TPU v7x, 32 devices: a whole 2x2x4 slice. The times are simulated.
32 devices in a mesh: space: 8 (over y, x, core), inst: 4 (over z).
Axes of the slice: x: 2, y: 2, z: 4, core: 2. Of those that a mesh axis runs over, the one named last changes fastest.
Arguments:
- state: float32 [4, 4, 16, 2048], P('inst', None, None, 'space'), may hold values from -1.3 to 5, as said below
- face_cell: int32 [6144], P('space'), may hold values from 0 to 4095
- face_node: int32 [6144], P('space'), may hold values from 0 to 4095
- face_area: float32 [3, 6144], P(None, 'space'), may hold values from -6 to 6
Outputs:
- increment: float32 [4, 4, 16, 2048], P('inst', None, None, 'space')
- blade_forces: float32 [4, 3, 4096], P('inst', None, 'space')
Inputs may be any that keep to these rules, and one draw needn't show every extreme that they name: state: density within 0.7 to 1.4, each velocity component within -0.9 to 0.9, pressure within 0.5 to 1.5. `face_node`: a shell node index.
All inputs are finite; a program needn't handle non-finite values.
Results may differ from a plain program's by a relative error of at most 0.0002.
Values sent between devices are 32-bit elements; how exact they have to be, the bound alone decides.
No kernel may reach another device: no remote copies, remote signals or barrier semaphores. Data moves between devices by JAX's collectives and lax.ppermute only.
A program may use at most 128 MiB of HBM per device.

v0:
```python
import math

import jax
import jax.numpy as jnp
import numpy as np
from jax import lax
from jax.sharding import PartitionSpec as P

NODE_DEV = 512


gamma_ratio = 1.4
omega_rate = 0.5
cfl_number = 0.8


def with_halo(value, sides, width):
    for axis, dim in sides:
        devices, length = (lax.axis_size(axis), value.shape[dim])
        up = [(i, (i + 1) % devices) for i in range(devices)]
        down = [(j, i) for i, j in up]
        last = lax.slice_in_dim(value, length - width, length, axis=dim)
        initial = lax.slice_in_dim(value, 0, width, axis=dim)
        before = lax.ppermute(last, axis, up)
        after = lax.ppermute(initial, axis, down)
        value = jnp.concatenate([before, value, after], axis=dim)
    return value


def spectral_table(count):
    values = np.zeros((count, count), np.float32)
    for row_index in range(count):
        for col_index in range(count):
            offset = row_index - col_index
            values[row_index, col_index] = (-1.0) ** offset / count
            if offset != 0:
                values[row_index, col_index] += (
                    0.5 * (-1.0) ** offset / math.tan(math.pi * offset / count)
                )
    return values


def primitives(extended):
    density = extended[..., 0, :, :]
    radial_velocity = extended[..., 1, :, :] / density
    around_velocity = extended[..., 2, :, :] / density
    pressure = (gamma_ratio - 1.0) * (
        extended[..., 3, :, :]
        - 0.5 * density * (radial_velocity * radial_velocity + around_velocity * around_velocity)
    )
    sound_speed = jnp.sqrt(gamma_ratio * pressure / density)
    return (radial_velocity, around_velocity, pressure, sound_speed)


def around_faces(cells, around_velocity, pressure, sound_speed):
    face_flux = jnp.stack(
        [
            cells[..., 2, :, :],
            cells[..., 1, :, :] * around_velocity,
            cells[..., 2, :, :] * around_velocity + pressure,
            (cells[..., 3, :, :] + pressure) * around_velocity,
        ],
        axis=-3,
    )
    speed = jnp.abs(around_velocity) + sound_speed
    dissipation = jnp.expand_dims(jnp.maximum(speed[..., :-1], speed[..., 1:]), -3)
    return 0.5 * (face_flux[..., :-1] + face_flux[..., 1:]) - 0.5 * dissipation * (
        cells[..., 1:] - cells[..., :-1]
    )


def radial_faces(cells, radial_velocity, pressure, sound_speed):
    face_flux = jnp.stack(
        [
            cells[..., 1, :, :],
            cells[..., 1, :, :] * radial_velocity + pressure,
            cells[..., 2, :, :] * radial_velocity,
            (cells[..., 3, :, :] + pressure) * radial_velocity,
        ],
        axis=-3,
    )
    speed = jnp.abs(radial_velocity) + sound_speed
    dissipation = jnp.expand_dims(jnp.maximum(speed[..., :-1, :], speed[..., 1:, :]), -3)
    interior = 0.5 * (face_flux[..., :-1, :] + face_flux[..., 1:, :]) - 0.5 * dissipation * (
        cells[..., 1:, :] - cells[..., :-1, :]
    )
    lower_wall = pressure[..., :1, :]
    upper_wall = pressure[..., -1:, :]
    nothing = jnp.zeros_like(lower_wall)
    lower = jnp.stack([nothing, lower_wall, nothing, nothing], axis=-3)
    upper = jnp.stack([nothing, upper_wall, nothing, nothing], axis=-3)
    return jnp.concatenate([lower, interior, upper], axis=-2)


def spatial_residual(extended):
    radial_velocity, around_velocity, pressure, sound_speed = primitives(extended)
    beside_all = around_faces(extended, around_velocity, pressure, sound_speed)
    div_around = beside_all[..., 1:] - beside_all[..., :-1]
    cells = extended[..., 1:-1]
    radial_velocity = radial_velocity[..., 1:-1]
    around_velocity = around_velocity[..., 1:-1]
    pressure = pressure[..., 1:-1]
    sound_speed = sound_speed[..., 1:-1]
    radial = radial_faces(cells, radial_velocity, pressure, sound_speed)
    div_radial = radial[..., 1:, :] - radial[..., :-1, :]
    return (div_around + div_radial, radial_velocity, around_velocity, pressure, sound_speed)


def per_device(state, face_cell, face_node, face_area):
    instances = lax.axis_size("inst")
    instance = lax.axis_index("inst")
    spectral = jnp.asarray(spectral_table(instances), jnp.float32)
    spectral_row = spectral[instance]
    time_term = (
        omega_rate
        * jnp.einsum(
            "m,mcrx->crx",
            spectral_row,
            lax.all_gather(state, "inst", axis=0, tiled=True),
            precision=lax.Precision.HIGHEST,
        )[None]
    )
    padded = with_halo(state[0], (("space", 2),), 1)
    divergence, radial_velocity, around_velocity, pressure, sound_speed = spatial_residual(
        padded[None]
    )
    residual = divergence + time_term
    step = cfl_number / (
        jnp.abs(radial_velocity)
        + jnp.abs(around_velocity)
        + 2.0 * sound_speed
        + omega_rate * instances / 2.0
    )
    increment = -step[:, None] * residual
    face_pressure = pressure[0].reshape(-1)[face_cell]
    contribution = face_pressure[None, :] * face_area
    node_total = NODE_DEV * lax.axis_size("space")
    dense_forces = jnp.zeros((3, node_total), jnp.float32).at[:, face_node].add(contribution)
    blade_forces = lax.psum_scatter(dense_forces[None], "space", scatter_dimension=2, tiled=True)
    return (increment, blade_forces)


def solution(mesh):
    in_specs = (P("inst", None, None, "space"), P("space"), P("space"), P(None, "space"))
    out_specs = (P("inst", None, None, "space"), P("inst", None, "space"))
    return jax.shard_map(
        per_device, mesh=mesh, in_specs=in_specs, out_specs=out_specs, check_vma=False
    )
```

profile of v0, /device:TPU:0, one launch (start us, length us, event | category | flops | bytes accessed | tf_op | source)
XLA Modules:
  0.0 93.0 jit_solution(13897368097923561530)
XLA Ops:
  7.2 0.0 reduce-scatter.2.cloned.1.call-start
  7.2 0.9 fusion.37
  8.1 0.5 collective-permute-start
  8.5 2.9 %collective-permute-start.1 = (f32[4,16,1]{2,1,0:T(8,128)S(1)}, f32[4,16,1]{2,1,0:T(8,128)S(1)}, u32[]{:S(2)}, u32[]{:S(2)}) collective-permute-start(f32[4,16,1]{2,1,0:T(8,128)S(1)} %get-tuple-element.22), channel_id=1, source_target_pairs={{4,0},{8,4},{12,8},{16,12},{20,16},{24,20},{28,24},{0,28},{5,1},{9... | collective-permute-start | bytes 776 | tf_op jit(solution)/shard_map/ppermute | solution.py:25
  11.5 15.0 %all_gather.3 = f32[4,4,16,256]{3,2,1,0:T(8,128)S(1)} all-gather(f32[1,4,16,256]{3,2,1,0:T(8,128)} %param.5), channel_id=1, replica_groups=mesh['space'=8,'inst'=4] {'inst'}, dimensions={0}, use_global_device_ids=true | all-gather | bytes 327680 | tf_op jit(solution)/shard_map/all_gather | solution.py:119
  26.4 0.7 compare_select_fusion
  27.1 0.7 compare_select_fusion.1
  27.8 1.4 %fusion.2 = f32[1,4,16,256]{3,0,2,1:T(1,128)S(1)} fusion(f32[4,4,16,256]{3,2,1,0:T(8,128)S(1)} %all_gather.3, f32[4,4]{1,0:T(4,128)} %constant.5.clone, s32[]{:T(128)S(6)} %select_n.9), kind=kOutput, calls=%fused_computation.4 | convolution fusion | flops 786432 | bytes 328196 | tf_op jit(solution)/shard_map/m,mcrx->crx/dot_general | solution.py:116
  29.2 0.1 pad.9.clone
  29.3 0.0 collective-permute-done
  29.3 0.0 collective-permute-done.1
  29.3 0.9 %maximum_bitcast_fusion = f32[1,4,16,258]{3,2,1,0:T(8,128)S(1)} fusion(f32[4,16,1]{2,1,0:T(8,128)S(1)} %collective-permute-done.1, f32[4,16,256]{2,1,0:T(8,128)} %bitcast.86, f32[4,16,1]{2,1,0:T(8,128)S(1)} %collective-permute-done), kind=kLoop, calls=%fused_computation.11 | loop fusion | flops 33024 | bytes 132096 | tf_op jit(solution)/shard_map/broadcast_in_dim | solution.py:125
  30.3 0.1 slice.152
  30.4 0.1 slice_bitcast_fusion.3
  30.5 0.1 maximum_maximum_fusion.1
  30.6 0.1 fusion.14
  30.7 0.1 fusion.31
  30.8 0.0 copy-start
  30.8 4.5 %gather_fusion = f32[768]{0:T(1024)S(1)} fusion(f32[4096]{0:T(1024)S(1)} %bitcast.83, s32[1024]{0:T(1024)S(1)} %pad_clamp_fusion), kind=kCustom, calls=%fused_computation | custom fusion | bytes 9216 | tf_op jit(solution)/shard_map/gather | solution.py:135
  35.3 0.0 copy-done
  35.3 0.2 copy.13
  35.5 7.5 %scatter_custom_fusion = f32[3,4096]{0,1:T(8,128)} fusion(s32[768]{0:T(1024)S(1)} %compare_select_fusion.1, f32[768,3]{1,0:T(8,128)S(1)} %copy.13, f32[]{:T(128)} %constant.18.clone.1), kind=kCustom, calls=%fused_computation.2 | custom fusion | flops 2304 | bytes 49156 | tf_op jit(solution)/shard_map/scatter-add | solution.py:138
  43.0 0.0 reduce-scatter.2.cloned.1.call-update
  43.0 0.1 fusion.8
  43.1 0.1 fusion.5
  43.2 0.7 fusion.12
  44.0 40.5 %reduce-scatter.2.cloned.1.call-done = f32[1,3,512]{1,2,0:T(8,128)} async-done(((f32[1,3,4096]{1,2,0:T(8,128)}), f32[1,3,512]{1,2,0:T(8,128)}) %reduce-scatter.2.cloned.1.call-update) | async-done | bytes 6160 | tf_op jit(solution)/shard_map/reduce_scatter | solution.py:139
  84.5 1.7 %copy.14 = f32[1,3,512]{2,0,1:T(1,128)} copy(f32[1,3,512]{1,2,0:T(8,128)} %reduce-scatter.2.cloned.1.call-done) | data formatting | bytes 12288
  (13 shorter events, 0.1 us)
Async XLA Ops:
  7.2 77.3 %reduce-scatter.2.cloned.1.call-start = ((), (), s32[]{:S(2)}) async-start(), calls=%async_computation.1 | async-start | bytes 2359296 | tf_op jit(solution)/shard_map/reduce_scatter | solution.py:139
  8.1 21.2 %collective-permute-start = (f32[4,16,1]{2,1,0:T(8,128)S(1)}, f32[4,16,1]{2,1,0:T(8,128)S(1)}, u32[]{:S(2)}, u32[]{:S(2)}) collective-permute-start(f32[4,16,1]{2,1,0:T(8,128)S(1)} %get-tuple-element.21), channel_id=1, source_target_pairs={{0,4},{4,8},{8,12},{12,16},{16,20},{20,24},{24,28},{28,0},{1,5},{5... | collective-permute-start | bytes 776 | tf_op jit(solution)/shard_map/ppermute | solution.py:24
  8.5 20.8 %collective-permute-start.1 = (f32[4,16,1]{2,1,0:T(8,128)S(1)}, f32[4,16,1]{2,1,0:T(8,128)S(1)}, u32[]{:S(2)}, u32[]{:S(2)}) collective-permute-start(f32[4,16,1]{2,1,0:T(8,128)S(1)} %get-tuple-element.22), channel_id=1, source_target_pairs={{4,0},{8,4},{12,8},{16,12},{20,16},{24,20},{28,24},{0,28},{5,1},{9... | collective-permute-start | bytes 776 | tf_op jit(solution)/shard_map/ppermute | solution.py:25
  30.8 4.5 %copy-start = (f32[3,768]{1,0:T(4,128)S(1)}, f32[3,768]{1,0:T(4,128)}, u32[]{:S(2)}) copy-start(f32[3,768]{1,0:T(4,128)} %param.8) | copy-start | bytes 27652
Sparse Core Ops, SparseCore 0:
  43.1 41.3 reduce-scatter.1
where the time goes:
time: 93.3 us; the launch traced here: 93 us
  waiting for transfers between devices  40.5 us (43%)
  blocking collectives  15 us (16%)
  between operations  14.2 us (15%)
  other arithmetic  11.1 us (12%)
  local copies, waits for them, and re-layouts  7.41 us (8%)
  starting transfers between devices  3.43 us (4%)
  matrix products  1.37 us (1%)
    reduce_scatter x1, waiting for transfers between devices, per_device(): lax.psum_scatter(dense_forces[None], 'space', scatter_dimension=2, tiled=...  40.5 us
    all_gather x1, blocking collectives, per_device(): lax.all_gather(state, 'inst', axis=0, tiled=True)  15 us
    scatter-add x1, other arithmetic, per_device(): jnp.zeros((3, node_total), jnp.float32).at[:, face_node].add(contribution)  7.46 us
    gather x1, local copies, waits for them, and re-layouts, per_device(): face_pressure = pressure[0].reshape(-1)[face_cell]  4.46 us
    ppermute x1, starting transfers between devices, with_halo(): after = lax.ppermute(initial, axis, down)  2.94 us
  transfers between devices with their start and end apart: 3, of which 1 were waited for; matrix products, arithmetic and copies ran while one was open for 4% of the time, Pallas kernels for 0%

commit v1 on v0

v1 whole, which is shorter than its diff:
```python
import functools
import math

import jax
import jax.numpy as jnp
import numpy as np
from jax import lax
from jax.experimental import pallas as pl
from jax.experimental.pallas import tpu as pltpu
from jax.sharding import PartitionSpec as P

gamma_ratio = 1.4
omega_rate = 0.5
cfl_number = 0.8

LANES = 128
ROWS = 16
DIRECT = 16


def spectral_row(count):
    row = np.zeros((count,), np.float32)
    for shift in range(count):
        row[shift] = (-1.0) ** shift / count
        if shift != 0:
            row[shift] += 0.5 * (-1.0) ** shift / math.tan(math.pi * shift / count)
    return [float(omega_rate * value) for value in row]


def pressure_of(q0, q1, q2, q3):
    inverse = 1.0 / q0
    vr = q1 * inverse
    vc = q2 * inverse
    p = (gamma_ratio - 1.0) * (q3 - 0.5 * q0 * (vr * vr + vc * vc))
    return inverse, vr, vc, p


def forces_kernel(blocks, relative, node_block, state, cell, node, area, *outs):
    radial, around = state.shape[2:]
    faces = cell.shape[0] * LANES
    chunks = faces // LANES
    _, _, _, p = pressure_of(state[0, 0], state[0, 1], state[0, 2], state[0, 3])
    sublane = lax.broadcasted_iota(jnp.int32, (8, LANES), 0)
    picked = []
    for c in range(chunks):
        index = jnp.broadcast_to(cell[c : c + 1, :], (8, LANES))
        row = index // around
        column = index % around
        lane = column % LANES
        half = column // LANES
        total = jnp.zeros((8, LANES), jnp.float32)
        for r in range(radial // 8):
            for h in range(around // LANES):
                part = p[r * 8 : (r + 1) * 8, h * LANES : (h + 1) * LANES]
                value = jnp.take_along_axis(part, lane, axis=1, mode="promise_in_bounds")
                total += jnp.where((row == sublane + r * 8) & (half == h), value, 0.0)
        picked.append(jnp.sum(total, axis=0, keepdims=True))
    face_pressure = jnp.concatenate(picked, axis=1)
    contribution = face_pressure * area[...]
    nodes = jnp.concatenate([node[c : c + 1, :] for c in range(chunks)], axis=1)

    high = node_block // LANES
    owner = nodes // node_block
    if relative:
        owner = (owner - lax.axis_index("space") + blocks) % blocks
    place = owner * high + (nodes % node_block) // LANES
    low = nodes % LANES
    pick_low = (
        lax.broadcasted_iota(jnp.int32, (LANES, faces), 0) == jnp.broadcast_to(low, (LANES, faces))
    ).astype(jnp.float32).astype(jnp.bfloat16)
    pattern = jnp.concatenate(
        [jnp.broadcast_to(contribution[k : k + 1], (high, faces)) for k in range(3)]
        + [jnp.zeros((ROWS - 3 * high, faces), jnp.float32)],
        axis=0,
    )
    first = pattern.astype(jnp.bfloat16).astype(jnp.float32)
    second = pattern - first
    place = jnp.broadcast_to(place, (ROWS, faces))
    row_high = lax.broadcasted_iota(jnp.int32, (ROWS, faces), 0) % high

    def dense(start, count):
        masks = [place == row_high + (start + b) * high for b in range(count)]
        result = None
        for part in (first, second):
            left = jnp.concatenate([jnp.where(m, part, 0.0) for m in masks], axis=0)
            product = lax.dot_general(
                left.astype(jnp.bfloat16),
                pick_low,
                (((1,), (1,)), ((), ())),
                preferred_element_type=jnp.float32,
            )
            result = product if result is None else result + product
        return result

    if relative:
        result = dense(0, blocks)
        for b in range(blocks):
            block = result[b * ROWS : (b + 1) * ROWS]
            outs[b][0:ROWS, :] = block
        edge = state[0].reshape(4 * radial, around)
        outs[1][ROWS:, :] = edge[:, around - LANES :]
        outs[blocks - 1][ROWS:, :] = edge[:, :LANES]
    else:
        group = 8

        @pl.loop(0, blocks // group)
        def _(g):
            result = dense(g * group, group)
            outs[0][pl.ds(g * group, group)] = result.reshape(group, ROWS, LANES)


def update_kernel(weights, instances, relative, state, before, after, *refs):
    others = refs[: instances - 1]
    forces = refs[instances - 1 : -2]
    increment, blade = refs[-2:]
    radial, around = state.shape[2:]
    base = ROWS if relative else 0
    lane = lax.broadcasted_iota(jnp.int32, (radial, LANES), 1)
    q = []
    for c in range(4):
        rows = pl.ds(base + c * radial, radial)
        edge = jnp.where(lane == LANES - 1, before[rows, :], after[rows, :])
        q.append(jnp.concatenate([state[0, c], edge], axis=1))
    inverse, vr, vc, p = pressure_of(*q)
    a = jnp.sqrt(gamma_ratio * p * inverse)
    width = around + LANES
    step = cfl_number / (
        jnp.abs(vr) + jnp.abs(vc) + 2.0 * a + omega_rate * instances / 2.0
    )

    def next_lane(x):
        return pltpu.roll(x, width - 1, 1)

    def last_lane(x):
        return pltpu.roll(x, 1, 1)

    speed = jnp.abs(vc) + a
    reach = 0.5 * jnp.maximum(speed, next_lane(speed))
    flux = (q[2], q[1] * vc, q[2] * vc + p, (q[3] + p) * vc)
    divergence = []
    for c in range(4):
        face = 0.5 * (flux[c] + next_lane(flux[c])) - reach * (next_lane(q[c]) - q[c])
        divergence.append((face - last_lane(face))[:, :around])

    own = slice(0, around)
    q = [x[:, own] for x in q]
    vr, p, a, step = vr[:, own], p[:, own], a[:, own], step[:, own]

    def above(x):
        return pltpu.roll(x, radial - 1, 0)

    def below(x):
        return pltpu.roll(x, 1, 0)

    row = lax.broadcasted_iota(jnp.int32, (radial, around), 0)
    hub, tip = row == 0, row == radial - 1
    speed = jnp.abs(vr) + a
    reach = 0.5 * jnp.maximum(speed, above(speed))
    flux = (q[1], q[1] * vr + p, q[2] * vr, (q[3] + p) * vr)
    for c in range(4):
        wall = p if c == 1 else 0.0
        face = 0.5 * (flux[c] + above(flux[c])) - reach * (above(q[c]) - q[c])
        upper = jnp.where(tip, wall, face)
        lower = jnp.where(hub, wall, below(face))
        residual = divergence[c] + (upper - lower) + weights[0] * q[c]
        for shift, other in enumerate(others, 1):
            residual += weights[shift] * other[0, c]
        increment[0, c] = -step * residual

    total = None
    for ref in forces:
        if relative:
            part = ref[0:ROWS, :]
        else:
            part = jnp.sum(ref[...], axis=0)
        total = part if total is None else total + part
    high = blade.shape[2] // LANES
    for k in range(3):
        for h in range(high):
            blade[k, :, pl.ds(h * LANES, LANES)] = total[k * high + h : k * high + h + 1, :]


def per_device(node_block, state, face_cell, face_node, face_area):
    blocks = lax.axis_size("space")
    instances = lax.axis_size("inst")
    radial, around = state.shape[2:]
    relative = 3 <= blocks <= DIRECT
    chunks = face_cell.shape[0] // LANES
    vmem = pl.BlockSpec(memory_space=pltpu.VMEM)
    params = pltpu.CompilerParams(vmem_limit_bytes=(4 if relative else 32) * 2**20)

    others = [
        lax.ppermute(state, "inst", [(i, (i + s) % instances) for i in range(instances)])
        for s in range(1, instances)
    ]

    rows = 4 * radial
    if relative:
        shapes = [
            jax.ShapeDtypeStruct((ROWS + (rows if b in (1, blocks - 1) else 0), LANES), jnp.float32)
            for b in range(blocks)
        ]
    else:
        shapes = [jax.ShapeDtypeStruct((blocks, ROWS, LANES), jnp.float32)]
    parts = pl.pallas_call(
        functools.partial(forces_kernel, blocks, relative, node_block),
        out_shape=shapes,
        in_specs=[vmem] * 4,
        out_specs=[vmem] * len(shapes),
        compiler_params=params,
        name="face_forces",
    )(
        state,
        face_cell.reshape(chunks, LANES),
        face_node.reshape(chunks, LANES),
        face_area,
    )

    def shifted(value, s):
        return lax.ppermute(value, "space", [(i, (i + s) % blocks) for i in range(blocks)])

    if relative:
        forces = [parts[0]] + [shifted(parts[s], s) for s in range(1, blocks)]
        before, after = forces[1], forces[blocks - 1]
    else:
        forces = [lax.all_to_all(parts[0], "space", 0, 0, tiled=True)]
        flat = state.reshape(rows, around)
        before = shifted(flat[:, around - LANES :], 1)
        after = shifted(flat[:, :LANES], blocks - 1)

    increment, blade = pl.pallas_call(
        functools.partial(update_kernel, spectral_row(instances), instances, relative),
        out_shape=[
            jax.ShapeDtypeStruct(state.shape, jnp.float32),
            jax.ShapeDtypeStruct((3, 1, node_block), jnp.float32),
        ],
        in_specs=[vmem] * (3 + len(others) + len(forces)),
        out_specs=[vmem] * 2,
        compiler_params=params,
        name="update",
    )(state, before, after, *others, *forces)
    return increment, jnp.transpose(blade, (1, 0, 2))


def solution(mesh):
    in_specs = (P("inst", None, None, "space"), P("space"), P("space"), P(None, "space"))
    out_specs = (P("inst", None, None, "space"), P("inst", None, "space"))
    return jax.shard_map(
        functools.partial(per_device, 512),
        mesh=mesh,
        in_specs=in_specs,
        out_specs=out_specs,
        check_vma=False,
    )
```

time: 93.3 us -> 26.2 us (0.28)
  the two profiles are of different devices: /device:TPU:0 before, /device:TPU:1 now
where the time goes in v1:
time: 26.2 us; the launch traced here: 25.9 us
  starting transfers between devices  16.2 us (62%)
  waiting for transfers between devices  4.83 us (18%)
  local copies, waits for them, and re-layouts  2.91 us (11%)
  Pallas kernels  1.23 us (5%)
  between operations  0.66 us (3%)
    ppermute x7, starting transfers between devices, shifted(): lax.ppermute(value, 'space', [(i, (i + s) % blocks) for i in range(blocks)])  10.6 us
    ppermute x3, starting transfers between devices, per_device(): lax.ppermute(state, 'inst', [(i, (i + s) % instances) for i in range(inst...  5.57 us
    ppermute x7, waiting for transfers between devices, shifted(): lax.ppermute(value, 'space', [(i, (i + s) % blocks) for i in range(blocks)])  4.82 us
    unnamed x8, local copies, waits for them, and re-layouts  2.91 us
    pallas_call x1, Pallas kernels, per_device(): pl.pallas_call(functools.partial(update_kernel, spectral_row(instances),...  0.86 us
  transfers between devices with their start and end apart: 10, of which 4 were waited for; matrix products, arithmetic and copies ran while one was open for 0% of the time, Pallas kernels for 0%

profile of v1, /device:TPU:1, one launch (start us, length us, event | category | flops | bytes accessed | tf_op | source)
XLA Modules:
  0.0 25.9 jit_solution(2365587494365612422)
XLA Ops:
  0.6 0.0 copy-start
  0.6 0.8 %copy-done = f32[1,4,16,256]{3,2,1,0:T(8,128)S(1)} copy-done((f32[1,4,16,256]{3,2,1,0:T(8,128)S(1)}, f32[1,4,16,256]{3,2,1,0:T(8,128)}, u32[]{:S(2)}) %copy-start) | copy-done | bytes 65560
  1.5 0.0 copy-start.1
  1.5 0.7 %copy-done.1 = f32[3,768]{1,0:T(4,128)S(1)} copy-done((f32[3,768]{1,0:T(4,128)S(1)}, f32[3,768]{1,0:T(4,128)}, u32[]{:S(2)}) %copy-start.1) | copy-done | bytes 9240
  2.2 0.0 copy-start.2
  2.2 0.7 %copy-done.2 = s32[768]{0:T(1024)S(1)} copy-done((s32[768]{0:T(1024)S(1)}, s32[768]{0:T(1024)}, u32[]{:S(2)}) %copy-start.2) | copy-done | bytes 3096
  2.9 0.0 copy-start.3
  2.9 0.7 %copy-done.3 = s32[768]{0:T(1024)S(1)} copy-done((s32[768]{0:T(1024)S(1)}, s32[768]{0:T(1024)}, u32[]{:S(2)}) %copy-start.3) | copy-done | bytes 3096
  3.6 0.4 %face_forces.1 = (f32[16,128]{1,0:T(8,128)S(1)}, f32[80,128]{1,0:T(8,128)S(1)}, f32[16,128]{1,0:T(8,128)S(1)}, f32[16,128]{1,0:T(8,128)S(1)}, f32[16,128]{1,0:T(...) custom-call(f32[1,4,16,256]{3,2,1,0:T(8,128)S(1)} %copy-done, ...), custom_call_target="tpu_custom_call" | custom-call | tf_op jit(solution)/shard_map/face_forces/pallas_call | solution.py:205
  3.9 2.1 %collective-permute-start.5 = (f32[16,128]{1,0:T(8,128)S(1)}, f32[16,128]{1,0:T(8,128)S(1)}, u32[]{:S(2)}, u32[]{:S(2)}) collective-permute-start(f32[16,128]{1,0:T(8,128)S(1)} %get-tuple-element.15), channel_id=1, source_target_pairs={{0,8},{4,12},{8,16},{12,20},{16,24},{20,28},{24,0},{28,4},{1,9},{5... | collective-permute-start | bytes 24584 | tf_op jit(solution)/shard_map/ppermute | solution.py:220
  6.0 2.3 %collective-permute-start.3 = (f32[1,4,16,256]{3,2,1,0:T(8,128)S(1)}, f32[1,4,16,256]{3,2,1,0:T(8,128)S(1)}, u32[]{:S(2)}, u32[]{:S(2)}) collective-permute-start(f32[1,4,16,256]{3,2,1,0:T(8,128)S(1)} %copy-done), channel_id=1, source_target_pairs={{0,2},{1,3},{2,0},{3,1},{4,6},{5,7},{6,4},{7,5},{8,10},{9,11},{10,... | collective-permute-start | bytes 196616 | tf_op jit(solution)/shard_map/ppermute | solution.py:193
  8.3 1.3 %collective-permute-start.2 = (f32[1,4,16,256]{3,2,1,0:T(8,128)S(1)}, f32[1,4,16,256]{3,2,1,0:T(8,128)S(1)}, u32[]{:S(2)}, u32[]{:S(2)}) collective-permute-start(f32[1,4,16,256]{3,2,1,0:T(8,128)S(1)} %copy-done), channel_id=1, source_target_pairs={{0,1},{1,2},{2,3},{3,0},{4,5},{5,6},{6,7},{7,4},{8,9},{9,10},{10,1... | collective-permute-start | bytes 196616 | tf_op jit(solution)/shard_map/ppermute | solution.py:193
  9.6 2.0 %collective-permute-start.4 = (f32[1,4,16,256]{3,2,1,0:T(8,128)S(1)}, f32[1,4,16,256]{3,2,1,0:T(8,128)S(1)}, u32[]{:S(2)}, u32[]{:S(2)}) collective-permute-start(f32[1,4,16,256]{3,2,1,0:T(8,128)S(1)} %copy-done), channel_id=1, source_target_pairs={{0,3},{1,0},{2,1},{3,2},{4,7},{5,4},{6,5},{7,6},{8,11},{9,8},{10,9... | collective-permute-start | bytes 196616 | tf_op jit(solution)/shard_map/ppermute | solution.py:193
  11.6 2.9 %collective-permute-start.6 = (f32[16,128]{1,0:T(8,128)S(1)}, f32[16,128]{1,0:T(8,128)S(1)}, u32[]{:S(2)}, u32[]{:S(2)}) collective-permute-start(f32[16,128]{1,0:T(8,128)S(1)} %get-tuple-element.16), channel_id=1, source_target_pairs={{0,12},{4,16},{8,20},{12,24},{16,28},{20,0},{24,4},{28,8},{1,13},{... | collective-permute-start | bytes 24584 | tf_op jit(solution)/shard_map/ppermute | solution.py:220
  14.5 0.0 collective-permute-done.5.refs_5_
  14.5 0.2 collective-permute-start.7
  14.7 1.0 %collective-permute-done.6.refs_6_ = f32[16,128]{1,0:T(8,128)S(1)} collective-permute-done((f32[16,128]{1,0:T(8,128)S(1)}, f32[16,128]{1,0:T(8,128)S(1)}, u32[]{:S(2)}, u32[]{:S(2)}) %collective-permute-start.6) | collective-permute-done | bytes 8224 | tf_op jit(solution)/shard_map/ppermute | solution.py:220
  15.8 1.7 %collective-permute-start.8 = (f32[16,128]{1,0:T(8,128)S(1)}, f32[16,128]{1,0:T(8,128)S(1)}, u32[]{:S(2)}, u32[]{:S(2)}) collective-permute-start(f32[16,128]{1,0:T(8,128)S(1)} %get-tuple-element.18), channel_id=1, source_target_pairs={{0,20},{4,24},{8,28},{12,0},{16,4},{20,8},{24,12},{28,16},{1,21},{... | collective-permute-start | bytes 24584 | tf_op jit(solution)/shard_map/ppermute | solution.py:220
  17.5 0.0 collective-permute-done.7.refs_7_
  17.5 1.3 %collective-permute-start.9 = (f32[16,128]{1,0:T(8,128)S(1)}, f32[16,128]{1,0:T(8,128)S(1)}, u32[]{:S(2)}, u32[]{:S(2)}) collective-permute-start(f32[16,128]{1,0:T(8,128)S(1)} %get-tuple-element.19), channel_id=1, source_target_pairs={{0,24},{4,28},{8,0},{12,4},{16,8},{20,12},{24,16},{28,20},{1,25},{... | collective-permute-start | bytes 24584 | tf_op jit(solution)/shard_map/ppermute | solution.py:220
  18.9 0.4 %collective-permute-done.8.refs_8_ = f32[16,128]{1,0:T(8,128)S(1)} collective-permute-done((f32[16,128]{1,0:T(8,128)S(1)}, f32[16,128]{1,0:T(8,128)S(1)}, u32[]{:S(2)}, u32[]{:S(2)}) %collective-permute-start.8) | collective-permute-done | bytes 8224 | tf_op jit(solution)/shard_map/ppermute | solution.py:220
  19.2 2.3 %collective-permute-start = (f32[80,128]{1,0:T(8,128)S(1)}, f32[80,128]{1,0:T(8,128)S(1)}, u32[]{:S(2)}, u32[]{:S(2)}) collective-permute-start(f32[80,128]{1,0:T(8,128)S(1)} %get-tuple-element.12), channel_id=1, source_target_pairs={{0,4},{4,8},{8,12},{12,16},{16,20},{20,24},{24,28},{28,0},{1,5},{5... | collective-permute-start | bytes 122888 | tf_op jit(solution)/shard_map/ppermute | solution.py:220
  21.5 0.0 collective-permute-done.9.refs_9_
  21.5 0.0 collective-permute-start.1
  21.5 1.1 %collective-permute-done.before.refs_4_ = f32[80,128]{1,0:T(8,128)S(1)} collective-permute-done((f32[80,128]{1,0:T(8,128)S(1)}, f32[80,128]{1,0:T(8,128)S(1)}, u32[]{:S(2)}, u32[]{:S(2)}) %collective-permute-start) | collective-permute-done | bytes 40992 | tf_op jit(solution)/shard_map/ppermute | solution.py:220
  22.6 2.3 %collective-permute-done.1.after.refs_10_ = f32[80,128]{1,0:T(8,128)S(1)} collective-permute-done((f32[80,128]{1,0:T(8,128)S(1)}, f32[80,128]{1,0:T(8,128)S(1)}, u32[]{:S(2)}, u32[]{:S(2)}) %collective-permute-start.1) | collective-permute-done | bytes 40992 | tf_op jit(solution)/shard_map/ppermute | solution.py:220
  25.0 0.0 collective-permute-done.3.refs_1_
  25.0 0.0 collective-permute-done.2.refs_0_
  25.0 0.0 collective-permute-done.4.refs_2_
  25.0 0.9 %update.1 = (f32[1,4,16,256]{3,2,1,0:T(8,128)}, f32[3,1,512]{2,1,0:T(1,128)}) custom-call(f32[1,4,16,256]{3,2,1,0:T(8,128)S(1)} %copy-done, f32[80,128]{1,0:T(8,128)S(1)} %collective-permute-done.before.refs_4_, f32[80,128]{1,0:T(8,128)S(1)} %collective-permute-done.1.after.refs_10_, f32[1,4,16,256]{3,2,1,0:T(8,128)S(1)} %collective-permute-done.2.refs_0_, ...), custom_call_target="tpu_custom_call" | custom-call | tf_op jit(solution)/shard_map/update/pallas_call | solution.py:231
Async XLA Ops:
  0.6 0.8 %copy-start = (f32[1,4,16,256]{3,2,1,0:T(8,128)S(1)}, f32[1,4,16,256]{3,2,1,0:T(8,128)}, u32[]{:S(2)}) copy-start(f32[1,4,16,256]{3,2,1,0:T(8,128)} %state.3) | copy-start | bytes 196612
  1.5 0.7 %copy-start.1 = (f32[3,768]{1,0:T(4,128)S(1)}, f32[3,768]{1,0:T(4,128)}, u32[]{:S(2)}) copy-start(f32[3,768]{1,0:T(4,128)} %area.1) | copy-start | bytes 27652
  2.2 0.7 %copy-start.2 = (s32[768]{0:T(1024)S(1)}, s32[768]{0:T(1024)}, u32[]{:S(2)}) copy-start(s32[768]{0:T(1024)} %param.5) | copy-start | bytes 9220
  2.9 0.7 %copy-start.3 = (s32[768]{0:T(1024)S(1)}, s32[768]{0:T(1024)}, u32[]{:S(2)}) copy-start(s32[768]{0:T(1024)} %param.6) | copy-start | bytes 9220
  3.9 10.6 %collective-permute-start.5 = (f32[16,128]{1,0:T(8,128)S(1)}, f32[16,128]{1,0:T(8,128)S(1)}, u32[]{:S(2)}, u32[]{:S(2)}) collective-permute-start(f32[16,128]{1,0:T(8,128)S(1)} %get-tuple-element.15), channel_id=1, source_target_pairs={{0,8},{4,12},{8,16},{12,20},{16,24},{20,28},{24,0},{28,4},{1,9},{5... | collective-permute-start | bytes 24584 | tf_op jit(solution)/shard_map/ppermute | solution.py:220
  6.0 19.0 %collective-permute-start.3 = (f32[1,4,16,256]{3,2,1,0:T(8,128)S(1)}, f32[1,4,16,256]{3,2,1,0:T(8,128)S(1)}, u32[]{:S(2)}, u32[]{:S(2)}) collective-permute-start(f32[1,4,16,256]{3,2,1,0:T(8,128)S(1)} %copy-done), channel_id=1, source_target_pairs={{0,2},{1,3},{2,0},{3,1},{4,6},{5,7},{6,4},{7,5},{8,10},{9,11},{10,... | collective-permute-start | bytes 196616 | tf_op jit(solution)/shard_map/ppermute | solution.py:193
  8.3 16.6 %collective-permute-start.2 = (f32[1,4,16,256]{3,2,1,0:T(8,128)S(1)}, f32[1,4,16,256]{3,2,1,0:T(8,128)S(1)}, u32[]{:S(2)}, u32[]{:S(2)}) collective-permute-start(f32[1,4,16,256]{3,2,1,0:T(8,128)S(1)} %copy-done), channel_id=1, source_target_pairs={{0,1},{1,2},{2,3},{3,0},{4,5},{5,6},{6,7},{7,4},{8,9},{9,10},{10,1... | collective-permute-start | bytes 196616 | tf_op jit(solution)/shard_map/ppermute | solution.py:193
  9.6 15.4 %collective-permute-start.4 = (f32[1,4,16,256]{3,2,1,0:T(8,128)S(1)}, f32[1,4,16,256]{3,2,1,0:T(8,128)S(1)}, u32[]{:S(2)}, u32[]{:S(2)}) collective-permute-start(f32[1,4,16,256]{3,2,1,0:T(8,128)S(1)} %copy-done), channel_id=1, source_target_pairs={{0,3},{1,0},{2,1},{3,2},{4,7},{5,4},{6,5},{7,6},{8,11},{9,8},{10,9... | collective-permute-start | bytes 196616 | tf_op jit(solution)/shard_map/ppermute | solution.py:193
  11.6 4.2 %collective-permute-start.6 = (f32[16,128]{1,0:T(8,128)S(1)}, f32[16,128]{1,0:T(8,128)S(1)}, u32[]{:S(2)}, u32[]{:S(2)}) collective-permute-start(f32[16,128]{1,0:T(8,128)S(1)} %get-tuple-element.16), channel_id=1, source_target_pairs={{0,12},{4,16},{8,20},{12,24},{16,28},{20,0},{24,4},{28,8},{1,13},{... | collective-permute-start | bytes 24584 | tf_op jit(solution)/shard_map/ppermute | solution.py:220
  14.5 3.0 %collective-permute-start.7 = (f32[16,128]{1,0:T(8,128)S(1)}, f32[16,128]{1,0:T(8,128)S(1)}, u32[]{:S(2)}, u32[]{:S(2)}) collective-permute-start(f32[16,128]{1,0:T(8,128)S(1)} %get-tuple-element.17), channel_id=1, source_target_pairs={{0,16},{4,20},{8,24},{12,28},{16,0},{20,4},{24,8},{28,12},{1,17},{... | collective-permute-start | bytes 24584 | tf_op jit(solution)/shard_map/ppermute | solution.py:220
  15.8 3.5 %collective-permute-start.8 = (f32[16,128]{1,0:T(8,128)S(1)}, f32[16,128]{1,0:T(8,128)S(1)}, u32[]{:S(2)}, u32[]{:S(2)}) collective-permute-start(f32[16,128]{1,0:T(8,128)S(1)} %get-tuple-element.18), channel_id=1, source_target_pairs={{0,20},{4,24},{8,28},{12,0},{16,4},{20,8},{24,12},{28,16},{1,21},{... | collective-permute-start | bytes 24584 | tf_op jit(solution)/shard_map/ppermute | solution.py:220
  17.5 4.0 %collective-permute-start.9 = (f32[16,128]{1,0:T(8,128)S(1)}, f32[16,128]{1,0:T(8,128)S(1)}, u32[]{:S(2)}, u32[]{:S(2)}) collective-permute-start(f32[16,128]{1,0:T(8,128)S(1)} %get-tuple-element.19), channel_id=1, source_target_pairs={{0,24},{4,28},{8,0},{12,4},{16,8},{20,12},{24,16},{28,20},{1,25},{... | collective-permute-start | bytes 24584 | tf_op jit(solution)/shard_map/ppermute | solution.py:220
  19.2 3.4 %collective-permute-start = (f32[80,128]{1,0:T(8,128)S(1)}, f32[80,128]{1,0:T(8,128)S(1)}, u32[]{:S(2)}, u32[]{:S(2)}) collective-permute-start(f32[80,128]{1,0:T(8,128)S(1)} %get-tuple-element.12), channel_id=1, source_target_pairs={{0,4},{4,8},{8,12},{12,16},{16,20},{20,24},{24,28},{28,0},{1,5},{5... | collective-permute-start | bytes 122888 | tf_op jit(solution)/shard_map/ppermute | solution.py:220
  21.5 3.4 %collective-permute-start.1 = (f32[80,128]{1,0:T(8,128)S(1)}, f32[80,128]{1,0:T(8,128)S(1)}, u32[]{:S(2)}, u32[]{:S(2)}) collective-permute-start(f32[80,128]{1,0:T(8,128)S(1)} %get-tuple-element.13), channel_id=1, source_target_pairs={{0,28},{4,0},{8,4},{12,8},{16,12},{20,16},{24,20},{28,24},{1,29},{... | collective-permute-start | bytes 122888 | tf_op jit(solution)/shard_map/ppermute | solution.py:220

commit v2 on v1

--- a/solution.py
+++ b/solution.py
@@ -15,7 +15,6 @@
 
 LANES = 128
 ROWS = 16
-DIRECT = 16
 
 
 def spectral_row(count):
@@ -35,7 +34,17 @@
     return inverse, vr, vc, p
 
 
-def forces_kernel(blocks, relative, node_block, state, cell, node, area, *outs):
+def forces_kernel(blocks, node_block, state_hbm, cell_hbm, node_hbm, area_hbm, out, state, cell, node, area, sems):
+    loads = [
+        pltpu.make_async_copy(source, target, sems.at[i])
+        for i, (source, target) in enumerate(
+            ((state_hbm, state), (cell_hbm, cell), (node_hbm, node), (area_hbm, area))
+        )
+    ]
+    for load in loads:
+        load.start()
+    for load in loads:
+        load.wait()
     radial, around = state.shape[2:]
     faces = cell.shape[0] * LANES
     chunks = faces // LANES
@@ -60,10 +69,7 @@
     nodes = jnp.concatenate([node[c : c + 1, :] for c in range(chunks)], axis=1)
 
     high = node_block // LANES
-    owner = nodes // node_block
-    if relative:
-        owner = (owner - lax.axis_index("space") + blocks) % blocks
-    place = owner * high + (nodes % node_block) // LANES
+    place = nodes // LANES
     low = nodes % LANES
     pick_low = (
         lax.broadcasted_iota(jnp.int32, (LANES, faces), 0) == jnp.broadcast_to(low, (LANES, faces))
@@ -90,36 +96,40 @@
                 preferred_element_type=jnp.float32,
             )
             result = product if result is None else result + product
-        return result
-
-    if relative:
-        result = dense(0, blocks)
-        for b in range(blocks):
-            block = result[b * ROWS : (b + 1) * ROWS]
-            outs[b][0:ROWS, :] = block
-        edge = state[0].reshape(4 * radial, around)
-        outs[1][ROWS:, :] = edge[:, around - LANES :]
-        outs[blocks - 1][ROWS:, :] = edge[:, :LANES]
+        return result.reshape(count, ROWS, LANES)
+
+    group = math.gcd(blocks, 8)
+    if group == blocks:
+        out[:, 0:ROWS, :] = dense(0, blocks)
     else:
-        group = 8
 
         @pl.loop(0, blocks // group)
         def _(g):
-            result = dense(g * group, group)
-            outs[0][pl.ds(g * group, group)] = result.reshape(group, ROWS, LANES)
-
-
-def update_kernel(weights, instances, relative, state, before, after, *refs):
+            out[pl.ds(g * group, group), 0:ROWS, :] = dense(g * group, group)
+
+    lane = lax.broadcasted_iota(jnp.int32, (radial, LANES), 1)
+    edge = jnp.zeros((radial, LANES), jnp.float32)
+    for c in range(4):
+        last = pltpu.roll(state[0, c, :, around - LANES :], (c + 1) % LANES, 1)
+        initial = pltpu.roll(state[0, c, :, :LANES], 4 + c, 1)
+        edge = jnp.where(lane == c, last, jnp.where(lane == 4 + c, initial, edge))
+    out[:, ROWS:, :] = jnp.broadcast_to(edge[None], (blocks, radial, LANES))
+
+
+def update_kernel(weights, blocks, instances, state, parts, *refs):
     others = refs[: instances - 1]
-    forces = refs[instances - 1 : -2]
     increment, blade = refs[-2:]
     radial, around = state.shape[2:]
-    base = ROWS if relative else 0
+    me = lax.axis_index("space")
+    before = parts[(me + blocks - 1) % blocks, ROWS:, :]
+    after = parts[(me + 1) % blocks, ROWS:, :]
     lane = lax.broadcasted_iota(jnp.int32, (radial, LANES), 1)
     q = []
     for c in range(4):
-        rows = pl.ds(base + c * radial, radial)
-        edge = jnp.where(lane == LANES - 1, before[rows, :], after[rows, :])
+        last = pltpu.roll(before, LANES - 1 - c, 1)
+        initial = pltpu.roll(after, LANES - 4 - c, 1)
+        edge = jnp.where(lane == LANES - 1, last, initial)
+        edge = jnp.where((lane == LANES - 1) | (lane == 0), edge, state[0, c, :, :LANES])
         q.append(jnp.concatenate([state[0, c], edge], axis=1))
     inverse, vr, vc, p = pressure_of(*q)
     a = jnp.sqrt(gamma_ratio * p * inverse)
@@ -167,13 +177,7 @@
             residual += weights[shift] * other[0, c]
         increment[0, c] = -step * residual
 
-    total = None
-    for ref in forces:
-        if relative:
-            part = ref[0:ROWS, :]
-        else:
-            part = jnp.sum(ref[...], axis=0)
-        total = part if total is None else total + part
+    total = jnp.sum(parts[:, 0:ROWS, :], axis=0)
     high = blade.shape[2] // LANES
     for k in range(3):
         for h in range(high):
@@ -184,61 +188,48 @@
     blocks = lax.axis_size("space")
     instances = lax.axis_size("inst")
     radial, around = state.shape[2:]
-    relative = 3 <= blocks <= DIRECT
     chunks = face_cell.shape[0] // LANES
     vmem = pl.BlockSpec(memory_space=pltpu.VMEM)
-    params = pltpu.CompilerParams(vmem_limit_bytes=(4 if relative else 32) * 2**20)
+    params = pltpu.CompilerParams(vmem_limit_bytes=(4 if blocks <= 16 else 16) * 2**20)
 
     others = [
         lax.ppermute(state, "inst", [(i, (i + s) % instances) for i in range(instances)])
         for s in range(1, instances)
     ]
 
-    rows = 4 * radial
-    if relative:
-        shapes = [
-            jax.ShapeDtypeStruct((ROWS + (rows if b in (1, blocks - 1) else 0), LANES), jnp.float32)
-            for b in range(blocks)
-        ]
-    else:
-        shapes = [jax.ShapeDtypeStruct((blocks, ROWS, LANES), jnp.float32)]
-    parts = pl.pallas_call(
-        functools.partial(forces_kernel, blocks, relative, node_block),
-        out_shape=shapes,
-        in_specs=[vmem] * 4,
-        out_specs=[vmem] * len(shapes),
-        compiler_params=params,
-        name="face_forces",
-    )(
+    faces = (
         state,
         face_cell.reshape(chunks, LANES),
         face_node.reshape(chunks, LANES),
         face_area,
     )
-
-    def shifted(value, s):
-        return lax.ppermute(value, "space", [(i, (i + s) % blocks) for i in range(blocks)])
-
-    if relative:
-        forces = [parts[0]] + [shifted(parts[s], s) for s in range(1, blocks)]
-        before, after = forces[1], forces[blocks - 1]
-    else:
-        forces = [lax.all_to_all(parts[0], "space", 0, 0, tiled=True)]
-        flat = state.reshape(rows, around)
-        before = shifted(flat[:, around - LANES :], 1)
-        after = shifted(flat[:, :LANES], blocks - 1)
+    parts, near_state = pl.pallas_call(
+        functools.partial(forces_kernel, blocks, node_block),
+        out_shape=[
+            jax.ShapeDtypeStruct((blocks, ROWS + radial, LANES), jnp.float32),
+            jax.ShapeDtypeStruct(state.shape, jnp.float32),
+        ],
+        in_specs=[pl.BlockSpec(memory_space=pltpu.HBM)] * 4,
+        out_specs=[vmem] * 2,
+        scratch_shapes=[pltpu.VMEM(x.shape, x.dtype) for x in faces[1:]]
+        + [pltpu.SemaphoreType.DMA((4,))],
+        compiler_params=params,
+        cost_estimate=pl.CostEstimate(flops=10**9, bytes_accessed=10**7, transcendentals=0),
+        name="face_forces",
+    )(*(pltpu.with_memory_space_constraint(x, pltpu.HBM) for x in faces))
+    parts = lax.all_to_all(parts, "space", 0, 0, tiled=True)
 
     increment, blade = pl.pallas_call(
-        functools.partial(update_kernel, spectral_row(instances), instances, relative),
+        functools.partial(update_kernel, spectral_row(instances), blocks, instances),
         out_shape=[
             jax.ShapeDtypeStruct(state.shape, jnp.float32),
             jax.ShapeDtypeStruct((3, 1, node_block), jnp.float32),
         ],
-        in_specs=[vmem] * (3 + len(others) + len(forces)),
+        in_specs=[vmem] * (2 + len(others)),
         out_specs=[vmem] * 2,
         compiler_params=params,
         name="update",
-    )(state, before, after, *others, *forces)
+    )(near_state, parts, *others)
     return increment, jnp.transpose(blade, (1, 0, 2))
 
 

time: 26.2 us -> 18.6 us (0.71)
  the two profiles are of different devices: /device:TPU:1 before, /device:TPU:0 now
where the time goes in v2:
time: 18.6 us; the launch traced here: 18.3 us
  starting transfers between devices  10.9 us (59%)
  waiting for transfers between devices  3.96 us (21%)
  Pallas kernels  2.8 us (15%)
  between operations  0.65 us (3%)
    ppermute x3, starting transfers between devices, per_device(): lax.ppermute(state, 'inst', [(i, (i + s) % instances) for i in range(inst...  5.57 us
    all_to_all x1, starting transfers between devices, per_device(): parts = lax.all_to_all(parts, 'space', 0, 0, tiled=True)  5.31 us
    ppermute x3, waiting for transfers between devices, per_device(): lax.ppermute(state, 'inst', [(i, (i + s) % instances) for i in range(inst...  3.96 us
    pallas_call x1, Pallas kernels, per_device(): pl.pallas_call(functools.partial(forces_kernel, blocks, node_block), out_...  1.88 us
    pallas_call x1, Pallas kernels, per_device(): pl.pallas_call(functools.partial(update_kernel, spectral_row(instances),...  0.92 us
  transfers between devices with their start and end apart: 4, of which 3 were waited for; matrix products, arithmetic and copies ran while one was open for 0% of the time, Pallas kernels for 0%

profile of v2, /device:TPU:0, one launch (start us, length us, event | category | flops | bytes accessed | tf_op | source)
XLA Modules:
  0.0 18.3 jit_solution(18434193656794800385)
XLA Ops:
  0.6 1.9 %face_forces.1 = (f32[8,32,128]{2,1,0:T(8,128)}, f32[1,4,16,256]{3,2,1,0:T(8,128)S(1)}) custom-call(f32[1,4,16,256]{3,2,1,0:T(8,128)} %state_hbm.1, s32[6,128]{1,0:T(8,128)} %bitcast.4, s32[6,128]{1,0:T(8,128)} %bitcast.5, f32[3,768]{1,0:T(4,128)} %area_hbm.1), custom_call_target="tpu_custom_call" | custom-call | flops 1000000000 | bytes 10000000 | tf_op jit(solution)/shard_map/face_forces/pallas_call | solution.py:206
  2.5 0.0 copy-start
  2.5 5.3 %all-to-all-start = ((f32[8,32,128]{2,1,0:T(8,128)}), f32[8,32,128]{2,1,0:T(8,128)S(1)}, u32[]{:S(2)}, u32[]{:S(2)}) async-start(f32[8,32,128]{2,1,0:T(8,128)} %get-tuple-element.7), calls=%async_computation | async-start | bytes 262144 | tf_op jit(solution)/shard_map/all_to_all | solution.py:220
  7.8 0.0 copy-done
  7.9 1.6 %collective-permute-start = (f32[1,4,16,256]{3,2,1,0:T(8,128)S(1)}, f32[1,4,16,256]{3,2,1,0:T(8,128)S(1)}, u32[]{:S(2)}, u32[]{:S(2)}) collective-permute-start(f32[1,4,16,256]{3,2,1,0:T(8,128)S(1)} %copy-done), channel_id=1, source_target_pairs={{0,1},{1,2},{2,3},{3,0},{4,5},{5,6},{6,7},{7,4},{8,9},{9,10},{10,1... | collective-permute-start | bytes 196616 | tf_op jit(solution)/shard_map/ppermute | solution.py:196
  9.5 2.6 %collective-permute-start.1 = (f32[1,4,16,256]{3,2,1,0:T(8,128)S(1)}, f32[1,4,16,256]{3,2,1,0:T(8,128)S(1)}, u32[]{:S(2)}, u32[]{:S(2)}) collective-permute-start(f32[1,4,16,256]{3,2,1,0:T(8,128)S(1)} %copy-done), channel_id=1, source_target_pairs={{0,2},{1,3},{2,0},{3,1},{4,6},{5,7},{6,4},{7,5},{8,10},{9,11},{10,... | collective-permute-start | bytes 196616 | tf_op jit(solution)/shard_map/ppermute | solution.py:196
  12.1 1.3 %collective-permute-start.2 = (f32[1,4,16,256]{3,2,1,0:T(8,128)S(1)}, f32[1,4,16,256]{3,2,1,0:T(8,128)S(1)}, u32[]{:S(2)}, u32[]{:S(2)}) collective-permute-start(f32[1,4,16,256]{3,2,1,0:T(8,128)S(1)} %copy-done), channel_id=1, source_target_pairs={{0,3},{1,0},{2,1},{3,2},{4,7},{5,4},{6,5},{7,6},{8,11},{9,8},{10,9... | collective-permute-start | bytes 196616 | tf_op jit(solution)/shard_map/ppermute | solution.py:196
  13.4 1.0 %collective-permute-done.refs_0_ = f32[1,4,16,256]{3,2,1,0:T(8,128)S(1)} collective-permute-done((f32[1,4,16,256]{3,2,1,0:T(8,128)S(1)}, f32[1,4,16,256]{3,2,1,0:T(8,128)S(1)}, u32[]{:S(2)}, u32[]{:S(2)}) %collective-permute-start) | collective-permute-done | bytes 65568 | tf_op jit(solution)/shard_map/ppermute | solution.py:196
  14.4 2.7 %collective-permute-done.1.refs_1_ = f32[1,4,16,256]{3,2,1,0:T(8,128)S(1)} collective-permute-done((f32[1,4,16,256]{3,2,1,0:T(8,128)S(1)}, f32[1,4,16,256]{3,2,1,0:T(8,128)S(1)}, u32[]{:S(2)}, u32[]{:S(2)}) %collective-permute-start.1) | collective-permute-done | bytes 65568 | tf_op jit(solution)/shard_map/ppermute | solution.py:196
  17.1 0.3 %collective-permute-done.2.refs_2_ = f32[1,4,16,256]{3,2,1,0:T(8,128)S(1)} collective-permute-done((f32[1,4,16,256]{3,2,1,0:T(8,128)S(1)}, f32[1,4,16,256]{3,2,1,0:T(8,128)S(1)}, u32[]{:S(2)}, u32[]{:S(2)}) %collective-permute-start.2) | collective-permute-done | bytes 65568 | tf_op jit(solution)/shard_map/ppermute | solution.py:196
  17.4 0.0 all-to-all-done.parts
  17.4 0.9 %update.1 = (f32[1,4,16,256]{3,2,1,0:T(8,128)}, f32[3,1,512]{2,1,0:T(1,128)}) custom-call(f32[1,4,16,256]{3,2,1,0:T(8,128)S(1)} %get-tuple-element.6.state, f32[8,32,128]{2,1,0:T(8,128)S(1)} %all-to-all-done.parts, f32[1,4,16,256]{3,2,1,0:T(8,128)S(1)} %collective-permute-done.refs_0_, f32[1,4,16,256]{3,2,1,0:T(8,128)S(1)} %collective-permute-done.1.refs_1_, ...), custom_call_target="tpu_custom_call" | custom-call | tf_op jit(solution)/shard_map/update/pallas_call | solution.py:222
Async XLA Ops:
  2.5 5.3 %copy-start = (f32[1,4,16,256]{3,2,1,0:T(8,128)S(1)}, f32[1,4,16,256]{3,2,1,0:T(8,128)}, u32[]{:S(2)}) copy-start(f32[1,4,16,256]{3,2,1,0:T(8,128)} %state_hbm.1) | copy-start | bytes 196612
  2.5 14.8 %all-to-all-start = ((f32[8,32,128]{2,1,0:T(8,128)}), f32[8,32,128]{2,1,0:T(8,128)S(1)}, u32[]{:S(2)}, u32[]{:S(2)}) async-start(f32[8,32,128]{2,1,0:T(8,128)} %get-tuple-element.7), calls=%async_computation | async-start | bytes 262144 | tf_op jit(solution)/shard_map/all_to_all | solution.py:220
  7.9 6.5 %collective-permute-start = (f32[1,4,16,256]{3,2,1,0:T(8,128)S(1)}, f32[1,4,16,256]{3,2,1,0:T(8,128)S(1)}, u32[]{:S(2)}, u32[]{:S(2)}) collective-permute-start(f32[1,4,16,256]{3,2,1,0:T(8,128)S(1)} %copy-done), channel_id=1, source_target_pairs={{0,1},{1,2},{2,3},{3,0},{4,5},{5,6},{6,7},{7,4},{8,9},{9,10},{10,1... | collective-permute-start | bytes 196616 | tf_op jit(solution)/shard_map/ppermute | solution.py:196
  9.5 7.6 %collective-permute-start.1 = (f32[1,4,16,256]{3,2,1,0:T(8,128)S(1)}, f32[1,4,16,256]{3,2,1,0:T(8,128)S(1)}, u32[]{:S(2)}, u32[]{:S(2)}) collective-permute-start(f32[1,4,16,256]{3,2,1,0:T(8,128)S(1)} %copy-done), channel_id=1, source_target_pairs={{0,2},{1,3},{2,0},{3,1},{4,6},{5,7},{6,4},{7,5},{8,10},{9,11},{10,... | collective-permute-start | bytes 196616 | tf_op jit(solution)/shard_map/ppermute | solution.py:196
  12.1 5.3 %collective-permute-start.2 = (f32[1,4,16,256]{3,2,1,0:T(8,128)S(1)}, f32[1,4,16,256]{3,2,1,0:T(8,128)S(1)}, u32[]{:S(2)}, u32[]{:S(2)}) collective-permute-start(f32[1,4,16,256]{3,2,1,0:T(8,128)S(1)} %copy-done), channel_id=1, source_target_pairs={{0,3},{1,0},{2,1},{3,2},{4,7},{5,4},{6,5},{7,6},{8,11},{9,8},{10,9... | collective-permute-start | bytes 196616 | tf_op jit(solution)/shard_map/ppermute | solution.py:196

commit v3 on v2

--- a/solution.py
+++ b/solution.py
@@ -98,38 +98,41 @@
             result = product if result is None else result + product
         return result.reshape(count, ROWS, LANES)
 
+    flat = state[0].reshape(4 * radial, around)
+    turned = jnp.concatenate([flat[:, around - LANES :], flat[:, :LANES]], axis=0).T
+    lane = lax.broadcasted_iota(jnp.int32, (1, LANES), 1)
+    edge = jnp.where(lane < LANES // 2, turned[LANES - 1 :, :], turned[:1, :])
+
     group = math.gcd(blocks, 8)
+    edge = jnp.broadcast_to(edge[None], (group, 1, LANES))
     if group == blocks:
-        out[:, 0:ROWS, :] = dense(0, blocks)
+        out[...] = dense(0, blocks)
+        out[:, 3 * high : 3 * high + 1, :] = edge
     else:
 
         @pl.loop(0, blocks // group)
         def _(g):
-            out[pl.ds(g * group, group), 0:ROWS, :] = dense(g * group, group)
-
-    lane = lax.broadcasted_iota(jnp.int32, (radial, LANES), 1)
-    edge = jnp.zeros((radial, LANES), jnp.float32)
-    for c in range(4):
-        last = pltpu.roll(state[0, c, :, around - LANES :], (c + 1) % LANES, 1)
-        initial = pltpu.roll(state[0, c, :, :LANES], 4 + c, 1)
-        edge = jnp.where(lane == c, last, jnp.where(lane == 4 + c, initial, edge))
-    out[:, ROWS:, :] = jnp.broadcast_to(edge[None], (blocks, radial, LANES))
+            out[pl.ds(g * group, group)] = dense(g * group, group)
+            out[pl.ds(g * group, group), 3 * high : 3 * high + 1, :] = edge
 
 
 def update_kernel(weights, blocks, instances, state, parts, *refs):
     others = refs[: instances - 1]
     increment, blade = refs[-2:]
     radial, around = state.shape[2:]
+    high = blade.shape[2] // LANES
     me = lax.axis_index("space")
-    before = parts[(me + blocks - 1) % blocks, ROWS:, :]
-    after = parts[(me + 1) % blocks, ROWS:, :]
+    before = parts[(me + blocks - 1) % blocks, 3 * high : 3 * high + 1, :]
+    after = parts[(me + 1) % blocks, 3 * high : 3 * high + 1, :]
+    lane = lax.broadcasted_iota(jnp.int32, (1, LANES), 1)
+    edge = jnp.where(lane < LANES // 2, before, after)
+    columns = jnp.broadcast_to(edge, (LANES, LANES)).T
     lane = lax.broadcasted_iota(jnp.int32, (radial, LANES), 1)
     q = []
     for c in range(4):
-        last = pltpu.roll(before, LANES - 1 - c, 1)
-        initial = pltpu.roll(after, LANES - 4 - c, 1)
+        last = columns[c * radial : (c + 1) * radial]
+        initial = columns[LANES // 2 + c * radial : LANES // 2 + (c + 1) * radial]
         edge = jnp.where(lane == LANES - 1, last, initial)
-        edge = jnp.where((lane == LANES - 1) | (lane == 0), edge, state[0, c, :, :LANES])
         q.append(jnp.concatenate([state[0, c], edge], axis=1))
     inverse, vr, vc, p = pressure_of(*q)
     a = jnp.sqrt(gamma_ratio * p * inverse)
@@ -177,8 +180,7 @@
             residual += weights[shift] * other[0, c]
         increment[0, c] = -step * residual
 
-    total = jnp.sum(parts[:, 0:ROWS, :], axis=0)
-    high = blade.shape[2] // LANES
+    total = jnp.sum(parts[...], axis=0)
     for k in range(3):
         for h in range(high):
             blade[k, :, pl.ds(h * LANES, LANES)] = total[k * high + h : k * high + h + 1, :]
@@ -206,7 +208,7 @@
     parts, near_state = pl.pallas_call(
         functools.partial(forces_kernel, blocks, node_block),
         out_shape=[
-            jax.ShapeDtypeStruct((blocks, ROWS + radial, LANES), jnp.float32),
+            jax.ShapeDtypeStruct((blocks, ROWS, LANES), jnp.float32),
             jax.ShapeDtypeStruct(state.shape, jnp.float32),
         ],
         in_specs=[pl.BlockSpec(memory_space=pltpu.HBM)] * 4,

time: 18.6 us -> 18.6 us (level)
  blocking collectives: 0 us -> 8.54 us
  waiting for transfers between devices: 3.96 us -> 0.01 us
  starting transfers between devices: 10.9 us -> 7.01 us
  Pallas kernels: 2.8 us -> 2.2 us
    all_to_all x0 -> x1, blocking collectives: none -> 8.54 us  [per_device(): parts = lax.all_to_all(parts, 'space', 0, 0, tiled=True)]
    all_to_all x1 -> x0, starting transfers between devices: 5.31 us -> none  [per_device(): parts = lax.all_to_all(parts, 'space', 0, 0, tiled=True)]
    ppermute x3, waiting for transfers between devices: 3.96 us -> 0.01 us  [per_device(): lax.ppermute(state, 'inst', [(i, (i + s) % instances) for i in range(inst...]
    ppermute x3, starting transfers between devices: 5.57 us -> 7.01 us  [per_device(): lax.ppermute(state, 'inst', [(i, (i + s) % instances) for i in range(inst...]
    pallas_call x1, Pallas kernels: 1.88 us -> 1.26 us  [per_device(): pl.pallas_call(functools.partial(forces_kernel, blocks, node_block), out_...]
  transfers between devices with their start and end apart: 4 -> 3, of which waited for: 3 -> 0; matrix products, arithmetic and copies ran while one was open for 0% -> 0% of each run, Pallas kernels for 0% -> 7%
where the time goes in v3:
time: 18.6 us; the launch traced here: 18.4 us
  blocking collectives  8.54 us (46%)
  starting transfers between devices  7.01 us (38%)
  Pallas kernels  2.2 us (12%)
  between operations  0.65 us (3%)
    all_to_all x1, blocking collectives, per_device(): parts = lax.all_to_all(parts, 'space', 0, 0, tiled=True)  8.54 us
    ppermute x3, starting transfers between devices, per_device(): lax.ppermute(state, 'inst', [(i, (i + s) % instances) for i in range(inst...  7.01 us
    pallas_call x1, Pallas kernels, per_device(): pl.pallas_call(functools.partial(forces_kernel, blocks, node_block), out_...  1.26 us
    pallas_call x1, Pallas kernels, per_device(): pl.pallas_call(functools.partial(update_kernel, spectral_row(instances),...  0.94 us
  transfers between devices with their start and end apart: 3, of which 0 were waited for; matrix products, arithmetic and copies ran while one was open for 0% of the time, Pallas kernels for 7%

profile of v3, /device:TPU:0, one launch (start us, length us, event | category | flops | bytes accessed | tf_op | source)
XLA Modules:
  0.0 18.4 jit_solution(12262443364758696789)
XLA Ops:
  0.6 3.1 %collective-permute-start = (f32[1,4,16,256]{3,2,1,0:T(8,128)}, f32[1,4,16,256]{3,2,1,0:T(8,128)S(1)}, u32[]{:S(2)}, u32[]{:S(2)}) collective-permute-start(f32[1,4,16,256]{3,2,1,0:T(8,128)} %state_hbm.1), channel_id=1, source_target_pairs={{0,1},{1,2},{2,3},{3,0},{4,5},{5,6},{6,7},{7,4},{8,9},{9,10},{10,1... | collective-permute-start | bytes 196616 | tf_op jit(solution)/shard_map/ppermute | solution.py:198
  3.7 2.6 %collective-permute-start.1 = (f32[1,4,16,256]{3,2,1,0:T(8,128)}, f32[1,4,16,256]{3,2,1,0:T(8,128)S(1)}, u32[]{:S(2)}, u32[]{:S(2)}) collective-permute-start(f32[1,4,16,256]{3,2,1,0:T(8,128)} %state_hbm.1), channel_id=1, source_target_pairs={{0,2},{1,3},{2,0},{3,1},{4,6},{5,7},{6,4},{7,5},{8,10},{9,11},{10,... | collective-permute-start | bytes 196616 | tf_op jit(solution)/shard_map/ppermute | solution.py:198
  6.3 1.3 %collective-permute-start.2 = (f32[1,4,16,256]{3,2,1,0:T(8,128)}, f32[1,4,16,256]{3,2,1,0:T(8,128)S(1)}, u32[]{:S(2)}, u32[]{:S(2)}) collective-permute-start(f32[1,4,16,256]{3,2,1,0:T(8,128)} %state_hbm.1), channel_id=1, source_target_pairs={{0,3},{1,0},{2,1},{3,2},{4,7},{5,4},{6,5},{7,6},{8,11},{9,8},{10,9... | collective-permute-start | bytes 196616 | tf_op jit(solution)/shard_map/ppermute | solution.py:198
  7.6 1.3 %face_forces.1 = (f32[8,16,128]{2,1,0:T(8,128)S(1)}, f32[1,4,16,256]{3,2,1,0:T(8,128)S(1)}) custom-call(f32[1,4,16,256]{3,2,1,0:T(8,128)} %state_hbm.1, s32[6,128]{1,0:T(8,128)} %bitcast.4, s32[6,128]{1,0:T(8,128)} %bitcast.5, f32[3,768]{1,0:T(4,128)} %area_hbm.1), custom_call_target="tpu_custom_call" | custom-call | flops 1000000000 | bytes 10000000 | tf_op jit(solution)/shard_map/face_forces/pallas_call | solution.py:208
  8.9 8.5 %all_to_all.5.parts = f32[8,16,128]{2,1,0:T(8,128)S(1)} all-to-all(f32[8,16,128]{2,1,0:T(8,128)S(1)} %get-tuple-element.7), channel_id=1, replica_groups=mesh['space'=8,'inst'=4] {'space'}, dimensions={0} | all-to-all | bytes 131072 | tf_op jit(solution)/shard_map/all_to_all | solution.py:222
  17.5 0.0 collective-permute-done.refs_0_
  17.5 0.0 collective-permute-done.1.refs_1_
  17.5 0.0 collective-permute-done.2.refs_2_
  17.5 0.9 %update.1 = (f32[1,4,16,256]{3,2,1,0:T(8,128)}, f32[3,1,512]{2,1,0:T(1,128)}) custom-call(f32[1,4,16,256]{3,2,1,0:T(8,128)S(1)} %get-tuple-element.6.state, f32[8,16,128]{2,1,0:T(8,128)S(1)} %all_to_all.5.parts, f32[1,4,16,256]{3,2,1,0:T(8,128)S(1)} %collective-permute-done.refs_0_, f32[1,4,16,256]{3,2,1,0:T(8,128)S(1)} %collective-permute-done.1.refs_1_, ...), custom_call_target="tpu_custom_call" | custom-call | tf_op jit(solution)/shard_map/update/pallas_call | solution.py:224
Async XLA Ops:
  0.6 16.8 %collective-permute-start = (f32[1,4,16,256]{3,2,1,0:T(8,128)}, f32[1,4,16,256]{3,2,1,0:T(8,128)S(1)}, u32[]{:S(2)}, u32[]{:S(2)}) collective-permute-start(f32[1,4,16,256]{3,2,1,0:T(8,128)} %state_hbm.1), channel_id=1, source_target_pairs={{0,1},{1,2},{2,3},{3,0},{4,5},{5,6},{6,7},{7,4},{8,9},{9,10},{10,1... | collective-permute-start | bytes 196616 | tf_op jit(solution)/shard_map/ppermute | solution.py:198
  3.7 13.8 %collective-permute-start.1 = (f32[1,4,16,256]{3,2,1,0:T(8,128)}, f32[1,4,16,256]{3,2,1,0:T(8,128)S(1)}, u32[]{:S(2)}, u32[]{:S(2)}) collective-permute-start(f32[1,4,16,256]{3,2,1,0:T(8,128)} %state_hbm.1), channel_id=1, source_target_pairs={{0,2},{1,3},{2,0},{3,1},{4,6},{5,7},{6,4},{7,5},{8,10},{9,11},{10,... | collective-permute-start | bytes 196616 | tf_op jit(solution)/shard_map/ppermute | solution.py:198
  6.3 11.2 %collective-permute-start.2 = (f32[1,4,16,256]{3,2,1,0:T(8,128)}, f32[1,4,16,256]{3,2,1,0:T(8,128)S(1)}, u32[]{:S(2)}, u32[]{:S(2)}) collective-permute-start(f32[1,4,16,256]{3,2,1,0:T(8,128)} %state_hbm.1), channel_id=1, source_target_pairs={{0,3},{1,0},{2,1},{3,2},{4,7},{5,4},{6,5},{7,6},{8,11},{9,8},{10,9... | collective-permute-start | bytes 196616 | tf_op jit(solution)/shard_map/ppermute | solution.py:198

commit v4 on v3

--- a/solution.py
+++ b/solution.py
@@ -15,6 +15,8 @@
 
 LANES = 128
 ROWS = 16
+EDGE = 12
+RIDING = 8
 
 
 def spectral_row(count):
@@ -34,7 +36,7 @@
     return inverse, vr, vc, p
 
 
-def forces_kernel(blocks, node_block, state_hbm, cell_hbm, node_hbm, area_hbm, out, state, cell, node, area, sems):
+def forces_kernel(blocks, node_block, state_hbm, cell_hbm, node_hbm, area_hbm, kept, sent, state, cell, node, area, sems):
     loads = [
         pltpu.make_async_copy(source, target, sems.at[i])
         for i, (source, target) in enumerate(
@@ -69,7 +71,7 @@
     nodes = jnp.concatenate([node[c : c + 1, :] for c in range(chunks)], axis=1)
 
     high = node_block // LANES
-    place = nodes // LANES
+    place = nodes // LANES ^ lax.axis_index("space") * high
     low = nodes % LANES
     pick_low = (
         lax.broadcasted_iota(jnp.int32, (LANES, faces), 0) == jnp.broadcast_to(low, (LANES, faces))
@@ -98,32 +100,77 @@
             result = product if result is None else result + product
         return result.reshape(count, ROWS, LANES)
 
+    group = min(blocks, 8)
+
+    def halves(g):
+        result = dense(g * group, group).reshape(group // 2, 2, ROWS, LANES)
+        return result[:, 0], result[:, 1]
+
+    if group == blocks:
+        kept[...], sent[...] = halves(0)
+    else:
+
+        @pl.loop(0, blocks // group)
+        def _(g):
+            span = pl.ds(g * (group // 2), group // 2)
+            kept[span], sent[span] = halves(g)
+
     flat = state[0].reshape(4 * radial, around)
     turned = jnp.concatenate([flat[:, around - LANES :], flat[:, :LANES]], axis=0).T
     lane = lax.broadcasted_iota(jnp.int32, (1, LANES), 1)
     edge = jnp.where(lane < LANES // 2, turned[LANES - 1 :, :], turned[:1, :])
-
-    group = math.gcd(blocks, 8)
-    edge = jnp.broadcast_to(edge[None], (group, 1, LANES))
-    if group == blocks:
-        out[...] = dense(0, blocks)
-        out[:, 3 * high : 3 * high + 1, :] = edge
-    else:
-
-        @pl.loop(0, blocks // group)
-        def _(g):
-            out[pl.ds(g * group, group)] = dense(g * group, group)
-            out[pl.ds(g * group, group), 3 * high : 3 * high + 1, :] = edge
-
-
-def update_kernel(weights, blocks, instances, state, parts, *refs):
-    others = refs[: instances - 1]
+    for out in (kept, sent):
+        out[0, EDGE : EDGE + 1, :] = edge
+
+
+def halving_kernel(edges, kept, came, kept_next, sent):
+    half = kept_next.shape[0]
+    for b in range(half):
+        kept_next[b] = kept[2 * b] + came[2 * b]
+        sent[b] = kept[2 * b + 1] + came[2 * b + 1]
+    if edges:
+        own, others = (gather_edges(ref, edges) for ref in (kept, came))
+        put_edges(kept_next, own + others)
+        put_edges(sent, own + others)
+
+
+def gather_edges(ref, count):
+    spare = ROWS - EDGE
+    return [ref[i // spare, EDGE + i % spare : EDGE + i % spare + 1, :] for i in range(count)]
+
+
+def put_edges(ref, rows):
+    spare = ROWS - EDGE
+    for i, row in enumerate(rows):
+        ref[i // spare, EDGE + i % spare : EDGE + i % spare + 1, :] = row
+
+
+def pair_kernel(weights, instances, state, partner, *outs):
+    odd = lax.axis_index("inst") % 2
+    for i, out in enumerate(outs):
+        shift = 2 * (i + 1)
+        weight = jnp.where(odd == 1, weights[(shift + 1) % instances], weights[shift - 1])
+        out[...] = weights[shift] * state[...] + weight * partner[...]
+
+
+def update_kernel(weights, blocks, instances, state, kept, came, partner, *refs):
+    sums = refs[: instances // 2 - 1]
     increment, blade = refs[-2:]
     radial, around = state.shape[2:]
     high = blade.shape[2] // LANES
-    me = lax.axis_index("space")
-    before = parts[(me + blocks - 1) % blocks, 3 * high : 3 * high + 1, :]
-    after = parts[(me + 1) % blocks, 3 * high : 3 * high + 1, :]
+    if blocks <= RIDING:
+        me = lax.axis_index("space")
+        known = [kept[0, EDGE:, :], came[0, EDGE:, :]]
+        known = jnp.concatenate(known, axis=0)
+        row = lax.broadcasted_iota(jnp.int32, known.shape, 0)
+
+        def edge_of(device):
+            return jnp.sum(jnp.where(row == device ^ me, known, 0.0), axis=0, keepdims=True)
+
+        before = edge_of((me + blocks - 1) % blocks)
+        after = edge_of((me + 1) % blocks)
+    else:
+        before, after = (ref[0:1, :] for ref in refs[instances // 2 - 1 : -2])
     lane = lax.broadcasted_iota(jnp.int32, (1, LANES), 1)
     edge = jnp.where(lane < LANES // 2, before, after)
     columns = jnp.broadcast_to(edge, (LANES, LANES)).T
@@ -170,17 +217,21 @@
     speed = jnp.abs(vr) + a
     reach = 0.5 * jnp.maximum(speed, above(speed))
     flux = (q[1], q[1] * vr + p, q[2] * vr, (q[3] + p) * vr)
+    partner_weight = jnp.where(
+        lax.axis_index("inst") % 2 == 1, weights[1], weights[instances - 1]
+    )
     for c in range(4):
         wall = p if c == 1 else 0.0
         face = 0.5 * (flux[c] + above(flux[c])) - reach * (above(q[c]) - q[c])
         upper = jnp.where(tip, wall, face)
         lower = jnp.where(hub, wall, below(face))
         residual = divergence[c] + (upper - lower) + weights[0] * q[c]
-        for shift, other in enumerate(others, 1):
-            residual += weights[shift] * other[0, c]
+        residual += partner_weight * partner[0, c]
+        for ref in sums:
+            residual += ref[0, c]
         increment[0, c] = -step * residual
 
-    total = jnp.sum(parts[...], axis=0)
+    total = kept[0] + came[0]
     for k in range(3):
         for h in range(high):
             blade[k, :, pl.ds(h * LANES, LANES)] = total[k * high + h : k * high + h + 1, :]
@@ -194,10 +245,25 @@
     vmem = pl.BlockSpec(memory_space=pltpu.VMEM)
     params = pltpu.CompilerParams(vmem_limit_bytes=(4 if blocks <= 16 else 16) * 2**20)
 
-    others = [
-        lax.ppermute(state, "inst", [(i, (i + s) % instances) for i in range(instances)])
-        for s in range(1, instances)
-    ]
+    def swapped(value, axis, bit):
+        return lax.ppermute(value, axis, [(i, i ^ bit) for i in range(lax.axis_size(axis))])
+
+    def shifted(value, axis, s):
+        count = lax.axis_size(axis)
+        return lax.ppermute(value, axis, [(i, (i + s) % count) for i in range(count)])
+
+    def call(kernel, name, shapes, *operands):
+        return pl.pallas_call(
+            kernel,
+            out_shape=[jax.ShapeDtypeStruct(shape, jnp.float32) for shape in shapes],
+            in_specs=[vmem] * len(operands),
+            out_specs=[vmem] * len(shapes),
+            compiler_params=params,
+            name=name,
+        )(*operands)
+
+    weights = spectral_row(instances)
+    partner = swapped(state, "inst", 1)
 
     faces = (
         state,
@@ -205,33 +271,59 @@
         face_node.reshape(chunks, LANES),
         face_area,
     )
-    parts, near_state = pl.pallas_call(
+    half = jax.ShapeDtypeStruct((blocks // 2, ROWS, LANES), jnp.float32)
+    kept, sent, near_state = pl.pallas_call(
         functools.partial(forces_kernel, blocks, node_block),
-        out_shape=[
-            jax.ShapeDtypeStruct((blocks, ROWS, LANES), jnp.float32),
-            jax.ShapeDtypeStruct(state.shape, jnp.float32),
-        ],
+        out_shape=[half, half, jax.ShapeDtypeStruct(state.shape, jnp.float32)],
         in_specs=[pl.BlockSpec(memory_space=pltpu.HBM)] * 4,
-        out_specs=[vmem] * 2,
+        out_specs=[vmem] * 3,
         scratch_shapes=[pltpu.VMEM(x.shape, x.dtype) for x in faces[1:]]
         + [pltpu.SemaphoreType.DMA((4,))],
         compiler_params=params,
         cost_estimate=pl.CostEstimate(flops=10**9, bytes_accessed=10**7, transcendentals=0),
         name="face_forces",
     )(*(pltpu.with_memory_space_constraint(x, pltpu.HBM) for x in faces))
-    parts = lax.all_to_all(parts, "space", 0, 0, tiled=True)
-
-    increment, blade = pl.pallas_call(
-        functools.partial(update_kernel, spectral_row(instances), blocks, instances),
-        out_shape=[
-            jax.ShapeDtypeStruct(state.shape, jnp.float32),
-            jax.ShapeDtypeStruct((3, 1, node_block), jnp.float32),
-        ],
-        in_specs=[vmem] * (2 + len(others)),
-        out_specs=[vmem] * 2,
-        compiler_params=params,
-        name="update",
-    )(near_state, parts, *others)
+
+    riding = blocks <= RIDING
+    edges = []
+    if not riding:
+        row = jnp.broadcast_to(kept[0, EDGE : EDGE + 1, :], (8, LANES))
+        edges = [shifted(row, "space", 1), shifted(row, "space", blocks - 1)]
+    came = swapped(sent, "space", 1)
+
+    sums = call(
+        functools.partial(pair_kernel, weights, instances),
+        "pair_sums",
+        [state.shape] * (instances // 2 - 1),
+        near_state,
+        partner,
+    )
+    sums = [shifted(value, "inst", 2 * (i + 1)) for i, value in enumerate(sums)]
+
+    bit = 2
+    while bit < blocks:
+        shape = (blocks // (2 * bit), ROWS, LANES)
+        kept, sent = call(
+            functools.partial(halving_kernel, bit // 2 if riding else 0),
+            "halving",
+            [shape] * 2,
+            kept,
+            came,
+        )
+        came = swapped(sent, "space", bit)
+        bit *= 2
+
+    increment, blade = call(
+        functools.partial(update_kernel, weights, blocks, instances),
+        "update",
+        [state.shape, (3, 1, node_block)],
+        near_state,
+        kept,
+        came,
+        partner,
+        *sums,
+        *edges,
+    )
     return increment, jnp.transpose(blade, (1, 0, 2))
 
 

time: 18.6 us -> 19 us (1.022)
  blocking collectives: 8.54 us -> 0 us
  waiting for transfers between devices: 0.01 us -> 6.76 us
  starting transfers between devices: 7.01 us -> 9.2 us
    all_to_all x1 -> x0, blocking collectives: 8.54 us -> none  [per_device(): parts = lax.all_to_all(parts, 'space', 0, 0, tiled=True)]
    ppermute x3 -> x5, waiting for transfers between devices: 0.01 us -> 6.76 us  [the longest x4 6.76 us: swapped(): lax.ppermute(value, axis, [(i, i ^ bit) for i in range(lax.axis_size(axis...]
    ppermute x3 -> x5, starting transfers between devices: 7.01 us -> 9.2 us  [the longest x4 6.1 us: swapped(): lax.ppermute(value, axis, [(i, i ^ bit) for i in range(lax.axis_size(axis...]
    pallas_call x1 -> x4, Pallas kernels: 0.94 us -> 0.96 us  [call(): pl.pallas_call(kernel, out_shape=[jax.ShapeDtypeStruct(shape, jnp.float32...]
  transfers between devices with their start and end apart: 3 -> 5, of which waited for: 0 -> 4; matrix products, arithmetic and copies ran while one was open for 0% -> 0% of each run, Pallas kernels for 7% -> 7%
where the time goes in v4:
time: 19 us; the launch traced here: 18.8 us
  starting transfers between devices  9.2 us (48%)
  waiting for transfers between devices  6.76 us (36%)
  Pallas kernels  2.23 us (12%)
  between operations  0.65 us (3%)
    ppermute x4, waiting for transfers between devices, swapped(): lax.ppermute(value, axis, [(i, i ^ bit) for i in range(lax.axis_size(axis...  6.76 us
    ppermute x4, starting transfers between devices, swapped(): lax.ppermute(value, axis, [(i, i ^ bit) for i in range(lax.axis_size(axis...  6.1 us
    ppermute x1, starting transfers between devices, shifted(): lax.ppermute(value, axis, [(i, (i + s) % count) for i in range(count)])  3.1 us
    pallas_call x1, Pallas kernels, per_device(): pl.pallas_call(functools.partial(forces_kernel, blocks, node_block), out_...  1.27 us
    pallas_call x4, Pallas kernels, call(): pl.pallas_call(kernel, out_shape=[jax.ShapeDtypeStruct(shape, jnp.float32...  0.96 us
  transfers between devices with their start and end apart: 5, of which 4 were waited for; matrix products, arithmetic and copies ran while one was open for 0% of the time, Pallas kernels for 7%

profile of v4, /device:TPU:0, one launch (start us, length us, event | category | flops | bytes accessed | tf_op | source)
XLA Modules:
  0.0 18.8 jit_solution(14167160380944571382)
XLA Ops:
  0.6 3.1 %collective-permute-start.3 = (f32[1,4,16,256]{3,2,1,0:T(8,128)}, f32[1,4,16,256]{3,2,1,0:T(8,128)S(1)}, u32[]{:S(2)}, u32[]{:S(2)}) collective-permute-start(f32[1,4,16,256]{3,2,1,0:T(8,128)} %state_hbm.1), channel_id=1, source_target_pairs={{0,1},{1,0},{2,3},{3,2},{4,5},{5,4},{6,7},{7,6},{8,9},{9,8},{10,11... | collective-permute-start | bytes 196616 | tf_op jit(solution)/shard_map/ppermute | solution.py:249
  3.7 1.3 %face_forces.1 = (f32[4,16,128]{2,1,0:T(8,128)S(1)}, f32[4,16,128]{2,1,0:T(8,128)S(1)}, f32[1,4,16,256]{3,2,1,0:T(8,128)S(1)}) custom-call(f32[1,4,16,256]{3,2,1,0:T(8,128)} %state_hbm.1, s32[6,128]{1,0:T(8,128)} %bitcast.4, s32[6,128]{1,0:T(8,128)} %bitcast.5, f32[3,768]{1,0:T(4,128)} %area_hbm.1), custom_call_target="tpu_custom_call" | custom-call | flops 1000000000 | bytes 10000000 | tf_op jit(solution)/shard_map/face_forces/pallas_call | solution.py:275
  5.0 1.2 %collective-permute-done.3.partner = f32[1,4,16,256]{3,2,1,0:T(8,128)S(1)} collective-permute-done((f32[1,4,16,256]{3,2,1,0:T(8,128)}, f32[1,4,16,256]{3,2,1,0:T(8,128)S(1)}, u32[]{:S(2)}, u32[]{:S(2)}) %collective-permute-start.3) | collective-permute-done | bytes 65568 | tf_op jit(solution)/shard_map/ppermute | solution.py:249
  6.2 3.1 %collective-permute-start.4 = (f32[1,4,16,256]{3,2,1,0:T(8,128)S(1)}, f32[1,4,16,256]{3,2,1,0:T(8,128)S(1)}, u32[]{:S(2)}, u32[]{:S(2)}) collective-permute-start(f32[1,4,16,256]{3,2,1,0:T(8,128)S(1)} %pair_sums.1), channel_id=1, source_target_pairs={{0,2},{1,3},{2,0},{3,1},{4,6},{5,7},{6,4},{7,5},{8,10},{9,11},{10,... | collective-permute-start | bytes 196616 | tf_op jit(solution)/shard_map/ppermute | solution.py:253
  9.3 0.0 collective-permute-start
  9.3 1.2 %collective-permute-done.came = f32[4,16,128]{2,1,0:T(8,128)S(1)} collective-permute-done((f32[4,16,128]{2,1,0:T(8,128)S(1)}, f32[4,16,128]{2,1,0:T(8,128)S(1)}, u32[]{:S(2)}, u32[]{:S(2)}) %collective-permute-start) | collective-permute-done | bytes 32800 | tf_op jit(solution)/shard_map/ppermute | solution.py:249
  10.5 1.5 %collective-permute-start.1 = (f32[2,16,128]{2,1,0:T(8,128)S(1)}, f32[2,16,128]{2,1,0:T(8,128)S(1)}, u32[]{:S(2)}, u32[]{:S(2)}) collective-permute-start(f32[2,16,128]{2,1,0:T(8,128)S(1)} %get-tuple-element.15), channel_id=1, source_target_pairs={{0,8},{4,12},{8,0},{12,4},{16,24},{20,28},{24,16},{28,20},{1,9},{5... | collective-permute-start | bytes 49160 | tf_op jit(solution)/shard_map/ppermute | solution.py:249
  12.0 2.2 %collective-permute-done.1.came = f32[2,16,128]{2,1,0:T(8,128)S(1)} collective-permute-done((f32[2,16,128]{2,1,0:T(8,128)S(1)}, f32[2,16,128]{2,1,0:T(8,128)S(1)}, u32[]{:S(2)}, u32[]{:S(2)}) %collective-permute-start.1) | collective-permute-done | bytes 16416 | tf_op jit(solution)/shard_map/ppermute | solution.py:249
  14.3 1.5 %collective-permute-start.2 = (f32[1,16,128]{2,1,0:T(8,128)S(1)}, f32[1,16,128]{2,1,0:T(8,128)S(1)}, u32[]{:S(2)}, u32[]{:S(2)}) collective-permute-start(f32[1,16,128]{2,1,0:T(8,128)S(1)} %get-tuple-element.17), channel_id=1, source_target_pairs={{0,16},{4,20},{8,24},{12,28},{16,0},{20,4},{24,8},{28,12},{1,17},{... | collective-permute-start | bytes 24584 | tf_op jit(solution)/shard_map/ppermute | solution.py:249
  15.8 2.1 %collective-permute-done.2.came = f32[1,16,128]{2,1,0:T(8,128)S(1)} collective-permute-done((f32[1,16,128]{2,1,0:T(8,128)S(1)}, f32[1,16,128]{2,1,0:T(8,128)S(1)}, u32[]{:S(2)}, u32[]{:S(2)}) %collective-permute-start.2) | collective-permute-done | bytes 8224 | tf_op jit(solution)/shard_map/ppermute | solution.py:249
  17.9 0.0 collective-permute-done.4.refs_0_
  17.9 0.9 %update.1 = (f32[1,4,16,256]{3,2,1,0:T(8,128)}, f32[3,1,512]{2,1,0:T(1,128)}) custom-call(f32[1,4,16,256]{3,2,1,0:T(8,128)S(1)} %get-tuple-element.11.state, f32[1,16,128]{2,1,0:T(8,128)S(1)} %get-tuple-element.16.kept, f32[1,16,128]{2,1,0:T(8,128)S(1)} %collective-permute-done.2.came, f32[1,4,16,256]{3,2,1,0:T(8,128)S(1)} %collective-permute-done.3.partner, ...), custom_call_target="tpu_custom_call" | custom-call | tf_op jit(solution)/shard_map/update/pallas_call | solution.py:256
  (3 shorter events, 0.0 us)
Async XLA Ops:
  0.6 5.5 %collective-permute-start.3 = (f32[1,4,16,256]{3,2,1,0:T(8,128)}, f32[1,4,16,256]{3,2,1,0:T(8,128)S(1)}, u32[]{:S(2)}, u32[]{:S(2)}) collective-permute-start(f32[1,4,16,256]{3,2,1,0:T(8,128)} %state_hbm.1), channel_id=1, source_target_pairs={{0,1},{1,0},{2,3},{3,2},{4,5},{5,4},{6,7},{7,6},{8,9},{9,8},{10,11... | collective-permute-start | bytes 196616 | tf_op jit(solution)/shard_map/ppermute | solution.py:249
  6.2 11.7 %collective-permute-start.4 = (f32[1,4,16,256]{3,2,1,0:T(8,128)S(1)}, f32[1,4,16,256]{3,2,1,0:T(8,128)S(1)}, u32[]{:S(2)}, u32[]{:S(2)}) collective-permute-start(f32[1,4,16,256]{3,2,1,0:T(8,128)S(1)} %pair_sums.1), channel_id=1, source_target_pairs={{0,2},{1,3},{2,0},{3,1},{4,6},{5,7},{6,4},{7,5},{8,10},{9,11},{10,... | collective-permute-start | bytes 196616 | tf_op jit(solution)/shard_map/ppermute | solution.py:253
  9.3 1.2 %collective-permute-start = (f32[4,16,128]{2,1,0:T(8,128)S(1)}, f32[4,16,128]{2,1,0:T(8,128)S(1)}, u32[]{:S(2)}, u32[]{:S(2)}) collective-permute-start(f32[4,16,128]{2,1,0:T(8,128)S(1)} %get-tuple-element.13), channel_id=1, source_target_pairs={{0,4},{4,0},{8,12},{12,8},{16,20},{20,16},{24,28},{28,24},{1,5},{5... | collective-permute-start | bytes 98312 | tf_op jit(solution)/shard_map/ppermute | solution.py:249
  10.5 3.7 %collective-permute-start.1 = (f32[2,16,128]{2,1,0:T(8,128)S(1)}, f32[2,16,128]{2,1,0:T(8,128)S(1)}, u32[]{:S(2)}, u32[]{:S(2)}) collective-permute-start(f32[2,16,128]{2,1,0:T(8,128)S(1)} %get-tuple-element.15), channel_id=1, source_target_pairs={{0,8},{4,12},{8,0},{12,4},{16,24},{20,28},{24,16},{28,20},{1,9},{5... | collective-permute-start | bytes 49160 | tf_op jit(solution)/shard_map/ppermute | solution.py:249
  14.3 3.7 %collective-permute-start.2 = (f32[1,16,128]{2,1,0:T(8,128)S(1)}, f32[1,16,128]{2,1,0:T(8,128)S(1)}, u32[]{:S(2)}, u32[]{:S(2)}) collective-permute-start(f32[1,16,128]{2,1,0:T(8,128)S(1)} %get-tuple-element.17), channel_id=1, source_target_pairs={{0,16},{4,20},{8,24},{12,28},{16,0},{20,4},{24,8},{28,12},{1,17},{... | collective-permute-start | bytes 24584 | tf_op jit(solution)/shard_map/ppermute | solution.py:249

commit v5 on v4

--- a/solution.py
+++ b/solution.py
@@ -16,6 +16,7 @@
 LANES = 128
 ROWS = 16
 EDGE = 12
+PLACING = 10**10
 RIDING = 8
 
 
@@ -36,7 +37,8 @@
     return inverse, vr, vc, p
 
 
-def forces_kernel(blocks, node_block, state_hbm, cell_hbm, node_hbm, area_hbm, kept, sent, state, cell, node, area, sems):
+def forces_kernel(blocks, node_block, state_hbm, cell_hbm, node_hbm, area_hbm, state, *refs):
+    *outs, cell, node, area, sems = refs
     loads = [
         pltpu.make_async_copy(source, target, sems.at[i])
         for i, (source, target) in enumerate(
@@ -100,57 +102,50 @@
             result = product if result is None else result + product
         return result.reshape(count, ROWS, LANES)
 
-    group = min(blocks, 8)
-
-    def halves(g):
-        result = dense(g * group, group).reshape(group // 2, 2, ROWS, LANES)
-        return result[:, 0], result[:, 1]
-
-    if group == blocks:
-        kept[...], sent[...] = halves(0)
+    size = blocks // len(outs)
+    group = min(size, 8)
+    if size == group:
+        for i, out in enumerate(outs):
+            out[...] = dense(i * size, size)
     else:
-
-        @pl.loop(0, blocks // group)
-        def _(g):
-            span = pl.ds(g * (group // 2), group // 2)
-            kept[span], sent[span] = halves(g)
+        for i, out in enumerate(outs):
+
+            @pl.loop(0, size // group)
+            def _(g):
+                out[pl.ds(g * group, group)] = dense(i * size + g * group, group)
 
     flat = state[0].reshape(4 * radial, around)
     turned = jnp.concatenate([flat[:, around - LANES :], flat[:, :LANES]], axis=0).T
     lane = lax.broadcasted_iota(jnp.int32, (1, LANES), 1)
     edge = jnp.where(lane < LANES // 2, turned[LANES - 1 :, :], turned[:1, :])
-    for out in (kept, sent):
+    for out in outs:
         out[0, EDGE : EDGE + 1, :] = edge
 
 
-def halving_kernel(edges, kept, came, kept_next, sent):
-    half = kept_next.shape[0]
-    for b in range(half):
-        kept_next[b] = kept[2 * b] + came[2 * b]
-        sent[b] = kept[2 * b + 1] + came[2 * b + 1]
-    if edges:
-        own, others = (gather_edges(ref, edges) for ref in (kept, came))
-        put_edges(kept_next, own + others)
-        put_edges(sent, own + others)
-
-
-def gather_edges(ref, count):
-    spare = ROWS - EDGE
-    return [ref[i // spare, EDGE + i % spare : EDGE + i % spare + 1, :] for i in range(count)]
-
-
-def put_edges(ref, rows):
-    spare = ROWS - EDGE
-    for i, row in enumerate(rows):
-        ref[i // spare, EDGE + i % spare : EDGE + i % spare + 1, :] = row
-
-
-def pair_kernel(weights, instances, state, partner, *outs):
-    odd = lax.axis_index("inst") % 2
+def halving_kernel(arrived, riding, *refs):
+    outs = refs[arrived:]
+    size = outs[0].shape[0]
     for i, out in enumerate(outs):
-        shift = 2 * (i + 1)
-        weight = jnp.where(odd == 1, weights[(shift + 1) % instances], weights[shift - 1])
-        out[...] = weights[shift] * state[...] + weight * partner[...]
+        for b in range(size):
+            out[b] = functools.reduce(jnp.add, [ref[i * size + b] for ref in refs[:arrived]])
+        if riding:
+            for j, ref in enumerate(refs[:arrived]):
+                out[0, EDGE + j : EDGE + j + 1, :] = ref[0, EDGE : EDGE + 1, :]
+
+
+def pair_kernel(weights, instances, state, partner, _, *outs):
+    me = lax.axis_index("inst")
+
+    def weight(shift):
+        value = weights[0]
+        for i in range(1, instances):
+            value = jnp.where(shift == i, weights[i], value)
+        return value
+
+    for i, out in enumerate(outs):
+        shift = ((me ^ (i + 1)) - me + instances) % instances
+        far = (shift + instances // 2) % instances
+        out[...] = weight(shift) * state[...] + weight(far) * partner[...]
 
 
 def update_kernel(weights, blocks, instances, state, kept, came, partner, *refs):
@@ -158,14 +153,16 @@
     increment, blade = refs[-2:]
     radial, around = state.shape[2:]
     high = blade.shape[2] // LANES
-    if blocks <= RIDING:
+    if blocks == RIDING:
         me = lax.axis_index("space")
         known = [kept[0, EDGE:, :], came[0, EDGE:, :]]
         known = jnp.concatenate(known, axis=0)
         row = lax.broadcasted_iota(jnp.int32, known.shape, 0)
 
         def edge_of(device):
-            return jnp.sum(jnp.where(row == device ^ me, known, 0.0), axis=0, keepdims=True)
+            relative = device ^ me
+            place = relative // 2 + (relative % 2) * (RIDING // 2)
+            return jnp.sum(jnp.where(row == place, known, 0.0), axis=0, keepdims=True)
 
         before = edge_of((me + blocks - 1) % blocks)
         after = edge_of((me + 1) % blocks)
@@ -217,16 +214,13 @@
     speed = jnp.abs(vr) + a
     reach = 0.5 * jnp.maximum(speed, above(speed))
     flux = (q[1], q[1] * vr + p, q[2] * vr, (q[3] + p) * vr)
-    partner_weight = jnp.where(
-        lax.axis_index("inst") % 2 == 1, weights[1], weights[instances - 1]
-    )
     for c in range(4):
         wall = p if c == 1 else 0.0
         face = 0.5 * (flux[c] + above(flux[c])) - reach * (above(q[c]) - q[c])
         upper = jnp.where(tip, wall, face)
         lower = jnp.where(hub, wall, below(face))
         residual = divergence[c] + (upper - lower) + weights[0] * q[c]
-        residual += partner_weight * partner[0, c]
+        residual += weights[instances // 2] * partner[0, c]
         for ref in sums:
             residual += ref[0, c]
         increment[0, c] = -step * residual
@@ -252,18 +246,19 @@
         count = lax.axis_size(axis)
         return lax.ppermute(value, axis, [(i, (i + s) % count) for i in range(count)])
 
-    def call(kernel, name, shapes, *operands):
+    def call(kernel, name, shapes, *operands, flops=0):
         return pl.pallas_call(
             kernel,
             out_shape=[jax.ShapeDtypeStruct(shape, jnp.float32) for shape in shapes],
             in_specs=[vmem] * len(operands),
             out_specs=[vmem] * len(shapes),
             compiler_params=params,
+            cost_estimate=pl.CostEstimate(flops=flops, bytes_accessed=0, transcendentals=0),
             name=name,
         )(*operands)
 
     weights = spectral_row(instances)
-    partner = swapped(state, "inst", 1)
+    partner = shifted(state, "inst", instances // 2)
 
     faces = (
         state,
@@ -271,47 +266,50 @@
         face_node.reshape(chunks, LANES),
         face_area,
     )
-    half = jax.ShapeDtypeStruct((blocks // 2, ROWS, LANES), jnp.float32)
-    kept, sent, near_state = pl.pallas_call(
+    riding = blocks == RIDING
+    steps = [4, 2] if riding else [2] * (blocks.bit_length() - 1)
+    size = blocks // steps[0]
+    block = jax.ShapeDtypeStruct((size, ROWS, LANES), jnp.float32)
+    near_state, kept, *sent = pl.pallas_call(
         functools.partial(forces_kernel, blocks, node_block),
-        out_shape=[half, half, jax.ShapeDtypeStruct(state.shape, jnp.float32)],
+        out_shape=[jax.ShapeDtypeStruct(state.shape, jnp.float32)] + [block] * steps[0],
         in_specs=[pl.BlockSpec(memory_space=pltpu.HBM)] * 4,
-        out_specs=[vmem] * 3,
+        out_specs=[vmem] * (1 + steps[0]),
         scratch_shapes=[pltpu.VMEM(x.shape, x.dtype) for x in faces[1:]]
         + [pltpu.SemaphoreType.DMA((4,))],
         compiler_params=params,
-        cost_estimate=pl.CostEstimate(flops=10**9, bytes_accessed=10**7, transcendentals=0),
+        cost_estimate=pl.CostEstimate(flops=PLACING, bytes_accessed=0, transcendentals=0),
         name="face_forces",
     )(*(pltpu.with_memory_space_constraint(x, pltpu.HBM) for x in faces))
 
-    riding = blocks <= RIDING
     edges = []
     if not riding:
         row = jnp.broadcast_to(kept[0, EDGE : EDGE + 1, :], (8, LANES))
         edges = [shifted(row, "space", 1), shifted(row, "space", blocks - 1)]
-    came = swapped(sent, "space", 1)
-
+
+    came = [swapped(value, "space", (i + 1) * size) for i, value in enumerate(sent)]
     sums = call(
         functools.partial(pair_kernel, weights, instances),
         "pair_sums",
         [state.shape] * (instances // 2 - 1),
         near_state,
         partner,
-    )
-    sums = [shifted(value, "inst", 2 * (i + 1)) for i, value in enumerate(sums)]
-
-    bit = 2
-    while bit < blocks:
-        shape = (blocks // (2 * bit), ROWS, LANES)
-        kept, sent = call(
-            functools.partial(halving_kernel, bit // 2 if riding else 0),
+        came[0],
+        flops=PLACING,
+    )
+    sums = [swapped(value, "inst", i + 1) for i, value in enumerate(sums)]
+
+    for step in steps[1:]:
+        size //= step
+        kept, *sent = call(
+            functools.partial(halving_kernel, 1 + len(came), riding),
             "halving",
-            [shape] * 2,
+            [(size, ROWS, LANES)] * step,
             kept,
-            came,
+            *came,
+            flops=PLACING,
         )
-        came = swapped(sent, "space", bit)
-        bit *= 2
+        came = [swapped(value, "space", (i + 1) * size) for i, value in enumerate(sent)]
 
     increment, blade = call(
         functools.partial(update_kernel, weights, blocks, instances),
@@ -319,7 +317,7 @@
         [state.shape, (3, 1, node_block)],
         near_state,
         kept,
-        came,
+        *came,
         partner,
         *sums,
         *edges,

time: 19 us -> 16.5 us (0.87)
  waiting for transfers between devices: 6.76 us -> 3.64 us
  Pallas kernels: 2.23 us -> 2.61 us
    ppermute x4 -> x5, waiting for transfers between devices: 6.76 us -> 3.64 us  [swapped(): lax.ppermute(value, axis, [(i, i ^ bit) for i in range(lax.axis_size(axis...]
    ppermute x1, starting transfers between devices: 3.1 us -> 4.1 us  [shifted(): lax.ppermute(value, axis, [(i, (i + s) % count) for i in range(count)])]
    ppermute x4 -> x5, starting transfers between devices: 6.1 us -> 5.27 us  [swapped(): lax.ppermute(value, axis, [(i, i ^ bit) for i in range(lax.axis_size(axis...]
    pallas_call x1, Pallas kernels: 1.27 us -> 1.64 us  [per_device(): pl.pallas_call(functools.partial(forces_kernel, blocks, node_block), out_...]
    pallas_call x4 -> x3, Pallas kernels: 0.96 us -> 0.98 us  [call(): pl.pallas_call(kernel, out_shape=[jax.ShapeDtypeStruct(shape, jnp.float32...]
  transfers between devices with their start and end apart: 5 -> 6, of which waited for: 4 -> 3; matrix products, arithmetic and copies ran while one was open for 0% -> 0% of each run, Pallas kernels for 7% -> 10%
where the time goes in v5:
time: 16.5 us; the launch traced here: 16.3 us
  starting transfers between devices  9.37 us (57%)
  waiting for transfers between devices  3.64 us (22%)
  Pallas kernels  2.61 us (16%)
  between operations  0.66 us (4%)
    ppermute x5, starting transfers between devices, swapped(): lax.ppermute(value, axis, [(i, i ^ bit) for i in range(lax.axis_size(axis...  5.27 us
    ppermute x1, starting transfers between devices, shifted(): lax.ppermute(value, axis, [(i, (i + s) % count) for i in range(count)])  4.1 us
    ppermute x5, waiting for transfers between devices, swapped(): lax.ppermute(value, axis, [(i, i ^ bit) for i in range(lax.axis_size(axis...  3.64 us
    pallas_call x1, Pallas kernels, per_device(): pl.pallas_call(functools.partial(forces_kernel, blocks, node_block), out_...  1.64 us
    pallas_call x3, Pallas kernels, call(): pl.pallas_call(kernel, out_shape=[jax.ShapeDtypeStruct(shape, jnp.float32...  0.98 us
  transfers between devices with their start and end apart: 6, of which 3 were waited for; matrix products, arithmetic and copies ran while one was open for 0% of the time, Pallas kernels for 10%

profile of v5, /device:TPU:0, one launch (start us, length us, event | category | flops | bytes accessed | tf_op | source)
XLA Modules:
  0.0 16.3 jit_solution(14671846576972505937)
XLA Ops:
  0.6 4.1 %collective-permute-start.4 = (f32[1,4,16,256]{3,2,1,0:T(8,128)}, f32[1,4,16,256]{3,2,1,0:T(8,128)S(1)}, u32[]{:S(2)}, u32[]{:S(2)}) collective-permute-start(f32[1,4,16,256]{3,2,1,0:T(8,128)} %state_hbm.1), channel_id=1, source_target_pairs={{0,2},{1,3},{2,0},{3,1},{4,6},{5,7},{6,4},{7,5},{8,10},{9,11},{10,... | collective-permute-start | bytes 196616 | tf_op jit(solution)/shard_map/ppermute | solution.py:247
  4.7 1.6 %face_forces.1 = (f32[1,4,16,256]{3,2,1,0:T(8,128)S(1)}, f32[2,16,128]{2,1,0:T(8,128)S(1)}, f32[2,16,128]{2,1,0:T(8,128)S(1)}, f32[2,16,128]{2,1,0:T(8,128)S(1)}, f32[2,16,128]{2,1,0:T(8,128)S(1)}) custom-call(f32[1,4,16,256]{3,2,1,0:T(8,128)} %state_hbm.1, s32[6,128]{1,0:T(8,128)} %bitcast.4, s32[6,128]{1,0:T(8,128)} %bitcast.5, f32[3,768]{1,0:T(4,128)} %area_hbm.1), custom_call_target="tpu_custom_call" | custom-call | flops 10000000000 | tf_op jit(solution)/shard_map/face_forces/pallas_call | solution.py:273
  6.4 1.6 %collective-permute-start = (f32[2,16,128]{2,1,0:T(8,128)S(1)}, f32[2,16,128]{2,1,0:T(8,128)S(1)}, u32[]{:S(2)}, u32[]{:S(2)}) collective-permute-start(f32[2,16,128]{2,1,0:T(8,128)S(1)} %get-tuple-element.13), channel_id=1, source_target_pairs={{0,8},{4,12},{8,0},{12,4},{16,24},{20,28},{24,16},{28,20},{1,9},{5... | collective-permute-start | bytes 49160 | tf_op jit(solution)/shard_map/ppermute | solution.py:243
  7.9 1.5 %collective-permute-start.1 = (f32[2,16,128]{2,1,0:T(8,128)S(1)}, f32[2,16,128]{2,1,0:T(8,128)S(1)}, u32[]{:S(2)}, u32[]{:S(2)}) collective-permute-start(f32[2,16,128]{2,1,0:T(8,128)S(1)} %get-tuple-element.14), channel_id=1, source_target_pairs={{0,16},{4,20},{8,24},{12,28},{16,0},{20,4},{24,8},{28,12},{1,17},{... | collective-permute-start | bytes 49160 | tf_op jit(solution)/shard_map/ppermute | solution.py:243
  9.5 0.5 %collective-permute-start.2 = (f32[2,16,128]{2,1,0:T(8,128)S(1)}, f32[2,16,128]{2,1,0:T(8,128)S(1)}, u32[]{:S(2)}, u32[]{:S(2)}) collective-permute-start(f32[2,16,128]{2,1,0:T(8,128)S(1)} %get-tuple-element.15), channel_id=1, source_target_pairs={{0,24},{4,28},{8,16},{12,20},{16,8},{20,12},{24,0},{28,4},{1,25},{... | collective-permute-start | bytes 49160 | tf_op jit(solution)/shard_map/ppermute | solution.py:243
  9.9 0.2 %collective-permute-done.refs_1_._ = f32[2,16,128]{2,1,0:T(8,128)S(1)} collective-permute-done((f32[2,16,128]{2,1,0:T(8,128)S(1)}, f32[2,16,128]{2,1,0:T(8,128)S(1)}, u32[]{:S(2)}, u32[]{:S(2)}) %collective-permute-start) | collective-permute-done | bytes 16416 | tf_op jit(solution)/shard_map/ppermute | solution.py:243
  10.2 0.0 collective-permute-done.4.partner
  10.2 1.6 %collective-permute-start.5 = (f32[1,4,16,256]{3,2,1,0:T(8,128)S(1)}, f32[1,4,16,256]{3,2,1,0:T(8,128)S(1)}, u32[]{:S(2)}, u32[]{:S(2)}) collective-permute-start(f32[1,4,16,256]{3,2,1,0:T(8,128)S(1)} %pair_sums.1), channel_id=1, source_target_pairs={{0,1},{1,0},{2,3},{3,2},{4,5},{5,4},{6,7},{7,6},{8,9},{9,8},{10,11... | collective-permute-start | bytes 196616 | tf_op jit(solution)/shard_map/ppermute | solution.py:243
  11.9 0.0 collective-permute-done.1.refs_2_
  11.9 2.2 %collective-permute-done.2.refs_3_ = f32[2,16,128]{2,1,0:T(8,128)S(1)} collective-permute-done((f32[2,16,128]{2,1,0:T(8,128)S(1)}, f32[2,16,128]{2,1,0:T(8,128)S(1)}, u32[]{:S(2)}, u32[]{:S(2)}) %collective-permute-start.2) | collective-permute-done | bytes 16416 | tf_op jit(solution)/shard_map/ppermute | solution.py:243
  14.1 0.1 collective-permute-start.3
  14.2 1.2 %collective-permute-done.3.came = f32[1,16,128]{2,1,0:T(8,128)S(1)} collective-permute-done((f32[1,16,128]{2,1,0:T(8,128)S(1)}, f32[1,16,128]{2,1,0:T(8,128)S(1)}, u32[]{:S(2)}, u32[]{:S(2)}) %collective-permute-start.3) | collective-permute-done | bytes 8224 | tf_op jit(solution)/shard_map/ppermute | solution.py:243
  15.3 0.0 collective-permute-done.5.refs_0_
  15.3 0.9 %update.1 = (f32[1,4,16,256]{3,2,1,0:T(8,128)}, f32[3,1,512]{2,1,0:T(1,128)}) custom-call(f32[1,4,16,256]{3,2,1,0:T(8,128)S(1)} %get-tuple-element.11.state, f32[1,16,128]{2,1,0:T(8,128)S(1)} %get-tuple-element.16.kept, f32[1,16,128]{2,1,0:T(8,128)S(1)} %collective-permute-done.3.came, f32[1,4,16,256]{3,2,1,0:T(8,128)S(1)} %collective-permute-done.4.partner, ...), custom_call_target="tpu_custom_call" | custom-call | tf_op jit(solution)/shard_map/update/pallas_call | solution.py:250
  (2 shorter events, 0.0 us)
Async XLA Ops:
  0.6 9.6 %collective-permute-start.4 = (f32[1,4,16,256]{3,2,1,0:T(8,128)}, f32[1,4,16,256]{3,2,1,0:T(8,128)S(1)}, u32[]{:S(2)}, u32[]{:S(2)}) collective-permute-start(f32[1,4,16,256]{3,2,1,0:T(8,128)} %state_hbm.1), channel_id=1, source_target_pairs={{0,2},{1,3},{2,0},{3,1},{4,6},{5,7},{6,4},{7,5},{8,10},{9,11},{10,... | collective-permute-start | bytes 196616 | tf_op jit(solution)/shard_map/ppermute | solution.py:247
  6.4 3.8 %collective-permute-start = (f32[2,16,128]{2,1,0:T(8,128)S(1)}, f32[2,16,128]{2,1,0:T(8,128)S(1)}, u32[]{:S(2)}, u32[]{:S(2)}) collective-permute-start(f32[2,16,128]{2,1,0:T(8,128)S(1)} %get-tuple-element.13), channel_id=1, source_target_pairs={{0,8},{4,12},{8,0},{12,4},{16,24},{20,28},{24,16},{28,20},{1,9},{5... | collective-permute-start | bytes 49160 | tf_op jit(solution)/shard_map/ppermute | solution.py:243
  7.9 3.9 %collective-permute-start.1 = (f32[2,16,128]{2,1,0:T(8,128)S(1)}, f32[2,16,128]{2,1,0:T(8,128)S(1)}, u32[]{:S(2)}, u32[]{:S(2)}) collective-permute-start(f32[2,16,128]{2,1,0:T(8,128)S(1)} %get-tuple-element.14), channel_id=1, source_target_pairs={{0,16},{4,20},{8,24},{12,28},{16,0},{20,4},{24,8},{28,12},{1,17},{... | collective-permute-start | bytes 49160 | tf_op jit(solution)/shard_map/ppermute | solution.py:243
  9.5 4.6 %collective-permute-start.2 = (f32[2,16,128]{2,1,0:T(8,128)S(1)}, f32[2,16,128]{2,1,0:T(8,128)S(1)}, u32[]{:S(2)}, u32[]{:S(2)}) collective-permute-start(f32[2,16,128]{2,1,0:T(8,128)S(1)} %get-tuple-element.15), channel_id=1, source_target_pairs={{0,24},{4,28},{8,16},{12,20},{16,8},{20,12},{24,0},{28,4},{1,25},{... | collective-permute-start | bytes 49160 | tf_op jit(solution)/shard_map/ppermute | solution.py:243
  10.2 5.1 %collective-permute-start.5 = (f32[1,4,16,256]{3,2,1,0:T(8,128)S(1)}, f32[1,4,16,256]{3,2,1,0:T(8,128)S(1)}, u32[]{:S(2)}, u32[]{:S(2)}) collective-permute-start(f32[1,4,16,256]{3,2,1,0:T(8,128)S(1)} %pair_sums.1), channel_id=1, source_target_pairs={{0,1},{1,0},{2,3},{3,2},{4,5},{5,4},{6,7},{7,6},{8,9},{9,8},{10,11... | collective-permute-start | bytes 196616 | tf_op jit(solution)/shard_map/ppermute | solution.py:243
  14.1 1.2 %collective-permute-start.3 = (f32[1,16,128]{2,1,0:T(8,128)S(1)}, f32[1,16,128]{2,1,0:T(8,128)S(1)}, u32[]{:S(2)}, u32[]{:S(2)}) collective-permute-start(f32[1,16,128]{2,1,0:T(8,128)S(1)} %get-tuple-element.17), channel_id=1, source_target_pairs={{0,4},{4,0},{8,12},{12,8},{16,20},{20,16},{24,28},{28,24},{1,5},{5... | collective-permute-start | bytes 24584 | tf_op jit(solution)/shard_map/ppermute | solution.py:243

commit v6 on v5

--- a/solution.py
+++ b/solution.py
@@ -103,16 +103,16 @@
         return result.reshape(count, ROWS, LANES)
 
     size = blocks // len(outs)
-    group = min(size, 8)
-    if size == group:
+    if blocks <= 16:
+        result = dense(0, blocks)
         for i, out in enumerate(outs):
-            out[...] = dense(i * size, size)
+            out[...] = result[i * size : (i + 1) * size]
     else:
         for i, out in enumerate(outs):
 
-            @pl.loop(0, size // group)
+            @pl.loop(0, size // 8)
             def _(g):
-                out[pl.ds(g * group, group)] = dense(i * size + g * group, group)
+                out[pl.ds(g * 8, 8)] = dense(i * size + g * 8, 8)
 
     flat = state[0].reshape(4 * radial, around)
     turned = jnp.concatenate([flat[:, around - LANES :], flat[:, :LANES]], axis=0).T
@@ -148,7 +148,46 @@
         out[...] = weight(shift) * state[...] + weight(far) * partner[...]
 
 
-def update_kernel(weights, blocks, instances, state, kept, came, partner, *refs):
+def around_flux(q, vc, p):
+    return (q[2], q[1] * vc, q[2] * vc + p, (q[3] + p) * vc)
+
+
+def flux_kernel(weight, instances, state, base, step):
+    radial, around = state.shape[2:]
+    q = [state[0, c] for c in range(4)]
+    inverse, vr, vc, p = pressure_of(*q)
+    a = jnp.sqrt(gamma_ratio * p * inverse)
+    step[...] = cfl_number / (
+        jnp.abs(vr) + jnp.abs(vc) + 2.0 * a + omega_rate * instances / 2.0
+    )
+
+    def after(x):
+        return pltpu.roll(x, around - 1, 1)
+
+    def above(x):
+        return pltpu.roll(x, radial - 1, 0)
+
+    column = lax.broadcasted_iota(jnp.int32, (radial, around), 1)
+    row = lax.broadcasted_iota(jnp.int32, (radial, around), 0)
+    hub, tip = row == 0, row == radial - 1
+    speed = jnp.abs(vc) + a
+    reach = 0.5 * jnp.maximum(speed, after(speed))
+    speed = jnp.abs(vr) + a
+    rise = 0.5 * jnp.maximum(speed, above(speed))
+    flux = around_flux(q, vc, p)
+    radial_flux = (q[1], q[1] * vr + p, q[2] * vr, (q[3] + p) * vr)
+    for c in range(4):
+        face = 0.5 * (flux[c] + after(flux[c])) - reach * (after(q[c]) - q[c])
+        face = jnp.where(column == around - 1, 0.0, face)
+        residual = weight * q[c] + (face - pltpu.roll(face, 1, 1))
+        wall = p if c == 1 else 0.0
+        face = 0.5 * (radial_flux[c] + above(radial_flux[c])) - rise * (above(q[c]) - q[c])
+        upper = jnp.where(tip, wall, face)
+        lower = jnp.where(hub, wall, pltpu.roll(face, 1, 0))
+        base[0, c] = residual + (upper - lower)
+
+
+def update_kernel(weight, blocks, instances, state, base, step, kept, came, partner, *refs):
     sums = refs[: instances // 2 - 1]
     increment, blade = refs[-2:]
     radial, around = state.shape[2:]
@@ -171,59 +210,37 @@
     lane = lax.broadcasted_iota(jnp.int32, (1, LANES), 1)
     edge = jnp.where(lane < LANES // 2, before, after)
     columns = jnp.broadcast_to(edge, (LANES, LANES)).T
+
     lane = lax.broadcasted_iota(jnp.int32, (radial, LANES), 1)
-    q = []
+    first, last = lane == 0, lane == LANES - 1
+    own, far = [], []
     for c in range(4):
-        last = columns[c * radial : (c + 1) * radial]
-        initial = columns[LANES // 2 + c * radial : LANES // 2 + (c + 1) * radial]
-        edge = jnp.where(lane == LANES - 1, last, initial)
-        q.append(jnp.concatenate([state[0, c], edge], axis=1))
-    inverse, vr, vc, p = pressure_of(*q)
-    a = jnp.sqrt(gamma_ratio * p * inverse)
-    width = around + LANES
-    step = cfl_number / (
-        jnp.abs(vr) + jnp.abs(vc) + 2.0 * a + omega_rate * instances / 2.0
-    )
-
-    def next_lane(x):
-        return pltpu.roll(x, width - 1, 1)
-
-    def last_lane(x):
-        return pltpu.roll(x, 1, 1)
-
-    speed = jnp.abs(vc) + a
-    reach = 0.5 * jnp.maximum(speed, next_lane(speed))
-    flux = (q[2], q[1] * vc, q[2] * vc + p, (q[3] + p) * vc)
-    divergence = []
+        own.append(jnp.where(first, state[0, c, :, :LANES], state[0, c, :, around - LANES :]))
+        far.append(
+            jnp.where(
+                last,
+                columns[LANES // 2 + c * radial : LANES // 2 + (c + 1) * radial],
+                columns[c * radial : (c + 1) * radial],
+            )
+        )
+    faces, speeds = [], []
+    for q in (own, far):
+        inverse, _, vc, p = pressure_of(*q)
+        speeds.append(jnp.abs(vc) + jnp.sqrt(gamma_ratio * p * inverse))
+        faces.append(around_flux(q, vc, p))
+    side = jnp.where(last, 0.5, -0.5)
+    reach = 0.5 * jnp.maximum(*speeds)
     for c in range(4):
-        face = 0.5 * (flux[c] + next_lane(flux[c])) - reach * (next_lane(q[c]) - q[c])
-        divergence.append((face - last_lane(face))[:, :around])
-
-    own = slice(0, around)
-    q = [x[:, own] for x in q]
-    vr, p, a, step = vr[:, own], p[:, own], a[:, own], step[:, own]
-
-    def above(x):
-        return pltpu.roll(x, radial - 1, 0)
-
-    def below(x):
-        return pltpu.roll(x, 1, 0)
-
-    row = lax.broadcasted_iota(jnp.int32, (radial, around), 0)
-    hub, tip = row == 0, row == radial - 1
-    speed = jnp.abs(vr) + a
-    reach = 0.5 * jnp.maximum(speed, above(speed))
-    flux = (q[1], q[1] * vr + p, q[2] * vr, (q[3] + p) * vr)
-    for c in range(4):
-        wall = p if c == 1 else 0.0
-        face = 0.5 * (flux[c] + above(flux[c])) - reach * (above(q[c]) - q[c])
-        upper = jnp.where(tip, wall, face)
-        lower = jnp.where(hub, wall, below(face))
-        residual = divergence[c] + (upper - lower) + weights[0] * q[c]
-        residual += weights[instances // 2] * partner[0, c]
+        outer = side * (faces[0][c] + faces[1][c]) - reach * (far[c] - own[c])
+        outer = [jnp.where(first, outer, 0.0), jnp.where(last, outer, 0.0)]
+        middle = around - 2 * LANES
+        if middle:
+            outer.insert(1, jnp.zeros((radial, middle), jnp.float32))
+        residual = base[0, c] + weight * partner[0, c]
         for ref in sums:
             residual += ref[0, c]
-        increment[0, c] = -step * residual
+        residual += jnp.concatenate(outer, axis=1)
+        increment[0, c] = -step[...] * residual
 
     total = kept[0] + came[0]
     for k in range(3):
@@ -245,6 +262,10 @@
     def shifted(value, axis, s):
         count = lax.axis_size(axis)
         return lax.ppermute(value, axis, [(i, (i + s) % count) for i in range(count)])
+
+    def exchanged(sent, size):
+        came = [swapped(sent[i], "space", (i + 1) * size) for i in reversed(range(len(sent)))]
+        return came[::-1]
 
     def call(kernel, name, shapes, *operands, flops=0):
         return pl.pallas_call(
@@ -287,14 +308,14 @@
         row = jnp.broadcast_to(kept[0, EDGE : EDGE + 1, :], (8, LANES))
         edges = [shifted(row, "space", 1), shifted(row, "space", blocks - 1)]
 
-    came = [swapped(value, "space", (i + 1) * size) for i, value in enumerate(sent)]
+    came = exchanged(sent, size)
     sums = call(
         functools.partial(pair_kernel, weights, instances),
         "pair_sums",
         [state.shape] * (instances // 2 - 1),
         near_state,
         partner,
-        came[0],
+        came[-1],
         flops=PLACING,
     )
     sums = [swapped(value, "inst", i + 1) for i, value in enumerate(sums)]
@@ -309,13 +330,21 @@
             *came,
             flops=PLACING,
         )
-        came = [swapped(value, "space", (i + 1) * size) for i, value in enumerate(sent)]
-
+        came = exchanged(sent, size)
+
+    base, step = call(
+        functools.partial(flux_kernel, weights[0], instances),
+        "flux",
+        [state.shape, (radial, around)],
+        near_state,
+    )
     increment, blade = call(
-        functools.partial(update_kernel, weights, blocks, instances),
+        functools.partial(update_kernel, weights[instances // 2], blocks, instances),
         "update",
         [state.shape, (3, 1, node_block)],
         near_state,
+        base,
+        step,
         kept,
         *came,
         partner,

time: 16.5 us -> 16 us (0.970)
  Pallas kernels: 2.61 us -> 2.28 us
    pallas_call x1, Pallas kernels: 1.64 us -> 1.27 us  [per_device(): pl.pallas_call(functools.partial(forces_kernel, blocks, node_block), out_...]
    pallas_call x3 -> x4, Pallas kernels: 0.98 us -> 1.01 us  [call(): pl.pallas_call(kernel, out_shape=[jax.ShapeDtypeStruct(shape, jnp.float32...]
  transfers between devices with their start and end apart: 6 -> 6, of which waited for: 3 -> 4; matrix products, arithmetic and copies ran while one was open for 0% -> 0% of each run, Pallas kernels for 10% -> 9%
where the time goes in v6:
time: 16 us; the launch traced here: 15.9 us
  starting transfers between devices  9.37 us (59%)
  waiting for transfers between devices  3.56 us (22%)
  Pallas kernels  2.28 us (14%)
  between operations  0.67 us (4%)
    ppermute x5, starting transfers between devices, swapped(): lax.ppermute(value, axis, [(i, i ^ bit) for i in range(lax.axis_size(axis...  5.27 us
    ppermute x1, starting transfers between devices, shifted(): lax.ppermute(value, axis, [(i, (i + s) % count) for i in range(count)])  4.1 us
    ppermute x5, waiting for transfers between devices, swapped(): lax.ppermute(value, axis, [(i, i ^ bit) for i in range(lax.axis_size(axis...  3.55 us
    pallas_call x1, Pallas kernels, per_device(): pl.pallas_call(functools.partial(forces_kernel, blocks, node_block), out_...  1.27 us
    pallas_call x4, Pallas kernels, call(): pl.pallas_call(kernel, out_shape=[jax.ShapeDtypeStruct(shape, jnp.float32...  1.01 us
  transfers between devices with their start and end apart: 6, of which 4 were waited for; matrix products, arithmetic and copies ran while one was open for 0% of the time, Pallas kernels for 9%

profile of v6, /device:TPU:0, one launch (start us, length us, event | category | flops | bytes accessed | tf_op | source)
XLA Modules:
  0.0 15.9 jit_solution(10126247331805361226)
XLA Ops:
  0.6 4.1 %collective-permute-start.4 = (f32[1,4,16,256]{3,2,1,0:T(8,128)}, f32[1,4,16,256]{3,2,1,0:T(8,128)S(1)}, u32[]{:S(2)}, u32[]{:S(2)}) collective-permute-start(f32[1,4,16,256]{3,2,1,0:T(8,128)} %state_hbm.1), channel_id=1, source_target_pairs={{0,2},{1,3},{2,0},{3,1},{4,6},{5,7},{6,4},{7,5},{8,10},{9,11},{10,... | collective-permute-start | bytes 196616 | tf_op jit(solution)/shard_map/ppermute | solution.py:264
  4.7 1.3 %face_forces.1 = (f32[1,4,16,256]{3,2,1,0:T(8,128)S(1)}, f32[2,16,128]{2,1,0:T(8,128)S(1)}, f32[2,16,128]{2,1,0:T(8,128)S(1)}, f32[2,16,128]{2,1,0:T(8,128)S(1)}, f32[2,16,128]{2,1,0:T(8,128)S(1)}) custom-call(f32[1,4,16,256]{3,2,1,0:T(8,128)} %state_hbm.1, s32[6,128]{1,0:T(8,128)} %bitcast.4, s32[6,128]{1,0:T(8,128)} %bitcast.5, f32[3,768]{1,0:T(4,128)} %area_hbm.1), custom_call_target="tpu_custom_call" | custom-call | flops 10000000000 | tf_op jit(solution)/shard_map/face_forces/pallas_call | solution.py:294
  6.0 2.5 %collective-permute-start.2 = (f32[2,16,128]{2,1,0:T(8,128)S(1)}, f32[2,16,128]{2,1,0:T(8,128)S(1)}, u32[]{:S(2)}, u32[]{:S(2)}) collective-permute-start(f32[2,16,128]{2,1,0:T(8,128)S(1)} %get-tuple-element.19), channel_id=1, source_target_pairs={{0,24},{4,28},{8,16},{12,20},{16,8},{20,12},{24,0},{28,4},{1,25},{... | collective-permute-start | bytes 49160 | tf_op jit(solution)/shard_map/ppermute | solution.py:260
  8.5 0.5 %collective-permute-start = (f32[2,16,128]{2,1,0:T(8,128)S(1)}, f32[2,16,128]{2,1,0:T(8,128)S(1)}, u32[]{:S(2)}, u32[]{:S(2)}) collective-permute-start(f32[2,16,128]{2,1,0:T(8,128)S(1)} %get-tuple-element.17), channel_id=1, source_target_pairs={{0,8},{4,12},{8,0},{12,4},{16,24},{20,28},{24,16},{28,20},{1,9},{5... | collective-permute-start | bytes 49160 | tf_op jit(solution)/shard_map/ppermute | solution.py:260
  9.1 0.5 %collective-permute-start.1 = (f32[2,16,128]{2,1,0:T(8,128)S(1)}, f32[2,16,128]{2,1,0:T(8,128)S(1)}, u32[]{:S(2)}, u32[]{:S(2)}) collective-permute-start(f32[2,16,128]{2,1,0:T(8,128)S(1)} %get-tuple-element.18), channel_id=1, source_target_pairs={{0,16},{4,20},{8,24},{12,28},{16,0},{20,4},{24,8},{28,12},{1,17},{... | collective-permute-start | bytes 49160 | tf_op jit(solution)/shard_map/ppermute | solution.py:260
  9.6 1.2 %collective-permute-done.2.refs_3_._ = f32[2,16,128]{2,1,0:T(8,128)S(1)} collective-permute-done((f32[2,16,128]{2,1,0:T(8,128)S(1)}, f32[2,16,128]{2,1,0:T(8,128)S(1)}, u32[]{:S(2)}, u32[]{:S(2)}) %collective-permute-start.2) | collective-permute-done | bytes 16416 | tf_op jit(solution)/shard_map/ppermute | solution.py:260
  10.7 0.0 collective-permute-done.4.partner
  10.8 1.6 %collective-permute-start.5 = (f32[1,4,16,256]{3,2,1,0:T(8,128)S(1)}, f32[1,4,16,256]{3,2,1,0:T(8,128)S(1)}, u32[]{:S(2)}, u32[]{:S(2)}) collective-permute-start(f32[1,4,16,256]{3,2,1,0:T(8,128)S(1)} %pair_sums.1), channel_id=1, source_target_pairs={{0,1},{1,0},{2,3},{3,2},{4,5},{5,4},{6,7},{7,6},{8,9},{9,8},{10,11... | collective-permute-start | bytes 196616 | tf_op jit(solution)/shard_map/ppermute | solution.py:260
  12.4 0.0 collective-permute-done.refs_1_
  12.4 0.4 %collective-permute-done.1.refs_2_ = f32[2,16,128]{2,1,0:T(8,128)S(1)} collective-permute-done((f32[2,16,128]{2,1,0:T(8,128)S(1)}, f32[2,16,128]{2,1,0:T(8,128)S(1)}, u32[]{:S(2)}, u32[]{:S(2)}) %collective-permute-start.1) | collective-permute-done | bytes 16416 | tf_op jit(solution)/shard_map/ppermute | solution.py:260
  12.8 0.1 collective-permute-start.3
  12.9 0.2 %flux.1 = (f32[1,4,16,256]{3,2,1,0:T(8,128)S(1)}, f32[16,256]{1,0:T(8,128)S(1)}) custom-call(f32[1,4,16,256]{3,2,1,0:T(8,128)S(1)} %get-tuple-element.13.state), custom_call_target="tpu_custom_call" | custom-call | tf_op jit(solution)/shard_map/flux/pallas_call | solution.py:271
  13.1 1.0 %collective-permute-done.3.came = f32[1,16,128]{2,1,0:T(8,128)S(1)} collective-permute-done((f32[1,16,128]{2,1,0:T(8,128)S(1)}, f32[1,16,128]{2,1,0:T(8,128)S(1)}, u32[]{:S(2)}, u32[]{:S(2)}) %collective-permute-start.3) | collective-permute-done | bytes 8224 | tf_op jit(solution)/shard_map/ppermute | solution.py:260
  14.1 1.0 %collective-permute-done.5.refs_0_ = f32[1,4,16,256]{3,2,1,0:T(8,128)S(1)} collective-permute-done((f32[1,4,16,256]{3,2,1,0:T(8,128)S(1)}, f32[1,4,16,256]{3,2,1,0:T(8,128)S(1)}, u32[]{:S(2)}, u32[]{:S(2)}) %collective-permute-start.5) | collective-permute-done | bytes 65568 | tf_op jit(solution)/shard_map/ppermute | solution.py:260
  15.1 0.8 %update.1 = (f32[1,4,16,256]{3,2,1,0:T(8,128)}, f32[3,1,512]{2,1,0:T(1,128)}) custom-call(f32[1,4,16,256]{3,2,1,0:T(8,128)S(1)} %get-tuple-element.13.state, f32[1,4,16,256]{3,2,1,0:T(8,128)S(1)} %get-tuple-element.14.base, f32[16,256]{1,0:T(8,128)S(1)} %get-tuple-element.15.step, f32[1,16,128]{2,1,0:T(8,128)S(1)} %get-tuple-element.20.kept, ...), custom_call_target="tpu_custom_call" | custom-call | tf_op jit(solution)/shard_map/update/pallas_call | solution.py:271
  (2 shorter events, 0.0 us)
Async XLA Ops:
  0.6 10.1 %collective-permute-start.4 = (f32[1,4,16,256]{3,2,1,0:T(8,128)}, f32[1,4,16,256]{3,2,1,0:T(8,128)S(1)}, u32[]{:S(2)}, u32[]{:S(2)}) collective-permute-start(f32[1,4,16,256]{3,2,1,0:T(8,128)} %state_hbm.1), channel_id=1, source_target_pairs={{0,2},{1,3},{2,0},{3,1},{4,6},{5,7},{6,4},{7,5},{8,10},{9,11},{10,... | collective-permute-start | bytes 196616 | tf_op jit(solution)/shard_map/ppermute | solution.py:264
  6.0 4.7 %collective-permute-start.2 = (f32[2,16,128]{2,1,0:T(8,128)S(1)}, f32[2,16,128]{2,1,0:T(8,128)S(1)}, u32[]{:S(2)}, u32[]{:S(2)}) collective-permute-start(f32[2,16,128]{2,1,0:T(8,128)S(1)} %get-tuple-element.19), channel_id=1, source_target_pairs={{0,24},{4,28},{8,16},{12,20},{16,8},{20,12},{24,0},{28,4},{1,25},{... | collective-permute-start | bytes 49160 | tf_op jit(solution)/shard_map/ppermute | solution.py:260
  8.5 3.9 %collective-permute-start = (f32[2,16,128]{2,1,0:T(8,128)S(1)}, f32[2,16,128]{2,1,0:T(8,128)S(1)}, u32[]{:S(2)}, u32[]{:S(2)}) collective-permute-start(f32[2,16,128]{2,1,0:T(8,128)S(1)} %get-tuple-element.17), channel_id=1, source_target_pairs={{0,8},{4,12},{8,0},{12,4},{16,24},{20,28},{24,16},{28,20},{1,9},{5... | collective-permute-start | bytes 49160 | tf_op jit(solution)/shard_map/ppermute | solution.py:260
  9.1 3.7 %collective-permute-start.1 = (f32[2,16,128]{2,1,0:T(8,128)S(1)}, f32[2,16,128]{2,1,0:T(8,128)S(1)}, u32[]{:S(2)}, u32[]{:S(2)}) collective-permute-start(f32[2,16,128]{2,1,0:T(8,128)S(1)} %get-tuple-element.18), channel_id=1, source_target_pairs={{0,16},{4,20},{8,24},{12,28},{16,0},{20,4},{24,8},{28,12},{1,17},{... | collective-permute-start | bytes 49160 | tf_op jit(solution)/shard_map/ppermute | solution.py:260
  10.8 4.3 %collective-permute-start.5 = (f32[1,4,16,256]{3,2,1,0:T(8,128)S(1)}, f32[1,4,16,256]{3,2,1,0:T(8,128)S(1)}, u32[]{:S(2)}, u32[]{:S(2)}) collective-permute-start(f32[1,4,16,256]{3,2,1,0:T(8,128)S(1)} %pair_sums.1), channel_id=1, source_target_pairs={{0,1},{1,0},{2,3},{3,2},{4,5},{5,4},{6,7},{7,6},{8,9},{9,8},{10,11... | collective-permute-start | bytes 196616 | tf_op jit(solution)/shard_map/ppermute | solution.py:260
  12.8 1.2 %collective-permute-start.3 = (f32[1,16,128]{2,1,0:T(8,128)S(1)}, f32[1,16,128]{2,1,0:T(8,128)S(1)}, u32[]{:S(2)}, u32[]{:S(2)}) collective-permute-start(f32[1,16,128]{2,1,0:T(8,128)S(1)} %get-tuple-element.21), channel_id=1, source_target_pairs={{0,4},{4,0},{8,12},{12,8},{16,20},{20,16},{24,28},{28,24},{1,5},{5... | collective-permute-start | bytes 24584 | tf_op jit(solution)/shard_map/ppermute | solution.py:260

commit v7 on v6

--- a/solution.py
+++ b/solution.py
@@ -102,13 +102,14 @@
             result = product if result is None else result + product
         return result.reshape(count, ROWS, LANES)
 
+    ordered = outs[:1] + outs[:0:-1]
     size = blocks // len(outs)
     if blocks <= 16:
         result = dense(0, blocks)
-        for i, out in enumerate(outs):
+        for i, out in enumerate(ordered):
             out[...] = result[i * size : (i + 1) * size]
     else:
-        for i, out in enumerate(outs):
+        for i, out in enumerate(ordered):
 
             @pl.loop(0, size // 8)
             def _(g):
@@ -133,7 +134,7 @@
                 out[0, EDGE + j : EDGE + j + 1, :] = ref[0, EDGE : EDGE + 1, :]
 
 
-def pair_kernel(weights, instances, state, partner, _, *outs):
+def pair_kernel(weights, instances, state, partner, *outs):
     me = lax.axis_index("inst")
 
     def weight(shift):
@@ -187,9 +188,8 @@
         base[0, c] = residual + (upper - lower)
 
 
-def update_kernel(weight, blocks, instances, state, base, step, kept, came, partner, *refs):
-    sums = refs[: instances // 2 - 1]
-    increment, blade = refs[-2:]
+def outer_kernel(weight, blocks, state, base, kept, came, partner, *refs):
+    *edges, residual, blade = refs
     radial, around = state.shape[2:]
     high = blade.shape[2] // LANES
     if blocks == RIDING:
@@ -200,13 +200,14 @@
 
         def edge_of(device):
             relative = device ^ me
-            place = relative // 2 + (relative % 2) * (RIDING // 2)
+            half = RIDING // 2
+            place = (half - relative // 2) % half + (relative % 2) * half
             return jnp.sum(jnp.where(row == place, known, 0.0), axis=0, keepdims=True)
 
         before = edge_of((me + blocks - 1) % blocks)
         after = edge_of((me + 1) % blocks)
     else:
-        before, after = (ref[0:1, :] for ref in refs[instances // 2 - 1 : -2])
+        before, after = (ref[0:1, :] for ref in edges)
     lane = lax.broadcasted_iota(jnp.int32, (1, LANES), 1)
     edge = jnp.where(lane < LANES // 2, before, after)
     columns = jnp.broadcast_to(edge, (LANES, LANES)).T
@@ -236,16 +237,19 @@
         middle = around - 2 * LANES
         if middle:
             outer.insert(1, jnp.zeros((radial, middle), jnp.float32))
-        residual = base[0, c] + weight * partner[0, c]
-        for ref in sums:
-            residual += ref[0, c]
-        residual += jnp.concatenate(outer, axis=1)
-        increment[0, c] = -step[...] * residual
+        residual[0, c] = base[0, c] + weight * partner[0, c] + jnp.concatenate(outer, axis=1)
 
     total = kept[0] + came[0]
     for k in range(3):
         for h in range(high):
             blade[k, :, pl.ds(h * LANES, LANES)] = total[k * high + h : k * high + h + 1, :]
+
+
+def update_kernel(residual, step, *refs):
+    *sums, increment = refs
+    for c in range(residual.shape[1]):
+        total = functools.reduce(jnp.add, [ref[0, c] for ref in (residual, *sums)])
+        increment[0, c] = -step[...] * total
 
 
 def per_device(node_block, state, face_cell, face_node, face_area):
@@ -264,8 +268,9 @@
         return lax.ppermute(value, axis, [(i, (i + s) % count) for i in range(count)])
 
     def exchanged(sent, size):
-        came = [swapped(sent[i], "space", (i + 1) * size) for i in reversed(range(len(sent)))]
-        return came[::-1]
+        return [
+            swapped(value, "space", (len(sent) - i) * size) for i, value in enumerate(sent)
+        ]
 
     def call(kernel, name, shapes, *operands, flops=0):
         return pl.pallas_call(
@@ -315,7 +320,6 @@
         [state.shape] * (instances // 2 - 1),
         near_state,
         partner,
-        came[-1],
         flops=PLACING,
     )
     sums = [swapped(value, "inst", i + 1) for i, value in enumerate(sums)]
@@ -338,19 +342,18 @@
         [state.shape, (radial, around)],
         near_state,
     )
-    increment, blade = call(
-        functools.partial(update_kernel, weights[instances // 2], blocks, instances),
-        "update",
+    residual, blade = call(
+        functools.partial(outer_kernel, weights[instances // 2], blocks),
+        "outer",
         [state.shape, (3, 1, node_block)],
         near_state,
         base,
-        step,
         kept,
         *came,
         partner,
-        *sums,
         *edges,
     )
+    (increment,) = call(update_kernel, "update", [state.shape], residual, step, *sums)
     return increment, jnp.transpose(blade, (1, 0, 2))
 
 

time: 16 us -> 15.4 us (0.963)
  waiting for transfers between devices: 3.56 us -> 2.49 us
  Pallas kernels: 2.28 us -> 2.75 us
    ppermute x5, waiting for transfers between devices: 3.55 us -> 2.49 us  [swapped(): lax.ppermute(value, axis, [(i, i ^ bit) for i in range(lax.axis_size(axis...]
    pallas_call x4 -> x5, Pallas kernels: 1.01 us -> 1.48 us  [call(): pl.pallas_call(kernel, out_shape=[jax.ShapeDtypeStruct(shape, jnp.float32...]
  transfers between devices with their start and end apart: 6 -> 6, of which waited for: 4 -> 3; matrix products, arithmetic and copies ran while one was open for 0% -> 0% of each run, Pallas kernels for 9% -> 14%
where the time goes in v7:
time: 15.4 us; the launch traced here: 15.3 us
  starting transfers between devices  9.37 us (61%)
  Pallas kernels  2.75 us (18%)
  waiting for transfers between devices  2.49 us (16%)
  between operations  0.67 us (4%)
    ppermute x5, starting transfers between devices, swapped(): lax.ppermute(value, axis, [(i, i ^ bit) for i in range(lax.axis_size(axis...  5.27 us
    ppermute x1, starting transfers between devices, shifted(): lax.ppermute(value, axis, [(i, (i + s) % count) for i in range(count)])  4.1 us
    ppermute x5, waiting for transfers between devices, swapped(): lax.ppermute(value, axis, [(i, i ^ bit) for i in range(lax.axis_size(axis...  2.49 us
    pallas_call x5, Pallas kernels, call(): pl.pallas_call(kernel, out_shape=[jax.ShapeDtypeStruct(shape, jnp.float32...  1.48 us
    pallas_call x1, Pallas kernels, per_device(): pl.pallas_call(functools.partial(forces_kernel, blocks, node_block), out_...  1.27 us
  transfers between devices with their start and end apart: 6, of which 3 were waited for; matrix products, arithmetic and copies ran while one was open for 0% of the time, Pallas kernels for 14%

profile of v7, /device:TPU:0, one launch (start us, length us, event | category | flops | bytes accessed | tf_op | source)
XLA Modules:
  0.0 15.3 jit_solution(5760175644875927354)
XLA Ops:
  0.6 4.1 %collective-permute-start.4 = (f32[1,4,16,256]{3,2,1,0:T(8,128)}, f32[1,4,16,256]{3,2,1,0:T(8,128)S(1)}, u32[]{:S(2)}, u32[]{:S(2)}) collective-permute-start(f32[1,4,16,256]{3,2,1,0:T(8,128)} %state_hbm.1), channel_id=1, source_target_pairs={{0,2},{1,3},{2,0},{3,1},{4,6},{5,7},{6,4},{7,5},{8,10},{9,11},{10,... | collective-permute-start | bytes 196616 | tf_op jit(solution)/shard_map/ppermute | solution.py:268
  4.7 1.3 %face_forces.1 = (f32[1,4,16,256]{3,2,1,0:T(8,128)S(1)}, f32[2,16,128]{2,1,0:T(8,128)S(1)}, f32[2,16,128]{2,1,0:T(8,128)S(1)}, f32[2,16,128]{2,1,0:T(8,128)S(1)}, f32[2,16,128]{2,1,0:T(8,128)S(1)}) custom-call(f32[1,4,16,256]{3,2,1,0:T(8,128)} %state_hbm.1, s32[6,128]{1,0:T(8,128)} %bitcast.4, s32[6,128]{1,0:T(8,128)} %bitcast.5, f32[3,768]{1,0:T(4,128)} %area_hbm.1), custom_call_target="tpu_custom_call" | custom-call | flops 10000000000 | tf_op jit(solution)/shard_map/face_forces/pallas_call | solution.py:299
  6.0 2.5 %collective-permute-start = (f32[2,16,128]{2,1,0:T(8,128)S(1)}, f32[2,16,128]{2,1,0:T(8,128)S(1)}, u32[]{:S(2)}, u32[]{:S(2)}) collective-permute-start(f32[2,16,128]{2,1,0:T(8,128)S(1)} %get-tuple-element.16), channel_id=1, source_target_pairs={{0,24},{4,28},{8,16},{12,20},{16,8},{20,12},{24,0},{28,4},{1,25},{... | collective-permute-start | bytes 49160 | tf_op jit(solution)/shard_map/ppermute | solution.py:264
  8.5 0.5 %collective-permute-start.1 = (f32[2,16,128]{2,1,0:T(8,128)S(1)}, f32[2,16,128]{2,1,0:T(8,128)S(1)}, u32[]{:S(2)}, u32[]{:S(2)}) collective-permute-start(f32[2,16,128]{2,1,0:T(8,128)S(1)} %get-tuple-element.17), channel_id=1, source_target_pairs={{0,16},{4,20},{8,24},{12,28},{16,0},{20,4},{24,8},{28,12},{1,17},{... | collective-permute-start | bytes 49160 | tf_op jit(solution)/shard_map/ppermute | solution.py:264
  9.0 0.5 %collective-permute-start.2 = (f32[2,16,128]{2,1,0:T(8,128)S(1)}, f32[2,16,128]{2,1,0:T(8,128)S(1)}, u32[]{:S(2)}, u32[]{:S(2)}) collective-permute-start(f32[2,16,128]{2,1,0:T(8,128)S(1)} %get-tuple-element.18), channel_id=1, source_target_pairs={{0,8},{4,12},{8,0},{12,4},{16,24},{20,28},{24,16},{28,20},{1,9},{5... | collective-permute-start | bytes 49160 | tf_op jit(solution)/shard_map/ppermute | solution.py:264
  9.6 0.0 collective-permute-done.4.partner
  9.6 1.6 %collective-permute-start.5 = (f32[1,4,16,256]{3,2,1,0:T(8,128)S(1)}, f32[1,4,16,256]{3,2,1,0:T(8,128)S(1)}, u32[]{:S(2)}, u32[]{:S(2)}) collective-permute-start(f32[1,4,16,256]{3,2,1,0:T(8,128)S(1)} %pair_sums.1), channel_id=1, source_target_pairs={{0,1},{1,0},{2,3},{3,2},{4,5},{5,4},{6,7},{7,6},{8,9},{9,8},{10,11... | collective-permute-start | bytes 196616 | tf_op jit(solution)/shard_map/ppermute | solution.py:264
  11.2 0.0 collective-permute-done.refs_1_
  11.2 1.0 %collective-permute-done.1.refs_2_ = f32[2,16,128]{2,1,0:T(8,128)S(1)} collective-permute-done((f32[2,16,128]{2,1,0:T(8,128)S(1)}, f32[2,16,128]{2,1,0:T(8,128)S(1)}, u32[]{:S(2)}, u32[]{:S(2)}) %collective-permute-start.1) | collective-permute-done | bytes 16416 | tf_op jit(solution)/shard_map/ppermute | solution.py:264
  12.3 0.5 %collective-permute-done.2.refs_3_ = f32[2,16,128]{2,1,0:T(8,128)S(1)} collective-permute-done((f32[2,16,128]{2,1,0:T(8,128)S(1)}, f32[2,16,128]{2,1,0:T(8,128)S(1)}, u32[]{:S(2)}, u32[]{:S(2)}) %collective-permute-start.2) | collective-permute-done | bytes 16416 | tf_op jit(solution)/shard_map/ppermute | solution.py:264
  12.8 0.1 collective-permute-start.3
  12.9 0.2 %flux.1 = (f32[1,4,16,256]{3,2,1,0:T(8,128)S(1)}, f32[16,256]{1,0:T(8,128)S(1)}) custom-call(f32[1,4,16,256]{3,2,1,0:T(8,128)S(1)} %get-tuple-element.13.state), custom_call_target="tpu_custom_call" | custom-call | tf_op jit(solution)/shard_map/flux/pallas_call | solution.py:276
  13.1 1.0 %collective-permute-done.3.came = f32[1,16,128]{2,1,0:T(8,128)S(1)} collective-permute-done((f32[1,16,128]{2,1,0:T(8,128)S(1)}, f32[1,16,128]{2,1,0:T(8,128)S(1)}, u32[]{:S(2)}, u32[]{:S(2)}) %collective-permute-start.3) | collective-permute-done | bytes 8224 | tf_op jit(solution)/shard_map/ppermute | solution.py:264
  14.0 0.6 %outer.1 = (f32[1,4,16,256]{3,2,1,0:T(8,128)S(1)}, f32[3,1,512]{2,1,0:T(1,128)}) custom-call(f32[1,4,16,256]{3,2,1,0:T(8,128)S(1)} %get-tuple-element.13.state, f32[1,4,16,256]{3,2,1,0:T(8,128)S(1)} %get-tuple-element.14.base, f32[1,16,128]{2,1,0:T(8,128)S(1)} %get-tuple-element.19.kept, f32[1,16,128]{2,1,0:T(8,128)S(1)} %collective-permute-done.3.came, ...), custom_call_target="tpu_custom_call" | custom-call | tf_op jit(solution)/shard_map/outer/pallas_call | solution.py:276
  14.6 0.0 collective-permute-done.5.refs_0_
  14.6 0.6 %update.1 = f32[1,4,16,256]{3,2,1,0:T(8,128)} custom-call(f32[1,4,16,256]{3,2,1,0:T(8,128)S(1)} %get-tuple-element.21.residual, f32[16,256]{1,0:T(8,128)S(1)} %get-tuple-element.22.step, f32[1,4,16,256]{3,2,1,0:T(8,128)S(1)} %collective-permute-done.5.refs_0_), custom_call_target="tpu_custom_call" | custom-call | tf_op jit(solution)/shard_map/update/pallas_call | solution.py:276
  (2 shorter events, 0.0 us)
Async XLA Ops:
  0.6 8.9 %collective-permute-start.4 = (f32[1,4,16,256]{3,2,1,0:T(8,128)}, f32[1,4,16,256]{3,2,1,0:T(8,128)S(1)}, u32[]{:S(2)}, u32[]{:S(2)}) collective-permute-start(f32[1,4,16,256]{3,2,1,0:T(8,128)} %state_hbm.1), channel_id=1, source_target_pairs={{0,2},{1,3},{2,0},{3,1},{4,6},{5,7},{6,4},{7,5},{8,10},{9,11},{10,... | collective-permute-start | bytes 196616 | tf_op jit(solution)/shard_map/ppermute | solution.py:268
  6.0 5.2 %collective-permute-start = (f32[2,16,128]{2,1,0:T(8,128)S(1)}, f32[2,16,128]{2,1,0:T(8,128)S(1)}, u32[]{:S(2)}, u32[]{:S(2)}) collective-permute-start(f32[2,16,128]{2,1,0:T(8,128)S(1)} %get-tuple-element.16), channel_id=1, source_target_pairs={{0,24},{4,28},{8,16},{12,20},{16,8},{20,12},{24,0},{28,4},{1,25},{... | collective-permute-start | bytes 49160 | tf_op jit(solution)/shard_map/ppermute | solution.py:264
  8.5 3.7 %collective-permute-start.1 = (f32[2,16,128]{2,1,0:T(8,128)S(1)}, f32[2,16,128]{2,1,0:T(8,128)S(1)}, u32[]{:S(2)}, u32[]{:S(2)}) collective-permute-start(f32[2,16,128]{2,1,0:T(8,128)S(1)} %get-tuple-element.17), channel_id=1, source_target_pairs={{0,16},{4,20},{8,24},{12,28},{16,0},{20,4},{24,8},{28,12},{1,17},{... | collective-permute-start | bytes 49160 | tf_op jit(solution)/shard_map/ppermute | solution.py:264
  9.0 3.7 %collective-permute-start.2 = (f32[2,16,128]{2,1,0:T(8,128)S(1)}, f32[2,16,128]{2,1,0:T(8,128)S(1)}, u32[]{:S(2)}, u32[]{:S(2)}) collective-permute-start(f32[2,16,128]{2,1,0:T(8,128)S(1)} %get-tuple-element.18), channel_id=1, source_target_pairs={{0,8},{4,12},{8,0},{12,4},{16,24},{20,28},{24,16},{28,20},{1,9},{5... | collective-permute-start | bytes 49160 | tf_op jit(solution)/shard_map/ppermute | solution.py:264
  9.6 5.0 %collective-permute-start.5 = (f32[1,4,16,256]{3,2,1,0:T(8,128)S(1)}, f32[1,4,16,256]{3,2,1,0:T(8,128)S(1)}, u32[]{:S(2)}, u32[]{:S(2)}) collective-permute-start(f32[1,4,16,256]{3,2,1,0:T(8,128)S(1)} %pair_sums.1), channel_id=1, source_target_pairs={{0,1},{1,0},{2,3},{3,2},{4,5},{5,4},{6,7},{7,6},{8,9},{9,8},{10,11... | collective-permute-start | bytes 196616 | tf_op jit(solution)/shard_map/ppermute | solution.py:264
  12.8 1.2 %collective-permute-start.3 = (f32[1,16,128]{2,1,0:T(8,128)S(1)}, f32[1,16,128]{2,1,0:T(8,128)S(1)}, u32[]{:S(2)}, u32[]{:S(2)}) collective-permute-start(f32[1,16,128]{2,1,0:T(8,128)S(1)} %get-tuple-element.20), channel_id=1, source_target_pairs={{0,4},{4,0},{8,12},{12,8},{16,20},{20,16},{24,28},{28,24},{1,5},{5... | collective-permute-start | bytes 24584 | tf_op jit(solution)/shard_map/ppermute | solution.py:264

commit v8 on v7

--- a/solution.py
+++ b/solution.py
@@ -37,18 +37,11 @@
     return inverse, vr, vc, p
 
 
-def forces_kernel(blocks, node_block, state_hbm, cell_hbm, node_hbm, area_hbm, state, *refs):
-    *outs, cell, node, area, sems = refs
-    loads = [
-        pltpu.make_async_copy(source, target, sems.at[i])
-        for i, (source, target) in enumerate(
-            ((state_hbm, state), (cell_hbm, cell), (node_hbm, node), (area_hbm, area))
-        )
-    ]
-    for load in loads:
-        load.start()
-    for load in loads:
-        load.wait()
+def own_kernel(high, out):
+    out[...] = jnp.full(out.shape, lax.axis_index("space") * high, jnp.int32)
+
+
+def forces_kernel(node_block, own, state, cell, node, area, *outs):
     radial, around = state.shape[2:]
     faces = cell.shape[0] * LANES
     chunks = faces // LANES
@@ -73,7 +66,7 @@
     nodes = jnp.concatenate([node[c : c + 1, :] for c in range(chunks)], axis=1)
 
     high = node_block // LANES
-    place = nodes // LANES ^ lax.axis_index("space") * high
+    place = nodes // LANES ^ jnp.broadcast_to(own[0:1, 0:1], nodes.shape)
     low = nodes % LANES
     pick_low = (
         lax.broadcasted_iota(jnp.int32, (LANES, faces), 0) == jnp.broadcast_to(low, (LANES, faces))
@@ -103,7 +96,8 @@
         return result.reshape(count, ROWS, LANES)
 
     ordered = outs[:1] + outs[:0:-1]
-    size = blocks // len(outs)
+    size = outs[0].shape[0]
+    blocks = size * len(outs)
     if blocks <= 16:
         result = dense(0, blocks)
         for i, out in enumerate(ordered):
@@ -189,9 +183,8 @@
 
 
 def outer_kernel(weight, blocks, state, base, kept, came, partner, *refs):
-    *edges, residual, blade = refs
+    *edges, residual, total = refs
     radial, around = state.shape[2:]
-    high = blade.shape[2] // LANES
     if blocks == RIDING:
         me = lax.axis_index("space")
         known = [kept[0, EDGE:, :], came[0, EDGE:, :]]
@@ -239,17 +232,18 @@
             outer.insert(1, jnp.zeros((radial, middle), jnp.float32))
         residual[0, c] = base[0, c] + weight * partner[0, c] + jnp.concatenate(outer, axis=1)
 
-    total = kept[0] + came[0]
+    total[...] = kept[0] + came[0]
+
+
+def update_kernel(residual, step, total, *refs):
+    *sums, increment, blade = refs
+    high = blade.shape[2] // LANES
     for k in range(3):
         for h in range(high):
             blade[k, :, pl.ds(h * LANES, LANES)] = total[k * high + h : k * high + h + 1, :]
-
-
-def update_kernel(residual, step, *refs):
-    *sums, increment = refs
     for c in range(residual.shape[1]):
-        total = functools.reduce(jnp.add, [ref[0, c] for ref in (residual, *sums)])
-        increment[0, c] = -step[...] * total
+        change = functools.reduce(jnp.add, [ref[0, c] for ref in (residual, *sums)])
+        increment[0, c] = -step[...] * change
 
 
 def per_device(node_block, state, face_cell, face_node, face_area):
@@ -272,10 +266,10 @@
             swapped(value, "space", (len(sent) - i) * size) for i, value in enumerate(sent)
         ]
 
-    def call(kernel, name, shapes, *operands, flops=0):
+    def call(kernel, name, shapes, *operands, flops=0, dtype=jnp.float32):
         return pl.pallas_call(
             kernel,
-            out_shape=[jax.ShapeDtypeStruct(shape, jnp.float32) for shape in shapes],
+            out_shape=[jax.ShapeDtypeStruct(shape, dtype) for shape in shapes],
             in_specs=[vmem] * len(operands),
             out_specs=[vmem] * len(shapes),
             compiler_params=params,
@@ -286,27 +280,27 @@
     weights = spectral_row(instances)
     partner = shifted(state, "inst", instances // 2)
 
-    faces = (
+    riding = blocks == RIDING
+    steps = [4, 2] if riding else [2] * (blocks.bit_length() - 1)
+    size = blocks // steps[0]
+    (own,) = call(
+        functools.partial(own_kernel, node_block // LANES),
+        "own",
+        [(8, LANES)],
+        dtype=jnp.int32,
+        flops=PLACING,
+    )
+    kept, *sent = call(
+        functools.partial(forces_kernel, node_block),
+        "face_forces",
+        [(size, ROWS, LANES)] * steps[0],
+        own,
         state,
         face_cell.reshape(chunks, LANES),
         face_node.reshape(chunks, LANES),
         face_area,
-    )
-    riding = blocks == RIDING
-    steps = [4, 2] if riding else [2] * (blocks.bit_length() - 1)
-    size = blocks // steps[0]
-    block = jax.ShapeDtypeStruct((size, ROWS, LANES), jnp.float32)
-    near_state, kept, *sent = pl.pallas_call(
-        functools.partial(forces_kernel, blocks, node_block),
-        out_shape=[jax.ShapeDtypeStruct(state.shape, jnp.float32)] + [block] * steps[0],
-        in_specs=[pl.BlockSpec(memory_space=pltpu.HBM)] * 4,
-        out_specs=[vmem] * (1 + steps[0]),
-        scratch_shapes=[pltpu.VMEM(x.shape, x.dtype) for x in faces[1:]]
-        + [pltpu.SemaphoreType.DMA((4,))],
-        compiler_params=params,
-        cost_estimate=pl.CostEstimate(flops=PLACING, bytes_accessed=0, transcendentals=0),
-        name="face_forces",
-    )(*(pltpu.with_memory_space_constraint(x, pltpu.HBM) for x in faces))
+        flops=PLACING,
+    )
 
     edges = []
     if not riding:
@@ -318,7 +312,7 @@
         functools.partial(pair_kernel, weights, instances),
         "pair_sums",
         [state.shape] * (instances // 2 - 1),
-        near_state,
+        state,
         partner,
         flops=PLACING,
     )
@@ -340,20 +334,28 @@
         functools.partial(flux_kernel, weights[0], instances),
         "flux",
         [state.shape, (radial, around)],
-        near_state,
-    )
-    residual, blade = call(
+        state,
+    )
+    residual, total = call(
         functools.partial(outer_kernel, weights[instances // 2], blocks),
         "outer",
-        [state.shape, (3, 1, node_block)],
-        near_state,
+        [state.shape, (ROWS, LANES)],
+        state,
         base,
         kept,
         *came,
         partner,
         *edges,
     )
-    (increment,) = call(update_kernel, "update", [state.shape], residual, step, *sums)
+    increment, blade = call(
+        update_kernel,
+        "update",
+        [state.shape, (3, 1, node_block)],
+        residual,
+        step,
+        total,
+        *sums,
+    )
     return increment, jnp.transpose(blade, (1, 0, 2))
 
 

time: 15.4 us -> 14.2 us (0.922)
  Pallas kernels: 2.75 us -> 1.41 us
    pallas_call x6 -> x7, Pallas kernels: 2.75 us -> 1.41 us  [call(): pl.pallas_call(kernel, out_shape=[jax.ShapeDtypeStruct(shape, dtype) for...]
  transfers between devices with their start and end apart: 6 -> 6, of which waited for: 3 -> 3; matrix products, arithmetic and copies ran while one was open for 0% -> 0% of each run, Pallas kernels for 14% -> 5%
where the time goes in v8:
time: 14.2 us; the launch traced here: 14 us
  starting transfers between devices  9.37 us (66%)
  waiting for transfers between devices  2.49 us (18%)
  Pallas kernels  1.41 us (10%)
  between operations  0.73 us (5%)
    ppermute x5, starting transfers between devices, swapped(): lax.ppermute(value, axis, [(i, i ^ bit) for i in range(lax.axis_size(axis...  5.27 us
    ppermute x1, starting transfers between devices, shifted(): lax.ppermute(value, axis, [(i, (i + s) % count) for i in range(count)])  4.1 us
    ppermute x5, waiting for transfers between devices, swapped(): lax.ppermute(value, axis, [(i, i ^ bit) for i in range(lax.axis_size(axis...  2.49 us
    pallas_call x7, Pallas kernels, call(): pl.pallas_call(kernel, out_shape=[jax.ShapeDtypeStruct(shape, dtype) for...  1.41 us
  transfers between devices with their start and end apart: 6, of which 3 were waited for; matrix products, arithmetic and copies ran while one was open for 0% of the time, Pallas kernels for 5%

profile of v8, /device:TPU:0, one launch (start us, length us, event | category | flops | bytes accessed | tf_op | source)
XLA Modules:
  0.0 14.0 jit_solution(9003114873645066294)
XLA Ops:
  0.6 0.0 copy-start
  0.6 0.0 copy-start.2
  0.7 0.0 copy-start.3
  0.7 0.0 copy-start.1
  0.7 4.1 %collective-permute-start.4 = (f32[1,4,16,256]{3,2,1,0:T(8,128)}, f32[1,4,16,256]{3,2,1,0:T(8,128)S(1)}, u32[]{:S(2)}, u32[]{:S(2)}) collective-permute-start(f32[1,4,16,256]{3,2,1,0:T(8,128)} %state.7), channel_id=1, source_target_pairs={{0,2},{1,3},{2,0},{3,1},{4,6},{5,7},{6,4},{7,5},{8,10},{9,11},{10,... | collective-permute-start | bytes 196616 | tf_op jit(solution)/shard_map/ppermute | solution.py:262
  4.8 0.0 copy-done
  4.8 0.0 copy-done.2
  4.8 0.0 copy-done.3
  4.8 0.0 copy-done.1
  4.8 0.4 %face_forces.1 = (f32[2,16,128]{2,1,0:T(8,128)S(1)}, f32[2,16,128]{2,1,0:T(8,128)S(1)}, f32[2,16,128]{2,1,0:T(8,128)S(1)}, f32[2,16,128]{2,1,0:T(8,128)S(1)}) custom-call(s32[8,128]{1,0:T(8,128)S(1)} %own.1, f32[1,4,16,256]{3,2,1,0:T(8,128)S(1)} %copy-done, s32[6,128]{1,0:T(8,128)S(1)} %bitcast.3, s32[6,128]{1,0:T(8,128)S(1)} %bitcast.4, f32[3,768]{1,0:T(4,128)S(1)} %copy-done.1), custom_call_target="tpu_custom_call" | custom-call | flops 10000000000 | tf_op jit(solution)/shard_map/face_forces/pallas_call | solution.py:270
  5.2 2.5 %collective-permute-start = (f32[2,16,128]{2,1,0:T(8,128)S(1)}, f32[2,16,128]{2,1,0:T(8,128)S(1)}, u32[]{:S(2)}, u32[]{:S(2)}) collective-permute-start(f32[2,16,128]{2,1,0:T(8,128)S(1)} %get-tuple-element.16), channel_id=1, source_target_pairs={{0,24},{4,28},{8,16},{12,20},{16,8},{20,12},{24,0},{28,4},{1,25},{... | collective-permute-start | bytes 49160 | tf_op jit(solution)/shard_map/ppermute | solution.py:258
  7.7 0.5 %collective-permute-start.1 = (f32[2,16,128]{2,1,0:T(8,128)S(1)}, f32[2,16,128]{2,1,0:T(8,128)S(1)}, u32[]{:S(2)}, u32[]{:S(2)}) collective-permute-start(f32[2,16,128]{2,1,0:T(8,128)S(1)} %get-tuple-element.17), channel_id=1, source_target_pairs={{0,16},{4,20},{8,24},{12,28},{16,0},{20,4},{24,8},{28,12},{1,17},{... | collective-permute-start | bytes 49160 | tf_op jit(solution)/shard_map/ppermute | solution.py:258
  8.2 0.5 %collective-permute-start.2 = (f32[2,16,128]{2,1,0:T(8,128)S(1)}, f32[2,16,128]{2,1,0:T(8,128)S(1)}, u32[]{:S(2)}, u32[]{:S(2)}) collective-permute-start(f32[2,16,128]{2,1,0:T(8,128)S(1)} %get-tuple-element.18), channel_id=1, source_target_pairs={{0,8},{4,12},{8,0},{12,4},{16,24},{20,28},{24,16},{28,20},{1,9},{5... | collective-permute-start | bytes 49160 | tf_op jit(solution)/shard_map/ppermute | solution.py:258
  8.7 0.0 collective-permute-done.4.partner
  8.8 1.6 %collective-permute-start.5 = (f32[1,4,16,256]{3,2,1,0:T(8,128)S(1)}, f32[1,4,16,256]{3,2,1,0:T(8,128)S(1)}, u32[]{:S(2)}, u32[]{:S(2)}) collective-permute-start(f32[1,4,16,256]{3,2,1,0:T(8,128)S(1)} %pair_sums.1), channel_id=1, source_target_pairs={{0,1},{1,0},{2,3},{3,2},{4,5},{5,4},{6,7},{7,6},{8,9},{9,8},{10,11... | collective-permute-start | bytes 196616 | tf_op jit(solution)/shard_map/ppermute | solution.py:258
  10.4 0.0 collective-permute-done.refs_1_
  10.4 1.0 %collective-permute-done.1.refs_2_ = f32[2,16,128]{2,1,0:T(8,128)S(1)} collective-permute-done((f32[2,16,128]{2,1,0:T(8,128)S(1)}, f32[2,16,128]{2,1,0:T(8,128)S(1)}, u32[]{:S(2)}, u32[]{:S(2)}) %collective-permute-start.1) | collective-permute-done | bytes 16416 | tf_op jit(solution)/shard_map/ppermute | solution.py:258
  11.4 0.5 %collective-permute-done.2.refs_3_ = f32[2,16,128]{2,1,0:T(8,128)S(1)} collective-permute-done((f32[2,16,128]{2,1,0:T(8,128)S(1)}, f32[2,16,128]{2,1,0:T(8,128)S(1)}, u32[]{:S(2)}, u32[]{:S(2)}) %collective-permute-start.2) | collective-permute-done | bytes 16416 | tf_op jit(solution)/shard_map/ppermute | solution.py:258
  12.0 0.1 collective-permute-start.3
  12.0 0.2 %flux.1 = (f32[1,4,16,256]{3,2,1,0:T(8,128)S(1)}, f32[16,256]{1,0:T(8,128)S(1)}) custom-call(f32[1,4,16,256]{3,2,1,0:T(8,128)S(1)} %copy-done), custom_call_target="tpu_custom_call" | custom-call | tf_op jit(solution)/shard_map/flux/pallas_call | solution.py:270
  12.2 1.0 %collective-permute-done.3.came = f32[1,16,128]{2,1,0:T(8,128)S(1)} collective-permute-done((f32[1,16,128]{2,1,0:T(8,128)S(1)}, f32[1,16,128]{2,1,0:T(8,128)S(1)}, u32[]{:S(2)}, u32[]{:S(2)}) %collective-permute-start.3) | collective-permute-done | bytes 8224 | tf_op jit(solution)/shard_map/ppermute | solution.py:258
  13.2 0.2 %outer.1 = (f32[1,4,16,256]{3,2,1,0:T(8,128)S(1)}, f32[16,128]{1,0:T(8,128)S(1)}) custom-call(f32[1,4,16,256]{3,2,1,0:T(8,128)S(1)} %copy-done, f32[1,4,16,256]{3,2,1,0:T(8,128)S(1)} %get-tuple-element.14.base, f32[1,16,128]{2,1,0:T(8,128)S(1)} %get-tuple-element.19.kept, f32[1,16,128]{2,1,0:T(8,128)S(1)} %collective-permute-done.3.came, ...), custom_call_target="tpu_custom_call" | custom-call | tf_op jit(solution)/shard_map/outer/pallas_call | solution.py:270
  13.4 0.0 collective-permute-done.5.refs_0_
  13.4 0.7 %update.1 = (f32[1,4,16,256]{3,2,1,0:T(8,128)}, f32[3,1,512]{2,1,0:T(1,128)}) custom-call(f32[1,4,16,256]{3,2,1,0:T(8,128)S(1)} %get-tuple-element.21.residual, f32[16,256]{1,0:T(8,128)S(1)} %get-tuple-element.22.step, f32[16,128]{1,0:T(8,128)S(1)} %get-tuple-element.23.total, f32[1,4,16,256]{3,2,1,0:T(8,128)S(1)} %collective-permute-done.5.refs_0_), custom_call_target="tpu_custom_call" | custom-call | tf_op jit(solution)/shard_map/update/pallas_call | solution.py:270
  (3 shorter events, 0.0 us)
Async XLA Ops:
  0.6 4.1 %copy-start = (f32[1,4,16,256]{3,2,1,0:T(8,128)S(1)}, f32[1,4,16,256]{3,2,1,0:T(8,128)}, u32[]{:S(2)}) copy-start(f32[1,4,16,256]{3,2,1,0:T(8,128)} %state.7) | copy-start | bytes 196612
  0.6 4.1 %copy-start.2 = (s32[768]{0:T(1024)S(1)}, s32[768]{0:T(1024)}, u32[]{:S(2)}) copy-start(s32[768]{0:T(1024)} %param.5) | copy-start | bytes 9220
  0.7 4.1 %copy-start.3 = (s32[768]{0:T(1024)S(1)}, s32[768]{0:T(1024)}, u32[]{:S(2)}) copy-start(s32[768]{0:T(1024)} %param.6) | copy-start | bytes 9220
  0.7 4.1 %copy-start.1 = (f32[3,768]{1,0:T(4,128)S(1)}, f32[3,768]{1,0:T(4,128)}, u32[]{:S(2)}) copy-start(f32[3,768]{1,0:T(4,128)} %area.1) | copy-start | bytes 27652
  0.7 8.1 %collective-permute-start.4 = (f32[1,4,16,256]{3,2,1,0:T(8,128)}, f32[1,4,16,256]{3,2,1,0:T(8,128)S(1)}, u32[]{:S(2)}, u32[]{:S(2)}) collective-permute-start(f32[1,4,16,256]{3,2,1,0:T(8,128)} %state.7), channel_id=1, source_target_pairs={{0,2},{1,3},{2,0},{3,1},{4,6},{5,7},{6,4},{7,5},{8,10},{9,11},{10,... | collective-permute-start | bytes 196616 | tf_op jit(solution)/shard_map/ppermute | solution.py:262
  5.2 5.2 %collective-permute-start = (f32[2,16,128]{2,1,0:T(8,128)S(1)}, f32[2,16,128]{2,1,0:T(8,128)S(1)}, u32[]{:S(2)}, u32[]{:S(2)}) collective-permute-start(f32[2,16,128]{2,1,0:T(8,128)S(1)} %get-tuple-element.16), channel_id=1, source_target_pairs={{0,24},{4,28},{8,16},{12,20},{16,8},{20,12},{24,0},{28,4},{1,25},{... | collective-permute-start | bytes 49160 | tf_op jit(solution)/shard_map/ppermute | solution.py:258
  7.7 3.7 %collective-permute-start.1 = (f32[2,16,128]{2,1,0:T(8,128)S(1)}, f32[2,16,128]{2,1,0:T(8,128)S(1)}, u32[]{:S(2)}, u32[]{:S(2)}) collective-permute-start(f32[2,16,128]{2,1,0:T(8,128)S(1)} %get-tuple-element.17), channel_id=1, source_target_pairs={{0,16},{4,20},{8,24},{12,28},{16,0},{20,4},{24,8},{28,12},{1,17},{... | collective-permute-start | bytes 49160 | tf_op jit(solution)/shard_map/ppermute | solution.py:258
  8.2 3.7 %collective-permute-start.2 = (f32[2,16,128]{2,1,0:T(8,128)S(1)}, f32[2,16,128]{2,1,0:T(8,128)S(1)}, u32[]{:S(2)}, u32[]{:S(2)}) collective-permute-start(f32[2,16,128]{2,1,0:T(8,128)S(1)} %get-tuple-element.18), channel_id=1, source_target_pairs={{0,8},{4,12},{8,0},{12,4},{16,24},{20,28},{24,16},{28,20},{1,9},{5... | collective-permute-start | bytes 49160 | tf_op jit(solution)/shard_map/ppermute | solution.py:258
  8.8 4.6 %collective-permute-start.5 = (f32[1,4,16,256]{3,2,1,0:T(8,128)S(1)}, f32[1,4,16,256]{3,2,1,0:T(8,128)S(1)}, u32[]{:S(2)}, u32[]{:S(2)}) collective-permute-start(f32[1,4,16,256]{3,2,1,0:T(8,128)S(1)} %pair_sums.1), channel_id=1, source_target_pairs={{0,1},{1,0},{2,3},{3,2},{4,5},{5,4},{6,7},{7,6},{8,9},{9,8},{10,11... | collective-permute-start | bytes 196616 | tf_op jit(solution)/shard_map/ppermute | solution.py:258
  12.0 1.2 %collective-permute-start.3 = (f32[1,16,128]{2,1,0:T(8,128)S(1)}, f32[1,16,128]{2,1,0:T(8,128)S(1)}, u32[]{:S(2)}, u32[]{:S(2)}) collective-permute-start(f32[1,16,128]{2,1,0:T(8,128)S(1)} %get-tuple-element.20), channel_id=1, source_target_pairs={{0,4},{4,0},{8,12},{12,8},{16,20},{20,16},{24,28},{28,24},{1,5},{5... | collective-permute-start | bytes 24584 | tf_op jit(solution)/shard_map/ppermute | solution.py:258

commit v9 on v8

--- a/solution.py
+++ b/solution.py
@@ -37,11 +37,12 @@
     return inverse, vr, vc, p
 
 
-def own_kernel(high, out):
-    out[...] = jnp.full(out.shape, lax.axis_index("space") * high, jnp.int32)
-
-
-def forces_kernel(node_block, own, state, cell, node, area, *outs):
+def own_kernel(high, riding, out):
+    me = lax.axis_index("space")
+    out[...] = jnp.full(out.shape, (me - me % 2 if riding else me) * high, jnp.int32)
+
+
+def forces_kernel(node_block, riding, own, state, cell, node, area, *outs):
     radial, around = state.shape[2:]
     faces = cell.shape[0] * LANES
     chunks = faces // LANES
@@ -95,15 +96,14 @@
             result = product if result is None else result + product
         return result.reshape(count, ROWS, LANES)
 
-    ordered = outs[:1] + outs[:0:-1]
     size = outs[0].shape[0]
     blocks = size * len(outs)
     if blocks <= 16:
         result = dense(0, blocks)
-        for i, out in enumerate(ordered):
+        for i, out in enumerate(outs):
             out[...] = result[i * size : (i + 1) * size]
     else:
-        for i, out in enumerate(ordered):
+        for i, out in enumerate(outs):
 
             @pl.loop(0, size // 8)
             def _(g):
@@ -113,19 +113,46 @@
     turned = jnp.concatenate([flat[:, around - LANES :], flat[:, :LANES]], axis=0).T
     lane = lax.broadcasted_iota(jnp.int32, (1, LANES), 1)
     edge = jnp.where(lane < LANES // 2, turned[LANES - 1 :, :], turned[:1, :])
-    for out in outs:
-        out[0, EDGE : EDGE + 1, :] = edge
-
-
-def halving_kernel(arrived, riding, *refs):
-    outs = refs[arrived:]
+    if riding:
+        core = lax.axis_index("space") % 2
+        row = lax.broadcasted_iota(jnp.int32, (2, LANES), 0)
+        outs[0][0, EDGE : EDGE + 2, :] = jnp.where(row == core, edge, 0.0)
+    else:
+        outs[0][0, EDGE : EDGE + 1, :] = edge
+
+
+def chip_kernel(blocks, came, _, *outs):
+    edges = blocks[0, EDGE:, :] + came[0, EDGE:, :]
+    for out, pair in zip(outs, (0, 3, 2, 1)):
+        for b in range(2):
+            out[b] = blocks[2 * pair + b] + came[2 * pair + b]
+        out[0, EDGE:, :] = edges
+
+
+def plane_kernel(own, diagonal, y, x, *outs):
+    chips = (own, x, y, diagonal)
+    me = lax.axis_index("space")
+    first = me - me % 2
+    lane = lax.broadcasted_iota(jnp.int32, (1, LANES), 1)
+    for core, out in enumerate(outs):
+        out[...] = functools.reduce(jnp.add, [ref[core] for ref in chips])
+        device = first + core
+        around = (device + (RIDING - 1 if core == 0 else 1)) % RIDING
+        place = (around ^ first) // 2
+        there = own[0, EDGE + 1 - core : EDGE + 2 - core, :]
+        for i, ref in enumerate(chips[1:], 1):
+            row = ref[0, EDGE + 1 - core : EDGE + 2 - core, :]
+            there = jnp.where(place == i, row, there)
+        here = own[0, EDGE + 1 - core : EDGE + 2 - core, :]
+        before, after = (there, here) if core == 0 else (here, there)
+        out[EDGE : EDGE + 1, :] = jnp.where(lane < LANES // 2, before, after)
+
+
+def halving_kernel(kept, came, *outs):
     size = outs[0].shape[0]
     for i, out in enumerate(outs):
         for b in range(size):
-            out[b] = functools.reduce(jnp.add, [ref[i * size + b] for ref in refs[:arrived]])
-        if riding:
-            for j, ref in enumerate(refs[:arrived]):
-                out[0, EDGE + j : EDGE + j + 1, :] = ref[0, EDGE : EDGE + 1, :]
+            out[b] = kept[i * size + b] + came[i * size + b]
 
 
 def pair_kernel(weights, instances, state, partner, *outs):
@@ -182,27 +209,18 @@
         base[0, c] = residual + (upper - lower)
 
 
-def outer_kernel(weight, blocks, state, base, kept, came, partner, *refs):
+def outer_kernel(weight, state, base, kept, came, partner, *refs):
     *edges, residual, total = refs
     radial, around = state.shape[2:]
-    if blocks == RIDING:
-        me = lax.axis_index("space")
-        known = [kept[0, EDGE:, :], came[0, EDGE:, :]]
-        known = jnp.concatenate(known, axis=0)
-        row = lax.broadcasted_iota(jnp.int32, known.shape, 0)
-
-        def edge_of(device):
-            relative = device ^ me
-            half = RIDING // 2
-            place = (half - relative // 2) % half + (relative % 2) * half
-            return jnp.sum(jnp.where(row == place, known, 0.0), axis=0, keepdims=True)
-
-        before = edge_of((me + blocks - 1) % blocks)
-        after = edge_of((me + 1) % blocks)
+    if edges:
+        before, after = (ref[0:1, :] for ref in edges)
+        lane = lax.broadcasted_iota(jnp.int32, (1, LANES), 1)
+        edge = jnp.where(lane < LANES // 2, before, after)
+        total[...] = kept[0] + came[0]
     else:
-        before, after = (ref[0:1, :] for ref in edges)
-    lane = lax.broadcasted_iota(jnp.int32, (1, LANES), 1)
-    edge = jnp.where(lane < LANES // 2, before, after)
+        held = jnp.where(lax.axis_index("space") % 2 == 1, kept[...], came[...])
+        edge = held[EDGE : EDGE + 1, :]
+        total[...] = held
     columns = jnp.broadcast_to(edge, (LANES, LANES)).T
 
     lane = lax.broadcasted_iota(jnp.int32, (radial, LANES), 1)
@@ -232,8 +250,6 @@
             outer.insert(1, jnp.zeros((radial, middle), jnp.float32))
         residual[0, c] = base[0, c] + weight * partner[0, c] + jnp.concatenate(outer, axis=1)
 
-    total[...] = kept[0] + came[0]
-
 
 def update_kernel(residual, step, total, *refs):
     *sums, increment, blade = refs
@@ -261,10 +277,9 @@
         count = lax.axis_size(axis)
         return lax.ppermute(value, axis, [(i, (i + s) % count) for i in range(count)])
 
-    def exchanged(sent, size):
-        return [
-            swapped(value, "space", (len(sent) - i) * size) for i, value in enumerate(sent)
-        ]
+    def moved(value, core, bit):
+        pairs = [(i, i ^ bit) for i in range(blocks) if i % 2 == core]
+        return lax.ppermute(value, "space", pairs)
 
     def call(kernel, name, shapes, *operands, flops=0, dtype=jnp.float32):
         return pl.pallas_call(
@@ -281,19 +296,18 @@
     partner = shifted(state, "inst", instances // 2)
 
     riding = blocks == RIDING
-    steps = [4, 2] if riding else [2] * (blocks.bit_length() - 1)
-    size = blocks // steps[0]
+    parts = 1 if riding else 2
     (own,) = call(
-        functools.partial(own_kernel, node_block // LANES),
+        functools.partial(own_kernel, node_block // LANES, riding),
         "own",
         [(8, LANES)],
         dtype=jnp.int32,
         flops=PLACING,
     )
-    kept, *sent = call(
-        functools.partial(forces_kernel, node_block),
+    dense = call(
+        functools.partial(forces_kernel, node_block, riding),
         "face_forces",
-        [(size, ROWS, LANES)] * steps[0],
+        [(blocks // parts, ROWS, LANES)] * parts,
         own,
         state,
         face_cell.reshape(chunks, LANES),
@@ -302,12 +316,33 @@
         flops=PLACING,
     )
 
+    base, step = call(
+        functools.partial(flux_kernel, weights[0], instances),
+        "flux",
+        [state.shape, (radial, around)],
+        state,
+        flops=PLACING,
+    )
     edges = []
-    if not riding:
-        row = jnp.broadcast_to(kept[0, EDGE : EDGE + 1, :], (8, LANES))
+    if riding:
+        came = moved(dense[0], 0, 1)
+        mine, *sent = call(chip_kernel, "chip_sums", [(2, ROWS, LANES)] * 4, dense[0], came, step)
+        came = [moved(value, 1, bit) for value, bit in zip(sent, (6, 4, 2))]
+        block, kept = call(
+            plane_kernel, "plane_sums", [(ROWS, LANES)] * 2, mine, *came, flops=PLACING
+        )
+        came = moved(block, 1, 1)
+    else:
+        row = jnp.broadcast_to(dense[0][0, EDGE : EDGE + 1, :], (8, LANES))
         edges = [shifted(row, "space", 1), shifted(row, "space", blocks - 1)]
-
-    came = exchanged(sent, size)
+        size = blocks // 2
+        kept, came = dense[0], swapped(dense[1], "space", size)
+        while size > 1:
+            size //= 2
+            shapes = [(size, ROWS, LANES)] * 2
+            kept, sent = call(halving_kernel, "halving", shapes, kept, came)
+            came = swapped(sent, "space", size)
+
     sums = call(
         functools.partial(pair_kernel, weights, instances),
         "pair_sums",
@@ -318,32 +353,14 @@
     )
     sums = [swapped(value, "inst", i + 1) for i, value in enumerate(sums)]
 
-    for step in steps[1:]:
-        size //= step
-        kept, *sent = call(
-            functools.partial(halving_kernel, 1 + len(came), riding),
-            "halving",
-            [(size, ROWS, LANES)] * step,
-            kept,
-            *came,
-            flops=PLACING,
-        )
-        came = exchanged(sent, size)
-
-    base, step = call(
-        functools.partial(flux_kernel, weights[0], instances),
-        "flux",
-        [state.shape, (radial, around)],
-        state,
-    )
     residual, total = call(
-        functools.partial(outer_kernel, weights[instances // 2], blocks),
+        functools.partial(outer_kernel, weights[instances // 2]),
         "outer",
         [state.shape, (ROWS, LANES)],
         state,
         base,
         kept,
-        *came,
+        came,
         partner,
         *edges,
     )

time: 14.2 us -> 21.6 us (1.52)
  waiting for transfers between devices: 2.49 us -> 8.66 us
  starting transfers between devices: 9.37 us -> 10.5 us
    ppermute x0 -> x5, waiting for transfers between devices: none -> 8.66 us  [moved(): return lax.ppermute(value, 'space', pairs)]
    ppermute x0 -> x5, starting transfers between devices: none -> 4.74 us  [moved(): return lax.ppermute(value, 'space', pairs)]
    ppermute x5 -> x1, starting transfers between devices: 5.27 us -> 1.64 us  [swapped(): lax.ppermute(value, axis, [(i, i ^ bit) for i in range(lax.axis_size(axis...]
    ppermute x5 -> x1, waiting for transfers between devices: 2.49 us -> 0.01 us  [swapped(): lax.ppermute(value, axis, [(i, i ^ bit) for i in range(lax.axis_size(axis...]
    pallas_call x7 -> x8, Pallas kernels: 1.41 us -> 1.44 us  [call(): pl.pallas_call(kernel, out_shape=[jax.ShapeDtypeStruct(shape, dtype) for...]
  transfers between devices with their start and end apart: 6 -> 7, of which waited for: 3 -> 2; matrix products, arithmetic and copies ran while one was open for 0% -> 0% of each run, Pallas kernels for 5% -> 4%
where the time goes in v9:
time: 21.6 us; the launch traced here: 21.4 us
  starting transfers between devices  10.5 us (49%)
  waiting for transfers between devices  8.66 us (40%)
  Pallas kernels  1.44 us (7%)
  between operations  0.78 us (4%)
    ppermute x5, waiting for transfers between devices, moved(): return lax.ppermute(value, 'space', pairs)  8.66 us
    ppermute x5, starting transfers between devices, moved(): return lax.ppermute(value, 'space', pairs)  4.74 us
    ppermute x1, starting transfers between devices, shifted(): lax.ppermute(value, axis, [(i, (i + s) % count) for i in range(count)])  4.1 us
    ppermute x1, starting transfers between devices, swapped(): lax.ppermute(value, axis, [(i, i ^ bit) for i in range(lax.axis_size(axis...  1.64 us
    pallas_call x8, Pallas kernels, call(): pl.pallas_call(kernel, out_shape=[jax.ShapeDtypeStruct(shape, dtype) for...  1.44 us
  transfers between devices with their start and end apart: 7, of which 2 were waited for; matrix products, arithmetic and copies ran while one was open for 0% of the time, Pallas kernels for 4%

profile of v9, /device:TPU:0, one launch (start us, length us, event | category | flops | bytes accessed | tf_op | source)
XLA Modules:
  0.0 21.4 jit_solution(370535522320731261)
XLA Ops:
  0.6 0.0 copy-start
  0.6 0.0 copy-start.2
  0.7 0.0 copy-start.3
  0.7 0.0 copy-start.1
  0.7 4.1 %collective-permute-start.5 = (f32[1,4,16,256]{3,2,1,0:T(8,128)}, f32[1,4,16,256]{3,2,1,0:T(8,128)S(1)}, u32[]{:S(2)}, u32[]{:S(2)}) collective-permute-start(f32[1,4,16,256]{3,2,1,0:T(8,128)} %state.7), channel_id=1, source_target_pairs={{0,2},{1,3},{2,0},{3,1},{4,6},{5,7},{6,4},{7,5},{8,10},{9,11},{10,... | collective-permute-start | bytes 196616 | tf_op jit(solution)/shard_map/ppermute | solution.py:278
  4.8 0.0 copy-done
  4.8 0.0 copy-done.2
  4.8 0.0 copy-done.3
  4.8 0.0 copy-done.1
  4.8 0.4 %face_forces.1.blocks = f32[8,16,128]{2,1,0:T(8,128)S(1)} custom-call(s32[8,128]{1,0:T(8,128)S(1)} %own.1, f32[1,4,16,256]{3,2,1,0:T(8,128)S(1)} %copy-done, s32[6,128]{1,0:T(8,128)S(1)} %bitcast.3, s32[6,128]{1,0:T(8,128)S(1)} %bitcast.4, f32[3,768]{1,0:T(4,128)S(1)} %copy-done.1), custom_call_target="tpu_custom_call" | custom-call | flops 10000000000 | tf_op jit(solution)/shard_map/face_forces/pallas_call | solution.py:285
  5.2 1.5 %collective-permute-start = (f32[8,16,128]{2,1,0:T(8,128)S(1)}, f32[8,16,128]{2,1,0:T(8,128)S(1)}, u32[]{:S(2)}, u32[]{:S(2)}) collective-permute-start(f32[8,16,128]{2,1,0:T(8,128)S(1)} %face_forces.1.blocks), channel_id=1, source_target_pairs={{0,4},{8,12},{16,20},{24,28},{1,5},{9,13},{17,21},{25,29},{2,6},{1... | collective-permute-start | bytes 196616 | tf_op jit(solution)/shard_map/ppermute | solution.py:282
  6.7 0.2 flux.1
  6.9 0.7 %collective-permute-done.came = f32[8,16,128]{2,1,0:T(8,128)S(1)} collective-permute-done((f32[8,16,128]{2,1,0:T(8,128)S(1)}, f32[8,16,128]{2,1,0:T(8,128)S(1)}, u32[]{:S(2)}, u32[]{:S(2)}) %collective-permute-start) | collective-permute-done | bytes 65568 | tf_op jit(solution)/shard_map/ppermute | solution.py:282
  7.5 0.7 %collective-permute-start.1 = (f32[2,16,128]{2,1,0:T(8,128)S(1)}, f32[2,16,128]{2,1,0:T(8,128)S(1)}, u32[]{:S(2)}, u32[]{:S(2)}) collective-permute-start(f32[2,16,128]{2,1,0:T(8,128)S(1)} %get-tuple-element.17), channel_id=1, source_target_pairs={{4,28},{12,20},{20,12},{28,4},{5,29},{13,21},{21,13},{29,5},{6,30}... | collective-permute-start | bytes 49160 | tf_op jit(solution)/shard_map/ppermute | solution.py:282
  8.2 0.7 %collective-permute-start.2 = (f32[2,16,128]{2,1,0:T(8,128)S(1)}, f32[2,16,128]{2,1,0:T(8,128)S(1)}, u32[]{:S(2)}, u32[]{:S(2)}) collective-permute-start(f32[2,16,128]{2,1,0:T(8,128)S(1)} %get-tuple-element.18), channel_id=1, source_target_pairs={{4,20},{12,28},{20,4},{28,12},{5,21},{13,29},{21,5},{29,13},{6,22}... | collective-permute-start | bytes 49160 | tf_op jit(solution)/shard_map/ppermute | solution.py:282
  8.9 0.7 %collective-permute-start.3 = (f32[2,16,128]{2,1,0:T(8,128)S(1)}, f32[2,16,128]{2,1,0:T(8,128)S(1)}, u32[]{:S(2)}, u32[]{:S(2)}) collective-permute-start(f32[2,16,128]{2,1,0:T(8,128)S(1)} %get-tuple-element.19), channel_id=1, source_target_pairs={{4,12},{12,4},{20,28},{28,20},{5,13},{13,5},{21,29},{29,21},{6,14}... | collective-permute-start | bytes 49160 | tf_op jit(solution)/shard_map/ppermute | solution.py:282
  9.6 0.0 collective-permute-done.5.partner
  9.6 1.6 %collective-permute-start.6 = (f32[1,4,16,256]{3,2,1,0:T(8,128)S(1)}, f32[1,4,16,256]{3,2,1,0:T(8,128)S(1)}, u32[]{:S(2)}, u32[]{:S(2)}) collective-permute-start(f32[1,4,16,256]{3,2,1,0:T(8,128)S(1)} %pair_sums.1), channel_id=1, source_target_pairs={{0,1},{1,0},{2,3},{3,2},{4,5},{5,4},{6,7},{7,6},{8,9},{9,8},{10,11... | collective-permute-start | bytes 196616 | tf_op jit(solution)/shard_map/ppermute | solution.py:274
  11.2 0.0 collective-permute-done.1.diagonal
  11.3 0.0 collective-permute-done.2.y
  11.3 0.0 collective-permute-done.3.x
  11.3 1.3 %collective-permute-start.4 = (f32[16,128]{1,0:T(8,128)S(1)}, f32[16,128]{1,0:T(8,128)S(1)}, u32[]{:S(2)}, u32[]{:S(2)}) collective-permute-start(f32[16,128]{1,0:T(8,128)S(1)} %get-tuple-element.21), channel_id=1, source_target_pairs={{4,0},{12,8},{20,16},{28,24},{5,1},{13,9},{21,17},{29,25},{6,2},{1... | collective-permute-start | bytes 24584 | tf_op jit(solution)/shard_map/ppermute | solution.py:282
  12.6 8.0 %collective-permute-done.4.came = f32[16,128]{1,0:T(8,128)S(1)} collective-permute-done((f32[16,128]{1,0:T(8,128)S(1)}, f32[16,128]{1,0:T(8,128)S(1)}, u32[]{:S(2)}, u32[]{:S(2)}) %collective-permute-start.4) | collective-permute-done | bytes 8224 | tf_op jit(solution)/shard_map/ppermute | solution.py:282
  20.6 0.1 outer.1
  20.7 0.0 collective-permute-done.6.refs_0_
  20.7 0.7 %update.1 = (f32[1,4,16,256]{3,2,1,0:T(8,128)}, f32[3,1,512]{2,1,0:T(1,128)}) custom-call(f32[1,4,16,256]{3,2,1,0:T(8,128)S(1)} %get-tuple-element.22.residual, f32[16,256]{1,0:T(8,128)S(1)} %get-tuple-element.15._.step, f32[16,128]{1,0:T(8,128)S(1)} %get-tuple-element.23.total, f32[1,4,16,256]{3,2,1,0:T(8,128)S(1)} %collective-permute-done.6.refs_0_), custom_call_target="tpu_custom_call" | custom-call | tf_op jit(solution)/shard_map/update/pallas_call | solution.py:285
  (4 shorter events, 0.1 us)
Async XLA Ops:
  0.6 4.1 %copy-start = (f32[1,4,16,256]{3,2,1,0:T(8,128)S(1)}, f32[1,4,16,256]{3,2,1,0:T(8,128)}, u32[]{:S(2)}) copy-start(f32[1,4,16,256]{3,2,1,0:T(8,128)} %state.7) | copy-start | bytes 196612
  0.6 4.1 %copy-start.2 = (s32[768]{0:T(1024)S(1)}, s32[768]{0:T(1024)}, u32[]{:S(2)}) copy-start(s32[768]{0:T(1024)} %param.5) | copy-start | bytes 9220
  0.7 4.1 %copy-start.3 = (s32[768]{0:T(1024)S(1)}, s32[768]{0:T(1024)}, u32[]{:S(2)}) copy-start(s32[768]{0:T(1024)} %param.6) | copy-start | bytes 9220
  0.7 4.1 %copy-start.1 = (f32[3,768]{1,0:T(4,128)S(1)}, f32[3,768]{1,0:T(4,128)}, u32[]{:S(2)}) copy-start(f32[3,768]{1,0:T(4,128)} %area.1) | copy-start | bytes 27652
  0.7 8.9 %collective-permute-start.5 = (f32[1,4,16,256]{3,2,1,0:T(8,128)}, f32[1,4,16,256]{3,2,1,0:T(8,128)S(1)}, u32[]{:S(2)}, u32[]{:S(2)}) collective-permute-start(f32[1,4,16,256]{3,2,1,0:T(8,128)} %state.7), channel_id=1, source_target_pairs={{0,2},{1,3},{2,0},{3,1},{4,6},{5,7},{6,4},{7,5},{8,10},{9,11},{10,... | collective-permute-start | bytes 196616 | tf_op jit(solution)/shard_map/ppermute | solution.py:278
  5.2 2.4 %collective-permute-start = (f32[8,16,128]{2,1,0:T(8,128)S(1)}, f32[8,16,128]{2,1,0:T(8,128)S(1)}, u32[]{:S(2)}, u32[]{:S(2)}) collective-permute-start(f32[8,16,128]{2,1,0:T(8,128)S(1)} %face_forces.1.blocks), channel_id=1, source_target_pairs={{0,4},{8,12},{16,20},{24,28},{1,5},{9,13},{17,21},{25,29},{2,6},{1... | collective-permute-start | bytes 196616 | tf_op jit(solution)/shard_map/ppermute | solution.py:282
  7.5 3.7 %collective-permute-start.1 = (f32[2,16,128]{2,1,0:T(8,128)S(1)}, f32[2,16,128]{2,1,0:T(8,128)S(1)}, u32[]{:S(2)}, u32[]{:S(2)}) collective-permute-start(f32[2,16,128]{2,1,0:T(8,128)S(1)} %get-tuple-element.17), channel_id=1, source_target_pairs={{4,28},{12,20},{20,12},{28,4},{5,29},{13,21},{21,13},{29,5},{6,30}... | collective-permute-start | bytes 49160 | tf_op jit(solution)/shard_map/ppermute | solution.py:282
  8.2 3.0 %collective-permute-start.2 = (f32[2,16,128]{2,1,0:T(8,128)S(1)}, f32[2,16,128]{2,1,0:T(8,128)S(1)}, u32[]{:S(2)}, u32[]{:S(2)}) collective-permute-start(f32[2,16,128]{2,1,0:T(8,128)S(1)} %get-tuple-element.18), channel_id=1, source_target_pairs={{4,20},{12,28},{20,4},{28,12},{5,21},{13,29},{21,5},{29,13},{6,22}... | collective-permute-start | bytes 49160 | tf_op jit(solution)/shard_map/ppermute | solution.py:282
  8.9 2.4 %collective-permute-start.3 = (f32[2,16,128]{2,1,0:T(8,128)S(1)}, f32[2,16,128]{2,1,0:T(8,128)S(1)}, u32[]{:S(2)}, u32[]{:S(2)}) collective-permute-start(f32[2,16,128]{2,1,0:T(8,128)S(1)} %get-tuple-element.19), channel_id=1, source_target_pairs={{4,12},{12,4},{20,28},{28,20},{5,13},{13,5},{21,29},{29,21},{6,14}... | collective-permute-start | bytes 49160 | tf_op jit(solution)/shard_map/ppermute | solution.py:282
  9.6 11.1 %collective-permute-start.6 = (f32[1,4,16,256]{3,2,1,0:T(8,128)S(1)}, f32[1,4,16,256]{3,2,1,0:T(8,128)S(1)}, u32[]{:S(2)}, u32[]{:S(2)}) collective-permute-start(f32[1,4,16,256]{3,2,1,0:T(8,128)S(1)} %pair_sums.1), channel_id=1, source_target_pairs={{0,1},{1,0},{2,3},{3,2},{4,5},{5,4},{6,7},{7,6},{8,9},{9,8},{10,11... | collective-permute-start | bytes 196616 | tf_op jit(solution)/shard_map/ppermute | solution.py:274
  11.3 9.3 %collective-permute-start.4 = (f32[16,128]{1,0:T(8,128)S(1)}, f32[16,128]{1,0:T(8,128)S(1)}, u32[]{:S(2)}, u32[]{:S(2)}) collective-permute-start(f32[16,128]{1,0:T(8,128)S(1)} %get-tuple-element.21), channel_id=1, source_target_pairs={{4,0},{12,8},{20,16},{28,24},{5,1},{13,9},{21,17},{29,25},{6,2},{1... | collective-permute-start | bytes 24584 | tf_op jit(solution)/shard_map/ppermute | solution.py:282

commit v10 on v9

--- a/solution.py
+++ b/solution.py
@@ -277,8 +277,8 @@
         count = lax.axis_size(axis)
         return lax.ppermute(value, axis, [(i, (i + s) % count) for i in range(count)])
 
-    def moved(value, core, bit):
-        pairs = [(i, i ^ bit) for i in range(blocks) if i % 2 == core]
+    def swapped_by_second(value, bit):
+        pairs = [(i, i ^ bit if i % 2 else i) for i in range(blocks)]
         return lax.ppermute(value, "space", pairs)
 
     def call(kernel, name, shapes, *operands, flops=0, dtype=jnp.float32):
@@ -325,13 +325,13 @@
     )
     edges = []
     if riding:
-        came = moved(dense[0], 0, 1)
+        came = swapped(dense[0], "space", 1)
         mine, *sent = call(chip_kernel, "chip_sums", [(2, ROWS, LANES)] * 4, dense[0], came, step)
-        came = [moved(value, 1, bit) for value, bit in zip(sent, (6, 4, 2))]
+        came = [swapped_by_second(value, bit) for value, bit in zip(sent, (6, 4, 2))]
         block, kept = call(
             plane_kernel, "plane_sums", [(ROWS, LANES)] * 2, mine, *came, flops=PLACING
         )
-        came = moved(block, 1, 1)
+        came = swapped(block, "space", 1)
     else:
         row = jnp.broadcast_to(dense[0][0, EDGE : EDGE + 1, :], (8, LANES))
         edges = [shifted(row, "space", 1), shifted(row, "space", blocks - 1)]

time: 21.6 us -> 19.3 us (0.89)
  waiting for transfers between devices: 8.66 us -> 1.99 us
  starting transfers between devices: 10.5 us -> 14.9 us
    ppermute x5 -> x3, waiting for transfers between devices: 8.66 us -> 0.01 us  [swapped_by_second(): return lax.ppermute(value, 'space', pairs)]
    ppermute x1 -> x3, starting transfers between devices: 1.64 us -> 8.83 us  [swapped(): lax.ppermute(value, axis, [(i, i ^ bit) for i in range(lax.axis_size(axis...]
    ppermute x5 -> x3, starting transfers between devices: 4.74 us -> 1.99 us  [swapped_by_second(): return lax.ppermute(value, 'space', pairs)]
    ppermute x1 -> x3, waiting for transfers between devices: 0.01 us -> 1.88 us  [swapped(): lax.ppermute(value, axis, [(i, i ^ bit) for i in range(lax.axis_size(axis...]
  transfers between devices with their start and end apart: 7 -> 7, of which waited for: 2 -> 3; matrix products, arithmetic and copies ran while one was open for 0% -> 0% of each run, Pallas kernels for 4% -> 4%
where the time goes in v10:
time: 19.3 us; the launch traced here: 19.1 us
  starting transfers between devices  14.9 us (77%)
  waiting for transfers between devices  1.99 us (10%)
  Pallas kernels  1.43 us (7%)
  between operations  0.76 us (4%)
    ppermute x3, starting transfers between devices, swapped(): lax.ppermute(value, axis, [(i, i ^ bit) for i in range(lax.axis_size(axis...  8.83 us
    ppermute x1, starting transfers between devices, shifted(): lax.ppermute(value, axis, [(i, (i + s) % count) for i in range(count)])  4.1 us
    ppermute x3, starting transfers between devices, swapped_by_second(): return lax.ppermute(value, 'space', pairs)  1.99 us
    ppermute x3, waiting for transfers between devices, swapped(): lax.ppermute(value, axis, [(i, i ^ bit) for i in range(lax.axis_size(axis...  1.88 us
    pallas_call x8, Pallas kernels, call(): pl.pallas_call(kernel, out_shape=[jax.ShapeDtypeStruct(shape, dtype) for...  1.43 us
  transfers between devices with their start and end apart: 7, of which 3 were waited for; matrix products, arithmetic and copies ran while one was open for 0% of the time, Pallas kernels for 4%

profile of v10, /device:TPU:0, one launch (start us, length us, event | category | flops | bytes accessed | tf_op | source)
XLA Modules:
  0.0 19.1 jit_solution(3943824948963945797)
XLA Ops:
  0.6 0.0 copy-start
  0.6 0.0 copy-start.2
  0.7 0.0 copy-start.3
  0.7 0.0 copy-start.1
  0.7 4.1 %collective-permute-start.5 = (f32[1,4,16,256]{3,2,1,0:T(8,128)}, f32[1,4,16,256]{3,2,1,0:T(8,128)S(1)}, u32[]{:S(2)}, u32[]{:S(2)}) collective-permute-start(f32[1,4,16,256]{3,2,1,0:T(8,128)} %state.7), channel_id=1, source_target_pairs={{0,2},{1,3},{2,0},{3,1},{4,6},{5,7},{6,4},{7,5},{8,10},{9,11},{10,... | collective-permute-start | bytes 196616 | tf_op jit(solution)/shard_map/ppermute | solution.py:278
  4.8 0.0 copy-done
  4.8 0.0 copy-done.2
  4.8 0.0 copy-done.3
  4.8 0.0 copy-done.1
  4.8 0.4 %face_forces.1.blocks = f32[8,16,128]{2,1,0:T(8,128)S(1)} custom-call(s32[8,128]{1,0:T(8,128)S(1)} %own.1, f32[1,4,16,256]{3,2,1,0:T(8,128)S(1)} %copy-done, s32[6,128]{1,0:T(8,128)S(1)} %bitcast.3, s32[6,128]{1,0:T(8,128)S(1)} %bitcast.4, f32[3,768]{1,0:T(4,128)S(1)} %copy-done.1), custom_call_target="tpu_custom_call" | custom-call | flops 10000000000 | tf_op jit(solution)/shard_map/face_forces/pallas_call | solution.py:285
  5.2 0.1 collective-permute-start
  5.3 0.2 flux.1
  5.5 1.0 %collective-permute-done.came = f32[8,16,128]{2,1,0:T(8,128)S(1)} collective-permute-done((f32[8,16,128]{2,1,0:T(8,128)S(1)}, f32[8,16,128]{2,1,0:T(8,128)S(1)}, u32[]{:S(2)}, u32[]{:S(2)}) %collective-permute-start) | collective-permute-done | bytes 65568 | tf_op jit(solution)/shard_map/ppermute | solution.py:274
  6.5 0.7 %collective-permute-start.1 = (f32[2,16,128]{2,1,0:T(8,128)S(1)}, f32[2,16,128]{2,1,0:T(8,128)S(1)}, u32[]{:S(2)}, u32[]{:S(2)}) collective-permute-start(f32[2,16,128]{2,1,0:T(8,128)S(1)} %get-tuple-element.17), channel_id=1, source_target_pairs={{0,0},{4,28},{8,8},{12,20},{16,16},{20,12},{24,24},{28,4},{1,1},{5... | collective-permute-start | bytes 49160 | tf_op jit(solution)/shard_map/ppermute | solution.py:282
  7.2 0.7 %collective-permute-start.2 = (f32[2,16,128]{2,1,0:T(8,128)S(1)}, f32[2,16,128]{2,1,0:T(8,128)S(1)}, u32[]{:S(2)}, u32[]{:S(2)}) collective-permute-start(f32[2,16,128]{2,1,0:T(8,128)S(1)} %get-tuple-element.18), channel_id=1, source_target_pairs={{0,0},{4,20},{8,8},{12,28},{16,16},{20,4},{24,24},{28,12},{1,1},{5... | collective-permute-start | bytes 49160 | tf_op jit(solution)/shard_map/ppermute | solution.py:282
  7.9 0.7 %collective-permute-start.3 = (f32[2,16,128]{2,1,0:T(8,128)S(1)}, f32[2,16,128]{2,1,0:T(8,128)S(1)}, u32[]{:S(2)}, u32[]{:S(2)}) collective-permute-start(f32[2,16,128]{2,1,0:T(8,128)S(1)} %get-tuple-element.19), channel_id=1, source_target_pairs={{0,0},{4,12},{8,8},{12,4},{16,16},{20,28},{24,24},{28,20},{1,1},{5... | collective-permute-start | bytes 49160 | tf_op jit(solution)/shard_map/ppermute | solution.py:282
  8.5 0.1 collective-permute-done.5.partner
  8.7 1.6 %collective-permute-start.6 = (f32[1,4,16,256]{3,2,1,0:T(8,128)S(1)}, f32[1,4,16,256]{3,2,1,0:T(8,128)S(1)}, u32[]{:S(2)}, u32[]{:S(2)}) collective-permute-start(f32[1,4,16,256]{3,2,1,0:T(8,128)S(1)} %pair_sums.1), channel_id=1, source_target_pairs={{0,1},{1,0},{2,3},{3,2},{4,5},{5,4},{6,7},{7,6},{8,9},{9,8},{10,11... | collective-permute-start | bytes 196616 | tf_op jit(solution)/shard_map/ppermute | solution.py:274
  10.2 0.0 collective-permute-done.1.diagonal
  10.2 0.0 collective-permute-done.2.y
  10.2 0.0 collective-permute-done.3.x
  10.3 7.2 %collective-permute-start.4 = (f32[16,128]{1,0:T(8,128)S(1)}, f32[16,128]{1,0:T(8,128)S(1)}, u32[]{:S(2)}, u32[]{:S(2)}) collective-permute-start(f32[16,128]{1,0:T(8,128)S(1)} %get-tuple-element.21), channel_id=1, source_target_pairs={{0,4},{4,0},{8,12},{12,8},{16,20},{20,16},{24,28},{28,24},{1,5},{5... | collective-permute-start | bytes 24584 | tf_op jit(solution)/shard_map/ppermute | solution.py:274
  17.5 0.8 %collective-permute-done.4.came = f32[16,128]{1,0:T(8,128)S(1)} collective-permute-done((f32[16,128]{1,0:T(8,128)S(1)}, f32[16,128]{1,0:T(8,128)S(1)}, u32[]{:S(2)}, u32[]{:S(2)}) %collective-permute-start.4) | collective-permute-done | bytes 8224 | tf_op jit(solution)/shard_map/ppermute | solution.py:274
  18.3 0.1 outer.1
  18.4 0.0 collective-permute-done.6.refs_0_
  18.5 0.7 %update.1 = (f32[1,4,16,256]{3,2,1,0:T(8,128)}, f32[3,1,512]{2,1,0:T(1,128)}) custom-call(f32[1,4,16,256]{3,2,1,0:T(8,128)S(1)} %get-tuple-element.22.residual, f32[16,256]{1,0:T(8,128)S(1)} %get-tuple-element.15._.step, f32[16,128]{1,0:T(8,128)S(1)} %get-tuple-element.23.total, f32[1,4,16,256]{3,2,1,0:T(8,128)S(1)} %collective-permute-done.6.refs_0_), custom_call_target="tpu_custom_call" | custom-call | tf_op jit(solution)/shard_map/update/pallas_call | solution.py:285
  (4 shorter events, 0.1 us)
Async XLA Ops:
  0.6 4.1 %copy-start = (f32[1,4,16,256]{3,2,1,0:T(8,128)S(1)}, f32[1,4,16,256]{3,2,1,0:T(8,128)}, u32[]{:S(2)}) copy-start(f32[1,4,16,256]{3,2,1,0:T(8,128)} %state.7) | copy-start | bytes 196612
  0.6 4.1 %copy-start.2 = (s32[768]{0:T(1024)S(1)}, s32[768]{0:T(1024)}, u32[]{:S(2)}) copy-start(s32[768]{0:T(1024)} %param.5) | copy-start | bytes 9220
  0.7 4.1 %copy-start.3 = (s32[768]{0:T(1024)S(1)}, s32[768]{0:T(1024)}, u32[]{:S(2)}) copy-start(s32[768]{0:T(1024)} %param.6) | copy-start | bytes 9220
  0.7 4.1 %copy-start.1 = (f32[3,768]{1,0:T(4,128)S(1)}, f32[3,768]{1,0:T(4,128)}, u32[]{:S(2)}) copy-start(f32[3,768]{1,0:T(4,128)} %area.1) | copy-start | bytes 27652
  0.7 8.0 %collective-permute-start.5 = (f32[1,4,16,256]{3,2,1,0:T(8,128)}, f32[1,4,16,256]{3,2,1,0:T(8,128)S(1)}, u32[]{:S(2)}, u32[]{:S(2)}) collective-permute-start(f32[1,4,16,256]{3,2,1,0:T(8,128)} %state.7), channel_id=1, source_target_pairs={{0,2},{1,3},{2,0},{3,1},{4,6},{5,7},{6,4},{7,5},{8,10},{9,11},{10,... | collective-permute-start | bytes 196616 | tf_op jit(solution)/shard_map/ppermute | solution.py:278
  5.2 1.3 %collective-permute-start = (f32[8,16,128]{2,1,0:T(8,128)S(1)}, f32[8,16,128]{2,1,0:T(8,128)S(1)}, u32[]{:S(2)}, u32[]{:S(2)}) collective-permute-start(f32[8,16,128]{2,1,0:T(8,128)S(1)} %face_forces.1.blocks), channel_id=1, source_target_pairs={{0,4},{4,0},{8,12},{12,8},{16,20},{20,16},{24,28},{28,24},{1,5},{5... | collective-permute-start | bytes 196616 | tf_op jit(solution)/shard_map/ppermute | solution.py:274
  6.5 3.7 %collective-permute-start.1 = (f32[2,16,128]{2,1,0:T(8,128)S(1)}, f32[2,16,128]{2,1,0:T(8,128)S(1)}, u32[]{:S(2)}, u32[]{:S(2)}) collective-permute-start(f32[2,16,128]{2,1,0:T(8,128)S(1)} %get-tuple-element.17), channel_id=1, source_target_pairs={{0,0},{4,28},{8,8},{12,20},{16,16},{20,12},{24,24},{28,4},{1,1},{5... | collective-permute-start | bytes 49160 | tf_op jit(solution)/shard_map/ppermute | solution.py:282
  7.2 3.0 %collective-permute-start.2 = (f32[2,16,128]{2,1,0:T(8,128)S(1)}, f32[2,16,128]{2,1,0:T(8,128)S(1)}, u32[]{:S(2)}, u32[]{:S(2)}) collective-permute-start(f32[2,16,128]{2,1,0:T(8,128)S(1)} %get-tuple-element.18), channel_id=1, source_target_pairs={{0,0},{4,20},{8,8},{12,28},{16,16},{20,4},{24,24},{28,12},{1,1},{5... | collective-permute-start | bytes 49160 | tf_op jit(solution)/shard_map/ppermute | solution.py:282
  7.9 2.4 %collective-permute-start.3 = (f32[2,16,128]{2,1,0:T(8,128)S(1)}, f32[2,16,128]{2,1,0:T(8,128)S(1)}, u32[]{:S(2)}, u32[]{:S(2)}) collective-permute-start(f32[2,16,128]{2,1,0:T(8,128)S(1)} %get-tuple-element.19), channel_id=1, source_target_pairs={{0,0},{4,12},{8,8},{12,4},{16,16},{20,28},{24,24},{28,20},{1,1},{5... | collective-permute-start | bytes 49160 | tf_op jit(solution)/shard_map/ppermute | solution.py:282
  8.7 9.8 %collective-permute-start.6 = (f32[1,4,16,256]{3,2,1,0:T(8,128)S(1)}, f32[1,4,16,256]{3,2,1,0:T(8,128)S(1)}, u32[]{:S(2)}, u32[]{:S(2)}) collective-permute-start(f32[1,4,16,256]{3,2,1,0:T(8,128)S(1)} %pair_sums.1), channel_id=1, source_target_pairs={{0,1},{1,0},{2,3},{3,2},{4,5},{5,4},{6,7},{7,6},{8,9},{9,8},{10,11... | collective-permute-start | bytes 196616 | tf_op jit(solution)/shard_map/ppermute | solution.py:274
  10.3 8.0 %collective-permute-start.4 = (f32[16,128]{1,0:T(8,128)S(1)}, f32[16,128]{1,0:T(8,128)S(1)}, u32[]{:S(2)}, u32[]{:S(2)}) collective-permute-start(f32[16,128]{1,0:T(8,128)S(1)} %get-tuple-element.21), channel_id=1, source_target_pairs={{0,4},{4,0},{8,12},{12,8},{16,20},{20,16},{24,28},{28,24},{1,5},{5... | collective-permute-start | bytes 24584 | tf_op jit(solution)/shard_map/ppermute | solution.py:274

commit v11 on v8

--- a/solution.py
+++ b/solution.py
@@ -17,6 +17,7 @@
 ROWS = 16
 EDGE = 12
 PLACING = 10**10
+PLACES = (2, 3, 1)
 RIDING = 8
 
 
@@ -95,7 +96,8 @@
             result = product if result is None else result + product
         return result.reshape(count, ROWS, LANES)
 
-    ordered = outs[:1] + outs[:0:-1]
+    places = (0, *PLACES) if len(outs) == 4 else (0, 1)
+    ordered = [outs[places.index(i)] for i in range(len(outs))]
     size = outs[0].shape[0]
     blocks = size * len(outs)
     if blocks <= 16:
@@ -128,19 +130,20 @@
                 out[0, EDGE + j : EDGE + j + 1, :] = ref[0, EDGE : EDGE + 1, :]
 
 
-def pair_kernel(weights, instances, state, partner, *outs):
+def weight_from(weights, instances, source, target):
+    shift = (target - source + instances) % instances
+    value = weights[0]
+    for i in range(1, instances):
+        value = jnp.where(shift == i, weights[i], value)
+    return value
+
+
+def pair_kernel(weights, instances, first, seconds, state, partner, *outs):
     me = lax.axis_index("inst")
-
-    def weight(shift):
-        value = weights[0]
-        for i in range(1, instances):
-            value = jnp.where(shift == i, weights[i], value)
-        return value
-
-    for i, out in enumerate(outs):
-        shift = ((me ^ (i + 1)) - me + instances) % instances
-        far = (shift + instances // 2) % instances
-        out[...] = weight(shift) * state[...] + weight(far) * partner[...]
+    for second, out in zip(seconds, outs):
+        own = weight_from(weights, instances, me, me ^ second)
+        other = weight_from(weights, instances, me ^ first, me ^ second)
+        out[...] = own * state[...] + other * partner[...]
 
 
 def around_flux(q, vc, p):
@@ -182,7 +185,7 @@
         base[0, c] = residual + (upper - lower)
 
 
-def outer_kernel(weight, blocks, state, base, kept, came, partner, *refs):
+def outer_kernel(weights, instances, first, blocks, state, base, kept, came, partner, *refs):
     *edges, residual, total = refs
     radial, around = state.shape[2:]
     if blocks == RIDING:
@@ -194,25 +197,30 @@
         def edge_of(device):
             relative = device ^ me
             half = RIDING // 2
-            place = (half - relative // 2) % half + (relative % 2) * half
+            place = 0
+            for row_place, chip in enumerate(PLACES, 1):
+                place = jnp.where(relative // 2 == chip, row_place, place)
+            place += (relative % 2) * half
             return jnp.sum(jnp.where(row == place, known, 0.0), axis=0, keepdims=True)
 
         before = edge_of((me + blocks - 1) % blocks)
         after = edge_of((me + 1) % blocks)
     else:
         before, after = (ref[0:1, :] for ref in edges)
+    me = lax.axis_index("inst")
+    weight = weight_from(weights, instances, me ^ first, me)
     lane = lax.broadcasted_iota(jnp.int32, (1, LANES), 1)
     edge = jnp.where(lane < LANES // 2, before, after)
     columns = jnp.broadcast_to(edge, (LANES, LANES)).T
 
     lane = lax.broadcasted_iota(jnp.int32, (radial, LANES), 1)
-    first, last = lane == 0, lane == LANES - 1
+    left, right = lane == 0, lane == LANES - 1
     own, far = [], []
     for c in range(4):
-        own.append(jnp.where(first, state[0, c, :, :LANES], state[0, c, :, around - LANES :]))
+        own.append(jnp.where(left, state[0, c, :, :LANES], state[0, c, :, around - LANES :]))
         far.append(
             jnp.where(
-                last,
+                right,
                 columns[LANES // 2 + c * radial : LANES // 2 + (c + 1) * radial],
                 columns[c * radial : (c + 1) * radial],
             )
@@ -222,11 +230,11 @@
         inverse, _, vc, p = pressure_of(*q)
         speeds.append(jnp.abs(vc) + jnp.sqrt(gamma_ratio * p * inverse))
         faces.append(around_flux(q, vc, p))
-    side = jnp.where(last, 0.5, -0.5)
+    side = jnp.where(right, 0.5, -0.5)
     reach = 0.5 * jnp.maximum(*speeds)
     for c in range(4):
         outer = side * (faces[0][c] + faces[1][c]) - reach * (far[c] - own[c])
-        outer = [jnp.where(first, outer, 0.0), jnp.where(last, outer, 0.0)]
+        outer = [jnp.where(left, outer, 0.0), jnp.where(right, outer, 0.0)]
         middle = around - 2 * LANES
         if middle:
             outer.insert(1, jnp.zeros((radial, middle), jnp.float32))
@@ -262,9 +270,8 @@
         return lax.ppermute(value, axis, [(i, (i + s) % count) for i in range(count)])
 
     def exchanged(sent, size):
-        return [
-            swapped(value, "space", (len(sent) - i) * size) for i, value in enumerate(sent)
-        ]
+        places = PLACES if len(sent) == 3 else (1,)
+        return [swapped(value, "space", place * size) for place, value in zip(places, sent)]
 
     def call(kernel, name, shapes, *operands, flops=0, dtype=jnp.float32):
         return pl.pallas_call(
@@ -278,7 +285,8 @@
         )(*operands)
 
     weights = spectral_row(instances)
-    partner = shifted(state, "inst", instances // 2)
+    first, seconds = 1, range(2, instances, 2)
+    partner = swapped(state, "inst", first)
 
     riding = blocks == RIDING
     steps = [4, 2] if riding else [2] * (blocks.bit_length() - 1)
@@ -309,14 +317,14 @@
 
     came = exchanged(sent, size)
     sums = call(
-        functools.partial(pair_kernel, weights, instances),
+        functools.partial(pair_kernel, weights, instances, first, seconds),
         "pair_sums",
-        [state.shape] * (instances // 2 - 1),
+        [state.shape] * len(seconds),
         state,
         partner,
         flops=PLACING,
     )
-    sums = [swapped(value, "inst", i + 1) for i, value in enumerate(sums)]
+    sums = [swapped(value, "inst", second) for second, value in zip(seconds, sums)]
 
     for step in steps[1:]:
         size //= step
@@ -337,7 +345,7 @@
         state,
     )
     residual, total = call(
-        functools.partial(outer_kernel, weights[instances // 2], blocks),
+        functools.partial(outer_kernel, weights, instances, first, blocks),
         "outer",
         [state.shape, (ROWS, LANES)],
         state,

time: 14.2 us -> 14.5 us (1.021)
  waiting for transfers between devices: 2.49 us -> 2.83 us
    ppermute x1 -> x0, starting transfers between devices: 4.1 us -> none  [shifted(): lax.ppermute(value, axis, [(i, (i + s) % count) for i in range(count)])]
    ppermute x5 -> x6, starting transfers between devices: 5.27 us -> 9.37 us  [swapped(): lax.ppermute(value, axis, [(i, i ^ bit) for i in range(lax.axis_size(axis...]
    ppermute x5 -> x6, waiting for transfers between devices: 2.49 us -> 2.83 us  [swapped(): lax.ppermute(value, axis, [(i, i ^ bit) for i in range(lax.axis_size(axis...]
where the time goes in v11:
time: 14.5 us; the launch traced here: 14.3 us
  starting transfers between devices  9.37 us (65%)
  waiting for transfers between devices  2.83 us (20%)
  Pallas kernels  1.4 us (10%)
  between operations  0.72 us (5%)
    ppermute x6, starting transfers between devices, swapped(): lax.ppermute(value, axis, [(i, i ^ bit) for i in range(lax.axis_size(axis...  9.37 us
    ppermute x6, waiting for transfers between devices, swapped(): lax.ppermute(value, axis, [(i, i ^ bit) for i in range(lax.axis_size(axis...  2.83 us
    pallas_call x7, Pallas kernels, call(): pl.pallas_call(kernel, out_shape=[jax.ShapeDtypeStruct(shape, dtype) for...  1.4 us
  transfers between devices with their start and end apart: 6, of which 3 were waited for; matrix products, arithmetic and copies ran while one was open for 0% of the time, Pallas kernels for 5%

profile of v11, /device:TPU:0, one launch (start us, length us, event | category | flops | bytes accessed | tf_op | source)
XLA Modules:
  0.0 14.3 jit_solution(16967060173650856388)
XLA Ops:
  0.6 0.0 copy-start
  0.6 0.0 copy-start.2
  0.7 0.0 copy-start.3
  0.7 0.0 copy-start.1
  0.7 3.1 %collective-permute-start.4 = (f32[1,4,16,256]{3,2,1,0:T(8,128)}, f32[1,4,16,256]{3,2,1,0:T(8,128)S(1)}, u32[]{:S(2)}, u32[]{:S(2)}) collective-permute-start(f32[1,4,16,256]{3,2,1,0:T(8,128)} %state.7), channel_id=1, source_target_pairs={{0,1},{1,0},{2,3},{3,2},{4,5},{5,4},{6,7},{7,6},{8,9},{9,8},{10,11... | collective-permute-start | bytes 196616 | tf_op jit(solution)/shard_map/ppermute | solution.py:266
  3.8 0.0 copy-done
  3.8 0.0 copy-done.2
  3.8 0.0 copy-done.3
  3.8 0.0 copy-done.1
  3.8 0.4 %face_forces.1 = (f32[2,16,128]{2,1,0:T(8,128)S(1)}, f32[2,16,128]{2,1,0:T(8,128)S(1)}, f32[2,16,128]{2,1,0:T(8,128)S(1)}, f32[2,16,128]{2,1,0:T(8,128)S(1)}) custom-call(s32[8,128]{1,0:T(8,128)S(1)} %own.1, f32[1,4,16,256]{3,2,1,0:T(8,128)S(1)} %copy-done, s32[6,128]{1,0:T(8,128)S(1)} %bitcast.3, s32[6,128]{1,0:T(8,128)S(1)} %bitcast.4, f32[3,768]{1,0:T(4,128)S(1)} %copy-done.1), custom_call_target="tpu_custom_call" | custom-call | flops 10000000000 | tf_op jit(solution)/shard_map/face_forces/pallas_call | solution.py:277
  4.2 1.6 %collective-permute-start = (f32[2,16,128]{2,1,0:T(8,128)S(1)}, f32[2,16,128]{2,1,0:T(8,128)S(1)}, u32[]{:S(2)}, u32[]{:S(2)}) collective-permute-start(f32[2,16,128]{2,1,0:T(8,128)S(1)} %get-tuple-element.16), channel_id=1, source_target_pairs={{0,16},{4,20},{8,24},{12,28},{16,0},{20,4},{24,8},{28,12},{1,17},{... | collective-permute-start | bytes 49160 | tf_op jit(solution)/shard_map/ppermute | solution.py:266
  5.8 1.4 %collective-permute-start.1 = (f32[2,16,128]{2,1,0:T(8,128)S(1)}, f32[2,16,128]{2,1,0:T(8,128)S(1)}, u32[]{:S(2)}, u32[]{:S(2)}) collective-permute-start(f32[2,16,128]{2,1,0:T(8,128)S(1)} %get-tuple-element.17), channel_id=1, source_target_pairs={{0,24},{4,28},{8,16},{12,20},{16,8},{20,12},{24,0},{28,4},{1,25},{... | collective-permute-start | bytes 49160 | tf_op jit(solution)/shard_map/ppermute | solution.py:266
  7.2 0.5 %collective-permute-start.2 = (f32[2,16,128]{2,1,0:T(8,128)S(1)}, f32[2,16,128]{2,1,0:T(8,128)S(1)}, u32[]{:S(2)}, u32[]{:S(2)}) collective-permute-start(f32[2,16,128]{2,1,0:T(8,128)S(1)} %get-tuple-element.18), channel_id=1, source_target_pairs={{0,8},{4,12},{8,0},{12,4},{16,24},{20,28},{24,16},{28,20},{1,9},{5... | collective-permute-start | bytes 49160 | tf_op jit(solution)/shard_map/ppermute | solution.py:266
  7.7 0.0 collective-permute-done.4.partner
  7.8 2.7 %collective-permute-start.5 = (f32[1,4,16,256]{3,2,1,0:T(8,128)S(1)}, f32[1,4,16,256]{3,2,1,0:T(8,128)S(1)}, u32[]{:S(2)}, u32[]{:S(2)}) collective-permute-start(f32[1,4,16,256]{3,2,1,0:T(8,128)S(1)} %pair_sums.1), channel_id=1, source_target_pairs={{0,2},{1,3},{2,0},{3,1},{4,6},{5,7},{6,4},{7,5},{8,10},{9,11},{10,... | collective-permute-start | bytes 196616 | tf_op jit(solution)/shard_map/ppermute | solution.py:266
  10.4 0.0 collective-permute-done.refs_1_
  10.4 0.0 collective-permute-done.1.refs_2_
  10.4 0.5 %collective-permute-done.2.refs_3_ = f32[2,16,128]{2,1,0:T(8,128)S(1)} collective-permute-done((f32[2,16,128]{2,1,0:T(8,128)S(1)}, f32[2,16,128]{2,1,0:T(8,128)S(1)}, u32[]{:S(2)}, u32[]{:S(2)}) %collective-permute-start.2) | collective-permute-done | bytes 16416 | tf_op jit(solution)/shard_map/ppermute | solution.py:266
  10.9 0.1 collective-permute-start.3
  11.0 0.2 %flux.1 = (f32[1,4,16,256]{3,2,1,0:T(8,128)S(1)}, f32[16,256]{1,0:T(8,128)S(1)}) custom-call(f32[1,4,16,256]{3,2,1,0:T(8,128)S(1)} %copy-done), custom_call_target="tpu_custom_call" | custom-call | tf_op jit(solution)/shard_map/flux/pallas_call | solution.py:277
  11.2 1.0 %collective-permute-done.3.came = f32[1,16,128]{2,1,0:T(8,128)S(1)} collective-permute-done((f32[1,16,128]{2,1,0:T(8,128)S(1)}, f32[1,16,128]{2,1,0:T(8,128)S(1)}, u32[]{:S(2)}, u32[]{:S(2)}) %collective-permute-start.3) | collective-permute-done | bytes 8224 | tf_op jit(solution)/shard_map/ppermute | solution.py:266
  12.2 0.2 %outer.1 = (f32[1,4,16,256]{3,2,1,0:T(8,128)S(1)}, f32[16,128]{1,0:T(8,128)S(1)}) custom-call(f32[1,4,16,256]{3,2,1,0:T(8,128)S(1)} %copy-done, f32[1,4,16,256]{3,2,1,0:T(8,128)S(1)} %get-tuple-element.14.base, f32[1,16,128]{2,1,0:T(8,128)S(1)} %get-tuple-element.19.kept, f32[1,16,128]{2,1,0:T(8,128)S(1)} %collective-permute-done.3.came, ...), custom_call_target="tpu_custom_call" | custom-call | tf_op jit(solution)/shard_map/outer/pallas_call | solution.py:277
  12.3 1.4 %collective-permute-done.5.refs_0_ = f32[1,4,16,256]{3,2,1,0:T(8,128)S(1)} collective-permute-done((f32[1,4,16,256]{3,2,1,0:T(8,128)S(1)}, f32[1,4,16,256]{3,2,1,0:T(8,128)S(1)}, u32[]{:S(2)}, u32[]{:S(2)}) %collective-permute-start.5) | collective-permute-done | bytes 65568 | tf_op jit(solution)/shard_map/ppermute | solution.py:266
  13.7 0.6 %update.1 = (f32[1,4,16,256]{3,2,1,0:T(8,128)}, f32[3,1,512]{2,1,0:T(1,128)}) custom-call(f32[1,4,16,256]{3,2,1,0:T(8,128)S(1)} %get-tuple-element.21.residual, f32[16,256]{1,0:T(8,128)S(1)} %get-tuple-element.22.step, f32[16,128]{1,0:T(8,128)S(1)} %get-tuple-element.23.total, f32[1,4,16,256]{3,2,1,0:T(8,128)S(1)} %collective-permute-done.5.refs_0_), custom_call_target="tpu_custom_call" | custom-call | tf_op jit(solution)/shard_map/update/pallas_call | solution.py:277
  (3 shorter events, 0.0 us)
Async XLA Ops:
  0.6 3.1 %copy-start = (f32[1,4,16,256]{3,2,1,0:T(8,128)S(1)}, f32[1,4,16,256]{3,2,1,0:T(8,128)}, u32[]{:S(2)}) copy-start(f32[1,4,16,256]{3,2,1,0:T(8,128)} %state.7) | copy-start | bytes 196612
  0.6 3.1 %copy-start.2 = (s32[768]{0:T(1024)S(1)}, s32[768]{0:T(1024)}, u32[]{:S(2)}) copy-start(s32[768]{0:T(1024)} %param.5) | copy-start | bytes 9220
  0.7 3.1 %copy-start.3 = (s32[768]{0:T(1024)S(1)}, s32[768]{0:T(1024)}, u32[]{:S(2)}) copy-start(s32[768]{0:T(1024)} %param.6) | copy-start | bytes 9220
  0.7 3.1 %copy-start.1 = (f32[3,768]{1,0:T(4,128)S(1)}, f32[3,768]{1,0:T(4,128)}, u32[]{:S(2)}) copy-start(f32[3,768]{1,0:T(4,128)} %area.1) | copy-start | bytes 27652
  0.7 7.1 %collective-permute-start.4 = (f32[1,4,16,256]{3,2,1,0:T(8,128)}, f32[1,4,16,256]{3,2,1,0:T(8,128)S(1)}, u32[]{:S(2)}, u32[]{:S(2)}) collective-permute-start(f32[1,4,16,256]{3,2,1,0:T(8,128)} %state.7), channel_id=1, source_target_pairs={{0,1},{1,0},{2,3},{3,2},{4,5},{5,4},{6,7},{7,6},{8,9},{9,8},{10,11... | collective-permute-start | bytes 196616 | tf_op jit(solution)/shard_map/ppermute | solution.py:266
  4.2 6.2 %collective-permute-start = (f32[2,16,128]{2,1,0:T(8,128)S(1)}, f32[2,16,128]{2,1,0:T(8,128)S(1)}, u32[]{:S(2)}, u32[]{:S(2)}) collective-permute-start(f32[2,16,128]{2,1,0:T(8,128)S(1)} %get-tuple-element.16), channel_id=1, source_target_pairs={{0,16},{4,20},{8,24},{12,28},{16,0},{20,4},{24,8},{28,12},{1,17},{... | collective-permute-start | bytes 49160 | tf_op jit(solution)/shard_map/ppermute | solution.py:266
  5.8 4.7 %collective-permute-start.1 = (f32[2,16,128]{2,1,0:T(8,128)S(1)}, f32[2,16,128]{2,1,0:T(8,128)S(1)}, u32[]{:S(2)}, u32[]{:S(2)}) collective-permute-start(f32[2,16,128]{2,1,0:T(8,128)S(1)} %get-tuple-element.17), channel_id=1, source_target_pairs={{0,24},{4,28},{8,16},{12,20},{16,8},{20,12},{24,0},{28,4},{1,25},{... | collective-permute-start | bytes 49160 | tf_op jit(solution)/shard_map/ppermute | solution.py:266
  7.2 3.7 %collective-permute-start.2 = (f32[2,16,128]{2,1,0:T(8,128)S(1)}, f32[2,16,128]{2,1,0:T(8,128)S(1)}, u32[]{:S(2)}, u32[]{:S(2)}) collective-permute-start(f32[2,16,128]{2,1,0:T(8,128)S(1)} %get-tuple-element.18), channel_id=1, source_target_pairs={{0,8},{4,12},{8,0},{12,4},{16,24},{20,28},{24,16},{28,20},{1,9},{5... | collective-permute-start | bytes 49160 | tf_op jit(solution)/shard_map/ppermute | solution.py:266
  7.8 5.9 %collective-permute-start.5 = (f32[1,4,16,256]{3,2,1,0:T(8,128)S(1)}, f32[1,4,16,256]{3,2,1,0:T(8,128)S(1)}, u32[]{:S(2)}, u32[]{:S(2)}) collective-permute-start(f32[1,4,16,256]{3,2,1,0:T(8,128)S(1)} %pair_sums.1), channel_id=1, source_target_pairs={{0,2},{1,3},{2,0},{3,1},{4,6},{5,7},{6,4},{7,5},{8,10},{9,11},{10,... | collective-permute-start | bytes 196616 | tf_op jit(solution)/shard_map/ppermute | solution.py:266
  10.9 1.2 %collective-permute-start.3 = (f32[1,16,128]{2,1,0:T(8,128)S(1)}, f32[1,16,128]{2,1,0:T(8,128)S(1)}, u32[]{:S(2)}, u32[]{:S(2)}) collective-permute-start(f32[1,16,128]{2,1,0:T(8,128)S(1)} %get-tuple-element.20), channel_id=1, source_target_pairs={{0,4},{4,0},{8,12},{12,8},{16,20},{20,16},{24,28},{28,24},{1,5},{5... | collective-permute-start | bytes 24584 | tf_op jit(solution)/shard_map/ppermute | solution.py:266

commit v12 on v11

--- a/solution.py
+++ b/solution.py
@@ -18,6 +18,7 @@
 EDGE = 12
 PLACING = 10**10
 PLACES = (2, 3, 1)
+ORDERS = ((1, 2), (2, 1))
 RIDING = 8
 
 
@@ -138,8 +139,14 @@
     return value
 
 
-def pair_kernel(weights, instances, first, seconds, state, partner, *outs):
+def of_core(orders):
+    odd = lax.axis_index("space") % 2
+    return [jnp.where(odd == 1, b, a) for a, b in zip(*orders)]
+
+
+def pair_kernel(weights, instances, orders, state, partner, *outs):
     me = lax.axis_index("inst")
+    first, *seconds = of_core(orders)
     for second, out in zip(seconds, outs):
         own = weight_from(weights, instances, me, me ^ second)
         other = weight_from(weights, instances, me ^ first, me ^ second)
@@ -185,7 +192,7 @@
         base[0, c] = residual + (upper - lower)
 
 
-def outer_kernel(weights, instances, first, blocks, state, base, kept, came, partner, *refs):
+def outer_kernel(weights, instances, orders, blocks, state, base, kept, came, partner, *refs):
     *edges, residual, total = refs
     radial, around = state.shape[2:]
     if blocks == RIDING:
@@ -208,7 +215,7 @@
     else:
         before, after = (ref[0:1, :] for ref in edges)
     me = lax.axis_index("inst")
-    weight = weight_from(weights, instances, me ^ first, me)
+    weight = weight_from(weights, instances, me ^ of_core(orders)[0], me)
     lane = lax.broadcasted_iota(jnp.int32, (1, LANES), 1)
     edge = jnp.where(lane < LANES // 2, before, after)
     columns = jnp.broadcast_to(edge, (LANES, LANES)).T
@@ -285,8 +292,16 @@
         )(*operands)
 
     weights = spectral_row(instances)
-    first, seconds = 1, range(2, instances, 2)
-    partner = swapped(state, "inst", first)
+    def partnered(value, place):
+        pairs = [
+            (i * instances + n, i * instances + (n ^ orders[i % 2][place]))
+            for i in range(blocks)
+            for n in range(instances)
+        ]
+        return lax.ppermute(value, ("space", "inst"), pairs)
+
+    orders = ORDERS if instances == 4 else ((1, *range(2, instances, 2)),) * 2
+    partner = partnered(state, 0)
 
     riding = blocks == RIDING
     steps = [4, 2] if riding else [2] * (blocks.bit_length() - 1)
@@ -317,14 +332,14 @@
 
     came = exchanged(sent, size)
     sums = call(
-        functools.partial(pair_kernel, weights, instances, first, seconds),
+        functools.partial(pair_kernel, weights, instances, orders),
         "pair_sums",
-        [state.shape] * len(seconds),
+        [state.shape] * (len(orders[0]) - 1),
         state,
         partner,
         flops=PLACING,
     )
-    sums = [swapped(value, "inst", second) for second, value in zip(seconds, sums)]
+    sums = [partnered(value, i) for i, value in enumerate(sums, 1)]
 
     for step in steps[1:]:
         size //= step
@@ -345,7 +360,7 @@
         state,
     )
     residual, total = call(
-        functools.partial(outer_kernel, weights, instances, first, blocks),
+        functools.partial(outer_kernel, weights, instances, orders, blocks),
         "outer",
         [state.shape, (ROWS, LANES)],
         state,

time: 14.5 us -> 14.5 us (level)
    ppermute x0 -> x2, starting transfers between devices: none -> 5.74 us  [partnered(): return lax.ppermute(value, ('space', 'inst'), pairs)]
    ppermute x6 -> x4, starting transfers between devices: 9.37 us -> 3.62 us  [swapped(): lax.ppermute(value, axis, [(i, i ^ bit) for i in range(lax.axis_size(axis...]
    ppermute x6 -> x4, waiting for transfers between devices: 2.83 us -> 1.47 us  [swapped(): lax.ppermute(value, axis, [(i, i ^ bit) for i in range(lax.axis_size(axis...]
    ppermute x0 -> x2, waiting for transfers between devices: none -> 1.36 us  [partnered(): return lax.ppermute(value, ('space', 'inst'), pairs)]
where the time goes in v12:
time: 14.5 us; the launch traced here: 14.4 us
  starting transfers between devices  9.37 us (65%)
  waiting for transfers between devices  2.83 us (20%)
  Pallas kernels  1.41 us (10%)
  between operations  0.72 us (5%)
    ppermute x2, starting transfers between devices, partnered(): return lax.ppermute(value, ('space', 'inst'), pairs)  5.74 us
    ppermute x4, starting transfers between devices, swapped(): lax.ppermute(value, axis, [(i, i ^ bit) for i in range(lax.axis_size(axis...  3.62 us
    ppermute x4, waiting for transfers between devices, swapped(): lax.ppermute(value, axis, [(i, i ^ bit) for i in range(lax.axis_size(axis...  1.47 us
    pallas_call x7, Pallas kernels, call(): pl.pallas_call(kernel, out_shape=[jax.ShapeDtypeStruct(shape, dtype) for...  1.41 us
    ppermute x2, waiting for transfers between devices, partnered(): return lax.ppermute(value, ('space', 'inst'), pairs)  1.36 us
  transfers between devices with their start and end apart: 6, of which 3 were waited for; matrix products, arithmetic and copies ran while one was open for 0% of the time, Pallas kernels for 5%

profile of v12, /device:TPU:0, one launch (start us, length us, event | category | flops | bytes accessed | tf_op | source)
XLA Modules:
  0.0 14.4 jit_solution(7583288937245160534)
XLA Ops:
  0.6 0.0 copy-start
  0.6 0.0 copy-start.2
  0.7 0.0 copy-start.3
  0.7 0.0 copy-start.1
  0.7 3.1 %collective-permute-start.4 = (f32[1,4,16,256]{3,2,1,0:T(8,128)}, f32[1,4,16,256]{3,2,1,0:T(8,128)S(1)}, u32[]{:S(2)}, u32[]{:S(2)}) collective-permute-start(f32[1,4,16,256]{3,2,1,0:T(8,128)} %state.7), channel_id=1, source_target_pairs={{0,1},{1,0},{2,3},{3,2},{4,6},{5,7},{6,4},{7,5},{8,9},{9,8},{10,11... | collective-permute-start | bytes 196616 | tf_op jit(solution)/shard_map/ppermute | solution.py:301
  3.8 0.0 copy-done
  3.8 0.0 copy-done.2
  3.8 0.0 copy-done.3
  3.8 0.0 copy-done.1
  3.8 0.4 %face_forces.1 = (f32[2,16,128]{2,1,0:T(8,128)S(1)}, f32[2,16,128]{2,1,0:T(8,128)S(1)}, f32[2,16,128]{2,1,0:T(8,128)S(1)}, f32[2,16,128]{2,1,0:T(8,128)S(1)}) custom-call(s32[8,128]{1,0:T(8,128)S(1)} %own.1, f32[1,4,16,256]{3,2,1,0:T(8,128)S(1)} %copy-done, s32[6,128]{1,0:T(8,128)S(1)} %bitcast.3, s32[6,128]{1,0:T(8,128)S(1)} %bitcast.4, f32[3,768]{1,0:T(4,128)S(1)} %copy-done.1), custom_call_target="tpu_custom_call" | custom-call | flops 10000000000 | tf_op jit(solution)/shard_map/face_forces/pallas_call | solution.py:284
  4.2 1.6 %collective-permute-start = (f32[2,16,128]{2,1,0:T(8,128)S(1)}, f32[2,16,128]{2,1,0:T(8,128)S(1)}, u32[]{:S(2)}, u32[]{:S(2)}) collective-permute-start(f32[2,16,128]{2,1,0:T(8,128)S(1)} %get-tuple-element.16), channel_id=1, source_target_pairs={{0,16},{4,20},{8,24},{12,28},{16,0},{20,4},{24,8},{28,12},{1,17},{... | collective-permute-start | bytes 49160 | tf_op jit(solution)/shard_map/ppermute | solution.py:273
  5.8 1.4 %collective-permute-start.1 = (f32[2,16,128]{2,1,0:T(8,128)S(1)}, f32[2,16,128]{2,1,0:T(8,128)S(1)}, u32[]{:S(2)}, u32[]{:S(2)}) collective-permute-start(f32[2,16,128]{2,1,0:T(8,128)S(1)} %get-tuple-element.17), channel_id=1, source_target_pairs={{0,24},{4,28},{8,16},{12,20},{16,8},{20,12},{24,0},{28,4},{1,25},{... | collective-permute-start | bytes 49160 | tf_op jit(solution)/shard_map/ppermute | solution.py:273
  7.2 0.5 %collective-permute-start.2 = (f32[2,16,128]{2,1,0:T(8,128)S(1)}, f32[2,16,128]{2,1,0:T(8,128)S(1)}, u32[]{:S(2)}, u32[]{:S(2)}) collective-permute-start(f32[2,16,128]{2,1,0:T(8,128)S(1)} %get-tuple-element.18), channel_id=1, source_target_pairs={{0,8},{4,12},{8,0},{12,4},{16,24},{20,28},{24,16},{28,20},{1,9},{5... | collective-permute-start | bytes 49160 | tf_op jit(solution)/shard_map/ppermute | solution.py:273
  7.7 0.0 collective-permute-done.4.partner
  7.8 2.7 %collective-permute-start.5 = (f32[1,4,16,256]{3,2,1,0:T(8,128)S(1)}, f32[1,4,16,256]{3,2,1,0:T(8,128)S(1)}, u32[]{:S(2)}, u32[]{:S(2)}) collective-permute-start(f32[1,4,16,256]{3,2,1,0:T(8,128)S(1)} %pair_sums.1), channel_id=1, source_target_pairs={{0,2},{1,3},{2,0},{3,1},{4,5},{5,4},{6,7},{7,6},{8,10},{9,11},{10,... | collective-permute-start | bytes 196616 | tf_op jit(solution)/shard_map/ppermute | solution.py:301
  10.4 0.0 collective-permute-done.refs_1_
  10.4 0.0 collective-permute-done.1.refs_2_
  10.4 0.5 %collective-permute-done.2.refs_3_ = f32[2,16,128]{2,1,0:T(8,128)S(1)} collective-permute-done((f32[2,16,128]{2,1,0:T(8,128)S(1)}, f32[2,16,128]{2,1,0:T(8,128)S(1)}, u32[]{:S(2)}, u32[]{:S(2)}) %collective-permute-start.2) | collective-permute-done | bytes 16416 | tf_op jit(solution)/shard_map/ppermute | solution.py:273
  10.9 0.1 collective-permute-start.3
  11.0 0.2 %flux.1 = (f32[1,4,16,256]{3,2,1,0:T(8,128)S(1)}, f32[16,256]{1,0:T(8,128)S(1)}) custom-call(f32[1,4,16,256]{3,2,1,0:T(8,128)S(1)} %copy-done), custom_call_target="tpu_custom_call" | custom-call | tf_op jit(solution)/shard_map/flux/pallas_call | solution.py:284
  11.2 1.0 %collective-permute-done.3.came = f32[1,16,128]{2,1,0:T(8,128)S(1)} collective-permute-done((f32[1,16,128]{2,1,0:T(8,128)S(1)}, f32[1,16,128]{2,1,0:T(8,128)S(1)}, u32[]{:S(2)}, u32[]{:S(2)}) %collective-permute-start.3) | collective-permute-done | bytes 8224 | tf_op jit(solution)/shard_map/ppermute | solution.py:273
  12.2 0.2 %outer.1 = (f32[1,4,16,256]{3,2,1,0:T(8,128)S(1)}, f32[16,128]{1,0:T(8,128)S(1)}) custom-call(f32[1,4,16,256]{3,2,1,0:T(8,128)S(1)} %copy-done, f32[1,4,16,256]{3,2,1,0:T(8,128)S(1)} %get-tuple-element.14.base, f32[1,16,128]{2,1,0:T(8,128)S(1)} %get-tuple-element.19.kept, f32[1,16,128]{2,1,0:T(8,128)S(1)} %collective-permute-done.3.came, ...), custom_call_target="tpu_custom_call" | custom-call | tf_op jit(solution)/shard_map/outer/pallas_call | solution.py:284
  12.3 1.4 %collective-permute-done.5.refs_0_ = f32[1,4,16,256]{3,2,1,0:T(8,128)S(1)} collective-permute-done((f32[1,4,16,256]{3,2,1,0:T(8,128)S(1)}, f32[1,4,16,256]{3,2,1,0:T(8,128)S(1)}, u32[]{:S(2)}, u32[]{:S(2)}) %collective-permute-start.5) | collective-permute-done | bytes 65568 | tf_op jit(solution)/shard_map/ppermute | solution.py:301
  13.7 0.6 %update.1 = (f32[1,4,16,256]{3,2,1,0:T(8,128)}, f32[3,1,512]{2,1,0:T(1,128)}) custom-call(f32[1,4,16,256]{3,2,1,0:T(8,128)S(1)} %get-tuple-element.21.residual, f32[16,256]{1,0:T(8,128)S(1)} %get-tuple-element.22.step, f32[16,128]{1,0:T(8,128)S(1)} %get-tuple-element.23.total, f32[1,4,16,256]{3,2,1,0:T(8,128)S(1)} %collective-permute-done.5.refs_0_), custom_call_target="tpu_custom_call" | custom-call | tf_op jit(solution)/shard_map/update/pallas_call | solution.py:284
  (3 shorter events, 0.0 us)
Async XLA Ops:
  0.6 3.1 %copy-start = (f32[1,4,16,256]{3,2,1,0:T(8,128)S(1)}, f32[1,4,16,256]{3,2,1,0:T(8,128)}, u32[]{:S(2)}) copy-start(f32[1,4,16,256]{3,2,1,0:T(8,128)} %state.7) | copy-start | bytes 196612
  0.6 3.1 %copy-start.2 = (s32[768]{0:T(1024)S(1)}, s32[768]{0:T(1024)}, u32[]{:S(2)}) copy-start(s32[768]{0:T(1024)} %param.5) | copy-start | bytes 9220
  0.7 3.1 %copy-start.3 = (s32[768]{0:T(1024)S(1)}, s32[768]{0:T(1024)}, u32[]{:S(2)}) copy-start(s32[768]{0:T(1024)} %param.6) | copy-start | bytes 9220
  0.7 3.1 %copy-start.1 = (f32[3,768]{1,0:T(4,128)S(1)}, f32[3,768]{1,0:T(4,128)}, u32[]{:S(2)}) copy-start(f32[3,768]{1,0:T(4,128)} %area.1) | copy-start | bytes 27652
  0.7 7.1 %collective-permute-start.4 = (f32[1,4,16,256]{3,2,1,0:T(8,128)}, f32[1,4,16,256]{3,2,1,0:T(8,128)S(1)}, u32[]{:S(2)}, u32[]{:S(2)}) collective-permute-start(f32[1,4,16,256]{3,2,1,0:T(8,128)} %state.7), channel_id=1, source_target_pairs={{0,1},{1,0},{2,3},{3,2},{4,6},{5,7},{6,4},{7,5},{8,9},{9,8},{10,11... | collective-permute-start | bytes 196616 | tf_op jit(solution)/shard_map/ppermute | solution.py:301
  4.2 6.3 %collective-permute-start = (f32[2,16,128]{2,1,0:T(8,128)S(1)}, f32[2,16,128]{2,1,0:T(8,128)S(1)}, u32[]{:S(2)}, u32[]{:S(2)}) collective-permute-start(f32[2,16,128]{2,1,0:T(8,128)S(1)} %get-tuple-element.16), channel_id=1, source_target_pairs={{0,16},{4,20},{8,24},{12,28},{16,0},{20,4},{24,8},{28,12},{1,17},{... | collective-permute-start | bytes 49160 | tf_op jit(solution)/shard_map/ppermute | solution.py:273
  5.8 4.7 %collective-permute-start.1 = (f32[2,16,128]{2,1,0:T(8,128)S(1)}, f32[2,16,128]{2,1,0:T(8,128)S(1)}, u32[]{:S(2)}, u32[]{:S(2)}) collective-permute-start(f32[2,16,128]{2,1,0:T(8,128)S(1)} %get-tuple-element.17), channel_id=1, source_target_pairs={{0,24},{4,28},{8,16},{12,20},{16,8},{20,12},{24,0},{28,4},{1,25},{... | collective-permute-start | bytes 49160 | tf_op jit(solution)/shard_map/ppermute | solution.py:273
  7.2 3.7 %collective-permute-start.2 = (f32[2,16,128]{2,1,0:T(8,128)S(1)}, f32[2,16,128]{2,1,0:T(8,128)S(1)}, u32[]{:S(2)}, u32[]{:S(2)}) collective-permute-start(f32[2,16,128]{2,1,0:T(8,128)S(1)} %get-tuple-element.18), channel_id=1, source_target_pairs={{0,8},{4,12},{8,0},{12,4},{16,24},{20,28},{24,16},{28,20},{1,9},{5... | collective-permute-start | bytes 49160 | tf_op jit(solution)/shard_map/ppermute | solution.py:273
  7.8 5.9 %collective-permute-start.5 = (f32[1,4,16,256]{3,2,1,0:T(8,128)S(1)}, f32[1,4,16,256]{3,2,1,0:T(8,128)S(1)}, u32[]{:S(2)}, u32[]{:S(2)}) collective-permute-start(f32[1,4,16,256]{3,2,1,0:T(8,128)S(1)} %pair_sums.1), channel_id=1, source_target_pairs={{0,2},{1,3},{2,0},{3,1},{4,5},{5,4},{6,7},{7,6},{8,10},{9,11},{10,... | collective-permute-start | bytes 196616 | tf_op jit(solution)/shard_map/ppermute | solution.py:301
  10.9 1.2 %collective-permute-start.3 = (f32[1,16,128]{2,1,0:T(8,128)S(1)}, f32[1,16,128]{2,1,0:T(8,128)S(1)}, u32[]{:S(2)}, u32[]{:S(2)}) collective-permute-start(f32[1,16,128]{2,1,0:T(8,128)S(1)} %get-tuple-element.20), channel_id=1, source_target_pairs={{0,4},{4,0},{8,12},{12,8},{16,20},{20,16},{24,28},{28,24},{1,5},{5... | collective-permute-start | bytes 24584 | tf_op jit(solution)/shard_map/ppermute | solution.py:273

commit v13 on v11

--- a/solution.py
+++ b/solution.py
@@ -18,6 +18,7 @@
 EDGE = 12
 PLACING = 10**10
 PLACES = (2, 3, 1)
+PARTS = 2
 RIDING = 8
 
 
@@ -140,10 +141,11 @@
 
 def pair_kernel(weights, instances, first, seconds, state, partner, *outs):
     me = lax.axis_index("inst")
-    for second, out in zip(seconds, outs):
+    for i, out in enumerate(outs):
+        second, part = seconds[i // PARTS], pl.ds(i % PARTS * out.shape[1], out.shape[1])
         own = weight_from(weights, instances, me, me ^ second)
         other = weight_from(weights, instances, me ^ first, me ^ second)
-        out[...] = own * state[...] + other * partner[...]
+        out[...] = own * state[:, part] + other * partner[:, part]
 
 
 def around_flux(q, vc, p):
@@ -250,7 +252,9 @@
         for h in range(high):
             blade[k, :, pl.ds(h * LANES, LANES)] = total[k * high + h : k * high + h + 1, :]
     for c in range(residual.shape[1]):
-        change = functools.reduce(jnp.add, [ref[0, c] for ref in (residual, *sums)])
+        size = residual.shape[1] // PARTS
+        parts = [ref[0, c % size] for ref in sums[c // size :: PARTS]]
+        change = functools.reduce(jnp.add, [residual[0, c], *parts])
         increment[0, c] = -step[...] * change
 
 
@@ -319,12 +323,12 @@
     sums = call(
         functools.partial(pair_kernel, weights, instances, first, seconds),
         "pair_sums",
-        [state.shape] * len(seconds),
+        [(1, 4 // PARTS, radial, around)] * (PARTS * len(seconds)),
         state,
         partner,
         flops=PLACING,
     )
-    sums = [swapped(value, "inst", second) for second, value in zip(seconds, sums)]
+    sums = [swapped(value, "inst", seconds[i // PARTS]) for i, value in enumerate(sums)]
 
     for step in steps[1:]:
         size //= step

time: 14.5 us -> 16.4 us (1.13)
  waiting for transfers between devices: 2.83 us -> 4.38 us
  starting transfers between devices: 9.37 us -> 9.7 us
    ppermute x6 -> x7, waiting for transfers between devices: 2.83 us -> 4.38 us  [swapped(): lax.ppermute(value, axis, [(i, i ^ bit) for i in range(lax.axis_size(axis...]
    ppermute x6 -> x7, starting transfers between devices: 9.37 us -> 9.7 us  [swapped(): lax.ppermute(value, axis, [(i, i ^ bit) for i in range(lax.axis_size(axis...]
  transfers between devices with their start and end apart: 6 -> 7, of which waited for: 3 -> 4; matrix products, arithmetic and copies ran while one was open for 0% -> 0% of each run, Pallas kernels for 5% -> 5%
where the time goes in v13:
time: 16.4 us; the launch traced here: 16.2 us
  starting transfers between devices  9.7 us (59%)
  waiting for transfers between devices  4.38 us (27%)
  Pallas kernels  1.4 us (9%)
  between operations  0.72 us (4%)
    ppermute x7, starting transfers between devices, swapped(): lax.ppermute(value, axis, [(i, i ^ bit) for i in range(lax.axis_size(axis...  9.7 us
    ppermute x7, waiting for transfers between devices, swapped(): lax.ppermute(value, axis, [(i, i ^ bit) for i in range(lax.axis_size(axis...  4.38 us
    pallas_call x7, Pallas kernels, call(): pl.pallas_call(kernel, out_shape=[jax.ShapeDtypeStruct(shape, dtype) for...  1.4 us
  transfers between devices with their start and end apart: 7, of which 4 were waited for; matrix products, arithmetic and copies ran while one was open for 0% of the time, Pallas kernels for 5%

profile of v13, /device:TPU:0, one launch (start us, length us, event | category | flops | bytes accessed | tf_op | source)
XLA Modules:
  0.0 16.2 jit_solution(4817240113309562257)
XLA Ops:
  0.6 0.0 copy-start
  0.6 0.0 copy-start.2
  0.7 0.0 copy-start.3
  0.7 0.0 copy-start.1
  0.7 3.1 %collective-permute-start.4 = (f32[1,4,16,256]{3,2,1,0:T(8,128)}, f32[1,4,16,256]{3,2,1,0:T(8,128)S(1)}, u32[]{:S(2)}, u32[]{:S(2)}) collective-permute-start(f32[1,4,16,256]{3,2,1,0:T(8,128)} %state.7), channel_id=1, source_target_pairs={{0,1},{1,0},{2,3},{3,2},{4,5},{5,4},{6,7},{7,6},{8,9},{9,8},{10,11... | collective-permute-start | bytes 196616 | tf_op jit(solution)/shard_map/ppermute | solution.py:270
  3.8 0.0 copy-done
  3.8 0.0 copy-done.2
  3.8 0.0 copy-done.3
  3.8 0.0 copy-done.1
  3.8 0.4 %face_forces.1 = (f32[2,16,128]{2,1,0:T(8,128)S(1)}, f32[2,16,128]{2,1,0:T(8,128)S(1)}, f32[2,16,128]{2,1,0:T(8,128)S(1)}, f32[2,16,128]{2,1,0:T(8,128)S(1)}) custom-call(s32[8,128]{1,0:T(8,128)S(1)} %own.1, f32[1,4,16,256]{3,2,1,0:T(8,128)S(1)} %copy-done, s32[6,128]{1,0:T(8,128)S(1)} %bitcast.3, s32[6,128]{1,0:T(8,128)S(1)} %bitcast.4, f32[3,768]{1,0:T(4,128)S(1)} %copy-done.1), custom_call_target="tpu_custom_call" | custom-call | flops 10000000000 | tf_op jit(solution)/shard_map/face_forces/pallas_call | solution.py:281
  4.2 1.6 %collective-permute-start = (f32[2,16,128]{2,1,0:T(8,128)S(1)}, f32[2,16,128]{2,1,0:T(8,128)S(1)}, u32[]{:S(2)}, u32[]{:S(2)}) collective-permute-start(f32[2,16,128]{2,1,0:T(8,128)S(1)} %get-tuple-element.18), channel_id=1, source_target_pairs={{0,16},{4,20},{8,24},{12,28},{16,0},{20,4},{24,8},{28,12},{1,17},{... | collective-permute-start | bytes 49160 | tf_op jit(solution)/shard_map/ppermute | solution.py:270
  5.8 1.4 %collective-permute-start.1 = (f32[2,16,128]{2,1,0:T(8,128)S(1)}, f32[2,16,128]{2,1,0:T(8,128)S(1)}, u32[]{:S(2)}, u32[]{:S(2)}) collective-permute-start(f32[2,16,128]{2,1,0:T(8,128)S(1)} %get-tuple-element.19), channel_id=1, source_target_pairs={{0,24},{4,28},{8,16},{12,20},{16,8},{20,12},{24,0},{28,4},{1,25},{... | collective-permute-start | bytes 49160 | tf_op jit(solution)/shard_map/ppermute | solution.py:270
  7.2 0.5 %collective-permute-start.2 = (f32[2,16,128]{2,1,0:T(8,128)S(1)}, f32[2,16,128]{2,1,0:T(8,128)S(1)}, u32[]{:S(2)}, u32[]{:S(2)}) collective-permute-start(f32[2,16,128]{2,1,0:T(8,128)S(1)} %get-tuple-element.20), channel_id=1, source_target_pairs={{0,8},{4,12},{8,0},{12,4},{16,24},{20,28},{24,16},{28,20},{1,9},{5... | collective-permute-start | bytes 49160 | tf_op jit(solution)/shard_map/ppermute | solution.py:270
  7.7 0.0 collective-permute-done.4.partner
  7.8 2.7 %collective-permute-start.5 = (f32[1,2,16,256]{3,2,1,0:T(8,128)S(1)}, f32[1,2,16,256]{3,2,1,0:T(8,128)S(1)}, u32[]{:S(2)}, u32[]{:S(2)}) collective-permute-start(f32[1,2,16,256]{3,2,1,0:T(8,128)S(1)} %get-tuple-element.26), channel_id=1, source_target_pairs={{0,2},{1,3},{2,0},{3,1},{4,6},{5,7},{6,4},{7,5},{8,10},{9,11},{10,... | collective-permute-start | bytes 98312 | tf_op jit(solution)/shard_map/ppermute | solution.py:270
  10.4 0.3 %collective-permute-start.6 = (f32[1,2,16,256]{3,2,1,0:T(8,128)S(1)}, f32[1,2,16,256]{3,2,1,0:T(8,128)S(1)}, u32[]{:S(2)}, u32[]{:S(2)}) collective-permute-start(f32[1,2,16,256]{3,2,1,0:T(8,128)S(1)} %get-tuple-element.27), channel_id=1, source_target_pairs={{0,2},{1,3},{2,0},{3,1},{4,6},{5,7},{6,4},{7,5},{8,10},{9,11},{10,... | collective-permute-start | bytes 98312 | tf_op jit(solution)/shard_map/ppermute | solution.py:270
  10.8 0.0 collective-permute-done.refs_1_
  10.8 0.0 collective-permute-done.1.refs_2_
  10.8 0.2 %collective-permute-done.2.refs_3_ = f32[2,16,128]{2,1,0:T(8,128)S(1)} collective-permute-done((f32[2,16,128]{2,1,0:T(8,128)S(1)}, f32[2,16,128]{2,1,0:T(8,128)S(1)}, u32[]{:S(2)}, u32[]{:S(2)}) %collective-permute-start.2) | collective-permute-done | bytes 16416 | tf_op jit(solution)/shard_map/ppermute | solution.py:270
  10.9 0.1 collective-permute-start.3
  11.0 0.2 %flux.1 = (f32[1,4,16,256]{3,2,1,0:T(8,128)S(1)}, f32[16,256]{1,0:T(8,128)S(1)}) custom-call(f32[1,4,16,256]{3,2,1,0:T(8,128)S(1)} %copy-done), custom_call_target="tpu_custom_call" | custom-call | tf_op jit(solution)/shard_map/flux/pallas_call | solution.py:281
  11.2 1.0 %collective-permute-done.3.came = f32[1,16,128]{2,1,0:T(8,128)S(1)} collective-permute-done((f32[1,16,128]{2,1,0:T(8,128)S(1)}, f32[1,16,128]{2,1,0:T(8,128)S(1)}, u32[]{:S(2)}, u32[]{:S(2)}) %collective-permute-start.3) | collective-permute-done | bytes 8224 | tf_op jit(solution)/shard_map/ppermute | solution.py:270
  12.2 0.2 outer.1
  12.3 1.3 %collective-permute-done.5.refs_0_ = f32[1,2,16,256]{3,2,1,0:T(8,128)S(1)} collective-permute-done((f32[1,2,16,256]{3,2,1,0:T(8,128)S(1)}, f32[1,2,16,256]{3,2,1,0:T(8,128)S(1)}, u32[]{:S(2)}, u32[]{:S(2)}) %collective-permute-start.5) | collective-permute-done | bytes 32800 | tf_op jit(solution)/shard_map/ppermute | solution.py:270
  13.6 1.9 %collective-permute-done.6.refs_1_ = f32[1,2,16,256]{3,2,1,0:T(8,128)S(1)} collective-permute-done((f32[1,2,16,256]{3,2,1,0:T(8,128)S(1)}, f32[1,2,16,256]{3,2,1,0:T(8,128)S(1)}, u32[]{:S(2)}, u32[]{:S(2)}) %collective-permute-start.6) | collective-permute-done | bytes 32800 | tf_op jit(solution)/shard_map/ppermute | solution.py:270
  15.6 0.6 %update.1 = (f32[1,4,16,256]{3,2,1,0:T(8,128)}, f32[3,1,512]{2,1,0:T(1,128)}) custom-call(f32[1,4,16,256]{3,2,1,0:T(8,128)S(1)} %get-tuple-element.23.residual, f32[16,256]{1,0:T(8,128)S(1)} %get-tuple-element.24.step, f32[16,128]{1,0:T(8,128)S(1)} %get-tuple-element.25.total, f32[1,2,16,256]{3,2,1,0:T(8,128)S(1)} %collective-permute-done.5.refs_0_, ...), custom_call_target="tpu_custom_call" | custom-call | tf_op jit(solution)/shard_map/update/pallas_call | solution.py:281
  (3 shorter events, 0.0 us)
Async XLA Ops:
  0.6 3.1 %copy-start = (f32[1,4,16,256]{3,2,1,0:T(8,128)S(1)}, f32[1,4,16,256]{3,2,1,0:T(8,128)}, u32[]{:S(2)}) copy-start(f32[1,4,16,256]{3,2,1,0:T(8,128)} %state.7) | copy-start | bytes 196612
  0.6 3.1 %copy-start.2 = (s32[768]{0:T(1024)S(1)}, s32[768]{0:T(1024)}, u32[]{:S(2)}) copy-start(s32[768]{0:T(1024)} %param.5) | copy-start | bytes 9220
  0.7 3.1 %copy-start.3 = (s32[768]{0:T(1024)S(1)}, s32[768]{0:T(1024)}, u32[]{:S(2)}) copy-start(s32[768]{0:T(1024)} %param.6) | copy-start | bytes 9220
  0.7 3.1 %copy-start.1 = (f32[3,768]{1,0:T(4,128)S(1)}, f32[3,768]{1,0:T(4,128)}, u32[]{:S(2)}) copy-start(f32[3,768]{1,0:T(4,128)} %area.1) | copy-start | bytes 27652
  0.7 7.1 %collective-permute-start.4 = (f32[1,4,16,256]{3,2,1,0:T(8,128)}, f32[1,4,16,256]{3,2,1,0:T(8,128)S(1)}, u32[]{:S(2)}, u32[]{:S(2)}) collective-permute-start(f32[1,4,16,256]{3,2,1,0:T(8,128)} %state.7), channel_id=1, source_target_pairs={{0,1},{1,0},{2,3},{3,2},{4,5},{5,4},{6,7},{7,6},{8,9},{9,8},{10,11... | collective-permute-start | bytes 196616 | tf_op jit(solution)/shard_map/ppermute | solution.py:270
  4.2 6.6 %collective-permute-start = (f32[2,16,128]{2,1,0:T(8,128)S(1)}, f32[2,16,128]{2,1,0:T(8,128)S(1)}, u32[]{:S(2)}, u32[]{:S(2)}) collective-permute-start(f32[2,16,128]{2,1,0:T(8,128)S(1)} %get-tuple-element.18), channel_id=1, source_target_pairs={{0,16},{4,20},{8,24},{12,28},{16,0},{20,4},{24,8},{28,12},{1,17},{... | collective-permute-start | bytes 49160 | tf_op jit(solution)/shard_map/ppermute | solution.py:270
  5.8 5.0 %collective-permute-start.1 = (f32[2,16,128]{2,1,0:T(8,128)S(1)}, f32[2,16,128]{2,1,0:T(8,128)S(1)}, u32[]{:S(2)}, u32[]{:S(2)}) collective-permute-start(f32[2,16,128]{2,1,0:T(8,128)S(1)} %get-tuple-element.19), channel_id=1, source_target_pairs={{0,24},{4,28},{8,16},{12,20},{16,8},{20,12},{24,0},{28,4},{1,25},{... | collective-permute-start | bytes 49160 | tf_op jit(solution)/shard_map/ppermute | solution.py:270
  7.2 3.7 %collective-permute-start.2 = (f32[2,16,128]{2,1,0:T(8,128)S(1)}, f32[2,16,128]{2,1,0:T(8,128)S(1)}, u32[]{:S(2)}, u32[]{:S(2)}) collective-permute-start(f32[2,16,128]{2,1,0:T(8,128)S(1)} %get-tuple-element.20), channel_id=1, source_target_pairs={{0,8},{4,12},{8,0},{12,4},{16,24},{20,28},{24,16},{28,20},{1,9},{5... | collective-permute-start | bytes 49160 | tf_op jit(solution)/shard_map/ppermute | solution.py:270
  7.8 5.9 %collective-permute-start.5 = (f32[1,2,16,256]{3,2,1,0:T(8,128)S(1)}, f32[1,2,16,256]{3,2,1,0:T(8,128)S(1)}, u32[]{:S(2)}, u32[]{:S(2)}) collective-permute-start(f32[1,2,16,256]{3,2,1,0:T(8,128)S(1)} %get-tuple-element.26), channel_id=1, source_target_pairs={{0,2},{1,3},{2,0},{3,1},{4,6},{5,7},{6,4},{7,5},{8,10},{9,11},{10,... | collective-permute-start | bytes 98312 | tf_op jit(solution)/shard_map/ppermute | solution.py:270
  10.4 5.2 %collective-permute-start.6 = (f32[1,2,16,256]{3,2,1,0:T(8,128)S(1)}, f32[1,2,16,256]{3,2,1,0:T(8,128)S(1)}, u32[]{:S(2)}, u32[]{:S(2)}) collective-permute-start(f32[1,2,16,256]{3,2,1,0:T(8,128)S(1)} %get-tuple-element.27), channel_id=1, source_target_pairs={{0,2},{1,3},{2,0},{3,1},{4,6},{5,7},{6,4},{7,5},{8,10},{9,11},{10,... | collective-permute-start | bytes 98312 | tf_op jit(solution)/shard_map/ppermute | solution.py:270
  10.9 1.2 %collective-permute-start.3 = (f32[1,16,128]{2,1,0:T(8,128)S(1)}, f32[1,16,128]{2,1,0:T(8,128)S(1)}, u32[]{:S(2)}, u32[]{:S(2)}) collective-permute-start(f32[1,16,128]{2,1,0:T(8,128)S(1)} %get-tuple-element.22), channel_id=1, source_target_pairs={{0,4},{4,0},{8,12},{12,8},{16,20},{20,16},{24,28},{28,24},{1,5},{5... | collective-permute-start | bytes 24584 | tf_op jit(solution)/shard_map/ppermute | solution.py:270

commit v14 on v12

--- a/solution.py
+++ b/solution.py
@@ -18,7 +18,7 @@
 EDGE = 12
 PLACING = 10**10
 PLACES = (2, 3, 1)
-ORDERS = ((1, 2), (2, 1))
+ORDERS = ((2, 1), (1, 2))
 RIDING = 8
 
 
@@ -139,14 +139,14 @@
     return value
 
 
-def of_core(orders):
-    odd = lax.axis_index("space") % 2
-    return [jnp.where(odd == 1, b, a) for a, b in zip(*orders)]
+def of_chip(orders):
+    chip = lax.axis_index("space") // 2
+    return [jnp.where(chip == 0, a, b) for a, b in zip(*orders)]
 
 
 def pair_kernel(weights, instances, orders, state, partner, *outs):
     me = lax.axis_index("inst")
-    first, *seconds = of_core(orders)
+    first, *seconds = of_chip(orders)
     for second, out in zip(seconds, outs):
         own = weight_from(weights, instances, me, me ^ second)
         other = weight_from(weights, instances, me ^ first, me ^ second)
@@ -215,7 +215,7 @@
     else:
         before, after = (ref[0:1, :] for ref in edges)
     me = lax.axis_index("inst")
-    weight = weight_from(weights, instances, me ^ of_core(orders)[0], me)
+    weight = weight_from(weights, instances, me ^ of_chip(orders)[0], me)
     lane = lax.broadcasted_iota(jnp.int32, (1, LANES), 1)
     edge = jnp.where(lane < LANES // 2, before, after)
     columns = jnp.broadcast_to(edge, (LANES, LANES)).T
@@ -294,7 +294,7 @@
     weights = spectral_row(instances)
     def partnered(value, place):
         pairs = [
-            (i * instances + n, i * instances + (n ^ orders[i % 2][place]))
+            (i * instances + n, i * instances + (n ^ orders[min(i // 2, 1)][place]))
             for i in range(blocks)
             for n in range(instances)
         ]

time: 14.5 us -> 13.9 us (0.959)
  waiting for transfers between devices: 2.83 us -> 2.24 us
    ppermute x2, waiting for transfers between devices: 1.36 us -> 0.78 us  [partnered(): return lax.ppermute(value, ('space', 'inst'), pairs)]
  transfers between devices with their start and end apart: 6 -> 6, of which waited for: 3 -> 3; matrix products, arithmetic and copies ran while one was open for 0% -> 0% of each run, Pallas kernels for 5% -> 6%
where the time goes in v14:
time: 13.9 us; the launch traced here: 13.8 us
  starting transfers between devices  9.37 us (67%)
  waiting for transfers between devices  2.24 us (16%)
  Pallas kernels  1.41 us (10%)
  between operations  0.72 us (5%)
    ppermute x2, starting transfers between devices, partnered(): return lax.ppermute(value, ('space', 'inst'), pairs)  5.74 us
    ppermute x4, starting transfers between devices, swapped(): lax.ppermute(value, axis, [(i, i ^ bit) for i in range(lax.axis_size(axis...  3.62 us
    ppermute x4, waiting for transfers between devices, swapped(): lax.ppermute(value, axis, [(i, i ^ bit) for i in range(lax.axis_size(axis...  1.47 us
    pallas_call x7, Pallas kernels, call(): pl.pallas_call(kernel, out_shape=[jax.ShapeDtypeStruct(shape, dtype) for...  1.41 us
    ppermute x2, waiting for transfers between devices, partnered(): return lax.ppermute(value, ('space', 'inst'), pairs)  0.78 us
  transfers between devices with their start and end apart: 6, of which 3 were waited for; matrix products, arithmetic and copies ran while one was open for 0% of the time, Pallas kernels for 6%

profile of v14, /device:TPU:0, one launch (start us, length us, event | category | flops | bytes accessed | tf_op | source)
XLA Modules:
  0.0 13.8 jit_solution(4378040723864217534)
XLA Ops:
  0.6 0.0 copy-start
  0.6 0.0 copy-start.2
  0.7 0.0 copy-start.3
  0.7 0.0 copy-start.1
  0.7 4.1 %collective-permute-start.4 = (f32[1,4,16,256]{3,2,1,0:T(8,128)}, f32[1,4,16,256]{3,2,1,0:T(8,128)S(1)}, u32[]{:S(2)}, u32[]{:S(2)}) collective-permute-start(f32[1,4,16,256]{3,2,1,0:T(8,128)} %state.7), channel_id=1, source_target_pairs={{0,2},{1,3},{2,0},{3,1},{4,6},{5,7},{6,4},{7,5},{8,9},{9,8},{10,11... | collective-permute-start | bytes 196616 | tf_op jit(solution)/shard_map/ppermute | solution.py:301
  4.8 0.0 copy-done
  4.8 0.0 copy-done.2
  4.8 0.0 copy-done.3
  4.8 0.0 copy-done.1
  4.8 0.4 %face_forces.1 = (f32[2,16,128]{2,1,0:T(8,128)S(1)}, f32[2,16,128]{2,1,0:T(8,128)S(1)}, f32[2,16,128]{2,1,0:T(8,128)S(1)}, f32[2,16,128]{2,1,0:T(8,128)S(1)}) custom-call(s32[8,128]{1,0:T(8,128)S(1)} %own.1, f32[1,4,16,256]{3,2,1,0:T(8,128)S(1)} %copy-done, s32[6,128]{1,0:T(8,128)S(1)} %bitcast.3, s32[6,128]{1,0:T(8,128)S(1)} %bitcast.4, f32[3,768]{1,0:T(4,128)S(1)} %copy-done.1), custom_call_target="tpu_custom_call" | custom-call | flops 10000000000 | tf_op jit(solution)/shard_map/face_forces/pallas_call | solution.py:284
  5.2 0.6 %collective-permute-start = (f32[2,16,128]{2,1,0:T(8,128)S(1)}, f32[2,16,128]{2,1,0:T(8,128)S(1)}, u32[]{:S(2)}, u32[]{:S(2)}) collective-permute-start(f32[2,16,128]{2,1,0:T(8,128)S(1)} %get-tuple-element.16), channel_id=1, source_target_pairs={{0,16},{4,20},{8,24},{12,28},{16,0},{20,4},{24,8},{28,12},{1,17},{... | collective-permute-start | bytes 49160 | tf_op jit(solution)/shard_map/ppermute | solution.py:273
  5.8 1.4 %collective-permute-start.1 = (f32[2,16,128]{2,1,0:T(8,128)S(1)}, f32[2,16,128]{2,1,0:T(8,128)S(1)}, u32[]{:S(2)}, u32[]{:S(2)}) collective-permute-start(f32[2,16,128]{2,1,0:T(8,128)S(1)} %get-tuple-element.17), channel_id=1, source_target_pairs={{0,24},{4,28},{8,16},{12,20},{16,8},{20,12},{24,0},{28,4},{1,25},{... | collective-permute-start | bytes 49160 | tf_op jit(solution)/shard_map/ppermute | solution.py:273
  7.2 1.5 %collective-permute-start.2 = (f32[2,16,128]{2,1,0:T(8,128)S(1)}, f32[2,16,128]{2,1,0:T(8,128)S(1)}, u32[]{:S(2)}, u32[]{:S(2)}) collective-permute-start(f32[2,16,128]{2,1,0:T(8,128)S(1)} %get-tuple-element.18), channel_id=1, source_target_pairs={{0,8},{4,12},{8,0},{12,4},{16,24},{20,28},{24,16},{28,20},{1,9},{5... | collective-permute-start | bytes 49160 | tf_op jit(solution)/shard_map/ppermute | solution.py:273
  8.7 0.0 collective-permute-done.4.partner
  8.8 1.6 %collective-permute-start.5 = (f32[1,4,16,256]{3,2,1,0:T(8,128)S(1)}, f32[1,4,16,256]{3,2,1,0:T(8,128)S(1)}, u32[]{:S(2)}, u32[]{:S(2)}) collective-permute-start(f32[1,4,16,256]{3,2,1,0:T(8,128)S(1)} %pair_sums.1), channel_id=1, source_target_pairs={{0,1},{1,0},{2,3},{3,2},{4,5},{5,4},{6,7},{7,6},{8,10},{9,11},{10,... | collective-permute-start | bytes 196616 | tf_op jit(solution)/shard_map/ppermute | solution.py:301
  10.4 0.0 collective-permute-done.refs_1_
  10.4 0.0 collective-permute-done.1.refs_2_
  10.4 0.5 %collective-permute-done.2.refs_3_ = f32[2,16,128]{2,1,0:T(8,128)S(1)} collective-permute-done((f32[2,16,128]{2,1,0:T(8,128)S(1)}, f32[2,16,128]{2,1,0:T(8,128)S(1)}, u32[]{:S(2)}, u32[]{:S(2)}) %collective-permute-start.2) | collective-permute-done | bytes 16416 | tf_op jit(solution)/shard_map/ppermute | solution.py:273
  10.9 0.1 collective-permute-start.3
  11.0 0.2 %flux.1 = (f32[1,4,16,256]{3,2,1,0:T(8,128)S(1)}, f32[16,256]{1,0:T(8,128)S(1)}) custom-call(f32[1,4,16,256]{3,2,1,0:T(8,128)S(1)} %copy-done), custom_call_target="tpu_custom_call" | custom-call | tf_op jit(solution)/shard_map/flux/pallas_call | solution.py:284
  11.2 1.0 %collective-permute-done.3.came = f32[1,16,128]{2,1,0:T(8,128)S(1)} collective-permute-done((f32[1,16,128]{2,1,0:T(8,128)S(1)}, f32[1,16,128]{2,1,0:T(8,128)S(1)}, u32[]{:S(2)}, u32[]{:S(2)}) %collective-permute-start.3) | collective-permute-done | bytes 8224 | tf_op jit(solution)/shard_map/ppermute | solution.py:273
  12.2 0.2 %outer.1 = (f32[1,4,16,256]{3,2,1,0:T(8,128)S(1)}, f32[16,128]{1,0:T(8,128)S(1)}) custom-call(f32[1,4,16,256]{3,2,1,0:T(8,128)S(1)} %copy-done, f32[1,4,16,256]{3,2,1,0:T(8,128)S(1)} %get-tuple-element.14.base, f32[1,16,128]{2,1,0:T(8,128)S(1)} %get-tuple-element.19.kept, f32[1,16,128]{2,1,0:T(8,128)S(1)} %collective-permute-done.3.came, ...), custom_call_target="tpu_custom_call" | custom-call | tf_op jit(solution)/shard_map/outer/pallas_call | solution.py:284
  12.3 0.8 %collective-permute-done.5.refs_0_ = f32[1,4,16,256]{3,2,1,0:T(8,128)S(1)} collective-permute-done((f32[1,4,16,256]{3,2,1,0:T(8,128)S(1)}, f32[1,4,16,256]{3,2,1,0:T(8,128)S(1)}, u32[]{:S(2)}, u32[]{:S(2)}) %collective-permute-start.5) | collective-permute-done | bytes 65568 | tf_op jit(solution)/shard_map/ppermute | solution.py:301
  13.1 0.6 %update.1 = (f32[1,4,16,256]{3,2,1,0:T(8,128)}, f32[3,1,512]{2,1,0:T(1,128)}) custom-call(f32[1,4,16,256]{3,2,1,0:T(8,128)S(1)} %get-tuple-element.21.residual, f32[16,256]{1,0:T(8,128)S(1)} %get-tuple-element.22.step, f32[16,128]{1,0:T(8,128)S(1)} %get-tuple-element.23.total, f32[1,4,16,256]{3,2,1,0:T(8,128)S(1)} %collective-permute-done.5.refs_0_), custom_call_target="tpu_custom_call" | custom-call | tf_op jit(solution)/shard_map/update/pallas_call | solution.py:284
  (3 shorter events, 0.0 us)
Async XLA Ops:
  0.6 4.1 %copy-start = (f32[1,4,16,256]{3,2,1,0:T(8,128)S(1)}, f32[1,4,16,256]{3,2,1,0:T(8,128)}, u32[]{:S(2)}) copy-start(f32[1,4,16,256]{3,2,1,0:T(8,128)} %state.7) | copy-start | bytes 196612
  0.6 4.1 %copy-start.2 = (s32[768]{0:T(1024)S(1)}, s32[768]{0:T(1024)}, u32[]{:S(2)}) copy-start(s32[768]{0:T(1024)} %param.5) | copy-start | bytes 9220
  0.7 4.1 %copy-start.3 = (s32[768]{0:T(1024)S(1)}, s32[768]{0:T(1024)}, u32[]{:S(2)}) copy-start(s32[768]{0:T(1024)} %param.6) | copy-start | bytes 9220
  0.7 4.1 %copy-start.1 = (f32[3,768]{1,0:T(4,128)S(1)}, f32[3,768]{1,0:T(4,128)}, u32[]{:S(2)}) copy-start(f32[3,768]{1,0:T(4,128)} %area.1) | copy-start | bytes 27652
  0.7 8.1 %collective-permute-start.4 = (f32[1,4,16,256]{3,2,1,0:T(8,128)}, f32[1,4,16,256]{3,2,1,0:T(8,128)S(1)}, u32[]{:S(2)}, u32[]{:S(2)}) collective-permute-start(f32[1,4,16,256]{3,2,1,0:T(8,128)} %state.7), channel_id=1, source_target_pairs={{0,2},{1,3},{2,0},{3,1},{4,6},{5,7},{6,4},{7,5},{8,9},{9,8},{10,11... | collective-permute-start | bytes 196616 | tf_op jit(solution)/shard_map/ppermute | solution.py:301
  5.2 5.2 %collective-permute-start = (f32[2,16,128]{2,1,0:T(8,128)S(1)}, f32[2,16,128]{2,1,0:T(8,128)S(1)}, u32[]{:S(2)}, u32[]{:S(2)}) collective-permute-start(f32[2,16,128]{2,1,0:T(8,128)S(1)} %get-tuple-element.16), channel_id=1, source_target_pairs={{0,16},{4,20},{8,24},{12,28},{16,0},{20,4},{24,8},{28,12},{1,17},{... | collective-permute-start | bytes 49160 | tf_op jit(solution)/shard_map/ppermute | solution.py:273
  5.8 4.7 %collective-permute-start.1 = (f32[2,16,128]{2,1,0:T(8,128)S(1)}, f32[2,16,128]{2,1,0:T(8,128)S(1)}, u32[]{:S(2)}, u32[]{:S(2)}) collective-permute-start(f32[2,16,128]{2,1,0:T(8,128)S(1)} %get-tuple-element.17), channel_id=1, source_target_pairs={{0,24},{4,28},{8,16},{12,20},{16,8},{20,12},{24,0},{28,4},{1,25},{... | collective-permute-start | bytes 49160 | tf_op jit(solution)/shard_map/ppermute | solution.py:273
  7.2 3.7 %collective-permute-start.2 = (f32[2,16,128]{2,1,0:T(8,128)S(1)}, f32[2,16,128]{2,1,0:T(8,128)S(1)}, u32[]{:S(2)}, u32[]{:S(2)}) collective-permute-start(f32[2,16,128]{2,1,0:T(8,128)S(1)} %get-tuple-element.18), channel_id=1, source_target_pairs={{0,8},{4,12},{8,0},{12,4},{16,24},{20,28},{24,16},{28,20},{1,9},{5... | collective-permute-start | bytes 49160 | tf_op jit(solution)/shard_map/ppermute | solution.py:273
  8.8 4.3 %collective-permute-start.5 = (f32[1,4,16,256]{3,2,1,0:T(8,128)S(1)}, f32[1,4,16,256]{3,2,1,0:T(8,128)S(1)}, u32[]{:S(2)}, u32[]{:S(2)}) collective-permute-start(f32[1,4,16,256]{3,2,1,0:T(8,128)S(1)} %pair_sums.1), channel_id=1, source_target_pairs={{0,1},{1,0},{2,3},{3,2},{4,5},{5,4},{6,7},{7,6},{8,10},{9,11},{10,... | collective-permute-start | bytes 196616 | tf_op jit(solution)/shard_map/ppermute | solution.py:301
  10.9 1.2 %collective-permute-start.3 = (f32[1,16,128]{2,1,0:T(8,128)S(1)}, f32[1,16,128]{2,1,0:T(8,128)S(1)}, u32[]{:S(2)}, u32[]{:S(2)}) collective-permute-start(f32[1,16,128]{2,1,0:T(8,128)S(1)} %get-tuple-element.20), channel_id=1, source_target_pairs={{0,4},{4,0},{8,12},{12,8},{16,20},{20,16},{24,28},{28,24},{1,5},{5... | collective-permute-start | bytes 24584 | tf_op jit(solution)/shard_map/ppermute | solution.py:273

commit v15 on v14

--- a/solution.py
+++ b/solution.py
@@ -17,7 +17,6 @@
 ROWS = 16
 EDGE = 12
 PLACING = 10**10
-PLACES = (2, 3, 1)
 ORDERS = ((2, 1), (1, 2))
 RIDING = 8
 
@@ -97,8 +96,7 @@
             result = product if result is None else result + product
         return result.reshape(count, ROWS, LANES)
 
-    places = (0, *PLACES) if len(outs) == 4 else (0, 1)
-    ordered = [outs[places.index(i)] for i in range(len(outs))]
+    ordered = outs[:1] + outs[:0:-1]
     size = outs[0].shape[0]
     blocks = size * len(outs)
     if blocks <= 16:
@@ -204,10 +202,7 @@
         def edge_of(device):
             relative = device ^ me
             half = RIDING // 2
-            place = 0
-            for row_place, chip in enumerate(PLACES, 1):
-                place = jnp.where(relative // 2 == chip, row_place, place)
-            place += (relative % 2) * half
+            place = (half - relative // 2) % half + (relative % 2) * half
             return jnp.sum(jnp.where(row == place, known, 0.0), axis=0, keepdims=True)
 
         before = edge_of((me + blocks - 1) % blocks)
@@ -277,8 +272,9 @@
         return lax.ppermute(value, axis, [(i, (i + s) % count) for i in range(count)])
 
     def exchanged(sent, size):
-        places = PLACES if len(sent) == 3 else (1,)
-        return [swapped(value, "space", place * size) for place, value in zip(places, sent)]
+        return [
+            swapped(value, "space", (len(sent) - i) * size) for i, value in enumerate(sent)
+        ]
 
     def call(kernel, name, shapes, *operands, flops=0, dtype=jnp.float32):
         return pl.pallas_call(

time: 13.9 us -> 13.9 us (level)
  no operation moved by 1% of the time
where the time goes in v15:
time: 13.9 us; the launch traced here: 13.8 us
  starting transfers between devices  9.37 us (67%)
  waiting for transfers between devices  2.24 us (16%)
  Pallas kernels  1.42 us (10%)
  between operations  0.72 us (5%)
    ppermute x2, starting transfers between devices, partnered(): return lax.ppermute(value, ('space', 'inst'), pairs)  5.74 us
    ppermute x4, starting transfers between devices, swapped(): lax.ppermute(value, axis, [(i, i ^ bit) for i in range(lax.axis_size(axis...  3.62 us
    ppermute x4, waiting for transfers between devices, swapped(): lax.ppermute(value, axis, [(i, i ^ bit) for i in range(lax.axis_size(axis...  1.47 us
    pallas_call x7, Pallas kernels, call(): pl.pallas_call(kernel, out_shape=[jax.ShapeDtypeStruct(shape, dtype) for...  1.42 us
    ppermute x2, waiting for transfers between devices, partnered(): return lax.ppermute(value, ('space', 'inst'), pairs)  0.78 us
  transfers between devices with their start and end apart: 6, of which 3 were waited for; matrix products, arithmetic and copies ran while one was open for 0% of the time, Pallas kernels for 6%

profile of v15, /device:TPU:0, one launch (start us, length us, event | category | flops | bytes accessed | tf_op | source)
XLA Modules:
  0.0 13.8 jit_solution(11575733530679981471)
XLA Ops:
  0.6 0.0 copy-start
  0.6 0.0 copy-start.2
  0.7 0.0 copy-start.3
  0.7 0.0 copy-start.1
  0.7 4.1 %collective-permute-start.4 = (f32[1,4,16,256]{3,2,1,0:T(8,128)}, f32[1,4,16,256]{3,2,1,0:T(8,128)S(1)}, u32[]{:S(2)}, u32[]{:S(2)}) collective-permute-start(f32[1,4,16,256]{3,2,1,0:T(8,128)} %state.7), channel_id=1, source_target_pairs={{0,2},{1,3},{2,0},{3,1},{4,6},{5,7},{6,4},{7,5},{8,9},{9,8},{10,11... | collective-permute-start | bytes 196616 | tf_op jit(solution)/shard_map/ppermute | solution.py:297
  4.8 0.0 copy-done
  4.8 0.0 copy-done.2
  4.8 0.0 copy-done.3
  4.8 0.0 copy-done.1
  4.8 0.4 %face_forces.1 = (f32[2,16,128]{2,1,0:T(8,128)S(1)}, f32[2,16,128]{2,1,0:T(8,128)S(1)}, f32[2,16,128]{2,1,0:T(8,128)S(1)}, f32[2,16,128]{2,1,0:T(8,128)S(1)}) custom-call(s32[8,128]{1,0:T(8,128)S(1)} %own.1, f32[1,4,16,256]{3,2,1,0:T(8,128)S(1)} %copy-done, s32[6,128]{1,0:T(8,128)S(1)} %bitcast.3, s32[6,128]{1,0:T(8,128)S(1)} %bitcast.4, f32[3,768]{1,0:T(4,128)S(1)} %copy-done.1), custom_call_target="tpu_custom_call" | custom-call | flops 10000000000 | tf_op jit(solution)/shard_map/face_forces/pallas_call | solution.py:280
  5.2 1.5 %collective-permute-start = (f32[2,16,128]{2,1,0:T(8,128)S(1)}, f32[2,16,128]{2,1,0:T(8,128)S(1)}, u32[]{:S(2)}, u32[]{:S(2)}) collective-permute-start(f32[2,16,128]{2,1,0:T(8,128)S(1)} %get-tuple-element.16), channel_id=1, source_target_pairs={{0,24},{4,28},{8,16},{12,20},{16,8},{20,12},{24,0},{28,4},{1,25},{... | collective-permute-start | bytes 49160 | tf_op jit(solution)/shard_map/ppermute | solution.py:268
  6.7 0.5 %collective-permute-start.1 = (f32[2,16,128]{2,1,0:T(8,128)S(1)}, f32[2,16,128]{2,1,0:T(8,128)S(1)}, u32[]{:S(2)}, u32[]{:S(2)}) collective-permute-start(f32[2,16,128]{2,1,0:T(8,128)S(1)} %get-tuple-element.17), channel_id=1, source_target_pairs={{0,16},{4,20},{8,24},{12,28},{16,0},{20,4},{24,8},{28,12},{1,17},{... | collective-permute-start | bytes 49160 | tf_op jit(solution)/shard_map/ppermute | solution.py:268
  7.2 1.5 %collective-permute-start.2 = (f32[2,16,128]{2,1,0:T(8,128)S(1)}, f32[2,16,128]{2,1,0:T(8,128)S(1)}, u32[]{:S(2)}, u32[]{:S(2)}) collective-permute-start(f32[2,16,128]{2,1,0:T(8,128)S(1)} %get-tuple-element.18), channel_id=1, source_target_pairs={{0,8},{4,12},{8,0},{12,4},{16,24},{20,28},{24,16},{28,20},{1,9},{5... | collective-permute-start | bytes 49160 | tf_op jit(solution)/shard_map/ppermute | solution.py:268
  8.7 0.0 collective-permute-done.4.partner
  8.8 1.6 %collective-permute-start.5 = (f32[1,4,16,256]{3,2,1,0:T(8,128)S(1)}, f32[1,4,16,256]{3,2,1,0:T(8,128)S(1)}, u32[]{:S(2)}, u32[]{:S(2)}) collective-permute-start(f32[1,4,16,256]{3,2,1,0:T(8,128)S(1)} %pair_sums.1), channel_id=1, source_target_pairs={{0,1},{1,0},{2,3},{3,2},{4,5},{5,4},{6,7},{7,6},{8,10},{9,11},{10,... | collective-permute-start | bytes 196616 | tf_op jit(solution)/shard_map/ppermute | solution.py:297
  10.4 0.0 collective-permute-done.refs_1_
  10.4 0.0 collective-permute-done.1.refs_2_
  10.4 0.5 %collective-permute-done.2.refs_3_ = f32[2,16,128]{2,1,0:T(8,128)S(1)} collective-permute-done((f32[2,16,128]{2,1,0:T(8,128)S(1)}, f32[2,16,128]{2,1,0:T(8,128)S(1)}, u32[]{:S(2)}, u32[]{:S(2)}) %collective-permute-start.2) | collective-permute-done | bytes 16416 | tf_op jit(solution)/shard_map/ppermute | solution.py:268
  10.9 0.1 collective-permute-start.3
  11.0 0.2 %flux.1 = (f32[1,4,16,256]{3,2,1,0:T(8,128)S(1)}, f32[16,256]{1,0:T(8,128)S(1)}) custom-call(f32[1,4,16,256]{3,2,1,0:T(8,128)S(1)} %copy-done), custom_call_target="tpu_custom_call" | custom-call | tf_op jit(solution)/shard_map/flux/pallas_call | solution.py:280
  11.2 1.0 %collective-permute-done.3.came = f32[1,16,128]{2,1,0:T(8,128)S(1)} collective-permute-done((f32[1,16,128]{2,1,0:T(8,128)S(1)}, f32[1,16,128]{2,1,0:T(8,128)S(1)}, u32[]{:S(2)}, u32[]{:S(2)}) %collective-permute-start.3) | collective-permute-done | bytes 8224 | tf_op jit(solution)/shard_map/ppermute | solution.py:268
  12.2 0.2 %outer.1 = (f32[1,4,16,256]{3,2,1,0:T(8,128)S(1)}, f32[16,128]{1,0:T(8,128)S(1)}) custom-call(f32[1,4,16,256]{3,2,1,0:T(8,128)S(1)} %copy-done, f32[1,4,16,256]{3,2,1,0:T(8,128)S(1)} %get-tuple-element.14.base, f32[1,16,128]{2,1,0:T(8,128)S(1)} %get-tuple-element.19.kept, f32[1,16,128]{2,1,0:T(8,128)S(1)} %collective-permute-done.3.came, ...), custom_call_target="tpu_custom_call" | custom-call | tf_op jit(solution)/shard_map/outer/pallas_call | solution.py:280
  12.3 0.8 %collective-permute-done.5.refs_0_ = f32[1,4,16,256]{3,2,1,0:T(8,128)S(1)} collective-permute-done((f32[1,4,16,256]{3,2,1,0:T(8,128)S(1)}, f32[1,4,16,256]{3,2,1,0:T(8,128)S(1)}, u32[]{:S(2)}, u32[]{:S(2)}) %collective-permute-start.5) | collective-permute-done | bytes 65568 | tf_op jit(solution)/shard_map/ppermute | solution.py:297
  13.1 0.6 %update.1 = (f32[1,4,16,256]{3,2,1,0:T(8,128)}, f32[3,1,512]{2,1,0:T(1,128)}) custom-call(f32[1,4,16,256]{3,2,1,0:T(8,128)S(1)} %get-tuple-element.21.residual, f32[16,256]{1,0:T(8,128)S(1)} %get-tuple-element.22.step, f32[16,128]{1,0:T(8,128)S(1)} %get-tuple-element.23.total, f32[1,4,16,256]{3,2,1,0:T(8,128)S(1)} %collective-permute-done.5.refs_0_), custom_call_target="tpu_custom_call" | custom-call | tf_op jit(solution)/shard_map/update/pallas_call | solution.py:280
  (3 shorter events, 0.0 us)
Async XLA Ops:
  0.6 4.1 %copy-start = (f32[1,4,16,256]{3,2,1,0:T(8,128)S(1)}, f32[1,4,16,256]{3,2,1,0:T(8,128)}, u32[]{:S(2)}) copy-start(f32[1,4,16,256]{3,2,1,0:T(8,128)} %state.7) | copy-start | bytes 196612
  0.6 4.1 %copy-start.2 = (s32[768]{0:T(1024)S(1)}, s32[768]{0:T(1024)}, u32[]{:S(2)}) copy-start(s32[768]{0:T(1024)} %param.5) | copy-start | bytes 9220
  0.7 4.1 %copy-start.3 = (s32[768]{0:T(1024)S(1)}, s32[768]{0:T(1024)}, u32[]{:S(2)}) copy-start(s32[768]{0:T(1024)} %param.6) | copy-start | bytes 9220
  0.7 4.1 %copy-start.1 = (f32[3,768]{1,0:T(4,128)S(1)}, f32[3,768]{1,0:T(4,128)}, u32[]{:S(2)}) copy-start(f32[3,768]{1,0:T(4,128)} %area.1) | copy-start | bytes 27652
  0.7 8.1 %collective-permute-start.4 = (f32[1,4,16,256]{3,2,1,0:T(8,128)}, f32[1,4,16,256]{3,2,1,0:T(8,128)S(1)}, u32[]{:S(2)}, u32[]{:S(2)}) collective-permute-start(f32[1,4,16,256]{3,2,1,0:T(8,128)} %state.7), channel_id=1, source_target_pairs={{0,2},{1,3},{2,0},{3,1},{4,6},{5,7},{6,4},{7,5},{8,9},{9,8},{10,11... | collective-permute-start | bytes 196616 | tf_op jit(solution)/shard_map/ppermute | solution.py:297
  5.2 5.2 %collective-permute-start = (f32[2,16,128]{2,1,0:T(8,128)S(1)}, f32[2,16,128]{2,1,0:T(8,128)S(1)}, u32[]{:S(2)}, u32[]{:S(2)}) collective-permute-start(f32[2,16,128]{2,1,0:T(8,128)S(1)} %get-tuple-element.16), channel_id=1, source_target_pairs={{0,24},{4,28},{8,16},{12,20},{16,8},{20,12},{24,0},{28,4},{1,25},{... | collective-permute-start | bytes 49160 | tf_op jit(solution)/shard_map/ppermute | solution.py:268
  6.7 3.7 %collective-permute-start.1 = (f32[2,16,128]{2,1,0:T(8,128)S(1)}, f32[2,16,128]{2,1,0:T(8,128)S(1)}, u32[]{:S(2)}, u32[]{:S(2)}) collective-permute-start(f32[2,16,128]{2,1,0:T(8,128)S(1)} %get-tuple-element.17), channel_id=1, source_target_pairs={{0,16},{4,20},{8,24},{12,28},{16,0},{20,4},{24,8},{28,12},{1,17},{... | collective-permute-start | bytes 49160 | tf_op jit(solution)/shard_map/ppermute | solution.py:268
  7.2 3.7 %collective-permute-start.2 = (f32[2,16,128]{2,1,0:T(8,128)S(1)}, f32[2,16,128]{2,1,0:T(8,128)S(1)}, u32[]{:S(2)}, u32[]{:S(2)}) collective-permute-start(f32[2,16,128]{2,1,0:T(8,128)S(1)} %get-tuple-element.18), channel_id=1, source_target_pairs={{0,8},{4,12},{8,0},{12,4},{16,24},{20,28},{24,16},{28,20},{1,9},{5... | collective-permute-start | bytes 49160 | tf_op jit(solution)/shard_map/ppermute | solution.py:268
  8.8 4.3 %collective-permute-start.5 = (f32[1,4,16,256]{3,2,1,0:T(8,128)S(1)}, f32[1,4,16,256]{3,2,1,0:T(8,128)S(1)}, u32[]{:S(2)}, u32[]{:S(2)}) collective-permute-start(f32[1,4,16,256]{3,2,1,0:T(8,128)S(1)} %pair_sums.1), channel_id=1, source_target_pairs={{0,1},{1,0},{2,3},{3,2},{4,5},{5,4},{6,7},{7,6},{8,10},{9,11},{10,... | collective-permute-start | bytes 196616 | tf_op jit(solution)/shard_map/ppermute | solution.py:297
  10.9 1.2 %collective-permute-start.3 = (f32[1,16,128]{2,1,0:T(8,128)S(1)}, f32[1,16,128]{2,1,0:T(8,128)S(1)}, u32[]{:S(2)}, u32[]{:S(2)}) collective-permute-start(f32[1,16,128]{2,1,0:T(8,128)S(1)} %get-tuple-element.20), channel_id=1, source_target_pairs={{0,4},{4,0},{8,12},{12,8},{16,20},{20,16},{24,28},{28,24},{1,5},{5... | collective-permute-start | bytes 24584 | tf_op jit(solution)/shard_map/ppermute | solution.py:268

commit v16 on v15

--- a/solution.py
+++ b/solution.py
@@ -38,8 +38,9 @@
     return inverse, vr, vc, p
 
 
-def own_kernel(high, out):
-    out[...] = jnp.full(out.shape, lax.axis_index("space") * high, jnp.int32)
+def own_kernel(high, riding, out):
+    me = 0 if riding else lax.axis_index("space")
+    out[...] = jnp.full(out.shape, me * high, jnp.int32)
 
 
 def forces_kernel(node_block, own, state, cell, node, area, *outs):
@@ -96,15 +97,16 @@
             result = product if result is None else result + product
         return result.reshape(count, ROWS, LANES)
 
-    ordered = outs[:1] + outs[:0:-1]
     size = outs[0].shape[0]
     blocks = size * len(outs)
     if blocks <= 16:
         result = dense(0, blocks)
-        for i, out in enumerate(ordered):
-            out[...] = result[i * size : (i + 1) * size]
+        for i, out in enumerate(outs):
+            out[:, 0:ROWS, :] = result[i * size : (i + 1) * size]
+            if out.shape[1] > ROWS:
+                out[:, ROWS:, :] = jnp.zeros((size, out.shape[1] - ROWS, LANES), jnp.float32)
     else:
-        for i, out in enumerate(ordered):
+        for i, out in enumerate(outs):
 
             @pl.loop(0, size // 8)
             def _(g):
@@ -114,19 +116,17 @@
     turned = jnp.concatenate([flat[:, around - LANES :], flat[:, :LANES]], axis=0).T
     lane = lax.broadcasted_iota(jnp.int32, (1, LANES), 1)
     edge = jnp.where(lane < LANES // 2, turned[LANES - 1 :, :], turned[:1, :])
-    for out in outs:
-        out[0, EDGE : EDGE + 1, :] = edge
-
-
-def halving_kernel(arrived, riding, *refs):
-    outs = refs[arrived:]
+    if len(outs) == 1:
+        outs[0][:, EDGE : EDGE + 1, :] = jnp.broadcast_to(edge[None], (blocks, 1, LANES))
+    else:
+        outs[0][0, EDGE : EDGE + 1, :] = edge
+
+
+def halving_kernel(kept, came, *outs):
     size = outs[0].shape[0]
     for i, out in enumerate(outs):
         for b in range(size):
-            out[b] = functools.reduce(jnp.add, [ref[i * size + b] for ref in refs[:arrived]])
-        if riding:
-            for j, ref in enumerate(refs[:arrived]):
-                out[0, EDGE + j : EDGE + j + 1, :] = ref[0, EDGE : EDGE + 1, :]
+            out[b] = kept[i * size + b] + came[i * size + b]
 
 
 def weight_from(weights, instances, source, target):
@@ -190,25 +190,18 @@
         base[0, c] = residual + (upper - lower)
 
 
-def outer_kernel(weights, instances, orders, blocks, state, base, kept, came, partner, *refs):
+def outer_kernel(weights, instances, orders, state, base, kept, came, partner, *refs):
     *edges, residual, total = refs
     radial, around = state.shape[2:]
-    if blocks == RIDING:
+    if edges:
+        before, after = (ref[0:1, :] for ref in edges)
+        total[...] = kept[0] + came[0]
+    else:
+        blocks = came.shape[0]
         me = lax.axis_index("space")
-        known = [kept[0, EDGE:, :], came[0, EDGE:, :]]
-        known = jnp.concatenate(known, axis=0)
-        row = lax.broadcasted_iota(jnp.int32, known.shape, 0)
-
-        def edge_of(device):
-            relative = device ^ me
-            half = RIDING // 2
-            place = (half - relative // 2) % half + (relative % 2) * half
-            return jnp.sum(jnp.where(row == place, known, 0.0), axis=0, keepdims=True)
-
-        before = edge_of((me + blocks - 1) % blocks)
-        after = edge_of((me + 1) % blocks)
-    else:
-        before, after = (ref[0:1, :] for ref in edges)
+        before = came[(me + blocks - 1) % blocks, EDGE : EDGE + 1, :]
+        after = came[(me + 1) % blocks, EDGE : EDGE + 1, :]
+        total[...] = jnp.sum(came[:, 0:ROWS, :], axis=0)
     me = lax.axis_index("inst")
     weight = weight_from(weights, instances, me ^ of_chip(orders)[0], me)
     lane = lax.broadcasted_iota(jnp.int32, (1, LANES), 1)
@@ -242,8 +235,6 @@
             outer.insert(1, jnp.zeros((radial, middle), jnp.float32))
         residual[0, c] = base[0, c] + weight * partner[0, c] + jnp.concatenate(outer, axis=1)
 
-    total[...] = kept[0] + came[0]
-
 
 def update_kernel(residual, step, total, *refs):
     *sums, increment, blade = refs
@@ -270,11 +261,6 @@
     def shifted(value, axis, s):
         count = lax.axis_size(axis)
         return lax.ppermute(value, axis, [(i, (i + s) % count) for i in range(count)])
-
-    def exchanged(sent, size):
-        return [
-            swapped(value, "space", (len(sent) - i) * size) for i, value in enumerate(sent)
-        ]
 
     def call(kernel, name, shapes, *operands, flops=0, dtype=jnp.float32):
         return pl.pallas_call(
@@ -300,19 +286,18 @@
     partner = partnered(state, 0)
 
     riding = blocks == RIDING
-    steps = [4, 2] if riding else [2] * (blocks.bit_length() - 1)
-    size = blocks // steps[0]
+    parts = 1 if riding else 2
     (own,) = call(
-        functools.partial(own_kernel, node_block // LANES),
+        functools.partial(own_kernel, node_block // LANES, riding),
         "own",
         [(8, LANES)],
         dtype=jnp.int32,
         flops=PLACING,
     )
-    kept, *sent = call(
+    dense = call(
         functools.partial(forces_kernel, node_block),
         "face_forces",
-        [(size, ROWS, LANES)] * steps[0],
+        [(blocks // parts, 2 * ROWS if riding else ROWS, LANES)] * parts,
         own,
         state,
         face_cell.reshape(chunks, LANES),
@@ -322,11 +307,19 @@
     )
 
     edges = []
-    if not riding:
-        row = jnp.broadcast_to(kept[0, EDGE : EDGE + 1, :], (8, LANES))
+    if riding:
+        kept, came = dense[0], lax.all_to_all(dense[0], "space", 0, 0, tiled=True)
+    else:
+        row = jnp.broadcast_to(dense[0][0, EDGE : EDGE + 1, :], (8, LANES))
         edges = [shifted(row, "space", 1), shifted(row, "space", blocks - 1)]
-
-    came = exchanged(sent, size)
+        size = blocks // 2
+        kept, came = dense[0], swapped(dense[1], "space", size)
+        while size > 1:
+            size //= 2
+            shapes = [(size, ROWS, LANES)] * 2
+            kept, sent = call(halving_kernel, "halving", shapes, kept, came)
+            came = swapped(sent, "space", size)
+
     sums = call(
         functools.partial(pair_kernel, weights, instances, orders),
         "pair_sums",
@@ -337,18 +330,6 @@
     )
     sums = [partnered(value, i) for i, value in enumerate(sums, 1)]
 
-    for step in steps[1:]:
-        size //= step
-        kept, *sent = call(
-            functools.partial(halving_kernel, 1 + len(came), riding),
-            "halving",
-            [(size, ROWS, LANES)] * step,
-            kept,
-            *came,
-            flops=PLACING,
-        )
-        came = exchanged(sent, size)
-
     base, step = call(
         functools.partial(flux_kernel, weights[0], instances),
         "flux",
@@ -356,13 +337,13 @@
         state,
     )
     residual, total = call(
-        functools.partial(outer_kernel, weights, instances, orders, blocks),
+        functools.partial(outer_kernel, weights, instances, orders),
         "outer",
         [state.shape, (ROWS, LANES)],
         state,
         base,
         kept,
-        *came,
+        came,
         partner,
         *edges,
     )

time: 13.9 us -> 16.7 us (1.20); the launches traced: 13.8 us -> 16.4 us
  Pallas kernels: 1.42 us -> 2.95 us
  waiting for transfers between devices: 2.24 us -> 3.55 us
  starting transfers between devices: 9.37 us -> 9.14 us
    ppermute x4 -> x0, starting transfers between devices: 3.62 us -> none  [swapped(): lax.ppermute(value, axis, [(i, i ^ bit) for i in range(lax.axis_size(axis...]
    all_to_all x0 -> x1, waiting for transfers between devices: none -> 3.54 us  [per_device(): kept, came = (dense[0], lax.all_to_all(dense[0], 'space', 0, 0, tiled=True))]
    all_to_all x0 -> x1, starting transfers between devices: none -> 3.37 us  [per_device(): kept, came = (dense[0], lax.all_to_all(dense[0], 'space', 0, 0, tiled=True))]
    pallas_call x7 -> x6, Pallas kernels: 1.42 us -> 2.95 us  [call(): pl.pallas_call(kernel, out_shape=[jax.ShapeDtypeStruct(shape, dtype) for...]
    ppermute x4 -> x0, waiting for transfers between devices: 1.47 us -> none  [swapped(): lax.ppermute(value, axis, [(i, i ^ bit) for i in range(lax.axis_size(axis...]
    ppermute x2, waiting for transfers between devices: 0.78 us -> 0.01 us  [partnered(): return lax.ppermute(value, ('space', 'inst'), pairs)]
  transfers between devices with their start and end apart: 6 -> 3, of which waited for: 3 -> 1; matrix products, arithmetic and copies ran while one was open for 0% -> 0% of each run, Pallas kernels for 6% -> 14%
where the time goes in v16:
time: 16.7 us; the launch traced here: 16.4 us
  starting transfers between devices  9.14 us (55%)
  waiting for transfers between devices  3.55 us (21%)
  Pallas kernels  2.95 us (18%)
  between operations  0.72 us (4%)
    ppermute x2, starting transfers between devices, partnered(): return lax.ppermute(value, ('space', 'inst'), pairs)  5.77 us
    all_to_all x1, waiting for transfers between devices, per_device(): kept, came = (dense[0], lax.all_to_all(dense[0], 'space', 0, 0, tiled=True))  3.54 us
    all_to_all x1, starting transfers between devices, per_device(): kept, came = (dense[0], lax.all_to_all(dense[0], 'space', 0, 0, tiled=True))  3.37 us
    pallas_call x6, Pallas kernels, call(): pl.pallas_call(kernel, out_shape=[jax.ShapeDtypeStruct(shape, dtype) for...  2.95 us
  transfers between devices with their start and end apart: 3, of which 1 were waited for; matrix products, arithmetic and copies ran while one was open for 0% of the time, Pallas kernels for 14%

profile of v16, /device:TPU:0, one launch (start us, length us, event | category | flops | bytes accessed | tf_op | source)
XLA Modules:
  0.0 16.4 jit_solution(17577800455950786069)
XLA Ops:
  0.6 0.0 copy-start
  0.6 0.0 copy-start.2
  0.7 0.0 copy-start.3
  0.7 0.0 copy-start.1
  0.7 4.1 %collective-permute-start = (f32[1,4,16,256]{3,2,1,0:T(8,128)}, f32[1,4,16,256]{3,2,1,0:T(8,128)S(1)}, u32[]{:S(2)}, u32[]{:S(2)}) collective-permute-start(f32[1,4,16,256]{3,2,1,0:T(8,128)} %state.7), channel_id=1, source_target_pairs={{0,2},{1,3},{2,0},{3,1},{4,6},{5,7},{6,4},{7,5},{8,9},{9,8},{10,11... | collective-permute-start | bytes 196616 | tf_op jit(solution)/shard_map/ppermute | solution.py:283
  4.8 0.0 copy-done
  4.8 0.0 copy-done.2
  4.8 0.0 copy-done.3
  4.8 0.0 copy-done.1
  4.8 1.0 %face_forces.1.kept = f32[8,32,128]{2,1,0:T(8,128)} custom-call(s32[8,128]{1,0:T(8,128)S(1)} %own.1, f32[1,4,16,256]{3,2,1,0:T(8,128)S(1)} %copy-done, s32[6,128]{1,0:T(8,128)S(1)} %bitcast.3, s32[6,128]{1,0:T(8,128)S(1)} %bitcast.4, f32[3,768]{1,0:T(4,128)S(1)} %copy-done.1), custom_call_target="tpu_custom_call" | custom-call | flops 10000000000 | tf_op jit(solution)/shard_map/face_forces/pallas_call | solution.py:266
  5.8 3.4 %all-to-all-start = ((f32[8,32,128]{2,1,0:T(8,128)}), f32[8,32,128]{2,1,0:T(8,128)S(1)}, u32[]{:S(2)}, u32[]{:S(2)}) async-start(f32[8,32,128]{2,1,0:T(8,128)} %face_forces.1.kept), calls=%async_computation | async-start | bytes 262144 | tf_op jit(solution)/shard_map/all_to_all | solution.py:311
  9.2 0.0 collective-permute-done.partner
  9.3 1.7 %collective-permute-start.1 = (f32[1,4,16,256]{3,2,1,0:T(8,128)S(1)}, f32[1,4,16,256]{3,2,1,0:T(8,128)S(1)}, u32[]{:S(2)}, u32[]{:S(2)}) collective-permute-start(f32[1,4,16,256]{3,2,1,0:T(8,128)S(1)} %pair_sums.1), channel_id=1, source_target_pairs={{0,1},{1,0},{2,3},{3,2},{4,5},{5,4},{6,7},{7,6},{8,10},{9,11},{10,... | collective-permute-start | bytes 196616 | tf_op jit(solution)/shard_map/ppermute | solution.py:283
  10.9 0.2 %flux.1 = (f32[1,4,16,256]{3,2,1,0:T(8,128)S(1)}, f32[16,256]{1,0:T(8,128)S(1)}) custom-call(f32[1,4,16,256]{3,2,1,0:T(8,128)S(1)} %copy-done), custom_call_target="tpu_custom_call" | custom-call | tf_op jit(solution)/shard_map/flux/pallas_call | solution.py:266
  11.1 3.5 %all-to-all-done.came = f32[8,32,128]{2,1,0:T(8,128)S(1)} async-done(((f32[8,32,128]{2,1,0:T(8,128)}), f32[8,32,128]{2,1,0:T(8,128)S(1)}, u32[]{:S(2)}, u32[]{:S(2)}) %all-to-all-start) | async-done | bytes 131104 | tf_op jit(solution)/shard_map/all_to_all | solution.py:311
  14.7 1.0 %outer.1 = (f32[1,4,16,256]{3,2,1,0:T(8,128)S(1)}, f32[16,128]{1,0:T(8,128)S(1)}) custom-call(f32[1,4,16,256]{3,2,1,0:T(8,128)S(1)} %copy-done, f32[1,4,16,256]{3,2,1,0:T(8,128)S(1)} %get-tuple-element.8.base, f32[8,32,128]{2,1,0:T(8,128)} %face_forces.1.kept, f32[8,32,128]{2,1,0:T(8,128)S(1)} %all-to-all-done.came, ...), custom_call_target="tpu_custom_call" | custom-call | tf_op jit(solution)/shard_map/outer/pallas_call | solution.py:266
  15.7 0.0 collective-permute-done.1.refs_0_
  15.7 0.6 %update.1 = (f32[1,4,16,256]{3,2,1,0:T(8,128)}, f32[3,1,512]{2,1,0:T(1,128)}) custom-call(f32[1,4,16,256]{3,2,1,0:T(8,128)S(1)} %get-tuple-element.9.residual, f32[16,256]{1,0:T(8,128)S(1)} %get-tuple-element.10.step, f32[16,128]{1,0:T(8,128)S(1)} %get-tuple-element.11.total, f32[1,4,16,256]{3,2,1,0:T(8,128)S(1)} %collective-permute-done.1.refs_0_), custom_call_target="tpu_custom_call" | custom-call | tf_op jit(solution)/shard_map/update/pallas_call | solution.py:266
  (2 shorter events, 0.0 us)
Async XLA Ops:
  0.6 4.1 %copy-start = (f32[1,4,16,256]{3,2,1,0:T(8,128)S(1)}, f32[1,4,16,256]{3,2,1,0:T(8,128)}, u32[]{:S(2)}) copy-start(f32[1,4,16,256]{3,2,1,0:T(8,128)} %state.7) | copy-start | bytes 196612
  0.6 4.1 %copy-start.2 = (s32[768]{0:T(1024)S(1)}, s32[768]{0:T(1024)}, u32[]{:S(2)}) copy-start(s32[768]{0:T(1024)} %param.5) | copy-start | bytes 9220
  0.7 4.1 %copy-start.3 = (s32[768]{0:T(1024)S(1)}, s32[768]{0:T(1024)}, u32[]{:S(2)}) copy-start(s32[768]{0:T(1024)} %param.6) | copy-start | bytes 9220
  0.7 4.1 %copy-start.1 = (f32[3,768]{1,0:T(4,128)S(1)}, f32[3,768]{1,0:T(4,128)}, u32[]{:S(2)}) copy-start(f32[3,768]{1,0:T(4,128)} %area.1) | copy-start | bytes 27652
  0.7 8.5 %collective-permute-start = (f32[1,4,16,256]{3,2,1,0:T(8,128)}, f32[1,4,16,256]{3,2,1,0:T(8,128)S(1)}, u32[]{:S(2)}, u32[]{:S(2)}) collective-permute-start(f32[1,4,16,256]{3,2,1,0:T(8,128)} %state.7), channel_id=1, source_target_pairs={{0,2},{1,3},{2,0},{3,1},{4,6},{5,7},{6,4},{7,5},{8,9},{9,8},{10,11... | collective-permute-start | bytes 196616 | tf_op jit(solution)/shard_map/ppermute | solution.py:283
  5.8 8.8 %all-to-all-start = ((f32[8,32,128]{2,1,0:T(8,128)}), f32[8,32,128]{2,1,0:T(8,128)S(1)}, u32[]{:S(2)}, u32[]{:S(2)}) async-start(f32[8,32,128]{2,1,0:T(8,128)} %face_forces.1.kept), calls=%async_computation | async-start | bytes 262144 | tf_op jit(solution)/shard_map/all_to_all | solution.py:311
  9.3 6.5 %collective-permute-start.1 = (f32[1,4,16,256]{3,2,1,0:T(8,128)S(1)}, f32[1,4,16,256]{3,2,1,0:T(8,128)S(1)}, u32[]{:S(2)}, u32[]{:S(2)}) collective-permute-start(f32[1,4,16,256]{3,2,1,0:T(8,128)S(1)} %pair_sums.1), channel_id=1, source_target_pairs={{0,1},{1,0},{2,3},{3,2},{4,5},{5,4},{6,7},{7,6},{8,10},{9,11},{10,... | collective-permute-start | bytes 196616 | tf_op jit(solution)/shard_map/ppermute | solution.py:283

commit v17 on v15

--- a/solution.py
+++ b/solution.py
@@ -17,7 +17,7 @@
 ROWS = 16
 EDGE = 12
 PLACING = 10**10
-ORDERS = ((2, 1), (1, 2))
+ORDERS = ((3, 1), (1, 2))
 RIDING = 8
 
 

time: 13.9 us -> 14.9 us (1.072)
  waiting for transfers between devices: 2.24 us -> 3.81 us
  starting transfers between devices: 9.37 us -> 8.81 us
    ppermute x4, waiting for transfers between devices: 1.47 us -> 2.55 us  [swapped(): lax.ppermute(value, axis, [(i, i ^ bit) for i in range(lax.axis_size(axis...]
    ppermute x2, starting transfers between devices: 5.74 us -> 5.19 us  [partnered(): return lax.ppermute(value, ('space', 'inst'), pairs)]
    ppermute x2, waiting for transfers between devices: 0.78 us -> 1.25 us  [partnered(): return lax.ppermute(value, ('space', 'inst'), pairs)]
  transfers between devices with their start and end apart: 6 -> 6, of which waited for: 3 -> 4; matrix products, arithmetic and copies ran while one was open for 0% -> 0% of each run, Pallas kernels for 6% -> 5%
where the time goes in v17:
time: 14.9 us; the launch traced here: 14.8 us
  starting transfers between devices  8.81 us (59%)
  waiting for transfers between devices  3.81 us (26%)
  Pallas kernels  1.42 us (10%)
  between operations  0.73 us (5%)
    ppermute x2, starting transfers between devices, partnered(): return lax.ppermute(value, ('space', 'inst'), pairs)  5.19 us
    ppermute x4, starting transfers between devices, swapped(): lax.ppermute(value, axis, [(i, i ^ bit) for i in range(lax.axis_size(axis...  3.62 us
    ppermute x4, waiting for transfers between devices, swapped(): lax.ppermute(value, axis, [(i, i ^ bit) for i in range(lax.axis_size(axis...  2.55 us
    pallas_call x7, Pallas kernels, call(): pl.pallas_call(kernel, out_shape=[jax.ShapeDtypeStruct(shape, dtype) for...  1.42 us
    ppermute x2, waiting for transfers between devices, partnered(): return lax.ppermute(value, ('space', 'inst'), pairs)  1.25 us
  transfers between devices with their start and end apart: 6, of which 4 were waited for; matrix products, arithmetic and copies ran while one was open for 0% of the time, Pallas kernels for 5%

profile of v17, /device:TPU:0, one launch (start us, length us, event | category | flops | bytes accessed | tf_op | source)
XLA Modules:
  0.0 14.8 jit_solution(6672375565176060001)
XLA Ops:
  0.6 0.0 copy-start
  0.6 0.0 copy-start.2
  0.7 0.0 copy-start.3
  0.7 0.0 copy-start.1
  0.7 5.1 %collective-permute-start.4 = (f32[1,4,16,256]{3,2,1,0:T(8,128)}, f32[1,4,16,256]{3,2,1,0:T(8,128)S(1)}, u32[]{:S(2)}, u32[]{:S(2)}) collective-permute-start(f32[1,4,16,256]{3,2,1,0:T(8,128)} %state.7), channel_id=1, source_target_pairs={{0,3},{1,2},{2,1},{3,0},{4,7},{5,6},{6,5},{7,4},{8,9},{9,8},{10,11... | collective-permute-start | bytes 196616 | tf_op jit(solution)/shard_map/ppermute | solution.py:297
  5.8 0.0 copy-done
  5.8 0.0 copy-done.2
  5.8 0.0 copy-done.3
  5.8 0.0 copy-done.1
  5.8 0.4 %face_forces.1 = (f32[2,16,128]{2,1,0:T(8,128)S(1)}, f32[2,16,128]{2,1,0:T(8,128)S(1)}, f32[2,16,128]{2,1,0:T(8,128)S(1)}, f32[2,16,128]{2,1,0:T(8,128)S(1)}) custom-call(s32[8,128]{1,0:T(8,128)S(1)} %own.1, f32[1,4,16,256]{3,2,1,0:T(8,128)S(1)} %copy-done, s32[6,128]{1,0:T(8,128)S(1)} %bitcast.3, s32[6,128]{1,0:T(8,128)S(1)} %bitcast.4, f32[3,768]{1,0:T(4,128)S(1)} %copy-done.1), custom_call_target="tpu_custom_call" | custom-call | flops 10000000000 | tf_op jit(solution)/shard_map/face_forces/pallas_call | solution.py:280
  6.2 0.5 %collective-permute-start = (f32[2,16,128]{2,1,0:T(8,128)S(1)}, f32[2,16,128]{2,1,0:T(8,128)S(1)}, u32[]{:S(2)}, u32[]{:S(2)}) collective-permute-start(f32[2,16,128]{2,1,0:T(8,128)S(1)} %get-tuple-element.16), channel_id=1, source_target_pairs={{0,24},{4,28},{8,16},{12,20},{16,8},{20,12},{24,0},{28,4},{1,25},{... | collective-permute-start | bytes 49160 | tf_op jit(solution)/shard_map/ppermute | solution.py:268
  6.7 0.5 %collective-permute-start.1 = (f32[2,16,128]{2,1,0:T(8,128)S(1)}, f32[2,16,128]{2,1,0:T(8,128)S(1)}, u32[]{:S(2)}, u32[]{:S(2)}) collective-permute-start(f32[2,16,128]{2,1,0:T(8,128)S(1)} %get-tuple-element.17), channel_id=1, source_target_pairs={{0,16},{4,20},{8,24},{12,28},{16,0},{20,4},{24,8},{28,12},{1,17},{... | collective-permute-start | bytes 49160 | tf_op jit(solution)/shard_map/ppermute | solution.py:268
  7.2 2.6 %collective-permute-start.2 = (f32[2,16,128]{2,1,0:T(8,128)S(1)}, f32[2,16,128]{2,1,0:T(8,128)S(1)}, u32[]{:S(2)}, u32[]{:S(2)}) collective-permute-start(f32[2,16,128]{2,1,0:T(8,128)S(1)} %get-tuple-element.18), channel_id=1, source_target_pairs={{0,8},{4,12},{8,0},{12,4},{16,24},{20,28},{24,16},{28,20},{1,9},{5... | collective-permute-start | bytes 49160 | tf_op jit(solution)/shard_map/ppermute | solution.py:268
  9.8 0.0 collective-permute-done.4.partner
  9.8 0.1 collective-permute-start.5
  9.9 1.0 %collective-permute-done.refs_1_ = f32[2,16,128]{2,1,0:T(8,128)S(1)} collective-permute-done((f32[2,16,128]{2,1,0:T(8,128)S(1)}, f32[2,16,128]{2,1,0:T(8,128)S(1)}, u32[]{:S(2)}, u32[]{:S(2)}) %collective-permute-start) | collective-permute-done | bytes 16416 | tf_op jit(solution)/shard_map/ppermute | solution.py:268
  10.9 0.0 collective-permute-done.1.refs_2_
  10.9 0.6 %collective-permute-done.2.refs_3_ = f32[2,16,128]{2,1,0:T(8,128)S(1)} collective-permute-done((f32[2,16,128]{2,1,0:T(8,128)S(1)}, f32[2,16,128]{2,1,0:T(8,128)S(1)}, u32[]{:S(2)}, u32[]{:S(2)}) %collective-permute-start.2) | collective-permute-done | bytes 16416 | tf_op jit(solution)/shard_map/ppermute | solution.py:268
  11.5 0.1 collective-permute-start.3
  11.6 0.2 %flux.1 = (f32[1,4,16,256]{3,2,1,0:T(8,128)S(1)}, f32[16,256]{1,0:T(8,128)S(1)}) custom-call(f32[1,4,16,256]{3,2,1,0:T(8,128)S(1)} %copy-done), custom_call_target="tpu_custom_call" | custom-call | tf_op jit(solution)/shard_map/flux/pallas_call | solution.py:280
  11.8 1.0 %collective-permute-done.3.came = f32[1,16,128]{2,1,0:T(8,128)S(1)} collective-permute-done((f32[1,16,128]{2,1,0:T(8,128)S(1)}, f32[1,16,128]{2,1,0:T(8,128)S(1)}, u32[]{:S(2)}, u32[]{:S(2)}) %collective-permute-start.3) | collective-permute-done | bytes 8224 | tf_op jit(solution)/shard_map/ppermute | solution.py:268
  12.7 0.2 %outer.1 = (f32[1,4,16,256]{3,2,1,0:T(8,128)S(1)}, f32[16,128]{1,0:T(8,128)S(1)}) custom-call(f32[1,4,16,256]{3,2,1,0:T(8,128)S(1)} %copy-done, f32[1,4,16,256]{3,2,1,0:T(8,128)S(1)} %get-tuple-element.14.base, f32[1,16,128]{2,1,0:T(8,128)S(1)} %get-tuple-element.19.kept, f32[1,16,128]{2,1,0:T(8,128)S(1)} %collective-permute-done.3.came, ...), custom_call_target="tpu_custom_call" | custom-call | tf_op jit(solution)/shard_map/outer/pallas_call | solution.py:280
  12.9 1.2 %collective-permute-done.5.refs_0_ = f32[1,4,16,256]{3,2,1,0:T(8,128)S(1)} collective-permute-done((f32[1,4,16,256]{3,2,1,0:T(8,128)S(1)}, f32[1,4,16,256]{3,2,1,0:T(8,128)S(1)}, u32[]{:S(2)}, u32[]{:S(2)}) %collective-permute-start.5) | collective-permute-done | bytes 65568 | tf_op jit(solution)/shard_map/ppermute | solution.py:297
  14.1 0.6 %update.1 = (f32[1,4,16,256]{3,2,1,0:T(8,128)}, f32[3,1,512]{2,1,0:T(1,128)}) custom-call(f32[1,4,16,256]{3,2,1,0:T(8,128)S(1)} %get-tuple-element.21.residual, f32[16,256]{1,0:T(8,128)S(1)} %get-tuple-element.22.step, f32[16,128]{1,0:T(8,128)S(1)} %get-tuple-element.23.total, f32[1,4,16,256]{3,2,1,0:T(8,128)S(1)} %collective-permute-done.5.refs_0_), custom_call_target="tpu_custom_call" | custom-call | tf_op jit(solution)/shard_map/update/pallas_call | solution.py:280
  (3 shorter events, 0.0 us)
Async XLA Ops:
  0.6 5.2 %copy-start = (f32[1,4,16,256]{3,2,1,0:T(8,128)S(1)}, f32[1,4,16,256]{3,2,1,0:T(8,128)}, u32[]{:S(2)}) copy-start(f32[1,4,16,256]{3,2,1,0:T(8,128)} %state.7) | copy-start | bytes 196612
  0.6 5.2 %copy-start.2 = (s32[768]{0:T(1024)S(1)}, s32[768]{0:T(1024)}, u32[]{:S(2)}) copy-start(s32[768]{0:T(1024)} %param.5) | copy-start | bytes 9220
  0.7 5.1 %copy-start.3 = (s32[768]{0:T(1024)S(1)}, s32[768]{0:T(1024)}, u32[]{:S(2)}) copy-start(s32[768]{0:T(1024)} %param.6) | copy-start | bytes 9220
  0.7 5.1 %copy-start.1 = (f32[3,768]{1,0:T(4,128)S(1)}, f32[3,768]{1,0:T(4,128)}, u32[]{:S(2)}) copy-start(f32[3,768]{1,0:T(4,128)} %area.1) | copy-start | bytes 27652
  0.7 9.1 %collective-permute-start.4 = (f32[1,4,16,256]{3,2,1,0:T(8,128)}, f32[1,4,16,256]{3,2,1,0:T(8,128)S(1)}, u32[]{:S(2)}, u32[]{:S(2)}) collective-permute-start(f32[1,4,16,256]{3,2,1,0:T(8,128)} %state.7), channel_id=1, source_target_pairs={{0,3},{1,2},{2,1},{3,0},{4,7},{5,6},{6,5},{7,4},{8,9},{9,8},{10,11... | collective-permute-start | bytes 196616 | tf_op jit(solution)/shard_map/ppermute | solution.py:297
  6.2 4.7 %collective-permute-start = (f32[2,16,128]{2,1,0:T(8,128)S(1)}, f32[2,16,128]{2,1,0:T(8,128)S(1)}, u32[]{:S(2)}, u32[]{:S(2)}) collective-permute-start(f32[2,16,128]{2,1,0:T(8,128)S(1)} %get-tuple-element.16), channel_id=1, source_target_pairs={{0,24},{4,28},{8,16},{12,20},{16,8},{20,12},{24,0},{28,4},{1,25},{... | collective-permute-start | bytes 49160 | tf_op jit(solution)/shard_map/ppermute | solution.py:268
  6.7 4.2 %collective-permute-start.1 = (f32[2,16,128]{2,1,0:T(8,128)S(1)}, f32[2,16,128]{2,1,0:T(8,128)S(1)}, u32[]{:S(2)}, u32[]{:S(2)}) collective-permute-start(f32[2,16,128]{2,1,0:T(8,128)S(1)} %get-tuple-element.17), channel_id=1, source_target_pairs={{0,16},{4,20},{8,24},{12,28},{16,0},{20,4},{24,8},{28,12},{1,17},{... | collective-permute-start | bytes 49160 | tf_op jit(solution)/shard_map/ppermute | solution.py:268
  7.2 4.3 %collective-permute-start.2 = (f32[2,16,128]{2,1,0:T(8,128)S(1)}, f32[2,16,128]{2,1,0:T(8,128)S(1)}, u32[]{:S(2)}, u32[]{:S(2)}) collective-permute-start(f32[2,16,128]{2,1,0:T(8,128)S(1)} %get-tuple-element.18), channel_id=1, source_target_pairs={{0,8},{4,12},{8,0},{12,4},{16,24},{20,28},{24,16},{28,20},{1,9},{5... | collective-permute-start | bytes 49160 | tf_op jit(solution)/shard_map/ppermute | solution.py:268
  9.8 4.3 %collective-permute-start.5 = (f32[1,4,16,256]{3,2,1,0:T(8,128)S(1)}, f32[1,4,16,256]{3,2,1,0:T(8,128)S(1)}, u32[]{:S(2)}, u32[]{:S(2)}) collective-permute-start(f32[1,4,16,256]{3,2,1,0:T(8,128)S(1)} %pair_sums.1), channel_id=1, source_target_pairs={{0,1},{1,0},{2,3},{3,2},{4,5},{5,4},{6,7},{7,6},{8,10},{9,11},{10,... | collective-permute-start | bytes 196616 | tf_op jit(solution)/shard_map/ppermute | solution.py:297
  11.5 1.2 %collective-permute-start.3 = (f32[1,16,128]{2,1,0:T(8,128)S(1)}, f32[1,16,128]{2,1,0:T(8,128)S(1)}, u32[]{:S(2)}, u32[]{:S(2)}) collective-permute-start(f32[1,16,128]{2,1,0:T(8,128)S(1)} %get-tuple-element.20), channel_id=1, source_target_pairs={{0,4},{4,0},{8,12},{12,8},{16,20},{20,16},{24,28},{28,24},{1,5},{5... | collective-permute-start | bytes 24584 | tf_op jit(solution)/shard_map/ppermute | solution.py:268

commit v18 on v15

--- a/solution.py
+++ b/solution.py
@@ -139,7 +139,7 @@
 
 def of_chip(orders):
     chip = lax.axis_index("space") // 2
-    return [jnp.where(chip == 0, a, b) for a, b in zip(*orders)]
+    return [jnp.where(chip % 2 == 0, a, b) for a, b in zip(*orders)]
 
 
 def pair_kernel(weights, instances, orders, state, partner, *outs):
@@ -290,7 +290,7 @@
     weights = spectral_row(instances)
     def partnered(value, place):
         pairs = [
-            (i * instances + n, i * instances + (n ^ orders[min(i // 2, 1)][place]))
+            (i * instances + n, i * instances + (n ^ orders[i // 2 % 2][place]))
             for i in range(blocks)
             for n in range(instances)
         ]

time: 13.9 us -> 13.9 us (level)
  no operation moved by 1% of the time
where the time goes in v18:
time: 13.9 us; the launch traced here: 13.8 us
  starting transfers between devices  9.37 us (67%)
  waiting for transfers between devices  2.24 us (16%)
  Pallas kernels  1.42 us (10%)
  between operations  0.72 us (5%)
    ppermute x2, starting transfers between devices, partnered(): return lax.ppermute(value, ('space', 'inst'), pairs)  5.74 us
    ppermute x4, starting transfers between devices, swapped(): lax.ppermute(value, axis, [(i, i ^ bit) for i in range(lax.axis_size(axis...  3.62 us
    ppermute x4, waiting for transfers between devices, swapped(): lax.ppermute(value, axis, [(i, i ^ bit) for i in range(lax.axis_size(axis...  1.46 us
    pallas_call x7, Pallas kernels, call(): pl.pallas_call(kernel, out_shape=[jax.ShapeDtypeStruct(shape, dtype) for...  1.42 us
    ppermute x2, waiting for transfers between devices, partnered(): return lax.ppermute(value, ('space', 'inst'), pairs)  0.78 us
  transfers between devices with their start and end apart: 6, of which 3 were waited for; matrix products, arithmetic and copies ran while one was open for 0% of the time, Pallas kernels for 6%

profile of v18, /device:TPU:0, one launch (start us, length us, event | category | flops | bytes accessed | tf_op | source)
XLA Modules:
  0.0 13.8 jit_solution(1961858922750341871)
XLA Ops:
  0.6 0.0 copy-start
  0.6 0.0 copy-start.2
  0.7 0.0 copy-start.3
  0.7 0.0 copy-start.1
  0.7 4.1 %collective-permute-start.4 = (f32[1,4,16,256]{3,2,1,0:T(8,128)}, f32[1,4,16,256]{3,2,1,0:T(8,128)S(1)}, u32[]{:S(2)}, u32[]{:S(2)}) collective-permute-start(f32[1,4,16,256]{3,2,1,0:T(8,128)} %state.7), channel_id=1, source_target_pairs={{0,2},{1,3},{2,0},{3,1},{4,6},{5,7},{6,4},{7,5},{8,9},{9,8},{10,11... | collective-permute-start | bytes 196616 | tf_op jit(solution)/shard_map/ppermute | solution.py:297
  4.8 0.0 copy-done
  4.8 0.0 copy-done.2
  4.8 0.0 copy-done.3
  4.8 0.0 copy-done.1
  4.8 0.4 %face_forces.1 = (f32[2,16,128]{2,1,0:T(8,128)S(1)}, f32[2,16,128]{2,1,0:T(8,128)S(1)}, f32[2,16,128]{2,1,0:T(8,128)S(1)}, f32[2,16,128]{2,1,0:T(8,128)S(1)}) custom-call(s32[8,128]{1,0:T(8,128)S(1)} %own.1, f32[1,4,16,256]{3,2,1,0:T(8,128)S(1)} %copy-done, s32[6,128]{1,0:T(8,128)S(1)} %bitcast.3, s32[6,128]{1,0:T(8,128)S(1)} %bitcast.4, f32[3,768]{1,0:T(4,128)S(1)} %copy-done.1), custom_call_target="tpu_custom_call" | custom-call | flops 10000000000 | tf_op jit(solution)/shard_map/face_forces/pallas_call | solution.py:280
  5.2 1.5 %collective-permute-start = (f32[2,16,128]{2,1,0:T(8,128)S(1)}, f32[2,16,128]{2,1,0:T(8,128)S(1)}, u32[]{:S(2)}, u32[]{:S(2)}) collective-permute-start(f32[2,16,128]{2,1,0:T(8,128)S(1)} %get-tuple-element.16), channel_id=1, source_target_pairs={{0,24},{4,28},{8,16},{12,20},{16,8},{20,12},{24,0},{28,4},{1,25},{... | collective-permute-start | bytes 49160 | tf_op jit(solution)/shard_map/ppermute | solution.py:268
  6.7 0.5 %collective-permute-start.1 = (f32[2,16,128]{2,1,0:T(8,128)S(1)}, f32[2,16,128]{2,1,0:T(8,128)S(1)}, u32[]{:S(2)}, u32[]{:S(2)}) collective-permute-start(f32[2,16,128]{2,1,0:T(8,128)S(1)} %get-tuple-element.17), channel_id=1, source_target_pairs={{0,16},{4,20},{8,24},{12,28},{16,0},{20,4},{24,8},{28,12},{1,17},{... | collective-permute-start | bytes 49160 | tf_op jit(solution)/shard_map/ppermute | solution.py:268
  7.2 1.5 %collective-permute-start.2 = (f32[2,16,128]{2,1,0:T(8,128)S(1)}, f32[2,16,128]{2,1,0:T(8,128)S(1)}, u32[]{:S(2)}, u32[]{:S(2)}) collective-permute-start(f32[2,16,128]{2,1,0:T(8,128)S(1)} %get-tuple-element.18), channel_id=1, source_target_pairs={{0,8},{4,12},{8,0},{12,4},{16,24},{20,28},{24,16},{28,20},{1,9},{5... | collective-permute-start | bytes 49160 | tf_op jit(solution)/shard_map/ppermute | solution.py:268
  8.7 0.0 collective-permute-done.4.partner
  8.8 1.6 %collective-permute-start.5 = (f32[1,4,16,256]{3,2,1,0:T(8,128)S(1)}, f32[1,4,16,256]{3,2,1,0:T(8,128)S(1)}, u32[]{:S(2)}, u32[]{:S(2)}) collective-permute-start(f32[1,4,16,256]{3,2,1,0:T(8,128)S(1)} %pair_sums.1), channel_id=1, source_target_pairs={{0,1},{1,0},{2,3},{3,2},{4,5},{5,4},{6,7},{7,6},{8,10},{9,11},{10,... | collective-permute-start | bytes 196616 | tf_op jit(solution)/shard_map/ppermute | solution.py:297
  10.4 0.0 collective-permute-done.refs_1_
  10.4 0.0 collective-permute-done.1.refs_2_
  10.4 0.5 %collective-permute-done.2.refs_3_ = f32[2,16,128]{2,1,0:T(8,128)S(1)} collective-permute-done((f32[2,16,128]{2,1,0:T(8,128)S(1)}, f32[2,16,128]{2,1,0:T(8,128)S(1)}, u32[]{:S(2)}, u32[]{:S(2)}) %collective-permute-start.2) | collective-permute-done | bytes 16416 | tf_op jit(solution)/shard_map/ppermute | solution.py:268
  10.9 0.1 collective-permute-start.3
  11.0 0.2 %flux.1 = (f32[1,4,16,256]{3,2,1,0:T(8,128)S(1)}, f32[16,256]{1,0:T(8,128)S(1)}) custom-call(f32[1,4,16,256]{3,2,1,0:T(8,128)S(1)} %copy-done), custom_call_target="tpu_custom_call" | custom-call | tf_op jit(solution)/shard_map/flux/pallas_call | solution.py:280
  11.2 1.0 %collective-permute-done.3.came = f32[1,16,128]{2,1,0:T(8,128)S(1)} collective-permute-done((f32[1,16,128]{2,1,0:T(8,128)S(1)}, f32[1,16,128]{2,1,0:T(8,128)S(1)}, u32[]{:S(2)}, u32[]{:S(2)}) %collective-permute-start.3) | collective-permute-done | bytes 8224 | tf_op jit(solution)/shard_map/ppermute | solution.py:268
  12.2 0.2 %outer.1 = (f32[1,4,16,256]{3,2,1,0:T(8,128)S(1)}, f32[16,128]{1,0:T(8,128)S(1)}) custom-call(f32[1,4,16,256]{3,2,1,0:T(8,128)S(1)} %copy-done, f32[1,4,16,256]{3,2,1,0:T(8,128)S(1)} %get-tuple-element.14.base, f32[1,16,128]{2,1,0:T(8,128)S(1)} %get-tuple-element.19.kept, f32[1,16,128]{2,1,0:T(8,128)S(1)} %collective-permute-done.3.came, ...), custom_call_target="tpu_custom_call" | custom-call | tf_op jit(solution)/shard_map/outer/pallas_call | solution.py:280
  12.3 0.8 %collective-permute-done.5.refs_0_ = f32[1,4,16,256]{3,2,1,0:T(8,128)S(1)} collective-permute-done((f32[1,4,16,256]{3,2,1,0:T(8,128)S(1)}, f32[1,4,16,256]{3,2,1,0:T(8,128)S(1)}, u32[]{:S(2)}, u32[]{:S(2)}) %collective-permute-start.5) | collective-permute-done | bytes 65568 | tf_op jit(solution)/shard_map/ppermute | solution.py:297
  13.1 0.6 %update.1 = (f32[1,4,16,256]{3,2,1,0:T(8,128)}, f32[3,1,512]{2,1,0:T(1,128)}) custom-call(f32[1,4,16,256]{3,2,1,0:T(8,128)S(1)} %get-tuple-element.21.residual, f32[16,256]{1,0:T(8,128)S(1)} %get-tuple-element.22.step, f32[16,128]{1,0:T(8,128)S(1)} %get-tuple-element.23.total, f32[1,4,16,256]{3,2,1,0:T(8,128)S(1)} %collective-permute-done.5.refs_0_), custom_call_target="tpu_custom_call" | custom-call | tf_op jit(solution)/shard_map/update/pallas_call | solution.py:280
  (3 shorter events, 0.0 us)
Async XLA Ops:
  0.6 4.1 %copy-start = (f32[1,4,16,256]{3,2,1,0:T(8,128)S(1)}, f32[1,4,16,256]{3,2,1,0:T(8,128)}, u32[]{:S(2)}) copy-start(f32[1,4,16,256]{3,2,1,0:T(8,128)} %state.7) | copy-start | bytes 196612
  0.6 4.1 %copy-start.2 = (s32[768]{0:T(1024)S(1)}, s32[768]{0:T(1024)}, u32[]{:S(2)}) copy-start(s32[768]{0:T(1024)} %param.5) | copy-start | bytes 9220
  0.7 4.1 %copy-start.3 = (s32[768]{0:T(1024)S(1)}, s32[768]{0:T(1024)}, u32[]{:S(2)}) copy-start(s32[768]{0:T(1024)} %param.6) | copy-start | bytes 9220
  0.7 4.1 %copy-start.1 = (f32[3,768]{1,0:T(4,128)S(1)}, f32[3,768]{1,0:T(4,128)}, u32[]{:S(2)}) copy-start(f32[3,768]{1,0:T(4,128)} %area.1) | copy-start | bytes 27652
  0.7 8.1 %collective-permute-start.4 = (f32[1,4,16,256]{3,2,1,0:T(8,128)}, f32[1,4,16,256]{3,2,1,0:T(8,128)S(1)}, u32[]{:S(2)}, u32[]{:S(2)}) collective-permute-start(f32[1,4,16,256]{3,2,1,0:T(8,128)} %state.7), channel_id=1, source_target_pairs={{0,2},{1,3},{2,0},{3,1},{4,6},{5,7},{6,4},{7,5},{8,9},{9,8},{10,11... | collective-permute-start | bytes 196616 | tf_op jit(solution)/shard_map/ppermute | solution.py:297
  5.2 5.2 %collective-permute-start = (f32[2,16,128]{2,1,0:T(8,128)S(1)}, f32[2,16,128]{2,1,0:T(8,128)S(1)}, u32[]{:S(2)}, u32[]{:S(2)}) collective-permute-start(f32[2,16,128]{2,1,0:T(8,128)S(1)} %get-tuple-element.16), channel_id=1, source_target_pairs={{0,24},{4,28},{8,16},{12,20},{16,8},{20,12},{24,0},{28,4},{1,25},{... | collective-permute-start | bytes 49160 | tf_op jit(solution)/shard_map/ppermute | solution.py:268
  6.7 3.8 %collective-permute-start.1 = (f32[2,16,128]{2,1,0:T(8,128)S(1)}, f32[2,16,128]{2,1,0:T(8,128)S(1)}, u32[]{:S(2)}, u32[]{:S(2)}) collective-permute-start(f32[2,16,128]{2,1,0:T(8,128)S(1)} %get-tuple-element.17), channel_id=1, source_target_pairs={{0,16},{4,20},{8,24},{12,28},{16,0},{20,4},{24,8},{28,12},{1,17},{... | collective-permute-start | bytes 49160 | tf_op jit(solution)/shard_map/ppermute | solution.py:268
  7.2 3.7 %collective-permute-start.2 = (f32[2,16,128]{2,1,0:T(8,128)S(1)}, f32[2,16,128]{2,1,0:T(8,128)S(1)}, u32[]{:S(2)}, u32[]{:S(2)}) collective-permute-start(f32[2,16,128]{2,1,0:T(8,128)S(1)} %get-tuple-element.18), channel_id=1, source_target_pairs={{0,8},{4,12},{8,0},{12,4},{16,24},{20,28},{24,16},{28,20},{1,9},{5... | collective-permute-start | bytes 49160 | tf_op jit(solution)/shard_map/ppermute | solution.py:268
  8.8 4.3 %collective-permute-start.5 = (f32[1,4,16,256]{3,2,1,0:T(8,128)S(1)}, f32[1,4,16,256]{3,2,1,0:T(8,128)S(1)}, u32[]{:S(2)}, u32[]{:S(2)}) collective-permute-start(f32[1,4,16,256]{3,2,1,0:T(8,128)S(1)} %pair_sums.1), channel_id=1, source_target_pairs={{0,1},{1,0},{2,3},{3,2},{4,5},{5,4},{6,7},{7,6},{8,10},{9,11},{10,... | collective-permute-start | bytes 196616 | tf_op jit(solution)/shard_map/ppermute | solution.py:297
  10.9 1.2 %collective-permute-start.3 = (f32[1,16,128]{2,1,0:T(8,128)S(1)}, f32[1,16,128]{2,1,0:T(8,128)S(1)}, u32[]{:S(2)}, u32[]{:S(2)}) collective-permute-start(f32[1,16,128]{2,1,0:T(8,128)S(1)} %get-tuple-element.20), channel_id=1, source_target_pairs={{0,4},{4,0},{8,12},{12,8},{16,20},{20,16},{24,28},{28,24},{1,5},{5... | collective-permute-start | bytes 24584 | tf_op jit(solution)/shard_map/ppermute | solution.py:268

commit v19 on v18

--- a/solution.py
+++ b/solution.py
@@ -40,6 +40,10 @@
 
 def own_kernel(high, out):
     out[...] = jnp.full(out.shape, lax.axis_index("space") * high, jnp.int32)
+
+
+def split(value, size):
+    return value >> (size.bit_length() - 1), value & (size - 1)
 
 
 def forces_kernel(node_block, own, state, cell, node, area, *outs):
@@ -50,51 +54,45 @@
     sublane = lax.broadcasted_iota(jnp.int32, (8, LANES), 0)
     picked = []
     for c in range(chunks):
-        index = jnp.broadcast_to(cell[c : c + 1, :], (8, LANES))
-        row = index // around
-        column = index % around
-        lane = column % LANES
-        half = column // LANES
+        tile, lane = split(jnp.broadcast_to(cell[c : c + 1, :], (8, LANES)), LANES)
         total = jnp.zeros((8, LANES), jnp.float32)
         for r in range(radial // 8):
             for h in range(around // LANES):
                 part = p[r * 8 : (r + 1) * 8, h * LANES : (h + 1) * LANES]
                 value = jnp.take_along_axis(part, lane, axis=1, mode="promise_in_bounds")
-                total += jnp.where((row == sublane + r * 8) & (half == h), value, 0.0)
+                place = (sublane + r * 8) * (around // LANES) + h
+                total += jnp.where(tile == place, value, 0.0)
         picked.append(jnp.sum(total, axis=0, keepdims=True))
     face_pressure = jnp.concatenate(picked, axis=1)
     contribution = face_pressure * area[...]
     nodes = jnp.concatenate([node[c : c + 1, :] for c in range(chunks)], axis=1)
 
     high = node_block // LANES
-    place = nodes // LANES ^ jnp.broadcast_to(own[0:1, 0:1], nodes.shape)
-    low = nodes % LANES
+    place, low = split(nodes, LANES)
+    place = place ^ jnp.broadcast_to(own[0:1, 0:1], nodes.shape)
     pick_low = (
         lax.broadcasted_iota(jnp.int32, (LANES, faces), 0) == jnp.broadcast_to(low, (LANES, faces))
     ).astype(jnp.float32).astype(jnp.bfloat16)
-    pattern = jnp.concatenate(
-        [jnp.broadcast_to(contribution[k : k + 1], (high, faces)) for k in range(3)]
-        + [jnp.zeros((ROWS - 3 * high, faces), jnp.float32)],
-        axis=0,
-    )
-    first = pattern.astype(jnp.bfloat16).astype(jnp.float32)
-    second = pattern - first
-    place = jnp.broadcast_to(place, (ROWS, faces))
-    row_high = lax.broadcasted_iota(jnp.int32, (ROWS, faces), 0) % high
+
+    row = lax.broadcasted_iota(jnp.int32, (8, faces), 0)
+    x, y, z = (jnp.broadcast_to(contribution[k : k + 1], (8, faces)) for k in range(3))
+    groups = []
+    for pattern in (jnp.where(row < high, x, y), jnp.where(row < high, z, 0.0)):
+        first = pattern.astype(jnp.bfloat16).astype(jnp.float32)
+        groups.append((first, pattern - first))
+    away = jnp.broadcast_to(place, (8, faces)) - (row & (high - 1))
 
     def dense(start, count):
-        masks = [place == row_high + (start + b) * high for b in range(count)]
-        result = None
-        for part in (first, second):
-            left = jnp.concatenate([jnp.where(m, part, 0.0) for m in masks], axis=0)
-            product = lax.dot_general(
-                left.astype(jnp.bfloat16),
-                pick_low,
-                (((1,), (1,)), ((), ())),
-                preferred_element_type=jnp.float32,
-            )
-            result = product if result is None else result + product
-        return result.reshape(count, ROWS, LANES)
+        masks = [away == (start + b) * high for b in range(count)]
+        left = [jnp.where(m, g[i], 0.0) for i in range(2) for m in masks for g in groups]
+        product = lax.dot_general(
+            jnp.concatenate(left, axis=0).astype(jnp.bfloat16),
+            pick_low,
+            (((1,), (1,)), ((), ())),
+            preferred_element_type=jnp.float32,
+        )
+        rows = count * ROWS
+        return (product[:rows] + product[rows:]).reshape(count, ROWS, LANES)
 
     ordered = outs[:1] + outs[:0:-1]
     size = outs[0].shape[0]
@@ -110,10 +108,18 @@
             def _(g):
                 out[pl.ds(g * 8, 8)] = dense(i * size + g * 8, 8)
 
-    flat = state[0].reshape(4 * radial, around)
-    turned = jnp.concatenate([flat[:, around - LANES :], flat[:, :LANES]], axis=0).T
-    lane = lax.broadcasted_iota(jnp.int32, (1, LANES), 1)
-    edge = jnp.where(lane < LANES // 2, turned[LANES - 1 :, :], turned[:1, :])
+    lane = lax.broadcasted_iota(jnp.int32, (8, LANES), 1)
+    columns = jnp.zeros((8, LANES), jnp.float32)
+    for i, column in enumerate((around - 1, 0)):
+        tile, index = divmod(column, LANES)
+        index = jnp.full((8, LANES), index, jnp.int32)
+        for c in range(4):
+            for r in range(radial // 8):
+                part = state[0, c, r * 8 : (r + 1) * 8, tile * LANES : (tile + 1) * LANES]
+                value = jnp.take_along_axis(part, index, axis=1, mode="promise_in_bounds")
+                place = (i * 4 + c) * radial + r * 8
+                columns = jnp.where(lane == sublane + place, value, columns)
+    edge = jnp.sum(columns, axis=0, keepdims=True)
     for out in outs:
         out[0, EDGE : EDGE + 1, :] = edge
 
@@ -213,20 +219,19 @@
     weight = weight_from(weights, instances, me ^ of_chip(orders)[0], me)
     lane = lax.broadcasted_iota(jnp.int32, (1, LANES), 1)
     edge = jnp.where(lane < LANES // 2, before, after)
-    columns = jnp.broadcast_to(edge, (LANES, LANES)).T
-
+    edge = jnp.broadcast_to(edge, (8, LANES))
+
+    sublane = lax.broadcasted_iota(jnp.int32, (8, LANES), 0)
     lane = lax.broadcasted_iota(jnp.int32, (radial, LANES), 1)
     left, right = lane == 0, lane == LANES - 1
     own, far = [], []
     for c in range(4):
         own.append(jnp.where(left, state[0, c, :, :LANES], state[0, c, :, around - LANES :]))
-        far.append(
-            jnp.where(
-                right,
-                columns[LANES // 2 + c * radial : LANES // 2 + (c + 1) * radial],
-                columns[c * radial : (c + 1) * radial],
-            )
-        )
+        halo = []
+        for r in range(radial // 8):
+            index = sublane + jnp.where(lane[:8] == LANES - 1, 4 * radial, 0) + c * radial + r * 8
+            halo.append(jnp.take_along_axis(edge, index, axis=1, mode="promise_in_bounds"))
+        far.append(jnp.concatenate(halo, axis=0))
     faces, speeds = [], []
     for q in (own, far):
         inverse, _, vc, p = pressure_of(*q)

time: 13.9 us -> 13.9 us (level)
  transfers between devices with their start and end apart: 6 -> 6, of which waited for: 3 -> 3; matrix products, arithmetic and copies ran while one was open for 0% -> 0% of each run, Pallas kernels for 6% -> 5%
where the time goes in v19:
time: 13.9 us; the launch traced here: 13.8 us
  starting transfers between devices  9.37 us (67%)
  waiting for transfers between devices  2.26 us (16%)
  Pallas kernels  1.39 us (10%)
  between operations  0.72 us (5%)
    ppermute x2, starting transfers between devices, partnered(): return lax.ppermute(value, ('space', 'inst'), pairs)  5.74 us
    ppermute x4, starting transfers between devices, swapped(): lax.ppermute(value, axis, [(i, i ^ bit) for i in range(lax.axis_size(axis...  3.62 us
    ppermute x4, waiting for transfers between devices, swapped(): lax.ppermute(value, axis, [(i, i ^ bit) for i in range(lax.axis_size(axis...  1.46 us
    pallas_call x7, Pallas kernels, call(): pl.pallas_call(kernel, out_shape=[jax.ShapeDtypeStruct(shape, dtype) for...  1.39 us
    ppermute x2, waiting for transfers between devices, partnered(): return lax.ppermute(value, ('space', 'inst'), pairs)  0.79 us
  transfers between devices with their start and end apart: 6, of which 3 were waited for; matrix products, arithmetic and copies ran while one was open for 0% of the time, Pallas kernels for 5%

profile of v19, /device:TPU:0, one launch (start us, length us, event | category | flops | bytes accessed | tf_op | source)
XLA Modules:
  0.0 13.8 jit_solution(2467380583219944461)
XLA Ops:
  0.6 0.0 copy-start
  0.6 0.0 copy-start.2
  0.7 0.0 copy-start.3
  0.7 0.0 copy-start.1
  0.7 4.1 %collective-permute-start.4 = (f32[1,4,16,256]{3,2,1,0:T(8,128)}, f32[1,4,16,256]{3,2,1,0:T(8,128)S(1)}, u32[]{:S(2)}, u32[]{:S(2)}) collective-permute-start(f32[1,4,16,256]{3,2,1,0:T(8,128)} %state.7), channel_id=1, source_target_pairs={{0,2},{1,3},{2,0},{3,1},{4,6},{5,7},{6,4},{7,5},{8,9},{9,8},{10,11... | collective-permute-start | bytes 196616 | tf_op jit(solution)/shard_map/ppermute | solution.py:302
  4.8 0.0 copy-done
  4.8 0.0 copy-done.2
  4.8 0.0 copy-done.3
  4.8 0.0 copy-done.1
  4.8 0.4 %face_forces.1 = (f32[2,16,128]{2,1,0:T(8,128)S(1)}, f32[2,16,128]{2,1,0:T(8,128)S(1)}, f32[2,16,128]{2,1,0:T(8,128)S(1)}, f32[2,16,128]{2,1,0:T(8,128)S(1)}) custom-call(s32[8,128]{1,0:T(8,128)S(1)} %own.1, f32[1,4,16,256]{3,2,1,0:T(8,128)S(1)} %copy-done, s32[6,128]{1,0:T(8,128)S(1)} %bitcast.3, s32[6,128]{1,0:T(8,128)S(1)} %bitcast.4, f32[3,768]{1,0:T(4,128)S(1)} %copy-done.1), custom_call_target="tpu_custom_call" | custom-call | flops 10000000000 | tf_op jit(solution)/shard_map/face_forces/pallas_call | solution.py:285
  5.2 1.5 %collective-permute-start = (f32[2,16,128]{2,1,0:T(8,128)S(1)}, f32[2,16,128]{2,1,0:T(8,128)S(1)}, u32[]{:S(2)}, u32[]{:S(2)}) collective-permute-start(f32[2,16,128]{2,1,0:T(8,128)S(1)} %get-tuple-element.16), channel_id=1, source_target_pairs={{0,24},{4,28},{8,16},{12,20},{16,8},{20,12},{24,0},{28,4},{1,25},{... | collective-permute-start | bytes 49160 | tf_op jit(solution)/shard_map/ppermute | solution.py:273
  6.7 0.5 %collective-permute-start.1 = (f32[2,16,128]{2,1,0:T(8,128)S(1)}, f32[2,16,128]{2,1,0:T(8,128)S(1)}, u32[]{:S(2)}, u32[]{:S(2)}) collective-permute-start(f32[2,16,128]{2,1,0:T(8,128)S(1)} %get-tuple-element.17), channel_id=1, source_target_pairs={{0,16},{4,20},{8,24},{12,28},{16,0},{20,4},{24,8},{28,12},{1,17},{... | collective-permute-start | bytes 49160 | tf_op jit(solution)/shard_map/ppermute | solution.py:273
  7.2 1.5 %collective-permute-start.2 = (f32[2,16,128]{2,1,0:T(8,128)S(1)}, f32[2,16,128]{2,1,0:T(8,128)S(1)}, u32[]{:S(2)}, u32[]{:S(2)}) collective-permute-start(f32[2,16,128]{2,1,0:T(8,128)S(1)} %get-tuple-element.18), channel_id=1, source_target_pairs={{0,8},{4,12},{8,0},{12,4},{16,24},{20,28},{24,16},{28,20},{1,9},{5... | collective-permute-start | bytes 49160 | tf_op jit(solution)/shard_map/ppermute | solution.py:273
  8.7 0.0 collective-permute-done.4.partner
  8.8 1.6 %collective-permute-start.5 = (f32[1,4,16,256]{3,2,1,0:T(8,128)S(1)}, f32[1,4,16,256]{3,2,1,0:T(8,128)S(1)}, u32[]{:S(2)}, u32[]{:S(2)}) collective-permute-start(f32[1,4,16,256]{3,2,1,0:T(8,128)S(1)} %pair_sums.1), channel_id=1, source_target_pairs={{0,1},{1,0},{2,3},{3,2},{4,5},{5,4},{6,7},{7,6},{8,10},{9,11},{10,... | collective-permute-start | bytes 196616 | tf_op jit(solution)/shard_map/ppermute | solution.py:302
  10.4 0.0 collective-permute-done.refs_1_
  10.4 0.0 collective-permute-done.1.refs_2_
  10.4 0.5 %collective-permute-done.2.refs_3_ = f32[2,16,128]{2,1,0:T(8,128)S(1)} collective-permute-done((f32[2,16,128]{2,1,0:T(8,128)S(1)}, f32[2,16,128]{2,1,0:T(8,128)S(1)}, u32[]{:S(2)}, u32[]{:S(2)}) %collective-permute-start.2) | collective-permute-done | bytes 16416 | tf_op jit(solution)/shard_map/ppermute | solution.py:273
  10.9 0.1 collective-permute-start.3
  11.0 0.2 %flux.1 = (f32[1,4,16,256]{3,2,1,0:T(8,128)S(1)}, f32[16,256]{1,0:T(8,128)S(1)}) custom-call(f32[1,4,16,256]{3,2,1,0:T(8,128)S(1)} %copy-done), custom_call_target="tpu_custom_call" | custom-call | tf_op jit(solution)/shard_map/flux/pallas_call | solution.py:285
  11.2 1.0 %collective-permute-done.3.came = f32[1,16,128]{2,1,0:T(8,128)S(1)} collective-permute-done((f32[1,16,128]{2,1,0:T(8,128)S(1)}, f32[1,16,128]{2,1,0:T(8,128)S(1)}, u32[]{:S(2)}, u32[]{:S(2)}) %collective-permute-start.3) | collective-permute-done | bytes 8224 | tf_op jit(solution)/shard_map/ppermute | solution.py:273
  12.2 0.1 %outer.1 = (f32[1,4,16,256]{3,2,1,0:T(8,128)S(1)}, f32[16,128]{1,0:T(8,128)S(1)}) custom-call(f32[1,4,16,256]{3,2,1,0:T(8,128)S(1)} %copy-done, f32[1,4,16,256]{3,2,1,0:T(8,128)S(1)} %get-tuple-element.14.base, f32[1,16,128]{2,1,0:T(8,128)S(1)} %get-tuple-element.19.kept, f32[1,16,128]{2,1,0:T(8,128)S(1)} %collective-permute-done.3.came, ...), custom_call_target="tpu_custom_call" | custom-call | tf_op jit(solution)/shard_map/outer/pallas_call | solution.py:285
  12.3 0.8 %collective-permute-done.5.refs_0_ = f32[1,4,16,256]{3,2,1,0:T(8,128)S(1)} collective-permute-done((f32[1,4,16,256]{3,2,1,0:T(8,128)S(1)}, f32[1,4,16,256]{3,2,1,0:T(8,128)S(1)}, u32[]{:S(2)}, u32[]{:S(2)}) %collective-permute-start.5) | collective-permute-done | bytes 65568 | tf_op jit(solution)/shard_map/ppermute | solution.py:302
  13.1 0.6 %update.1 = (f32[1,4,16,256]{3,2,1,0:T(8,128)}, f32[3,1,512]{2,1,0:T(1,128)}) custom-call(f32[1,4,16,256]{3,2,1,0:T(8,128)S(1)} %get-tuple-element.21.residual, f32[16,256]{1,0:T(8,128)S(1)} %get-tuple-element.22.step, f32[16,128]{1,0:T(8,128)S(1)} %get-tuple-element.23.total, f32[1,4,16,256]{3,2,1,0:T(8,128)S(1)} %collective-permute-done.5.refs_0_), custom_call_target="tpu_custom_call" | custom-call | tf_op jit(solution)/shard_map/update/pallas_call | solution.py:285
  (3 shorter events, 0.0 us)
Async XLA Ops:
  0.6 4.1 %copy-start = (f32[1,4,16,256]{3,2,1,0:T(8,128)S(1)}, f32[1,4,16,256]{3,2,1,0:T(8,128)}, u32[]{:S(2)}) copy-start(f32[1,4,16,256]{3,2,1,0:T(8,128)} %state.7) | copy-start | bytes 196612
  0.6 4.1 %copy-start.2 = (s32[768]{0:T(1024)S(1)}, s32[768]{0:T(1024)}, u32[]{:S(2)}) copy-start(s32[768]{0:T(1024)} %param.5) | copy-start | bytes 9220
  0.7 4.1 %copy-start.3 = (s32[768]{0:T(1024)S(1)}, s32[768]{0:T(1024)}, u32[]{:S(2)}) copy-start(s32[768]{0:T(1024)} %param.6) | copy-start | bytes 9220
  0.7 4.1 %copy-start.1 = (f32[3,768]{1,0:T(4,128)S(1)}, f32[3,768]{1,0:T(4,128)}, u32[]{:S(2)}) copy-start(f32[3,768]{1,0:T(4,128)} %area.1) | copy-start | bytes 27652
  0.7 8.1 %collective-permute-start.4 = (f32[1,4,16,256]{3,2,1,0:T(8,128)}, f32[1,4,16,256]{3,2,1,0:T(8,128)S(1)}, u32[]{:S(2)}, u32[]{:S(2)}) collective-permute-start(f32[1,4,16,256]{3,2,1,0:T(8,128)} %state.7), channel_id=1, source_target_pairs={{0,2},{1,3},{2,0},{3,1},{4,6},{5,7},{6,4},{7,5},{8,9},{9,8},{10,11... | collective-permute-start | bytes 196616 | tf_op jit(solution)/shard_map/ppermute | solution.py:302
  5.2 5.2 %collective-permute-start = (f32[2,16,128]{2,1,0:T(8,128)S(1)}, f32[2,16,128]{2,1,0:T(8,128)S(1)}, u32[]{:S(2)}, u32[]{:S(2)}) collective-permute-start(f32[2,16,128]{2,1,0:T(8,128)S(1)} %get-tuple-element.16), channel_id=1, source_target_pairs={{0,24},{4,28},{8,16},{12,20},{16,8},{20,12},{24,0},{28,4},{1,25},{... | collective-permute-start | bytes 49160 | tf_op jit(solution)/shard_map/ppermute | solution.py:273
  6.7 3.7 %collective-permute-start.1 = (f32[2,16,128]{2,1,0:T(8,128)S(1)}, f32[2,16,128]{2,1,0:T(8,128)S(1)}, u32[]{:S(2)}, u32[]{:S(2)}) collective-permute-start(f32[2,16,128]{2,1,0:T(8,128)S(1)} %get-tuple-element.17), channel_id=1, source_target_pairs={{0,16},{4,20},{8,24},{12,28},{16,0},{20,4},{24,8},{28,12},{1,17},{... | collective-permute-start | bytes 49160 | tf_op jit(solution)/shard_map/ppermute | solution.py:273
  7.2 3.7 %collective-permute-start.2 = (f32[2,16,128]{2,1,0:T(8,128)S(1)}, f32[2,16,128]{2,1,0:T(8,128)S(1)}, u32[]{:S(2)}, u32[]{:S(2)}) collective-permute-start(f32[2,16,128]{2,1,0:T(8,128)S(1)} %get-tuple-element.18), channel_id=1, source_target_pairs={{0,8},{4,12},{8,0},{12,4},{16,24},{20,28},{24,16},{28,20},{1,9},{5... | collective-permute-start | bytes 49160 | tf_op jit(solution)/shard_map/ppermute | solution.py:273
  8.8 4.3 %collective-permute-start.5 = (f32[1,4,16,256]{3,2,1,0:T(8,128)S(1)}, f32[1,4,16,256]{3,2,1,0:T(8,128)S(1)}, u32[]{:S(2)}, u32[]{:S(2)}) collective-permute-start(f32[1,4,16,256]{3,2,1,0:T(8,128)S(1)} %pair_sums.1), channel_id=1, source_target_pairs={{0,1},{1,0},{2,3},{3,2},{4,5},{5,4},{6,7},{7,6},{8,10},{9,11},{10,... | collective-permute-start | bytes 196616 | tf_op jit(solution)/shard_map/ppermute | solution.py:302
  10.9 1.2 %collective-permute-start.3 = (f32[1,16,128]{2,1,0:T(8,128)S(1)}, f32[1,16,128]{2,1,0:T(8,128)S(1)}, u32[]{:S(2)}, u32[]{:S(2)}) collective-permute-start(f32[1,16,128]{2,1,0:T(8,128)S(1)} %get-tuple-element.20), channel_id=1, source_target_pairs={{0,4},{4,0},{8,12},{12,8},{16,20},{20,16},{24,28},{28,24},{1,5},{5... | collective-permute-start | bytes 24584 | tf_op jit(solution)/shard_map/ppermute | solution.py:273

commit v20 on v19

--- a/solution.py
+++ b/solution.py
@@ -94,15 +94,15 @@
         rows = count * ROWS
         return (product[:rows] + product[rows:]).reshape(count, ROWS, LANES)
 
-    ordered = outs[:1] + outs[:0:-1]
     size = outs[0].shape[0]
-    blocks = size * len(outs)
-    if blocks <= 16:
-        result = dense(0, blocks)
-        for i, out in enumerate(ordered):
-            out[...] = result[i * size : (i + 1) * size]
+    if len(outs) == 4:
+        mine, x, y, diagonal = dense(0, 4 * size).reshape(4, size, ROWS, LANES)
+        swap = lax.axis_index("inst") % 2 == 1
+        sent = (jnp.where(swap, y, diagonal), jnp.where(swap, diagonal, y), x)
+        for out, part in zip(outs, (mine, *sent)):
+            out[...] = part
     else:
-        for i, out in enumerate(ordered):
+        for i, out in enumerate(outs):
 
             @pl.loop(0, size // 8)
             def _(g):
@@ -208,7 +208,9 @@
         def edge_of(device):
             relative = device ^ me
             half = RIDING // 2
-            place = (half - relative // 2) % half + (relative % 2) * half
+            place = (half - relative // 2) % half
+            swap = (lax.axis_index("inst") % 2 == 1) & (place >= 1) & (place <= 2)
+            place = jnp.where(swap, half - 1 - place, place) + (relative % 2) * half
             return jnp.sum(jnp.where(row == place, known, 0.0), axis=0, keepdims=True)
 
         before = edge_of((me + blocks - 1) % blocks)
@@ -276,9 +278,18 @@
         count = lax.axis_size(axis)
         return lax.ppermute(value, axis, [(i, (i + s) % count) for i in range(count)])
 
-    def exchanged(sent, size):
+    def exchanged(sent):
         return [
-            swapped(value, "space", (len(sent) - i) * size) for i, value in enumerate(sent)
+            lax.ppermute(
+                value,
+                ("space", "inst"),
+                [
+                    (i * instances + n, (i ^ bits[n % 2]) * instances + n)
+                    for i in range(blocks)
+                    for n in range(instances)
+                ],
+            )
+            for value, bits in zip(sent, ((6, 4), (4, 6), (2, 2)))
         ]
 
     def call(kernel, name, shapes, *operands, flops=0, dtype=jnp.float32):
@@ -331,7 +342,7 @@
         row = jnp.broadcast_to(kept[0, EDGE : EDGE + 1, :], (8, LANES))
         edges = [shifted(row, "space", 1), shifted(row, "space", blocks - 1)]
 
-    came = exchanged(sent, size)
+    came = exchanged(sent) if riding else [swapped(sent[0], "space", size)]
     sums = call(
         functools.partial(pair_kernel, weights, instances, orders),
         "pair_sums",
@@ -352,7 +363,7 @@
             *came,
             flops=PLACING,
         )
-        came = exchanged(sent, size)
+        came = [swapped(sent[0], "space", size)]
 
     base, step = call(
         functools.partial(flux_kernel, weights[0], instances),

time: 13.9 us -> 13.9 us (level)
    ppermute x4 -> x1, starting transfers between devices: 3.62 us -> 0.07 us  [swapped(): lax.ppermute(value, axis, [(i, i ^ bit) for i in range(lax.axis_size(axis...]
    ppermute x0 -> x3, starting transfers between devices: none -> 3.55 us  [exchanged(): lax.ppermute(value, ('space', 'inst'), [(i * instances + n, (i ^ bits[n %...]
    ppermute x4 -> x1, waiting for transfers between devices: 1.46 us -> 0.96 us  [swapped(): lax.ppermute(value, axis, [(i, i ^ bit) for i in range(lax.axis_size(axis...]
    ppermute x0 -> x3, waiting for transfers between devices: none -> 0.5 us  [exchanged(): lax.ppermute(value, ('space', 'inst'), [(i * instances + n, (i ^ bits[n %...]
where the time goes in v20:
time: 13.9 us; the launch traced here: 13.8 us
  starting transfers between devices  9.37 us (67%)
  waiting for transfers between devices  2.25 us (16%)
  Pallas kernels  1.4 us (10%)
  between operations  0.72 us (5%)
    ppermute x2, starting transfers between devices, partnered(): return lax.ppermute(value, ('space', 'inst'), pairs)  5.74 us
    ppermute x3, starting transfers between devices, exchanged(): lax.ppermute(value, ('space', 'inst'), [(i * instances + n, (i ^ bits[n %...  3.55 us
    pallas_call x7, Pallas kernels, call(): pl.pallas_call(kernel, out_shape=[jax.ShapeDtypeStruct(shape, dtype) for...  1.4 us
    ppermute x1, waiting for transfers between devices, swapped(): lax.ppermute(value, axis, [(i, i ^ bit) for i in range(lax.axis_size(axis...  0.96 us
    ppermute x2, waiting for transfers between devices, partnered(): return lax.ppermute(value, ('space', 'inst'), pairs)  0.78 us
    ppermute x3, waiting for transfers between devices, exchanged(): lax.ppermute(value, ('space', 'inst'), [(i * instances + n, (i ^ bits[n %...  0.5 us
  transfers between devices with their start and end apart: 6, of which 3 were waited for; matrix products, arithmetic and copies ran while one was open for 0% of the time, Pallas kernels for 5%

profile of v20, /device:TPU:0, one launch (start us, length us, event | category | flops | bytes accessed | tf_op | source)
XLA Modules:
  0.0 13.8 jit_solution(5969111541274825564)
XLA Ops:
  0.6 0.0 copy-start
  0.6 0.0 copy-start.2
  0.7 0.0 copy-start.3
  0.7 0.0 copy-start.1
  0.7 4.1 %collective-permute-start.4 = (f32[1,4,16,256]{3,2,1,0:T(8,128)}, f32[1,4,16,256]{3,2,1,0:T(8,128)S(1)}, u32[]{:S(2)}, u32[]{:S(2)}) collective-permute-start(f32[1,4,16,256]{3,2,1,0:T(8,128)} %state.7), channel_id=1, source_target_pairs={{0,2},{1,3},{2,0},{3,1},{4,6},{5,7},{6,4},{7,5},{8,9},{9,8},{10,11... | collective-permute-start | bytes 196616 | tf_op jit(solution)/shard_map/ppermute | solution.py:313
  4.8 0.0 copy-done
  4.8 0.0 copy-done.2
  4.8 0.0 copy-done.3
  4.8 0.0 copy-done.1
  4.8 0.4 %face_forces.1 = (f32[2,16,128]{2,1,0:T(8,128)S(1)}, f32[2,16,128]{2,1,0:T(8,128)S(1)}, f32[2,16,128]{2,1,0:T(8,128)S(1)}, f32[2,16,128]{2,1,0:T(8,128)S(1)}) custom-call(s32[8,128]{1,0:T(8,128)S(1)} %own.1, f32[1,4,16,256]{3,2,1,0:T(8,128)S(1)} %copy-done, s32[6,128]{1,0:T(8,128)S(1)} %bitcast.3, s32[6,128]{1,0:T(8,128)S(1)} %bitcast.4, f32[3,768]{1,0:T(4,128)S(1)} %copy-done.1), custom_call_target="tpu_custom_call" | custom-call | flops 10000000000 | tf_op jit(solution)/shard_map/face_forces/pallas_call | solution.py:296
  5.2 1.5 %collective-permute-start = (f32[2,16,128]{2,1,0:T(8,128)S(1)}, f32[2,16,128]{2,1,0:T(8,128)S(1)}, u32[]{:S(2)}, u32[]{:S(2)}) collective-permute-start(f32[2,16,128]{2,1,0:T(8,128)S(1)} %get-tuple-element.16), channel_id=1, source_target_pairs={{0,24},{1,17},{2,26},{3,19},{4,28},{5,21},{6,30},{7,23},{8,16},{9,... | collective-permute-start | bytes 49160 | tf_op jit(solution)/shard_map/ppermute | solution.py:283
  6.7 0.5 %collective-permute-start.1 = (f32[2,16,128]{2,1,0:T(8,128)S(1)}, f32[2,16,128]{2,1,0:T(8,128)S(1)}, u32[]{:S(2)}, u32[]{:S(2)}) collective-permute-start(f32[2,16,128]{2,1,0:T(8,128)S(1)} %get-tuple-element.17), channel_id=1, source_target_pairs={{0,16},{1,25},{2,18},{3,27},{4,20},{5,29},{6,22},{7,31},{8,24},{9,... | collective-permute-start | bytes 49160 | tf_op jit(solution)/shard_map/ppermute | solution.py:283
  7.2 1.5 %collective-permute-start.2 = (f32[2,16,128]{2,1,0:T(8,128)S(1)}, f32[2,16,128]{2,1,0:T(8,128)S(1)}, u32[]{:S(2)}, u32[]{:S(2)}) collective-permute-start(f32[2,16,128]{2,1,0:T(8,128)S(1)} %get-tuple-element.18), channel_id=1, source_target_pairs={{0,8},{1,9},{2,10},{3,11},{4,12},{5,13},{6,14},{7,15},{8,0},{9,1},... | collective-permute-start | bytes 49160 | tf_op jit(solution)/shard_map/ppermute | solution.py:283
  8.7 0.0 collective-permute-done.4.partner
  8.8 1.6 %collective-permute-start.5 = (f32[1,4,16,256]{3,2,1,0:T(8,128)S(1)}, f32[1,4,16,256]{3,2,1,0:T(8,128)S(1)}, u32[]{:S(2)}, u32[]{:S(2)}) collective-permute-start(f32[1,4,16,256]{3,2,1,0:T(8,128)S(1)} %pair_sums.1), channel_id=1, source_target_pairs={{0,1},{1,0},{2,3},{3,2},{4,5},{5,4},{6,7},{7,6},{8,10},{9,11},{10,... | collective-permute-start | bytes 196616 | tf_op jit(solution)/shard_map/ppermute | solution.py:313
  10.4 0.0 collective-permute-done.refs_1_
  10.4 0.0 collective-permute-done.1.refs_2_
  10.4 0.5 %collective-permute-done.2.refs_3_ = f32[2,16,128]{2,1,0:T(8,128)S(1)} collective-permute-done((f32[2,16,128]{2,1,0:T(8,128)S(1)}, f32[2,16,128]{2,1,0:T(8,128)S(1)}, u32[]{:S(2)}, u32[]{:S(2)}) %collective-permute-start.2) | collective-permute-done | bytes 16416 | tf_op jit(solution)/shard_map/ppermute | solution.py:283
  10.9 0.1 collective-permute-start.3
  11.0 0.2 %flux.1 = (f32[1,4,16,256]{3,2,1,0:T(8,128)S(1)}, f32[16,256]{1,0:T(8,128)S(1)}) custom-call(f32[1,4,16,256]{3,2,1,0:T(8,128)S(1)} %copy-done), custom_call_target="tpu_custom_call" | custom-call | tf_op jit(solution)/shard_map/flux/pallas_call | solution.py:296
  11.2 1.0 %collective-permute-done.3.came = f32[1,16,128]{2,1,0:T(8,128)S(1)} collective-permute-done((f32[1,16,128]{2,1,0:T(8,128)S(1)}, f32[1,16,128]{2,1,0:T(8,128)S(1)}, u32[]{:S(2)}, u32[]{:S(2)}) %collective-permute-start.3) | collective-permute-done | bytes 8224 | tf_op jit(solution)/shard_map/ppermute | solution.py:275
  12.2 0.1 %outer.1 = (f32[1,4,16,256]{3,2,1,0:T(8,128)S(1)}, f32[16,128]{1,0:T(8,128)S(1)}) custom-call(f32[1,4,16,256]{3,2,1,0:T(8,128)S(1)} %copy-done, f32[1,4,16,256]{3,2,1,0:T(8,128)S(1)} %get-tuple-element.14.base, f32[1,16,128]{2,1,0:T(8,128)S(1)} %get-tuple-element.19.kept, f32[1,16,128]{2,1,0:T(8,128)S(1)} %collective-permute-done.3.came, ...), custom_call_target="tpu_custom_call" | custom-call | tf_op jit(solution)/shard_map/outer/pallas_call | solution.py:296
  12.3 0.8 %collective-permute-done.5.refs_0_ = f32[1,4,16,256]{3,2,1,0:T(8,128)S(1)} collective-permute-done((f32[1,4,16,256]{3,2,1,0:T(8,128)S(1)}, f32[1,4,16,256]{3,2,1,0:T(8,128)S(1)}, u32[]{:S(2)}, u32[]{:S(2)}) %collective-permute-start.5) | collective-permute-done | bytes 65568 | tf_op jit(solution)/shard_map/ppermute | solution.py:313
  13.1 0.6 %update.1 = (f32[1,4,16,256]{3,2,1,0:T(8,128)}, f32[3,1,512]{2,1,0:T(1,128)}) custom-call(f32[1,4,16,256]{3,2,1,0:T(8,128)S(1)} %get-tuple-element.21.residual, f32[16,256]{1,0:T(8,128)S(1)} %get-tuple-element.22.step, f32[16,128]{1,0:T(8,128)S(1)} %get-tuple-element.23.total, f32[1,4,16,256]{3,2,1,0:T(8,128)S(1)} %collective-permute-done.5.refs_0_), custom_call_target="tpu_custom_call" | custom-call | tf_op jit(solution)/shard_map/update/pallas_call | solution.py:296
  (3 shorter events, 0.0 us)
Async XLA Ops:
  0.6 4.1 %copy-start = (f32[1,4,16,256]{3,2,1,0:T(8,128)S(1)}, f32[1,4,16,256]{3,2,1,0:T(8,128)}, u32[]{:S(2)}) copy-start(f32[1,4,16,256]{3,2,1,0:T(8,128)} %state.7) | copy-start | bytes 196612
  0.6 4.1 %copy-start.2 = (s32[768]{0:T(1024)S(1)}, s32[768]{0:T(1024)}, u32[]{:S(2)}) copy-start(s32[768]{0:T(1024)} %param.5) | copy-start | bytes 9220
  0.7 4.1 %copy-start.3 = (s32[768]{0:T(1024)S(1)}, s32[768]{0:T(1024)}, u32[]{:S(2)}) copy-start(s32[768]{0:T(1024)} %param.6) | copy-start | bytes 9220
  0.7 4.1 %copy-start.1 = (f32[3,768]{1,0:T(4,128)S(1)}, f32[3,768]{1,0:T(4,128)}, u32[]{:S(2)}) copy-start(f32[3,768]{1,0:T(4,128)} %area.1) | copy-start | bytes 27652
  0.7 8.1 %collective-permute-start.4 = (f32[1,4,16,256]{3,2,1,0:T(8,128)}, f32[1,4,16,256]{3,2,1,0:T(8,128)S(1)}, u32[]{:S(2)}, u32[]{:S(2)}) collective-permute-start(f32[1,4,16,256]{3,2,1,0:T(8,128)} %state.7), channel_id=1, source_target_pairs={{0,2},{1,3},{2,0},{3,1},{4,6},{5,7},{6,4},{7,5},{8,9},{9,8},{10,11... | collective-permute-start | bytes 196616 | tf_op jit(solution)/shard_map/ppermute | solution.py:313
  5.2 5.2 %collective-permute-start = (f32[2,16,128]{2,1,0:T(8,128)S(1)}, f32[2,16,128]{2,1,0:T(8,128)S(1)}, u32[]{:S(2)}, u32[]{:S(2)}) collective-permute-start(f32[2,16,128]{2,1,0:T(8,128)S(1)} %get-tuple-element.16), channel_id=1, source_target_pairs={{0,24},{1,17},{2,26},{3,19},{4,28},{5,21},{6,30},{7,23},{8,16},{9,... | collective-permute-start | bytes 49160 | tf_op jit(solution)/shard_map/ppermute | solution.py:283
  6.7 3.7 %collective-permute-start.1 = (f32[2,16,128]{2,1,0:T(8,128)S(1)}, f32[2,16,128]{2,1,0:T(8,128)S(1)}, u32[]{:S(2)}, u32[]{:S(2)}) collective-permute-start(f32[2,16,128]{2,1,0:T(8,128)S(1)} %get-tuple-element.17), channel_id=1, source_target_pairs={{0,16},{1,25},{2,18},{3,27},{4,20},{5,29},{6,22},{7,31},{8,24},{9,... | collective-permute-start | bytes 49160 | tf_op jit(solution)/shard_map/ppermute | solution.py:283
  7.2 3.7 %collective-permute-start.2 = (f32[2,16,128]{2,1,0:T(8,128)S(1)}, f32[2,16,128]{2,1,0:T(8,128)S(1)}, u32[]{:S(2)}, u32[]{:S(2)}) collective-permute-start(f32[2,16,128]{2,1,0:T(8,128)S(1)} %get-tuple-element.18), channel_id=1, source_target_pairs={{0,8},{1,9},{2,10},{3,11},{4,12},{5,13},{6,14},{7,15},{8,0},{9,1},... | collective-permute-start | bytes 49160 | tf_op jit(solution)/shard_map/ppermute | solution.py:283
  8.8 4.3 %collective-permute-start.5 = (f32[1,4,16,256]{3,2,1,0:T(8,128)S(1)}, f32[1,4,16,256]{3,2,1,0:T(8,128)S(1)}, u32[]{:S(2)}, u32[]{:S(2)}) collective-permute-start(f32[1,4,16,256]{3,2,1,0:T(8,128)S(1)} %pair_sums.1), channel_id=1, source_target_pairs={{0,1},{1,0},{2,3},{3,2},{4,5},{5,4},{6,7},{7,6},{8,10},{9,11},{10,... | collective-permute-start | bytes 196616 | tf_op jit(solution)/shard_map/ppermute | solution.py:313
  10.9 1.2 %collective-permute-start.3 = (f32[1,16,128]{2,1,0:T(8,128)S(1)}, f32[1,16,128]{2,1,0:T(8,128)S(1)}, u32[]{:S(2)}, u32[]{:S(2)}) collective-permute-start(f32[1,16,128]{2,1,0:T(8,128)S(1)} %get-tuple-element.20), channel_id=1, source_target_pairs={{0,4},{4,0},{8,12},{12,8},{16,20},{20,16},{24,28},{28,24},{1,5},{5... | collective-permute-start | bytes 24584 | tf_op jit(solution)/shard_map/ppermute | solution.py:275

commit v21 on v19

--- a/solution.py
+++ b/solution.py
@@ -94,7 +94,7 @@
         rows = count * ROWS
         return (product[:rows] + product[rows:]).reshape(count, ROWS, LANES)
 
-    ordered = outs[:1] + outs[:0:-1]
+    ordered = [outs[0], outs[2], outs[3], outs[1]] if len(outs) == 4 else outs
     size = outs[0].shape[0]
     blocks = size * len(outs)
     if blocks <= 16:
@@ -144,8 +144,8 @@
 
 
 def of_chip(orders):
-    chip = lax.axis_index("space") // 2
-    return [jnp.where(chip % 2 == 0, a, b) for a, b in zip(*orders)]
+    half = lax.axis_index("space") // 4
+    return [jnp.where(half % 2 == 0, a, b) for a, b in zip(*orders)]
 
 
 def pair_kernel(weights, instances, orders, state, partner, *outs):
@@ -208,7 +208,9 @@
         def edge_of(device):
             relative = device ^ me
             half = RIDING // 2
-            place = (half - relative // 2) % half + (relative % 2) * half
+            chip = relative // 2
+            place = jnp.where(chip == 3, 1, jnp.where(chip == 0, 0, chip + 1))
+            place += (relative % 2) * half
             return jnp.sum(jnp.where(row == place, known, 0.0), axis=0, keepdims=True)
 
         before = edge_of((me + blocks - 1) % blocks)
@@ -277,9 +279,8 @@
         return lax.ppermute(value, axis, [(i, (i + s) % count) for i in range(count)])
 
     def exchanged(sent, size):
-        return [
-            swapped(value, "space", (len(sent) - i) * size) for i, value in enumerate(sent)
-        ]
+        places = (3, 1, 2) if len(sent) == 3 else (1,)
+        return [swapped(value, "space", place * size) for place, value in zip(places, sent)]
 
     def call(kernel, name, shapes, *operands, flops=0, dtype=jnp.float32):
         return pl.pallas_call(
@@ -295,7 +296,7 @@
     weights = spectral_row(instances)
     def partnered(value, place):
         pairs = [
-            (i * instances + n, i * instances + (n ^ orders[i // 2 % 2][place]))
+            (i * instances + n, i * instances + (n ^ orders[i // 4 % 2][place]))
             for i in range(blocks)
             for n in range(instances)
         ]

time: 13.9 us -> 13.9 us (level)
  no operation moved by 1% of the time
where the time goes in v21:
time: 13.9 us; the launch traced here: 13.8 us
  starting transfers between devices  9.37 us (67%)
  waiting for transfers between devices  2.26 us (16%)
  Pallas kernels  1.39 us (10%)
  between operations  0.72 us (5%)
    ppermute x2, starting transfers between devices, partnered(): return lax.ppermute(value, ('space', 'inst'), pairs)  5.74 us
    ppermute x4, starting transfers between devices, swapped(): lax.ppermute(value, axis, [(i, i ^ bit) for i in range(lax.axis_size(axis...  3.62 us
    ppermute x4, waiting for transfers between devices, swapped(): lax.ppermute(value, axis, [(i, i ^ bit) for i in range(lax.axis_size(axis...  1.49 us
    pallas_call x7, Pallas kernels, call(): pl.pallas_call(kernel, out_shape=[jax.ShapeDtypeStruct(shape, dtype) for...  1.39 us
    ppermute x2, waiting for transfers between devices, partnered(): return lax.ppermute(value, ('space', 'inst'), pairs)  0.77 us
  transfers between devices with their start and end apart: 6, of which 3 were waited for; matrix products, arithmetic and copies ran while one was open for 0% of the time, Pallas kernels for 5%

profile of v21, /device:TPU:0, one launch (start us, length us, event | category | flops | bytes accessed | tf_op | source)
XLA Modules:
  0.0 13.8 jit_solution(13631257698039079382)
XLA Ops:
  0.6 0.0 copy-start
  0.6 0.0 copy-start.2
  0.7 0.0 copy-start.3
  0.7 0.0 copy-start.1
  0.7 4.1 %collective-permute-start.4 = (f32[1,4,16,256]{3,2,1,0:T(8,128)}, f32[1,4,16,256]{3,2,1,0:T(8,128)S(1)}, u32[]{:S(2)}, u32[]{:S(2)}) collective-permute-start(f32[1,4,16,256]{3,2,1,0:T(8,128)} %state.7), channel_id=1, source_target_pairs={{0,2},{1,3},{2,0},{3,1},{4,6},{5,7},{6,4},{7,5},{8,10},{9,11},{10,... | collective-permute-start | bytes 196616 | tf_op jit(solution)/shard_map/ppermute | solution.py:303
  4.8 0.0 copy-done
  4.8 0.0 copy-done.2
  4.8 0.0 copy-done.3
  4.8 0.0 copy-done.1
  4.8 0.4 %face_forces.1 = (f32[2,16,128]{2,1,0:T(8,128)S(1)}, f32[2,16,128]{2,1,0:T(8,128)S(1)}, f32[2,16,128]{2,1,0:T(8,128)S(1)}, f32[2,16,128]{2,1,0:T(8,128)S(1)}) custom-call(s32[8,128]{1,0:T(8,128)S(1)} %own.1, f32[1,4,16,256]{3,2,1,0:T(8,128)S(1)} %copy-done, s32[6,128]{1,0:T(8,128)S(1)} %bitcast.3, s32[6,128]{1,0:T(8,128)S(1)} %bitcast.4, f32[3,768]{1,0:T(4,128)S(1)} %copy-done.1), custom_call_target="tpu_custom_call" | custom-call | flops 10000000000 | tf_op jit(solution)/shard_map/face_forces/pallas_call | solution.py:286
  5.2 1.5 %collective-permute-start = (f32[2,16,128]{2,1,0:T(8,128)S(1)}, f32[2,16,128]{2,1,0:T(8,128)S(1)}, u32[]{:S(2)}, u32[]{:S(2)}) collective-permute-start(f32[2,16,128]{2,1,0:T(8,128)S(1)} %get-tuple-element.16), channel_id=1, source_target_pairs={{0,24},{4,28},{8,16},{12,20},{16,8},{20,12},{24,0},{28,4},{1,25},{... | collective-permute-start | bytes 49160 | tf_op jit(solution)/shard_map/ppermute | solution.py:275
  6.7 0.5 %collective-permute-start.1 = (f32[2,16,128]{2,1,0:T(8,128)S(1)}, f32[2,16,128]{2,1,0:T(8,128)S(1)}, u32[]{:S(2)}, u32[]{:S(2)}) collective-permute-start(f32[2,16,128]{2,1,0:T(8,128)S(1)} %get-tuple-element.17), channel_id=1, source_target_pairs={{0,8},{4,12},{8,0},{12,4},{16,24},{20,28},{24,16},{28,20},{1,9},{5... | collective-permute-start | bytes 49160 | tf_op jit(solution)/shard_map/ppermute | solution.py:275
  7.2 1.5 %collective-permute-start.2 = (f32[2,16,128]{2,1,0:T(8,128)S(1)}, f32[2,16,128]{2,1,0:T(8,128)S(1)}, u32[]{:S(2)}, u32[]{:S(2)}) collective-permute-start(f32[2,16,128]{2,1,0:T(8,128)S(1)} %get-tuple-element.18), channel_id=1, source_target_pairs={{0,16},{4,20},{8,24},{12,28},{16,0},{20,4},{24,8},{28,12},{1,17},{... | collective-permute-start | bytes 49160 | tf_op jit(solution)/shard_map/ppermute | solution.py:275
  8.7 0.0 collective-permute-done.4.partner
  8.8 1.6 %collective-permute-start.5 = (f32[1,4,16,256]{3,2,1,0:T(8,128)S(1)}, f32[1,4,16,256]{3,2,1,0:T(8,128)S(1)}, u32[]{:S(2)}, u32[]{:S(2)}) collective-permute-start(f32[1,4,16,256]{3,2,1,0:T(8,128)S(1)} %pair_sums.1), channel_id=1, source_target_pairs={{0,1},{1,0},{2,3},{3,2},{4,5},{5,4},{6,7},{7,6},{8,9},{9,8},{10,11... | collective-permute-start | bytes 196616 | tf_op jit(solution)/shard_map/ppermute | solution.py:303
  10.4 0.0 collective-permute-done.refs_1_
  10.4 0.0 collective-permute-done.1.refs_2_
  10.4 0.5 %collective-permute-done.2.refs_3_ = f32[2,16,128]{2,1,0:T(8,128)S(1)} collective-permute-done((f32[2,16,128]{2,1,0:T(8,128)S(1)}, f32[2,16,128]{2,1,0:T(8,128)S(1)}, u32[]{:S(2)}, u32[]{:S(2)}) %collective-permute-start.2) | collective-permute-done | bytes 16416 | tf_op jit(solution)/shard_map/ppermute | solution.py:275
  11.0 0.1 collective-permute-start.3
  11.0 0.2 %flux.1 = (f32[1,4,16,256]{3,2,1,0:T(8,128)S(1)}, f32[16,256]{1,0:T(8,128)S(1)}) custom-call(f32[1,4,16,256]{3,2,1,0:T(8,128)S(1)} %copy-done), custom_call_target="tpu_custom_call" | custom-call | tf_op jit(solution)/shard_map/flux/pallas_call | solution.py:286
  11.2 1.0 %collective-permute-done.3.came = f32[1,16,128]{2,1,0:T(8,128)S(1)} collective-permute-done((f32[1,16,128]{2,1,0:T(8,128)S(1)}, f32[1,16,128]{2,1,0:T(8,128)S(1)}, u32[]{:S(2)}, u32[]{:S(2)}) %collective-permute-start.3) | collective-permute-done | bytes 8224 | tf_op jit(solution)/shard_map/ppermute | solution.py:275
  12.2 0.1 %outer.1 = (f32[1,4,16,256]{3,2,1,0:T(8,128)S(1)}, f32[16,128]{1,0:T(8,128)S(1)}) custom-call(f32[1,4,16,256]{3,2,1,0:T(8,128)S(1)} %copy-done, f32[1,4,16,256]{3,2,1,0:T(8,128)S(1)} %get-tuple-element.14.base, f32[1,16,128]{2,1,0:T(8,128)S(1)} %get-tuple-element.19.kept, f32[1,16,128]{2,1,0:T(8,128)S(1)} %collective-permute-done.3.came, ...), custom_call_target="tpu_custom_call" | custom-call | tf_op jit(solution)/shard_map/outer/pallas_call | solution.py:286
  12.3 0.8 %collective-permute-done.5.refs_0_ = f32[1,4,16,256]{3,2,1,0:T(8,128)S(1)} collective-permute-done((f32[1,4,16,256]{3,2,1,0:T(8,128)S(1)}, f32[1,4,16,256]{3,2,1,0:T(8,128)S(1)}, u32[]{:S(2)}, u32[]{:S(2)}) %collective-permute-start.5) | collective-permute-done | bytes 65568 | tf_op jit(solution)/shard_map/ppermute | solution.py:303
  13.1 0.6 %update.1 = (f32[1,4,16,256]{3,2,1,0:T(8,128)}, f32[3,1,512]{2,1,0:T(1,128)}) custom-call(f32[1,4,16,256]{3,2,1,0:T(8,128)S(1)} %get-tuple-element.21.residual, f32[16,256]{1,0:T(8,128)S(1)} %get-tuple-element.22.step, f32[16,128]{1,0:T(8,128)S(1)} %get-tuple-element.23.total, f32[1,4,16,256]{3,2,1,0:T(8,128)S(1)} %collective-permute-done.5.refs_0_), custom_call_target="tpu_custom_call" | custom-call | tf_op jit(solution)/shard_map/update/pallas_call | solution.py:286
  (3 shorter events, 0.0 us)
Async XLA Ops:
  0.6 4.1 %copy-start = (f32[1,4,16,256]{3,2,1,0:T(8,128)S(1)}, f32[1,4,16,256]{3,2,1,0:T(8,128)}, u32[]{:S(2)}) copy-start(f32[1,4,16,256]{3,2,1,0:T(8,128)} %state.7) | copy-start | bytes 196612
  0.6 4.1 %copy-start.2 = (s32[768]{0:T(1024)S(1)}, s32[768]{0:T(1024)}, u32[]{:S(2)}) copy-start(s32[768]{0:T(1024)} %param.5) | copy-start | bytes 9220
  0.7 4.1 %copy-start.3 = (s32[768]{0:T(1024)S(1)}, s32[768]{0:T(1024)}, u32[]{:S(2)}) copy-start(s32[768]{0:T(1024)} %param.6) | copy-start | bytes 9220
  0.7 4.1 %copy-start.1 = (f32[3,768]{1,0:T(4,128)S(1)}, f32[3,768]{1,0:T(4,128)}, u32[]{:S(2)}) copy-start(f32[3,768]{1,0:T(4,128)} %area.1) | copy-start | bytes 27652
  0.7 8.1 %collective-permute-start.4 = (f32[1,4,16,256]{3,2,1,0:T(8,128)}, f32[1,4,16,256]{3,2,1,0:T(8,128)S(1)}, u32[]{:S(2)}, u32[]{:S(2)}) collective-permute-start(f32[1,4,16,256]{3,2,1,0:T(8,128)} %state.7), channel_id=1, source_target_pairs={{0,2},{1,3},{2,0},{3,1},{4,6},{5,7},{6,4},{7,5},{8,10},{9,11},{10,... | collective-permute-start | bytes 196616 | tf_op jit(solution)/shard_map/ppermute | solution.py:303
  5.2 5.2 %collective-permute-start = (f32[2,16,128]{2,1,0:T(8,128)S(1)}, f32[2,16,128]{2,1,0:T(8,128)S(1)}, u32[]{:S(2)}, u32[]{:S(2)}) collective-permute-start(f32[2,16,128]{2,1,0:T(8,128)S(1)} %get-tuple-element.16), channel_id=1, source_target_pairs={{0,24},{4,28},{8,16},{12,20},{16,8},{20,12},{24,0},{28,4},{1,25},{... | collective-permute-start | bytes 49160 | tf_op jit(solution)/shard_map/ppermute | solution.py:275
  6.7 3.7 %collective-permute-start.1 = (f32[2,16,128]{2,1,0:T(8,128)S(1)}, f32[2,16,128]{2,1,0:T(8,128)S(1)}, u32[]{:S(2)}, u32[]{:S(2)}) collective-permute-start(f32[2,16,128]{2,1,0:T(8,128)S(1)} %get-tuple-element.17), channel_id=1, source_target_pairs={{0,8},{4,12},{8,0},{12,4},{16,24},{20,28},{24,16},{28,20},{1,9},{5... | collective-permute-start | bytes 49160 | tf_op jit(solution)/shard_map/ppermute | solution.py:275
  7.2 3.7 %collective-permute-start.2 = (f32[2,16,128]{2,1,0:T(8,128)S(1)}, f32[2,16,128]{2,1,0:T(8,128)S(1)}, u32[]{:S(2)}, u32[]{:S(2)}) collective-permute-start(f32[2,16,128]{2,1,0:T(8,128)S(1)} %get-tuple-element.18), channel_id=1, source_target_pairs={{0,16},{4,20},{8,24},{12,28},{16,0},{20,4},{24,8},{28,12},{1,17},{... | collective-permute-start | bytes 49160 | tf_op jit(solution)/shard_map/ppermute | solution.py:275
  8.8 4.3 %collective-permute-start.5 = (f32[1,4,16,256]{3,2,1,0:T(8,128)S(1)}, f32[1,4,16,256]{3,2,1,0:T(8,128)S(1)}, u32[]{:S(2)}, u32[]{:S(2)}) collective-permute-start(f32[1,4,16,256]{3,2,1,0:T(8,128)S(1)} %pair_sums.1), channel_id=1, source_target_pairs={{0,1},{1,0},{2,3},{3,2},{4,5},{5,4},{6,7},{7,6},{8,9},{9,8},{10,11... | collective-permute-start | bytes 196616 | tf_op jit(solution)/shard_map/ppermute | solution.py:303
  11.0 1.2 %collective-permute-start.3 = (f32[1,16,128]{2,1,0:T(8,128)S(1)}, f32[1,16,128]{2,1,0:T(8,128)S(1)}, u32[]{:S(2)}, u32[]{:S(2)}) collective-permute-start(f32[1,16,128]{2,1,0:T(8,128)S(1)} %get-tuple-element.20), channel_id=1, source_target_pairs={{0,4},{4,0},{8,12},{12,8},{16,20},{20,16},{24,28},{28,24},{1,5},{5... | collective-permute-start | bytes 24584 | tf_op jit(solution)/shard_map/ppermute | solution.py:275

commit v22 on v21

--- a/solution.py
+++ b/solution.py
@@ -62,9 +62,10 @@
                 value = jnp.take_along_axis(part, lane, axis=1, mode="promise_in_bounds")
                 place = (sublane + r * 8) * (around // LANES) + h
                 total += jnp.where(tile == place, value, 0.0)
-        picked.append(jnp.sum(total, axis=0, keepdims=True))
+        for turn in (4, 2, 1):
+            total += pltpu.roll(total, turn, 0)
+        picked.append(total)
     face_pressure = jnp.concatenate(picked, axis=1)
-    contribution = face_pressure * area[...]
     nodes = jnp.concatenate([node[c : c + 1, :] for c in range(chunks)], axis=1)
 
     high = node_block // LANES
@@ -75,7 +76,7 @@
     ).astype(jnp.float32).astype(jnp.bfloat16)
 
     row = lax.broadcasted_iota(jnp.int32, (8, faces), 0)
-    x, y, z = (jnp.broadcast_to(contribution[k : k + 1], (8, faces)) for k in range(3))
+    x, y, z = (face_pressure * jnp.broadcast_to(area[k : k + 1, :], (8, faces)) for k in range(3))
     groups = []
     for pattern in (jnp.where(row < high, x, y), jnp.where(row < high, z, 0.0)):
         first = pattern.astype(jnp.bfloat16).astype(jnp.float32)
@@ -253,14 +254,21 @@
 
 
 def update_kernel(residual, step, total, *refs):
-    *sums, increment, blade = refs
+    *sums, increment_hbm, blade_hbm, increment, blade, sems = refs
     high = blade.shape[2] // LANES
     for k in range(3):
         for h in range(high):
             blade[k, :, pl.ds(h * LANES, LANES)] = total[k * high + h : k * high + h + 1, :]
+    copies = [pltpu.make_async_copy(blade, blade_hbm, sems.at[0])]
+    copies[0].start()
     for c in range(residual.shape[1]):
         change = functools.reduce(jnp.add, [ref[0, c] for ref in (residual, *sums)])
         increment[0, c] = -step[...] * change
+        copy = pltpu.make_async_copy(increment.at[0, c], increment_hbm.at[0, c], sems.at[1 + c])
+        copy.start()
+        copies.append(copy)
+    for copy in copies:
+        copy.wait()
 
 
 def per_device(node_block, state, face_cell, face_node, face_area):
@@ -372,15 +380,21 @@
         partner,
         *edges,
     )
-    increment, blade = call(
+    results = [
+        jax.ShapeDtypeStruct(state.shape, jnp.float32),
+        jax.ShapeDtypeStruct((3, 1, node_block), jnp.float32),
+    ]
+    increment, blade = pl.pallas_call(
         update_kernel,
-        "update",
-        [state.shape, (3, 1, node_block)],
-        residual,
-        step,
-        total,
-        *sums,
-    )
+        out_shape=results,
+        in_specs=[vmem] * (3 + len(sums)),
+        out_specs=[pl.BlockSpec(memory_space=pltpu.HBM)] * 2,
+        scratch_shapes=[pltpu.VMEM(x.shape, x.dtype) for x in results]
+        + [pltpu.SemaphoreType.DMA((5,))],
+        compiler_params=params,
+        cost_estimate=pl.CostEstimate(flops=0, bytes_accessed=0, transcendentals=0),
+        name="update",
+    )(residual, step, total, *sums)
     return increment, jnp.transpose(blade, (1, 0, 2))
 
 

time: 13.9 us -> 13.9 us (level)
    pallas_call x0 -> x1, Pallas kernels: none -> 0.68 us  [per_device(): pl.pallas_call(update_kernel, out_shape=results, in_specs=[vmem] * (3 + l...]
    pallas_call x7 -> x6, Pallas kernels: 1.39 us -> 0.73 us  [call(): pl.pallas_call(kernel, out_shape=[jax.ShapeDtypeStruct(shape, dtype) for...]
where the time goes in v22:
time: 13.9 us; the launch traced here: 13.8 us
  starting transfers between devices  9.37 us (67%)
  waiting for transfers between devices  2.26 us (16%)
  Pallas kernels  1.41 us (10%)
  between operations  0.72 us (5%)
    ppermute x2, starting transfers between devices, partnered(): return lax.ppermute(value, ('space', 'inst'), pairs)  5.74 us
    ppermute x4, starting transfers between devices, swapped(): lax.ppermute(value, axis, [(i, i ^ bit) for i in range(lax.axis_size(axis...  3.62 us
    ppermute x4, waiting for transfers between devices, swapped(): lax.ppermute(value, axis, [(i, i ^ bit) for i in range(lax.axis_size(axis...  1.49 us
    ppermute x2, waiting for transfers between devices, partnered(): return lax.ppermute(value, ('space', 'inst'), pairs)  0.76 us
    pallas_call x6, Pallas kernels, call(): pl.pallas_call(kernel, out_shape=[jax.ShapeDtypeStruct(shape, dtype) for...  0.73 us
    pallas_call x1, Pallas kernels, per_device(): pl.pallas_call(update_kernel, out_shape=results, in_specs=[vmem] * (3 + l...  0.68 us
  transfers between devices with their start and end apart: 6, of which 3 were waited for; matrix products, arithmetic and copies ran while one was open for 0% of the time, Pallas kernels for 5%

profile of v22, /device:TPU:0, one launch (start us, length us, event | category | flops | bytes accessed | tf_op | source)
XLA Modules:
  0.0 13.8 jit_solution(1901589008148153381)
XLA Ops:
  0.6 0.0 copy-start
  0.6 0.0 copy-start.2
  0.7 0.0 copy-start.3
  0.7 0.0 copy-start.1
  0.7 4.1 %collective-permute-start.4 = (f32[1,4,16,256]{3,2,1,0:T(8,128)}, f32[1,4,16,256]{3,2,1,0:T(8,128)S(1)}, u32[]{:S(2)}, u32[]{:S(2)}) collective-permute-start(f32[1,4,16,256]{3,2,1,0:T(8,128)} %state.7), channel_id=1, source_target_pairs={{0,2},{1,3},{2,0},{3,1},{4,6},{5,7},{6,4},{7,5},{8,10},{9,11},{10,... | collective-permute-start | bytes 196616 | tf_op jit(solution)/shard_map/ppermute | solution.py:311
  4.8 0.0 copy-done
  4.8 0.0 copy-done.2
  4.8 0.0 copy-done.3
  4.8 0.0 copy-done.1
  4.8 0.4 %face_forces.1 = (f32[2,16,128]{2,1,0:T(8,128)S(1)}, f32[2,16,128]{2,1,0:T(8,128)S(1)}, f32[2,16,128]{2,1,0:T(8,128)S(1)}, f32[2,16,128]{2,1,0:T(8,128)S(1)}) custom-call(s32[8,128]{1,0:T(8,128)S(1)} %own.1, f32[1,4,16,256]{3,2,1,0:T(8,128)S(1)} %copy-done, s32[6,128]{1,0:T(8,128)S(1)} %bitcast.3, s32[6,128]{1,0:T(8,128)S(1)} %bitcast.4, f32[3,768]{1,0:T(4,128)S(1)} %copy-done.1), custom_call_target="tpu_custom_call" | custom-call | flops 10000000000 | tf_op jit(solution)/shard_map/face_forces/pallas_call | solution.py:294
  5.2 1.5 %collective-permute-start = (f32[2,16,128]{2,1,0:T(8,128)S(1)}, f32[2,16,128]{2,1,0:T(8,128)S(1)}, u32[]{:S(2)}, u32[]{:S(2)}) collective-permute-start(f32[2,16,128]{2,1,0:T(8,128)S(1)} %get-tuple-element.16), channel_id=1, source_target_pairs={{0,24},{4,28},{8,16},{12,20},{16,8},{20,12},{24,0},{28,4},{1,25},{... | collective-permute-start | bytes 49160 | tf_op jit(solution)/shard_map/ppermute | solution.py:283
  6.7 0.5 %collective-permute-start.1 = (f32[2,16,128]{2,1,0:T(8,128)S(1)}, f32[2,16,128]{2,1,0:T(8,128)S(1)}, u32[]{:S(2)}, u32[]{:S(2)}) collective-permute-start(f32[2,16,128]{2,1,0:T(8,128)S(1)} %get-tuple-element.17), channel_id=1, source_target_pairs={{0,8},{4,12},{8,0},{12,4},{16,24},{20,28},{24,16},{28,20},{1,9},{5... | collective-permute-start | bytes 49160 | tf_op jit(solution)/shard_map/ppermute | solution.py:283
  7.2 1.5 %collective-permute-start.2 = (f32[2,16,128]{2,1,0:T(8,128)S(1)}, f32[2,16,128]{2,1,0:T(8,128)S(1)}, u32[]{:S(2)}, u32[]{:S(2)}) collective-permute-start(f32[2,16,128]{2,1,0:T(8,128)S(1)} %get-tuple-element.18), channel_id=1, source_target_pairs={{0,16},{4,20},{8,24},{12,28},{16,0},{20,4},{24,8},{28,12},{1,17},{... | collective-permute-start | bytes 49160 | tf_op jit(solution)/shard_map/ppermute | solution.py:283
  8.7 0.0 collective-permute-done.4.partner
  8.8 1.6 %collective-permute-start.5 = (f32[1,4,16,256]{3,2,1,0:T(8,128)S(1)}, f32[1,4,16,256]{3,2,1,0:T(8,128)S(1)}, u32[]{:S(2)}, u32[]{:S(2)}) collective-permute-start(f32[1,4,16,256]{3,2,1,0:T(8,128)S(1)} %pair_sums.1), channel_id=1, source_target_pairs={{0,1},{1,0},{2,3},{3,2},{4,5},{5,4},{6,7},{7,6},{8,9},{9,8},{10,11... | collective-permute-start | bytes 196616 | tf_op jit(solution)/shard_map/ppermute | solution.py:311
  10.4 0.0 collective-permute-done.refs_1_
  10.4 0.0 collective-permute-done.1.refs_2_
  10.4 0.5 %collective-permute-done.2.refs_3_ = f32[2,16,128]{2,1,0:T(8,128)S(1)} collective-permute-done((f32[2,16,128]{2,1,0:T(8,128)S(1)}, f32[2,16,128]{2,1,0:T(8,128)S(1)}, u32[]{:S(2)}, u32[]{:S(2)}) %collective-permute-start.2) | collective-permute-done | bytes 16416 | tf_op jit(solution)/shard_map/ppermute | solution.py:283
  10.9 0.1 collective-permute-start.3
  11.0 0.2 %flux.1 = (f32[1,4,16,256]{3,2,1,0:T(8,128)S(1)}, f32[16,256]{1,0:T(8,128)S(1)}) custom-call(f32[1,4,16,256]{3,2,1,0:T(8,128)S(1)} %copy-done), custom_call_target="tpu_custom_call" | custom-call | tf_op jit(solution)/shard_map/flux/pallas_call | solution.py:294
  11.2 1.0 %collective-permute-done.3.came = f32[1,16,128]{2,1,0:T(8,128)S(1)} collective-permute-done((f32[1,16,128]{2,1,0:T(8,128)S(1)}, f32[1,16,128]{2,1,0:T(8,128)S(1)}, u32[]{:S(2)}, u32[]{:S(2)}) %collective-permute-start.3) | collective-permute-done | bytes 8224 | tf_op jit(solution)/shard_map/ppermute | solution.py:283
  12.2 0.1 %outer.1 = (f32[1,4,16,256]{3,2,1,0:T(8,128)S(1)}, f32[16,128]{1,0:T(8,128)S(1)}) custom-call(f32[1,4,16,256]{3,2,1,0:T(8,128)S(1)} %copy-done, f32[1,4,16,256]{3,2,1,0:T(8,128)S(1)} %get-tuple-element.14.base, f32[1,16,128]{2,1,0:T(8,128)S(1)} %get-tuple-element.19.kept, f32[1,16,128]{2,1,0:T(8,128)S(1)} %collective-permute-done.3.came, ...), custom_call_target="tpu_custom_call" | custom-call | tf_op jit(solution)/shard_map/outer/pallas_call | solution.py:294
  12.3 0.8 %collective-permute-done.5.refs_0_ = f32[1,4,16,256]{3,2,1,0:T(8,128)S(1)} collective-permute-done((f32[1,4,16,256]{3,2,1,0:T(8,128)S(1)}, f32[1,4,16,256]{3,2,1,0:T(8,128)S(1)}, u32[]{:S(2)}, u32[]{:S(2)}) %collective-permute-start.5) | collective-permute-done | bytes 65568 | tf_op jit(solution)/shard_map/ppermute | solution.py:311
  13.1 0.7 %update.1 = (f32[1,4,16,256]{3,2,1,0:T(8,128)}, f32[3,1,512]{2,1,0:T(1,128)}) custom-call(f32[1,4,16,256]{3,2,1,0:T(8,128)S(1)} %get-tuple-element.21.residual, f32[16,256]{1,0:T(8,128)S(1)} %get-tuple-element.22.step, f32[16,128]{1,0:T(8,128)S(1)} %get-tuple-element.23.total, f32[1,4,16,256]{3,2,1,0:T(8,128)S(1)} %collective-permute-done.5.refs_0_), custom_call_target="tpu_custom_call" | custom-call | tf_op jit(solution)/shard_map/update/pallas_call | solution.py:387
  (3 shorter events, 0.0 us)
Async XLA Ops:
  0.6 4.1 %copy-start = (f32[1,4,16,256]{3,2,1,0:T(8,128)S(1)}, f32[1,4,16,256]{3,2,1,0:T(8,128)}, u32[]{:S(2)}) copy-start(f32[1,4,16,256]{3,2,1,0:T(8,128)} %state.7) | copy-start | bytes 196612
  0.6 4.1 %copy-start.2 = (s32[768]{0:T(1024)S(1)}, s32[768]{0:T(1024)}, u32[]{:S(2)}) copy-start(s32[768]{0:T(1024)} %param.5) | copy-start | bytes 9220
  0.7 4.1 %copy-start.3 = (s32[768]{0:T(1024)S(1)}, s32[768]{0:T(1024)}, u32[]{:S(2)}) copy-start(s32[768]{0:T(1024)} %param.6) | copy-start | bytes 9220
  0.7 4.1 %copy-start.1 = (f32[3,768]{1,0:T(4,128)S(1)}, f32[3,768]{1,0:T(4,128)}, u32[]{:S(2)}) copy-start(f32[3,768]{1,0:T(4,128)} %area.1) | copy-start | bytes 27652
  0.7 8.0 %collective-permute-start.4 = (f32[1,4,16,256]{3,2,1,0:T(8,128)}, f32[1,4,16,256]{3,2,1,0:T(8,128)S(1)}, u32[]{:S(2)}, u32[]{:S(2)}) collective-permute-start(f32[1,4,16,256]{3,2,1,0:T(8,128)} %state.7), channel_id=1, source_target_pairs={{0,2},{1,3},{2,0},{3,1},{4,6},{5,7},{6,4},{7,5},{8,10},{9,11},{10,... | collective-permute-start | bytes 196616 | tf_op jit(solution)/shard_map/ppermute | solution.py:311
  5.2 5.2 %collective-permute-start = (f32[2,16,128]{2,1,0:T(8,128)S(1)}, f32[2,16,128]{2,1,0:T(8,128)S(1)}, u32[]{:S(2)}, u32[]{:S(2)}) collective-permute-start(f32[2,16,128]{2,1,0:T(8,128)S(1)} %get-tuple-element.16), channel_id=1, source_target_pairs={{0,24},{4,28},{8,16},{12,20},{16,8},{20,12},{24,0},{28,4},{1,25},{... | collective-permute-start | bytes 49160 | tf_op jit(solution)/shard_map/ppermute | solution.py:283
  6.7 3.8 %collective-permute-start.1 = (f32[2,16,128]{2,1,0:T(8,128)S(1)}, f32[2,16,128]{2,1,0:T(8,128)S(1)}, u32[]{:S(2)}, u32[]{:S(2)}) collective-permute-start(f32[2,16,128]{2,1,0:T(8,128)S(1)} %get-tuple-element.17), channel_id=1, source_target_pairs={{0,8},{4,12},{8,0},{12,4},{16,24},{20,28},{24,16},{28,20},{1,9},{5... | collective-permute-start | bytes 49160 | tf_op jit(solution)/shard_map/ppermute | solution.py:283
  7.2 3.7 %collective-permute-start.2 = (f32[2,16,128]{2,1,0:T(8,128)S(1)}, f32[2,16,128]{2,1,0:T(8,128)S(1)}, u32[]{:S(2)}, u32[]{:S(2)}) collective-permute-start(f32[2,16,128]{2,1,0:T(8,128)S(1)} %get-tuple-element.18), channel_id=1, source_target_pairs={{0,16},{4,20},{8,24},{12,28},{16,0},{20,4},{24,8},{28,12},{1,17},{... | collective-permute-start | bytes 49160 | tf_op jit(solution)/shard_map/ppermute | solution.py:283
  8.8 4.3 %collective-permute-start.5 = (f32[1,4,16,256]{3,2,1,0:T(8,128)S(1)}, f32[1,4,16,256]{3,2,1,0:T(8,128)S(1)}, u32[]{:S(2)}, u32[]{:S(2)}) collective-permute-start(f32[1,4,16,256]{3,2,1,0:T(8,128)S(1)} %pair_sums.1), channel_id=1, source_target_pairs={{0,1},{1,0},{2,3},{3,2},{4,5},{5,4},{6,7},{7,6},{8,9},{9,8},{10,11... | collective-permute-start | bytes 196616 | tf_op jit(solution)/shard_map/ppermute | solution.py:311
  10.9 1.2 %collective-permute-start.3 = (f32[1,16,128]{2,1,0:T(8,128)S(1)}, f32[1,16,128]{2,1,0:T(8,128)S(1)}, u32[]{:S(2)}, u32[]{:S(2)}) collective-permute-start(f32[1,16,128]{2,1,0:T(8,128)S(1)} %get-tuple-element.20), channel_id=1, source_target_pairs={{0,4},{4,0},{8,12},{12,8},{16,20},{20,16},{24,28},{28,24},{1,5},{5... | collective-permute-start | bytes 24584 | tf_op jit(solution)/shard_map/ppermute | solution.py:283

commit v23 on v21

--- a/solution.py
+++ b/solution.py
@@ -38,8 +38,9 @@
     return inverse, vr, vc, p
 
 
-def own_kernel(high, out):
-    out[...] = jnp.full(out.shape, lax.axis_index("space") * high, jnp.int32)
+def own_kernel(high, riding, out):
+    me = lax.axis_index("space")
+    out[...] = jnp.full(out.shape, (me - me % 2 if riding else me) * high, jnp.int32)
 
 
 def split(value, size):
@@ -62,9 +63,10 @@
                 value = jnp.take_along_axis(part, lane, axis=1, mode="promise_in_bounds")
                 place = (sublane + r * 8) * (around // LANES) + h
                 total += jnp.where(tile == place, value, 0.0)
-        picked.append(jnp.sum(total, axis=0, keepdims=True))
+        for turn in (4, 2, 1):
+            total += pltpu.roll(total, turn, 0)
+        picked.append(total)
     face_pressure = jnp.concatenate(picked, axis=1)
-    contribution = face_pressure * area[...]
     nodes = jnp.concatenate([node[c : c + 1, :] for c in range(chunks)], axis=1)
 
     high = node_block // LANES
@@ -75,7 +77,7 @@
     ).astype(jnp.float32).astype(jnp.bfloat16)
 
     row = lax.broadcasted_iota(jnp.int32, (8, faces), 0)
-    x, y, z = (jnp.broadcast_to(contribution[k : k + 1], (8, faces)) for k in range(3))
+    x, y, z = (face_pressure * jnp.broadcast_to(area[k : k + 1, :], (8, faces)) for k in range(3))
     groups = []
     for pattern in (jnp.where(row < high, x, y), jnp.where(row < high, z, 0.0)):
         first = pattern.astype(jnp.bfloat16).astype(jnp.float32)
@@ -94,15 +96,15 @@
         rows = count * ROWS
         return (product[:rows] + product[rows:]).reshape(count, ROWS, LANES)
 
-    ordered = [outs[0], outs[2], outs[3], outs[1]] if len(outs) == 4 else outs
     size = outs[0].shape[0]
-    blocks = size * len(outs)
-    if blocks <= 16:
-        result = dense(0, blocks)
-        for i, out in enumerate(ordered):
-            out[...] = result[i * size : (i + 1) * size]
+    core = lax.axis_index("space") % 2
+    if len(outs) == 4:
+        mine, east, north, diagonal = dense(0, 4 * size).reshape(4, size, ROWS, LANES)
+        others = (jnp.where(core == 0, east, north), jnp.where(core == 0, north, east))
+        for out, part in zip(outs, (mine, diagonal, *others)):
+            out[...] = part
     else:
-        for i, out in enumerate(ordered):
+        for i, out in enumerate(outs):
 
             @pl.loop(0, size // 8)
             def _(g):
@@ -120,19 +122,35 @@
                 place = (i * 4 + c) * radial + r * 8
                 columns = jnp.where(lane == sublane + place, value, columns)
     edge = jnp.sum(columns, axis=0, keepdims=True)
+    row = lax.broadcasted_iota(jnp.int32, (2, LANES), 0)
+    pair = jnp.where(row == core, edge, 0.0) if len(outs) == 4 else jnp.where(row == 0, edge, 0.0)
     for out in outs:
-        out[0, EDGE : EDGE + 1, :] = edge
-
-
-def halving_kernel(arrived, riding, *refs):
-    outs = refs[arrived:]
+        out[0, EDGE : EDGE + 2, :] = pair
+
+
+def chip_kernel(kept, came, _, out):
+    out[...] = kept[...] + came[...]
+
+
+def plane_kernel(mine, diagonal, served, kept, sent):
+    core = lax.axis_index("space") % 2
+    first, second = (mine[b] + diagonal[b] + served[b] for b in range(2))
+    kept[0] = jnp.where(core == 0, first, second)
+    sent[0] = jnp.where(core == 0, second, first)
+    rows = [
+        jnp.where(core == 0, ref[0, EDGE : EDGE + 1, :], ref[0, EDGE + 1 : EDGE + 2, :])
+        for ref in (mine, diagonal)
+    ] + [served[0, EDGE : EDGE + 1, :], served[0, EDGE + 1 : EDGE + 2, :]]
+    for out in (kept, sent):
+        for i, edge in enumerate(rows):
+            out[0, EDGE + i : EDGE + i + 1, :] = edge
+
+
+def halving_kernel(kept, came, *outs):
     size = outs[0].shape[0]
     for i, out in enumerate(outs):
         for b in range(size):
-            out[b] = functools.reduce(jnp.add, [ref[i * size + b] for ref in refs[:arrived]])
-        if riding:
-            for j, ref in enumerate(refs[:arrived]):
-                out[0, EDGE + j : EDGE + j + 1, :] = ref[0, EDGE : EDGE + 1, :]
+            out[b] = kept[i * size + b] + came[i * size + b]
 
 
 def weight_from(weights, instances, source, target):
@@ -201,16 +219,20 @@
     radial, around = state.shape[2:]
     if blocks == RIDING:
         me = lax.axis_index("space")
+        core = me % 2
         known = [kept[0, EDGE:, :], came[0, EDGE:, :]]
+        known = [
+            jnp.where(core == 0, known[0], known[1]),
+            jnp.where(core == 0, known[1], known[0]),
+        ]
         known = jnp.concatenate(known, axis=0)
         row = lax.broadcasted_iota(jnp.int32, known.shape, 0)
 
         def edge_of(device):
-            relative = device ^ me
-            half = RIDING // 2
-            chip = relative // 2
-            place = jnp.where(chip == 3, 1, jnp.where(chip == 0, 0, chip + 1))
-            place += (relative % 2) * half
+            chip, of_core = (device ^ (me - core)) // 2, device % 2
+            place = jnp.where(chip == 1, 6 + of_core, 2 + of_core)
+            place = jnp.where(chip == 0, 4 * of_core, place)
+            place = jnp.where(chip == 3, 1 + 4 * of_core, place)
             return jnp.sum(jnp.where(row == place, known, 0.0), axis=0, keepdims=True)
 
         before = edge_of((me + blocks - 1) % blocks)
@@ -278,9 +300,9 @@
         count = lax.axis_size(axis)
         return lax.ppermute(value, axis, [(i, (i + s) % count) for i in range(count)])
 
-    def exchanged(sent, size):
-        places = (3, 1, 2) if len(sent) == 3 else (1,)
-        return [swapped(value, "space", place * size) for place, value in zip(places, sent)]
+    def served(value):
+        pairs = [(i, i ^ (2 if i % 2 else 4)) for i in range(blocks)]
+        return lax.ppermute(value, "space", pairs)
 
     def call(kernel, name, shapes, *operands, flops=0, dtype=jnp.float32):
         return pl.pallas_call(
@@ -306,19 +328,18 @@
     partner = partnered(state, 0)
 
     riding = blocks == RIDING
-    steps = [4, 2] if riding else [2] * (blocks.bit_length() - 1)
-    size = blocks // steps[0]
+    parts = 4 if riding else 2
     (own,) = call(
-        functools.partial(own_kernel, node_block // LANES),
+        functools.partial(own_kernel, node_block // LANES, riding),
         "own",
         [(8, LANES)],
         dtype=jnp.int32,
         flops=PLACING,
     )
-    kept, *sent = call(
+    dense = call(
         functools.partial(forces_kernel, node_block),
         "face_forces",
-        [(size, ROWS, LANES)] * steps[0],
+        [(blocks // parts, ROWS, LANES)] * parts,
         own,
         state,
         face_cell.reshape(chunks, LANES),
@@ -327,12 +348,40 @@
         flops=PLACING,
     )
 
+    base, step = call(
+        functools.partial(flux_kernel, weights[0], instances),
+        "flux",
+        [state.shape, (radial, around)],
+        state,
+        flops=PLACING,
+    )
     edges = []
-    if not riding:
-        row = jnp.broadcast_to(kept[0, EDGE : EDGE + 1, :], (8, LANES))
+    if riding:
+        mine, across, other, kept = dense
+        other = swapped(other, "space", 1)
+        across = swapped(across, "space", 6)
+        (kept,) = call(chip_kernel, "chip_sums", [kept.shape], kept, other, step, flops=PLACING)
+        kept, sent = call(
+            plane_kernel,
+            "plane_sums",
+            [(1, ROWS, LANES)] * 2,
+            mine,
+            across,
+            served(kept),
+            flops=PLACING,
+        )
+        came = swapped(sent, "space", 1)
+    else:
+        row = jnp.broadcast_to(dense[0][0, EDGE : EDGE + 1, :], (8, LANES))
         edges = [shifted(row, "space", 1), shifted(row, "space", blocks - 1)]
-
-    came = exchanged(sent, size)
+        size = blocks // 2
+        kept, came = dense[0], swapped(dense[1], "space", size)
+        while size > 1:
+            size //= 2
+            shapes = [(size, ROWS, LANES)] * 2
+            kept, sent = call(halving_kernel, "halving", shapes, kept, came)
+            came = swapped(sent, "space", size)
+
     sums = call(
         functools.partial(pair_kernel, weights, instances, orders),
         "pair_sums",
@@ -343,24 +392,6 @@
     )
     sums = [partnered(value, i) for i, value in enumerate(sums, 1)]
 
-    for step in steps[1:]:
-        size //= step
-        kept, *sent = call(
-            functools.partial(halving_kernel, 1 + len(came), riding),
-            "halving",
-            [(size, ROWS, LANES)] * step,
-            kept,
-            *came,
-            flops=PLACING,
-        )
-        came = exchanged(sent, size)
-
-    base, step = call(
-        functools.partial(flux_kernel, weights[0], instances),
-        "flux",
-        [state.shape, (radial, around)],
-        state,
-    )
     residual, total = call(
         functools.partial(outer_kernel, weights, instances, orders, blocks),
         "outer",
@@ -368,7 +399,7 @@
         state,
         base,
         kept,
-        *came,
+        came,
         partner,
         *edges,
     )

time: 13.9 us -> 13.8 us (level)
  starting transfers between devices: 9.37 us -> 8.91 us
  waiting for transfers between devices: 2.26 us -> 2.59 us
    ppermute x4 -> x3, starting transfers between devices: 3.62 us -> 1.64 us  [swapped(): lax.ppermute(value, axis, [(i, i ^ bit) for i in range(lax.axis_size(axis...]
    ppermute x0 -> x1, starting transfers between devices: none -> 1.59 us  [served(): return lax.ppermute(value, 'space', pairs)]
    ppermute x0 -> x1, waiting for transfers between devices: none -> 0.53 us  [served(): return lax.ppermute(value, 'space', pairs)]
    ppermute x4 -> x3, waiting for transfers between devices: 1.49 us -> 1.16 us  [swapped(): lax.ppermute(value, axis, [(i, i ^ bit) for i in range(lax.axis_size(axis...]
    pallas_call x7 -> x8, Pallas kernels: 1.39 us -> 1.37 us  [call(): pl.pallas_call(kernel, out_shape=[jax.ShapeDtypeStruct(shape, dtype) for...]
  transfers between devices with their start and end apart: 6 -> 6, of which waited for: 3 -> 4; matrix products, arithmetic and copies ran while one was open for 0% -> 0% of each run, Pallas kernels for 5% -> 5%
where the time goes in v23:
time: 13.8 us; the launch traced here: 13.6 us
  starting transfers between devices  8.91 us (65%)
  waiting for transfers between devices  2.59 us (19%)
  Pallas kernels  1.37 us (10%)
  between operations  0.74 us (5%)
    ppermute x2, starting transfers between devices, partnered(): return lax.ppermute(value, ('space', 'inst'), pairs)  5.68 us
    ppermute x3, starting transfers between devices, swapped(): lax.ppermute(value, axis, [(i, i ^ bit) for i in range(lax.axis_size(axis...  1.64 us
    ppermute x1, starting transfers between devices, served(): return lax.ppermute(value, 'space', pairs)  1.59 us
    pallas_call x8, Pallas kernels, call(): pl.pallas_call(kernel, out_shape=[jax.ShapeDtypeStruct(shape, dtype) for...  1.37 us
    ppermute x3, waiting for transfers between devices, swapped(): lax.ppermute(value, axis, [(i, i ^ bit) for i in range(lax.axis_size(axis...  1.16 us
    ppermute x2, waiting for transfers between devices, partnered(): return lax.ppermute(value, ('space', 'inst'), pairs)  0.9 us
    ppermute x1, waiting for transfers between devices, served(): return lax.ppermute(value, 'space', pairs)  0.53 us
  transfers between devices with their start and end apart: 6, of which 4 were waited for; matrix products, arithmetic and copies ran while one was open for 0% of the time, Pallas kernels for 5%

profile of v23, /device:TPU:0, one launch (start us, length us, event | category | flops | bytes accessed | tf_op | source)
XLA Modules:
  0.0 13.6 jit_solution(18389697920697697004)
XLA Ops:
  0.6 0.0 copy-start
  0.6 0.0 copy-start.2
  0.7 0.0 copy-start.3
  0.7 0.0 copy-start.1
  0.7 4.1 %collective-permute-start.4 = (f32[1,4,16,256]{3,2,1,0:T(8,128)}, f32[1,4,16,256]{3,2,1,0:T(8,128)S(1)}, u32[]{:S(2)}, u32[]{:S(2)}) collective-permute-start(f32[1,4,16,256]{3,2,1,0:T(8,128)} %state.7), channel_id=1, source_target_pairs={{0,2},{1,3},{2,0},{3,1},{4,6},{5,7},{6,4},{7,5},{8,10},{9,11},{10,... | collective-permute-start | bytes 196616 | tf_op jit(solution)/shard_map/ppermute | solution.py:325
  4.8 0.0 copy-done
  4.8 0.0 copy-done.2
  4.8 0.0 copy-done.3
  4.8 0.0 copy-done.1
  4.8 0.4 %face_forces.1 = (f32[2,16,128]{2,1,0:T(8,128)S(1)}, f32[2,16,128]{2,1,0:T(8,128)S(1)}, f32[2,16,128]{2,1,0:T(8,128)S(1)}, f32[2,16,128]{2,1,0:T(8,128)S(1)}) custom-call(s32[8,128]{1,0:T(8,128)S(1)} %own.1, f32[1,4,16,256]{3,2,1,0:T(8,128)S(1)} %copy-done, s32[6,128]{1,0:T(8,128)S(1)} %bitcast.3, s32[6,128]{1,0:T(8,128)S(1)} %bitcast.4, f32[3,768]{1,0:T(4,128)S(1)} %copy-done.1), custom_call_target="tpu_custom_call" | custom-call | flops 10000000000 | tf_op jit(solution)/shard_map/face_forces/pallas_call | solution.py:308
  5.2 0.1 collective-permute-start.1
  5.2 1.5 %collective-permute-start = (f32[2,16,128]{2,1,0:T(8,128)S(1)}, f32[2,16,128]{2,1,0:T(8,128)S(1)}, u32[]{:S(2)}, u32[]{:S(2)}) collective-permute-start(f32[2,16,128]{2,1,0:T(8,128)S(1)} %get-tuple-element.16), channel_id=1, source_target_pairs={{0,24},{4,28},{8,16},{12,20},{16,8},{20,12},{24,0},{28,4},{1,25},{... | collective-permute-start | bytes 49160 | tf_op jit(solution)/shard_map/ppermute | solution.py:297
  6.7 0.2 %flux.1 = (f32[1,4,16,256]{3,2,1,0:T(8,128)S(1)}, f32[16,256]{1,0:T(8,128)S(1)}) custom-call(f32[1,4,16,256]{3,2,1,0:T(8,128)S(1)} %copy-done), custom_call_target="tpu_custom_call" | custom-call | flops 10000000000 | tf_op jit(solution)/shard_map/flux/pallas_call | solution.py:308
  6.9 0.0 collective-permute-done.1.came
  7.0 1.6 %collective-permute-start.2 = (f32[2,16,128]{2,1,0:T(8,128)S(1)}, f32[2,16,128]{2,1,0:T(8,128)S(1)}, u32[]{:S(2)}, u32[]{:S(2)}) collective-permute-start(f32[2,16,128]{2,1,0:T(8,128)S(1)} %chip_sums.1), channel_id=1, source_target_pairs={{0,16},{4,12},{8,24},{12,4},{16,0},{20,28},{24,8},{28,20},{1,17},{... | collective-permute-start | bytes 49160 | tf_op jit(solution)/shard_map/ppermute | solution.py:305
  8.5 0.1 collective-permute-done.4.partner
  8.7 1.6 %collective-permute-start.5 = (f32[1,4,16,256]{3,2,1,0:T(8,128)S(1)}, f32[1,4,16,256]{3,2,1,0:T(8,128)S(1)}, u32[]{:S(2)}, u32[]{:S(2)}) collective-permute-start(f32[1,4,16,256]{3,2,1,0:T(8,128)S(1)} %pair_sums.1), channel_id=1, source_target_pairs={{0,1},{1,0},{2,3},{3,2},{4,5},{5,4},{6,7},{7,6},{8,9},{9,8},{10,11... | collective-permute-start | bytes 196616 | tf_op jit(solution)/shard_map/ppermute | solution.py:325
  10.2 0.0 collective-permute-done.diagonal
  10.2 0.5 %collective-permute-done.2.served = f32[2,16,128]{2,1,0:T(8,128)S(1)} collective-permute-done((f32[2,16,128]{2,1,0:T(8,128)S(1)}, f32[2,16,128]{2,1,0:T(8,128)S(1)}, u32[]{:S(2)}, u32[]{:S(2)}) %collective-permute-start.2) | collective-permute-done | bytes 16416 | tf_op jit(solution)/shard_map/ppermute | solution.py:305
  10.8 0.1 collective-permute-start.3
  10.9 1.2 %collective-permute-done.3.came = f32[1,16,128]{2,1,0:T(8,128)S(1)} collective-permute-done((f32[1,16,128]{2,1,0:T(8,128)S(1)}, f32[1,16,128]{2,1,0:T(8,128)S(1)}, u32[]{:S(2)}, u32[]{:S(2)}) %collective-permute-start.3) | collective-permute-done | bytes 8224 | tf_op jit(solution)/shard_map/ppermute | solution.py:297
  12.0 0.1 %outer.1 = (f32[1,4,16,256]{3,2,1,0:T(8,128)S(1)}, f32[16,128]{1,0:T(8,128)S(1)}) custom-call(f32[1,4,16,256]{3,2,1,0:T(8,128)S(1)} %copy-done, f32[1,4,16,256]{3,2,1,0:T(8,128)S(1)} %get-tuple-element.14.base, f32[1,16,128]{2,1,0:T(8,128)S(1)} %get-tuple-element.20.kept, f32[1,16,128]{2,1,0:T(8,128)S(1)} %collective-permute-done.3.came, ...), custom_call_target="tpu_custom_call" | custom-call | tf_op jit(solution)/shard_map/outer/pallas_call | solution.py:308
  12.2 0.8 %collective-permute-done.5.refs_0_ = f32[1,4,16,256]{3,2,1,0:T(8,128)S(1)} collective-permute-done((f32[1,4,16,256]{3,2,1,0:T(8,128)S(1)}, f32[1,4,16,256]{3,2,1,0:T(8,128)S(1)}, u32[]{:S(2)}, u32[]{:S(2)}) %collective-permute-start.5) | collective-permute-done | bytes 65568 | tf_op jit(solution)/shard_map/ppermute | solution.py:325
  13.0 0.6 %update.1 = (f32[1,4,16,256]{3,2,1,0:T(8,128)}, f32[3,1,512]{2,1,0:T(1,128)}) custom-call(f32[1,4,16,256]{3,2,1,0:T(8,128)S(1)} %get-tuple-element.22.residual, f32[16,256]{1,0:T(8,128)S(1)} %get-tuple-element.19._.step, f32[16,128]{1,0:T(8,128)S(1)} %get-tuple-element.23.total, f32[1,4,16,256]{3,2,1,0:T(8,128)S(1)} %collective-permute-done.5.refs_0_), custom_call_target="tpu_custom_call" | custom-call | tf_op jit(solution)/shard_map/update/pallas_call | solution.py:308
  (4 shorter events, 0.0 us)
Async XLA Ops:
  0.6 4.1 %copy-start = (f32[1,4,16,256]{3,2,1,0:T(8,128)S(1)}, f32[1,4,16,256]{3,2,1,0:T(8,128)}, u32[]{:S(2)}) copy-start(f32[1,4,16,256]{3,2,1,0:T(8,128)} %state.7) | copy-start | bytes 196612
  0.6 4.1 %copy-start.2 = (s32[768]{0:T(1024)S(1)}, s32[768]{0:T(1024)}, u32[]{:S(2)}) copy-start(s32[768]{0:T(1024)} %param.5) | copy-start | bytes 9220
  0.7 4.1 %copy-start.3 = (s32[768]{0:T(1024)S(1)}, s32[768]{0:T(1024)}, u32[]{:S(2)}) copy-start(s32[768]{0:T(1024)} %param.6) | copy-start | bytes 9220
  0.7 4.1 %copy-start.1 = (f32[3,768]{1,0:T(4,128)S(1)}, f32[3,768]{1,0:T(4,128)}, u32[]{:S(2)}) copy-start(f32[3,768]{1,0:T(4,128)} %area.1) | copy-start | bytes 27652
  0.7 8.0 %collective-permute-start.4 = (f32[1,4,16,256]{3,2,1,0:T(8,128)}, f32[1,4,16,256]{3,2,1,0:T(8,128)S(1)}, u32[]{:S(2)}, u32[]{:S(2)}) collective-permute-start(f32[1,4,16,256]{3,2,1,0:T(8,128)} %state.7), channel_id=1, source_target_pairs={{0,2},{1,3},{2,0},{3,1},{4,6},{5,7},{6,4},{7,5},{8,10},{9,11},{10,... | collective-permute-start | bytes 196616 | tf_op jit(solution)/shard_map/ppermute | solution.py:325
  5.2 1.8 %collective-permute-start.1 = (f32[2,16,128]{2,1,0:T(8,128)S(1)}, f32[2,16,128]{2,1,0:T(8,128)S(1)}, u32[]{:S(2)}, u32[]{:S(2)}) collective-permute-start(f32[2,16,128]{2,1,0:T(8,128)S(1)} %get-tuple-element.18), channel_id=1, source_target_pairs={{0,4},{4,0},{8,12},{12,8},{16,20},{20,16},{24,28},{28,24},{1,5},{5... | collective-permute-start | bytes 49160 | tf_op jit(solution)/shard_map/ppermute | solution.py:297
  5.2 5.0 %collective-permute-start = (f32[2,16,128]{2,1,0:T(8,128)S(1)}, f32[2,16,128]{2,1,0:T(8,128)S(1)}, u32[]{:S(2)}, u32[]{:S(2)}) collective-permute-start(f32[2,16,128]{2,1,0:T(8,128)S(1)} %get-tuple-element.16), channel_id=1, source_target_pairs={{0,24},{4,28},{8,16},{12,20},{16,8},{20,12},{24,0},{28,4},{1,25},{... | collective-permute-start | bytes 49160 | tf_op jit(solution)/shard_map/ppermute | solution.py:297
  7.0 3.8 %collective-permute-start.2 = (f32[2,16,128]{2,1,0:T(8,128)S(1)}, f32[2,16,128]{2,1,0:T(8,128)S(1)}, u32[]{:S(2)}, u32[]{:S(2)}) collective-permute-start(f32[2,16,128]{2,1,0:T(8,128)S(1)} %chip_sums.1), channel_id=1, source_target_pairs={{0,16},{4,12},{8,24},{12,4},{16,0},{20,28},{24,8},{28,20},{1,17},{... | collective-permute-start | bytes 49160 | tf_op jit(solution)/shard_map/ppermute | solution.py:305
  8.7 4.3 %collective-permute-start.5 = (f32[1,4,16,256]{3,2,1,0:T(8,128)S(1)}, f32[1,4,16,256]{3,2,1,0:T(8,128)S(1)}, u32[]{:S(2)}, u32[]{:S(2)}) collective-permute-start(f32[1,4,16,256]{3,2,1,0:T(8,128)S(1)} %pair_sums.1), channel_id=1, source_target_pairs={{0,1},{1,0},{2,3},{3,2},{4,5},{5,4},{6,7},{7,6},{8,9},{9,8},{10,11... | collective-permute-start | bytes 196616 | tf_op jit(solution)/shard_map/ppermute | solution.py:325
  10.8 1.2 %collective-permute-start.3 = (f32[1,16,128]{2,1,0:T(8,128)S(1)}, f32[1,16,128]{2,1,0:T(8,128)S(1)}, u32[]{:S(2)}, u32[]{:S(2)}) collective-permute-start(f32[1,16,128]{2,1,0:T(8,128)S(1)} %get-tuple-element.21), channel_id=1, source_target_pairs={{0,4},{4,0},{8,12},{12,8},{16,20},{20,16},{24,28},{28,24},{1,5},{5... | collective-permute-start | bytes 24584 | tf_op jit(solution)/shard_map/ppermute | solution.py:297

commit v24 on v23

--- a/solution.py
+++ b/solution.py
@@ -162,8 +162,8 @@
 
 
 def of_chip(orders):
-    half = lax.axis_index("space") // 4
-    return [jnp.where(half % 2 == 0, a, b) for a, b in zip(*orders)]
+    chip = lax.axis_index("space") // 2
+    return [jnp.where(chip == 0, a, b) for a, b in zip(*orders)]
 
 
 def pair_kernel(weights, instances, orders, state, partner, *outs):
@@ -318,7 +318,7 @@
     weights = spectral_row(instances)
     def partnered(value, place):
         pairs = [
-            (i * instances + n, i * instances + (n ^ orders[i // 4 % 2][place]))
+            (i * instances + n, i * instances + (n ^ orders[min(i // 2, 1)][place]))
             for i in range(blocks)
             for n in range(instances)
         ]

time: 13.8 us -> 13.8 us (level)
  starting transfers between devices: 8.91 us -> 7.05 us
  waiting for transfers between devices: 2.59 us -> 4.45 us
    ppermute x1, starting transfers between devices: 1.59 us -> 0.57 us  [served(): return lax.ppermute(value, 'space', pairs)]
    ppermute x2, waiting for transfers between devices: 0.9 us -> 1.92 us  [partnered(): return lax.ppermute(value, ('space', 'inst'), pairs)]
    ppermute x2, starting transfers between devices: 5.68 us -> 4.84 us  [partnered(): return lax.ppermute(value, ('space', 'inst'), pairs)]
    ppermute x3, waiting for transfers between devices: 1.16 us -> 1.85 us  [swapped(): lax.ppermute(value, axis, [(i, i ^ bit) for i in range(lax.axis_size(axis...]
    ppermute x1, waiting for transfers between devices: 0.53 us -> 0.69 us  [served(): return lax.ppermute(value, 'space', pairs)]
  transfers between devices with their start and end apart: 6 -> 6, of which waited for: 4 -> 5; matrix products, arithmetic and copies ran while one was open for 0% -> 0% of each run, Pallas kernels for 5% -> 5%
where the time goes in v24:
time: 13.8 us; the launch traced here: 13.6 us
  starting transfers between devices  7.05 us (51%)
  waiting for transfers between devices  4.45 us (32%)
  Pallas kernels  1.37 us (10%)
  between operations  0.74 us (5%)
    ppermute x2, starting transfers between devices, partnered(): return lax.ppermute(value, ('space', 'inst'), pairs)  4.84 us
    ppermute x2, waiting for transfers between devices, partnered(): return lax.ppermute(value, ('space', 'inst'), pairs)  1.92 us
    ppermute x3, waiting for transfers between devices, swapped(): lax.ppermute(value, axis, [(i, i ^ bit) for i in range(lax.axis_size(axis...  1.85 us
    ppermute x3, starting transfers between devices, swapped(): lax.ppermute(value, axis, [(i, i ^ bit) for i in range(lax.axis_size(axis...  1.64 us
    pallas_call x8, Pallas kernels, call(): pl.pallas_call(kernel, out_shape=[jax.ShapeDtypeStruct(shape, dtype) for...  1.37 us
    ppermute x1, waiting for transfers between devices, served(): return lax.ppermute(value, 'space', pairs)  0.69 us
    ppermute x1, starting transfers between devices, served(): return lax.ppermute(value, 'space', pairs)  0.57 us
  transfers between devices with their start and end apart: 6, of which 5 were waited for; matrix products, arithmetic and copies ran while one was open for 0% of the time, Pallas kernels for 5%

profile of v24, /device:TPU:0, one launch (start us, length us, event | category | flops | bytes accessed | tf_op | source)
XLA Modules:
  0.0 13.6 jit_solution(17093948255047677926)
XLA Ops:
  0.6 0.0 copy-start
  0.6 0.0 copy-start.2
  0.7 0.0 copy-start.3
  0.7 0.0 copy-start.1
  0.7 4.1 %collective-permute-start.4 = (f32[1,4,16,256]{3,2,1,0:T(8,128)}, f32[1,4,16,256]{3,2,1,0:T(8,128)S(1)}, u32[]{:S(2)}, u32[]{:S(2)}) collective-permute-start(f32[1,4,16,256]{3,2,1,0:T(8,128)} %state.7), channel_id=1, source_target_pairs={{0,2},{1,3},{2,0},{3,1},{4,6},{5,7},{6,4},{7,5},{8,9},{9,8},{10,11... | collective-permute-start | bytes 196616 | tf_op jit(solution)/shard_map/ppermute | solution.py:325
  4.8 0.0 copy-done
  4.8 0.0 copy-done.2
  4.8 0.0 copy-done.3
  4.8 0.0 copy-done.1
  4.8 0.4 %face_forces.1 = (f32[2,16,128]{2,1,0:T(8,128)S(1)}, f32[2,16,128]{2,1,0:T(8,128)S(1)}, f32[2,16,128]{2,1,0:T(8,128)S(1)}, f32[2,16,128]{2,1,0:T(8,128)S(1)}) custom-call(s32[8,128]{1,0:T(8,128)S(1)} %own.1, f32[1,4,16,256]{3,2,1,0:T(8,128)S(1)} %copy-done, s32[6,128]{1,0:T(8,128)S(1)} %bitcast.3, s32[6,128]{1,0:T(8,128)S(1)} %bitcast.4, f32[3,768]{1,0:T(4,128)S(1)} %copy-done.1), custom_call_target="tpu_custom_call" | custom-call | flops 10000000000 | tf_op jit(solution)/shard_map/face_forces/pallas_call | solution.py:308
  5.2 0.1 collective-permute-start.1
  5.2 1.5 %collective-permute-start = (f32[2,16,128]{2,1,0:T(8,128)S(1)}, f32[2,16,128]{2,1,0:T(8,128)S(1)}, u32[]{:S(2)}, u32[]{:S(2)}) collective-permute-start(f32[2,16,128]{2,1,0:T(8,128)S(1)} %get-tuple-element.16), channel_id=1, source_target_pairs={{0,24},{4,28},{8,16},{12,20},{16,8},{20,12},{24,0},{28,4},{1,25},{... | collective-permute-start | bytes 49160 | tf_op jit(solution)/shard_map/ppermute | solution.py:297
  6.7 0.2 %flux.1 = (f32[1,4,16,256]{3,2,1,0:T(8,128)S(1)}, f32[16,256]{1,0:T(8,128)S(1)}) custom-call(f32[1,4,16,256]{3,2,1,0:T(8,128)S(1)} %copy-done), custom_call_target="tpu_custom_call" | custom-call | flops 10000000000 | tf_op jit(solution)/shard_map/flux/pallas_call | solution.py:308
  6.9 0.0 collective-permute-done.1.came
  7.0 0.6 %collective-permute-start.2 = (f32[2,16,128]{2,1,0:T(8,128)S(1)}, f32[2,16,128]{2,1,0:T(8,128)S(1)}, u32[]{:S(2)}, u32[]{:S(2)}) collective-permute-start(f32[2,16,128]{2,1,0:T(8,128)S(1)} %chip_sums.1), channel_id=1, source_target_pairs={{0,16},{4,12},{8,24},{12,4},{16,0},{20,28},{24,8},{28,20},{1,17},{... | collective-permute-start | bytes 49160 | tf_op jit(solution)/shard_map/ppermute | solution.py:305
  7.5 1.1 %collective-permute-done.4.partner = f32[1,4,16,256]{3,2,1,0:T(8,128)S(1)} collective-permute-done((f32[1,4,16,256]{3,2,1,0:T(8,128)}, f32[1,4,16,256]{3,2,1,0:T(8,128)S(1)}, u32[]{:S(2)}, u32[]{:S(2)}) %collective-permute-start.4) | collective-permute-done | bytes 65568 | tf_op jit(solution)/shard_map/ppermute | solution.py:325
  8.7 0.7 %collective-permute-start.5 = (f32[1,4,16,256]{3,2,1,0:T(8,128)S(1)}, f32[1,4,16,256]{3,2,1,0:T(8,128)S(1)}, u32[]{:S(2)}, u32[]{:S(2)}) collective-permute-start(f32[1,4,16,256]{3,2,1,0:T(8,128)S(1)} %pair_sums.1), channel_id=1, source_target_pairs={{0,1},{1,0},{2,3},{3,2},{4,5},{5,4},{6,7},{7,6},{8,10},{9,11},{10,... | collective-permute-start | bytes 196616 | tf_op jit(solution)/shard_map/ppermute | solution.py:325
  9.4 0.7 %collective-permute-done.diagonal = f32[2,16,128]{2,1,0:T(8,128)S(1)} collective-permute-done((f32[2,16,128]{2,1,0:T(8,128)S(1)}, f32[2,16,128]{2,1,0:T(8,128)S(1)}, u32[]{:S(2)}, u32[]{:S(2)}) %collective-permute-start) | collective-permute-done | bytes 16416 | tf_op jit(solution)/shard_map/ppermute | solution.py:297
  10.1 0.7 %collective-permute-done.2.served = f32[2,16,128]{2,1,0:T(8,128)S(1)} collective-permute-done((f32[2,16,128]{2,1,0:T(8,128)S(1)}, f32[2,16,128]{2,1,0:T(8,128)S(1)}, u32[]{:S(2)}, u32[]{:S(2)}) %collective-permute-start.2) | collective-permute-done | bytes 16416 | tf_op jit(solution)/shard_map/ppermute | solution.py:305
  10.8 0.1 collective-permute-start.3
  10.9 1.2 %collective-permute-done.3.came = f32[1,16,128]{2,1,0:T(8,128)S(1)} collective-permute-done((f32[1,16,128]{2,1,0:T(8,128)S(1)}, f32[1,16,128]{2,1,0:T(8,128)S(1)}, u32[]{:S(2)}, u32[]{:S(2)}) %collective-permute-start.3) | collective-permute-done | bytes 8224 | tf_op jit(solution)/shard_map/ppermute | solution.py:297
  12.0 0.1 %outer.1 = (f32[1,4,16,256]{3,2,1,0:T(8,128)S(1)}, f32[16,128]{1,0:T(8,128)S(1)}) custom-call(f32[1,4,16,256]{3,2,1,0:T(8,128)S(1)} %copy-done, f32[1,4,16,256]{3,2,1,0:T(8,128)S(1)} %get-tuple-element.14.base, f32[1,16,128]{2,1,0:T(8,128)S(1)} %get-tuple-element.20.kept, f32[1,16,128]{2,1,0:T(8,128)S(1)} %collective-permute-done.3.came, ...), custom_call_target="tpu_custom_call" | custom-call | tf_op jit(solution)/shard_map/outer/pallas_call | solution.py:308
  12.2 0.8 %collective-permute-done.5.refs_0_ = f32[1,4,16,256]{3,2,1,0:T(8,128)S(1)} collective-permute-done((f32[1,4,16,256]{3,2,1,0:T(8,128)S(1)}, f32[1,4,16,256]{3,2,1,0:T(8,128)S(1)}, u32[]{:S(2)}, u32[]{:S(2)}) %collective-permute-start.5) | collective-permute-done | bytes 65568 | tf_op jit(solution)/shard_map/ppermute | solution.py:325
  13.0 0.6 %update.1 = (f32[1,4,16,256]{3,2,1,0:T(8,128)}, f32[3,1,512]{2,1,0:T(1,128)}) custom-call(f32[1,4,16,256]{3,2,1,0:T(8,128)S(1)} %get-tuple-element.22.residual, f32[16,256]{1,0:T(8,128)S(1)} %get-tuple-element.19._.step, f32[16,128]{1,0:T(8,128)S(1)} %get-tuple-element.23.total, f32[1,4,16,256]{3,2,1,0:T(8,128)S(1)} %collective-permute-done.5.refs_0_), custom_call_target="tpu_custom_call" | custom-call | tf_op jit(solution)/shard_map/update/pallas_call | solution.py:308
  (4 shorter events, 0.0 us)
Async XLA Ops:
  0.6 4.1 %copy-start = (f32[1,4,16,256]{3,2,1,0:T(8,128)S(1)}, f32[1,4,16,256]{3,2,1,0:T(8,128)}, u32[]{:S(2)}) copy-start(f32[1,4,16,256]{3,2,1,0:T(8,128)} %state.7) | copy-start | bytes 196612
  0.6 4.1 %copy-start.2 = (s32[768]{0:T(1024)S(1)}, s32[768]{0:T(1024)}, u32[]{:S(2)}) copy-start(s32[768]{0:T(1024)} %param.5) | copy-start | bytes 9220
  0.7 4.1 %copy-start.3 = (s32[768]{0:T(1024)S(1)}, s32[768]{0:T(1024)}, u32[]{:S(2)}) copy-start(s32[768]{0:T(1024)} %param.6) | copy-start | bytes 9220
  0.7 4.1 %copy-start.1 = (f32[3,768]{1,0:T(4,128)S(1)}, f32[3,768]{1,0:T(4,128)}, u32[]{:S(2)}) copy-start(f32[3,768]{1,0:T(4,128)} %area.1) | copy-start | bytes 27652
  0.7 8.0 %collective-permute-start.4 = (f32[1,4,16,256]{3,2,1,0:T(8,128)}, f32[1,4,16,256]{3,2,1,0:T(8,128)S(1)}, u32[]{:S(2)}, u32[]{:S(2)}) collective-permute-start(f32[1,4,16,256]{3,2,1,0:T(8,128)} %state.7), channel_id=1, source_target_pairs={{0,2},{1,3},{2,0},{3,1},{4,6},{5,7},{6,4},{7,5},{8,9},{9,8},{10,11... | collective-permute-start | bytes 196616 | tf_op jit(solution)/shard_map/ppermute | solution.py:325
  5.2 1.8 %collective-permute-start.1 = (f32[2,16,128]{2,1,0:T(8,128)S(1)}, f32[2,16,128]{2,1,0:T(8,128)S(1)}, u32[]{:S(2)}, u32[]{:S(2)}) collective-permute-start(f32[2,16,128]{2,1,0:T(8,128)S(1)} %get-tuple-element.18), channel_id=1, source_target_pairs={{0,4},{4,0},{8,12},{12,8},{16,20},{20,16},{24,28},{28,24},{1,5},{5... | collective-permute-start | bytes 49160 | tf_op jit(solution)/shard_map/ppermute | solution.py:297
  5.2 4.8 %collective-permute-start = (f32[2,16,128]{2,1,0:T(8,128)S(1)}, f32[2,16,128]{2,1,0:T(8,128)S(1)}, u32[]{:S(2)}, u32[]{:S(2)}) collective-permute-start(f32[2,16,128]{2,1,0:T(8,128)S(1)} %get-tuple-element.16), channel_id=1, source_target_pairs={{0,24},{4,28},{8,16},{12,20},{16,8},{20,12},{24,0},{28,4},{1,25},{... | collective-permute-start | bytes 49160 | tf_op jit(solution)/shard_map/ppermute | solution.py:297
  7.0 3.8 %collective-permute-start.2 = (f32[2,16,128]{2,1,0:T(8,128)S(1)}, f32[2,16,128]{2,1,0:T(8,128)S(1)}, u32[]{:S(2)}, u32[]{:S(2)}) collective-permute-start(f32[2,16,128]{2,1,0:T(8,128)S(1)} %chip_sums.1), channel_id=1, source_target_pairs={{0,16},{4,12},{8,24},{12,4},{16,0},{20,28},{24,8},{28,20},{1,17},{... | collective-permute-start | bytes 49160 | tf_op jit(solution)/shard_map/ppermute | solution.py:305
  8.7 4.3 %collective-permute-start.5 = (f32[1,4,16,256]{3,2,1,0:T(8,128)S(1)}, f32[1,4,16,256]{3,2,1,0:T(8,128)S(1)}, u32[]{:S(2)}, u32[]{:S(2)}) collective-permute-start(f32[1,4,16,256]{3,2,1,0:T(8,128)S(1)} %pair_sums.1), channel_id=1, source_target_pairs={{0,1},{1,0},{2,3},{3,2},{4,5},{5,4},{6,7},{7,6},{8,10},{9,11},{10,... | collective-permute-start | bytes 196616 | tf_op jit(solution)/shard_map/ppermute | solution.py:325
  10.8 1.2 %collective-permute-start.3 = (f32[1,16,128]{2,1,0:T(8,128)S(1)}, f32[1,16,128]{2,1,0:T(8,128)S(1)}, u32[]{:S(2)}, u32[]{:S(2)}) collective-permute-start(f32[1,16,128]{2,1,0:T(8,128)S(1)} %get-tuple-element.21), channel_id=1, source_target_pairs={{0,4},{4,0},{8,12},{12,8},{16,20},{20,16},{24,28},{28,24},{1,5},{5... | collective-permute-start | bytes 24584 | tf_op jit(solution)/shard_map/ppermute | solution.py:297

commit v25 on v23

--- a/solution.py
+++ b/solution.py
@@ -100,7 +100,7 @@
     core = lax.axis_index("space") % 2
     if len(outs) == 4:
         mine, east, north, diagonal = dense(0, 4 * size).reshape(4, size, ROWS, LANES)
-        others = (jnp.where(core == 0, east, north), jnp.where(core == 0, north, east))
+        others = (jnp.where(core == 0, north, east), jnp.where(core == 0, east, north))
         for out, part in zip(outs, (mine, diagonal, *others)):
             out[...] = part
     else:
@@ -230,7 +230,7 @@
 
         def edge_of(device):
             chip, of_core = (device ^ (me - core)) // 2, device % 2
-            place = jnp.where(chip == 1, 6 + of_core, 2 + of_core)
+            place = jnp.where(chip == 1, 2 + of_core, 6 + of_core)
             place = jnp.where(chip == 0, 4 * of_core, place)
             place = jnp.where(chip == 3, 1 + 4 * of_core, place)
             return jnp.sum(jnp.where(row == place, known, 0.0), axis=0, keepdims=True)
@@ -301,7 +301,7 @@
         return lax.ppermute(value, axis, [(i, (i + s) % count) for i in range(count)])
 
     def served(value):
-        pairs = [(i, i ^ (2 if i % 2 else 4)) for i in range(blocks)]
+        pairs = [(i, i ^ (4 if i % 2 else 2)) for i in range(blocks)]
         return lax.ppermute(value, "space", pairs)
 
     def call(kernel, name, shapes, *operands, flops=0, dtype=jnp.float32):

time: 13.8 us -> 13.8 us (level)
  starting transfers between devices: 8.91 us -> 7.64 us
  waiting for transfers between devices: 2.59 us -> 3.86 us
    ppermute x2, starting transfers between devices: 5.68 us -> 5.04 us  [partnered(): return lax.ppermute(value, ('space', 'inst'), pairs)]
    ppermute x2, waiting for transfers between devices: 0.9 us -> 1.53 us  [partnered(): return lax.ppermute(value, ('space', 'inst'), pairs)]
    ppermute x1, starting transfers between devices: 1.59 us -> 0.95 us  [served(): return lax.ppermute(value, 'space', pairs)]
    ppermute x3, waiting for transfers between devices: 1.16 us -> 1.52 us  [swapped(): lax.ppermute(value, axis, [(i, i ^ bit) for i in range(lax.axis_size(axis...]
    ppermute x1, waiting for transfers between devices: 0.53 us -> 0.8 us  [served(): return lax.ppermute(value, 'space', pairs)]
  transfers between devices with their start and end apart: 6 -> 6, of which waited for: 4 -> 5; matrix products, arithmetic and copies ran while one was open for 0% -> 0% of each run, Pallas kernels for 5% -> 5%
where the time goes in v25:
time: 13.8 us; the launch traced here: 13.6 us
  starting transfers between devices  7.64 us (55%)
  waiting for transfers between devices  3.86 us (28%)
  Pallas kernels  1.37 us (10%)
  between operations  0.74 us (5%)
    ppermute x2, starting transfers between devices, partnered(): return lax.ppermute(value, ('space', 'inst'), pairs)  5.04 us
    ppermute x3, starting transfers between devices, swapped(): lax.ppermute(value, axis, [(i, i ^ bit) for i in range(lax.axis_size(axis...  1.64 us
    ppermute x2, waiting for transfers between devices, partnered(): return lax.ppermute(value, ('space', 'inst'), pairs)  1.53 us
    ppermute x3, waiting for transfers between devices, swapped(): lax.ppermute(value, axis, [(i, i ^ bit) for i in range(lax.axis_size(axis...  1.52 us
    pallas_call x8, Pallas kernels, call(): pl.pallas_call(kernel, out_shape=[jax.ShapeDtypeStruct(shape, dtype) for...  1.37 us
    ppermute x1, starting transfers between devices, served(): return lax.ppermute(value, 'space', pairs)  0.95 us
    ppermute x1, waiting for transfers between devices, served(): return lax.ppermute(value, 'space', pairs)  0.8 us
  transfers between devices with their start and end apart: 6, of which 5 were waited for; matrix products, arithmetic and copies ran while one was open for 0% of the time, Pallas kernels for 5%

profile of v25, /device:TPU:0, one launch (start us, length us, event | category | flops | bytes accessed | tf_op | source)
XLA Modules:
  0.0 13.6 jit_solution(12957365376218080163)
XLA Ops:
  0.6 0.0 copy-start
  0.6 0.0 copy-start.2
  0.7 0.0 copy-start.3
  0.7 0.0 copy-start.1
  0.7 4.1 %collective-permute-start.4 = (f32[1,4,16,256]{3,2,1,0:T(8,128)}, f32[1,4,16,256]{3,2,1,0:T(8,128)S(1)}, u32[]{:S(2)}, u32[]{:S(2)}) collective-permute-start(f32[1,4,16,256]{3,2,1,0:T(8,128)} %state.7), channel_id=1, source_target_pairs={{0,2},{1,3},{2,0},{3,1},{4,6},{5,7},{6,4},{7,5},{8,10},{9,11},{10,... | collective-permute-start | bytes 196616 | tf_op jit(solution)/shard_map/ppermute | solution.py:325
  4.8 0.0 copy-done
  4.8 0.0 copy-done.2
  4.8 0.0 copy-done.3
  4.8 0.0 copy-done.1
  4.8 0.4 %face_forces.1 = (f32[2,16,128]{2,1,0:T(8,128)S(1)}, f32[2,16,128]{2,1,0:T(8,128)S(1)}, f32[2,16,128]{2,1,0:T(8,128)S(1)}, f32[2,16,128]{2,1,0:T(8,128)S(1)}) custom-call(s32[8,128]{1,0:T(8,128)S(1)} %own.1, f32[1,4,16,256]{3,2,1,0:T(8,128)S(1)} %copy-done, s32[6,128]{1,0:T(8,128)S(1)} %bitcast.3, s32[6,128]{1,0:T(8,128)S(1)} %bitcast.4, f32[3,768]{1,0:T(4,128)S(1)} %copy-done.1), custom_call_target="tpu_custom_call" | custom-call | flops 10000000000 | tf_op jit(solution)/shard_map/face_forces/pallas_call | solution.py:308
  5.2 0.1 collective-permute-start.1
  5.2 1.5 %collective-permute-start = (f32[2,16,128]{2,1,0:T(8,128)S(1)}, f32[2,16,128]{2,1,0:T(8,128)S(1)}, u32[]{:S(2)}, u32[]{:S(2)}) collective-permute-start(f32[2,16,128]{2,1,0:T(8,128)S(1)} %get-tuple-element.16), channel_id=1, source_target_pairs={{0,24},{4,28},{8,16},{12,20},{16,8},{20,12},{24,0},{28,4},{1,25},{... | collective-permute-start | bytes 49160 | tf_op jit(solution)/shard_map/ppermute | solution.py:297
  6.7 0.2 %flux.1 = (f32[1,4,16,256]{3,2,1,0:T(8,128)S(1)}, f32[16,256]{1,0:T(8,128)S(1)}) custom-call(f32[1,4,16,256]{3,2,1,0:T(8,128)S(1)} %copy-done), custom_call_target="tpu_custom_call" | custom-call | flops 10000000000 | tf_op jit(solution)/shard_map/flux/pallas_call | solution.py:308
  6.9 0.0 collective-permute-done.1.came
  7.0 1.0 %collective-permute-start.2 = (f32[2,16,128]{2,1,0:T(8,128)S(1)}, f32[2,16,128]{2,1,0:T(8,128)S(1)}, u32[]{:S(2)}, u32[]{:S(2)}) collective-permute-start(f32[2,16,128]{2,1,0:T(8,128)S(1)} %chip_sums.1), channel_id=1, source_target_pairs={{0,8},{4,20},{8,0},{12,28},{16,24},{20,4},{24,16},{28,12},{1,9},{5... | collective-permute-start | bytes 49160 | tf_op jit(solution)/shard_map/ppermute | solution.py:305
  7.9 0.7 %collective-permute-done.4.partner = f32[1,4,16,256]{3,2,1,0:T(8,128)S(1)} collective-permute-done((f32[1,4,16,256]{3,2,1,0:T(8,128)}, f32[1,4,16,256]{3,2,1,0:T(8,128)S(1)}, u32[]{:S(2)}, u32[]{:S(2)}) %collective-permute-start.4) | collective-permute-done | bytes 65568 | tf_op jit(solution)/shard_map/ppermute | solution.py:325
  8.7 0.9 %collective-permute-start.5 = (f32[1,4,16,256]{3,2,1,0:T(8,128)S(1)}, f32[1,4,16,256]{3,2,1,0:T(8,128)S(1)}, u32[]{:S(2)}, u32[]{:S(2)}) collective-permute-start(f32[1,4,16,256]{3,2,1,0:T(8,128)S(1)} %pair_sums.1), channel_id=1, source_target_pairs={{0,1},{1,0},{2,3},{3,2},{4,5},{5,4},{6,7},{7,6},{8,9},{9,8},{10,11... | collective-permute-start | bytes 196616 | tf_op jit(solution)/shard_map/ppermute | solution.py:325
  9.6 0.4 %collective-permute-done.diagonal = f32[2,16,128]{2,1,0:T(8,128)S(1)} collective-permute-done((f32[2,16,128]{2,1,0:T(8,128)S(1)}, f32[2,16,128]{2,1,0:T(8,128)S(1)}, u32[]{:S(2)}, u32[]{:S(2)}) %collective-permute-start) | collective-permute-done | bytes 16416 | tf_op jit(solution)/shard_map/ppermute | solution.py:297
  10.0 0.8 %collective-permute-done.2.served = f32[2,16,128]{2,1,0:T(8,128)S(1)} collective-permute-done((f32[2,16,128]{2,1,0:T(8,128)S(1)}, f32[2,16,128]{2,1,0:T(8,128)S(1)}, u32[]{:S(2)}, u32[]{:S(2)}) %collective-permute-start.2) | collective-permute-done | bytes 16416 | tf_op jit(solution)/shard_map/ppermute | solution.py:305
  10.8 0.1 collective-permute-start.3
  10.9 1.2 %collective-permute-done.3.came = f32[1,16,128]{2,1,0:T(8,128)S(1)} collective-permute-done((f32[1,16,128]{2,1,0:T(8,128)S(1)}, f32[1,16,128]{2,1,0:T(8,128)S(1)}, u32[]{:S(2)}, u32[]{:S(2)}) %collective-permute-start.3) | collective-permute-done | bytes 8224 | tf_op jit(solution)/shard_map/ppermute | solution.py:297
  12.0 0.1 %outer.1 = (f32[1,4,16,256]{3,2,1,0:T(8,128)S(1)}, f32[16,128]{1,0:T(8,128)S(1)}) custom-call(f32[1,4,16,256]{3,2,1,0:T(8,128)S(1)} %copy-done, f32[1,4,16,256]{3,2,1,0:T(8,128)S(1)} %get-tuple-element.14.base, f32[1,16,128]{2,1,0:T(8,128)S(1)} %get-tuple-element.20.kept, f32[1,16,128]{2,1,0:T(8,128)S(1)} %collective-permute-done.3.came, ...), custom_call_target="tpu_custom_call" | custom-call | tf_op jit(solution)/shard_map/outer/pallas_call | solution.py:308
  12.2 0.8 %collective-permute-done.5.refs_0_ = f32[1,4,16,256]{3,2,1,0:T(8,128)S(1)} collective-permute-done((f32[1,4,16,256]{3,2,1,0:T(8,128)S(1)}, f32[1,4,16,256]{3,2,1,0:T(8,128)S(1)}, u32[]{:S(2)}, u32[]{:S(2)}) %collective-permute-start.5) | collective-permute-done | bytes 65568 | tf_op jit(solution)/shard_map/ppermute | solution.py:325
  13.0 0.6 %update.1 = (f32[1,4,16,256]{3,2,1,0:T(8,128)}, f32[3,1,512]{2,1,0:T(1,128)}) custom-call(f32[1,4,16,256]{3,2,1,0:T(8,128)S(1)} %get-tuple-element.22.residual, f32[16,256]{1,0:T(8,128)S(1)} %get-tuple-element.19._.step, f32[16,128]{1,0:T(8,128)S(1)} %get-tuple-element.23.total, f32[1,4,16,256]{3,2,1,0:T(8,128)S(1)} %collective-permute-done.5.refs_0_), custom_call_target="tpu_custom_call" | custom-call | tf_op jit(solution)/shard_map/update/pallas_call | solution.py:308
  (4 shorter events, 0.0 us)
Async XLA Ops:
  0.6 4.1 %copy-start = (f32[1,4,16,256]{3,2,1,0:T(8,128)S(1)}, f32[1,4,16,256]{3,2,1,0:T(8,128)}, u32[]{:S(2)}) copy-start(f32[1,4,16,256]{3,2,1,0:T(8,128)} %state.7) | copy-start | bytes 196612
  0.6 4.1 %copy-start.2 = (s32[768]{0:T(1024)S(1)}, s32[768]{0:T(1024)}, u32[]{:S(2)}) copy-start(s32[768]{0:T(1024)} %param.5) | copy-start | bytes 9220
  0.7 4.1 %copy-start.3 = (s32[768]{0:T(1024)S(1)}, s32[768]{0:T(1024)}, u32[]{:S(2)}) copy-start(s32[768]{0:T(1024)} %param.6) | copy-start | bytes 9220
  0.7 4.1 %copy-start.1 = (f32[3,768]{1,0:T(4,128)S(1)}, f32[3,768]{1,0:T(4,128)}, u32[]{:S(2)}) copy-start(f32[3,768]{1,0:T(4,128)} %area.1) | copy-start | bytes 27652
  0.7 8.0 %collective-permute-start.4 = (f32[1,4,16,256]{3,2,1,0:T(8,128)}, f32[1,4,16,256]{3,2,1,0:T(8,128)S(1)}, u32[]{:S(2)}, u32[]{:S(2)}) collective-permute-start(f32[1,4,16,256]{3,2,1,0:T(8,128)} %state.7), channel_id=1, source_target_pairs={{0,2},{1,3},{2,0},{3,1},{4,6},{5,7},{6,4},{7,5},{8,10},{9,11},{10,... | collective-permute-start | bytes 196616 | tf_op jit(solution)/shard_map/ppermute | solution.py:325
  5.2 1.8 %collective-permute-start.1 = (f32[2,16,128]{2,1,0:T(8,128)S(1)}, f32[2,16,128]{2,1,0:T(8,128)S(1)}, u32[]{:S(2)}, u32[]{:S(2)}) collective-permute-start(f32[2,16,128]{2,1,0:T(8,128)S(1)} %get-tuple-element.18), channel_id=1, source_target_pairs={{0,4},{4,0},{8,12},{12,8},{16,20},{20,16},{24,28},{28,24},{1,5},{5... | collective-permute-start | bytes 49160 | tf_op jit(solution)/shard_map/ppermute | solution.py:297
  5.2 4.7 %collective-permute-start = (f32[2,16,128]{2,1,0:T(8,128)S(1)}, f32[2,16,128]{2,1,0:T(8,128)S(1)}, u32[]{:S(2)}, u32[]{:S(2)}) collective-permute-start(f32[2,16,128]{2,1,0:T(8,128)S(1)} %get-tuple-element.16), channel_id=1, source_target_pairs={{0,24},{4,28},{8,16},{12,20},{16,8},{20,12},{24,0},{28,4},{1,25},{... | collective-permute-start | bytes 49160 | tf_op jit(solution)/shard_map/ppermute | solution.py:297
  7.0 3.8 %collective-permute-start.2 = (f32[2,16,128]{2,1,0:T(8,128)S(1)}, f32[2,16,128]{2,1,0:T(8,128)S(1)}, u32[]{:S(2)}, u32[]{:S(2)}) collective-permute-start(f32[2,16,128]{2,1,0:T(8,128)S(1)} %chip_sums.1), channel_id=1, source_target_pairs={{0,8},{4,20},{8,0},{12,28},{16,24},{20,4},{24,16},{28,12},{1,9},{5... | collective-permute-start | bytes 49160 | tf_op jit(solution)/shard_map/ppermute | solution.py:305
  8.7 4.3 %collective-permute-start.5 = (f32[1,4,16,256]{3,2,1,0:T(8,128)S(1)}, f32[1,4,16,256]{3,2,1,0:T(8,128)S(1)}, u32[]{:S(2)}, u32[]{:S(2)}) collective-permute-start(f32[1,4,16,256]{3,2,1,0:T(8,128)S(1)} %pair_sums.1), channel_id=1, source_target_pairs={{0,1},{1,0},{2,3},{3,2},{4,5},{5,4},{6,7},{7,6},{8,9},{9,8},{10,11... | collective-permute-start | bytes 196616 | tf_op jit(solution)/shard_map/ppermute | solution.py:325
  10.8 1.2 %collective-permute-start.3 = (f32[1,16,128]{2,1,0:T(8,128)S(1)}, f32[1,16,128]{2,1,0:T(8,128)S(1)}, u32[]{:S(2)}, u32[]{:S(2)}) collective-permute-start(f32[1,16,128]{2,1,0:T(8,128)S(1)} %get-tuple-element.21), channel_id=1, source_target_pairs={{0,4},{4,0},{8,12},{12,8},{16,20},{20,16},{24,28},{28,24},{1,5},{5... | collective-permute-start | bytes 24584 | tf_op jit(solution)/shard_map/ppermute | solution.py:297

commit v26 on v25

--- a/solution.py
+++ b/solution.py
@@ -162,8 +162,8 @@
 
 
 def of_chip(orders):
-    half = lax.axis_index("space") // 4
-    return [jnp.where(half % 2 == 0, a, b) for a, b in zip(*orders)]
+    chip = lax.axis_index("space") // 2
+    return [jnp.where(chip == 0, a, b) for a, b in zip(*orders)]
 
 
 def pair_kernel(weights, instances, orders, state, partner, *outs):
@@ -318,7 +318,7 @@
     weights = spectral_row(instances)
     def partnered(value, place):
         pairs = [
-            (i * instances + n, i * instances + (n ^ orders[i // 4 % 2][place]))
+            (i * instances + n, i * instances + (n ^ orders[min(i // 2, 1)][place]))
             for i in range(blocks)
             for n in range(instances)
         ]

time: 13.8 us -> 13.8 us (level)
  waiting for transfers between devices: 3.86 us -> 4.42 us
  starting transfers between devices: 7.64 us -> 7.08 us
    ppermute x1, starting transfers between devices: 0.95 us -> 0.6 us  [served(): return lax.ppermute(value, 'space', pairs)]
    ppermute x2, waiting for transfers between devices: 1.53 us -> 1.89 us  [partnered(): return lax.ppermute(value, ('space', 'inst'), pairs)]
    ppermute x3, waiting for transfers between devices: 1.52 us -> 1.73 us  [swapped(): lax.ppermute(value, axis, [(i, i ^ bit) for i in range(lax.axis_size(axis...]
    ppermute x2, starting transfers between devices: 5.04 us -> 4.84 us  [partnered(): return lax.ppermute(value, ('space', 'inst'), pairs)]
where the time goes in v26:
time: 13.8 us; the launch traced here: 13.6 us
  starting transfers between devices  7.08 us (51%)
  waiting for transfers between devices  4.42 us (32%)
  Pallas kernels  1.37 us (10%)
  between operations  0.74 us (5%)
    ppermute x2, starting transfers between devices, partnered(): return lax.ppermute(value, ('space', 'inst'), pairs)  4.84 us
    ppermute x2, waiting for transfers between devices, partnered(): return lax.ppermute(value, ('space', 'inst'), pairs)  1.89 us
    ppermute x3, waiting for transfers between devices, swapped(): lax.ppermute(value, axis, [(i, i ^ bit) for i in range(lax.axis_size(axis...  1.73 us
    ppermute x3, starting transfers between devices, swapped(): lax.ppermute(value, axis, [(i, i ^ bit) for i in range(lax.axis_size(axis...  1.64 us
    pallas_call x8, Pallas kernels, call(): pl.pallas_call(kernel, out_shape=[jax.ShapeDtypeStruct(shape, dtype) for...  1.37 us
    ppermute x1, waiting for transfers between devices, served(): return lax.ppermute(value, 'space', pairs)  0.8 us
    ppermute x1, starting transfers between devices, served(): return lax.ppermute(value, 'space', pairs)  0.6 us
  transfers between devices with their start and end apart: 6, of which 5 were waited for; matrix products, arithmetic and copies ran while one was open for 0% of the time, Pallas kernels for 5%

profile of v26, /device:TPU:0, one launch (start us, length us, event | category | flops | bytes accessed | tf_op | source)
XLA Modules:
  0.0 13.6 jit_solution(2965951235991868165)
XLA Ops:
  0.6 0.0 copy-start
  0.6 0.0 copy-start.2
  0.7 0.0 copy-start.3
  0.7 0.0 copy-start.1
  0.7 4.1 %collective-permute-start.4 = (f32[1,4,16,256]{3,2,1,0:T(8,128)}, f32[1,4,16,256]{3,2,1,0:T(8,128)S(1)}, u32[]{:S(2)}, u32[]{:S(2)}) collective-permute-start(f32[1,4,16,256]{3,2,1,0:T(8,128)} %state.7), channel_id=1, source_target_pairs={{0,2},{1,3},{2,0},{3,1},{4,6},{5,7},{6,4},{7,5},{8,9},{9,8},{10,11... | collective-permute-start | bytes 196616 | tf_op jit(solution)/shard_map/ppermute | solution.py:325
  4.8 0.0 copy-done
  4.8 0.0 copy-done.2
  4.8 0.0 copy-done.3
  4.8 0.0 copy-done.1
  4.8 0.4 %face_forces.1 = (f32[2,16,128]{2,1,0:T(8,128)S(1)}, f32[2,16,128]{2,1,0:T(8,128)S(1)}, f32[2,16,128]{2,1,0:T(8,128)S(1)}, f32[2,16,128]{2,1,0:T(8,128)S(1)}) custom-call(s32[8,128]{1,0:T(8,128)S(1)} %own.1, f32[1,4,16,256]{3,2,1,0:T(8,128)S(1)} %copy-done, s32[6,128]{1,0:T(8,128)S(1)} %bitcast.3, s32[6,128]{1,0:T(8,128)S(1)} %bitcast.4, f32[3,768]{1,0:T(4,128)S(1)} %copy-done.1), custom_call_target="tpu_custom_call" | custom-call | flops 10000000000 | tf_op jit(solution)/shard_map/face_forces/pallas_call | solution.py:308
  5.2 0.1 collective-permute-start.1
  5.2 1.5 %collective-permute-start = (f32[2,16,128]{2,1,0:T(8,128)S(1)}, f32[2,16,128]{2,1,0:T(8,128)S(1)}, u32[]{:S(2)}, u32[]{:S(2)}) collective-permute-start(f32[2,16,128]{2,1,0:T(8,128)S(1)} %get-tuple-element.16), channel_id=1, source_target_pairs={{0,24},{4,28},{8,16},{12,20},{16,8},{20,12},{24,0},{28,4},{1,25},{... | collective-permute-start | bytes 49160 | tf_op jit(solution)/shard_map/ppermute | solution.py:297
  6.7 0.2 %flux.1 = (f32[1,4,16,256]{3,2,1,0:T(8,128)S(1)}, f32[16,256]{1,0:T(8,128)S(1)}) custom-call(f32[1,4,16,256]{3,2,1,0:T(8,128)S(1)} %copy-done), custom_call_target="tpu_custom_call" | custom-call | flops 10000000000 | tf_op jit(solution)/shard_map/flux/pallas_call | solution.py:308
  6.9 0.0 collective-permute-done.1.came
  7.0 0.6 %collective-permute-start.2 = (f32[2,16,128]{2,1,0:T(8,128)S(1)}, f32[2,16,128]{2,1,0:T(8,128)S(1)}, u32[]{:S(2)}, u32[]{:S(2)}) collective-permute-start(f32[2,16,128]{2,1,0:T(8,128)S(1)} %chip_sums.1), channel_id=1, source_target_pairs={{0,8},{4,20},{8,0},{12,28},{16,24},{20,4},{24,16},{28,12},{1,9},{5... | collective-permute-start | bytes 49160 | tf_op jit(solution)/shard_map/ppermute | solution.py:305
  7.6 1.1 %collective-permute-done.4.partner = f32[1,4,16,256]{3,2,1,0:T(8,128)S(1)} collective-permute-done((f32[1,4,16,256]{3,2,1,0:T(8,128)}, f32[1,4,16,256]{3,2,1,0:T(8,128)S(1)}, u32[]{:S(2)}, u32[]{:S(2)}) %collective-permute-start.4) | collective-permute-done | bytes 65568 | tf_op jit(solution)/shard_map/ppermute | solution.py:325
  8.7 0.7 %collective-permute-start.5 = (f32[1,4,16,256]{3,2,1,0:T(8,128)S(1)}, f32[1,4,16,256]{3,2,1,0:T(8,128)S(1)}, u32[]{:S(2)}, u32[]{:S(2)}) collective-permute-start(f32[1,4,16,256]{3,2,1,0:T(8,128)S(1)} %pair_sums.1), channel_id=1, source_target_pairs={{0,1},{1,0},{2,3},{3,2},{4,5},{5,4},{6,7},{7,6},{8,10},{9,11},{10,... | collective-permute-start | bytes 196616 | tf_op jit(solution)/shard_map/ppermute | solution.py:325
  9.4 0.6 %collective-permute-done.diagonal = f32[2,16,128]{2,1,0:T(8,128)S(1)} collective-permute-done((f32[2,16,128]{2,1,0:T(8,128)S(1)}, f32[2,16,128]{2,1,0:T(8,128)S(1)}, u32[]{:S(2)}, u32[]{:S(2)}) %collective-permute-start) | collective-permute-done | bytes 16416 | tf_op jit(solution)/shard_map/ppermute | solution.py:297
  10.0 0.8 %collective-permute-done.2.served = f32[2,16,128]{2,1,0:T(8,128)S(1)} collective-permute-done((f32[2,16,128]{2,1,0:T(8,128)S(1)}, f32[2,16,128]{2,1,0:T(8,128)S(1)}, u32[]{:S(2)}, u32[]{:S(2)}) %collective-permute-start.2) | collective-permute-done | bytes 16416 | tf_op jit(solution)/shard_map/ppermute | solution.py:305
  10.8 0.1 collective-permute-start.3
  10.9 1.2 %collective-permute-done.3.came = f32[1,16,128]{2,1,0:T(8,128)S(1)} collective-permute-done((f32[1,16,128]{2,1,0:T(8,128)S(1)}, f32[1,16,128]{2,1,0:T(8,128)S(1)}, u32[]{:S(2)}, u32[]{:S(2)}) %collective-permute-start.3) | collective-permute-done | bytes 8224 | tf_op jit(solution)/shard_map/ppermute | solution.py:297
  12.0 0.1 %outer.1 = (f32[1,4,16,256]{3,2,1,0:T(8,128)S(1)}, f32[16,128]{1,0:T(8,128)S(1)}) custom-call(f32[1,4,16,256]{3,2,1,0:T(8,128)S(1)} %copy-done, f32[1,4,16,256]{3,2,1,0:T(8,128)S(1)} %get-tuple-element.14.base, f32[1,16,128]{2,1,0:T(8,128)S(1)} %get-tuple-element.20.kept, f32[1,16,128]{2,1,0:T(8,128)S(1)} %collective-permute-done.3.came, ...), custom_call_target="tpu_custom_call" | custom-call | tf_op jit(solution)/shard_map/outer/pallas_call | solution.py:308
  12.2 0.8 %collective-permute-done.5.refs_0_ = f32[1,4,16,256]{3,2,1,0:T(8,128)S(1)} collective-permute-done((f32[1,4,16,256]{3,2,1,0:T(8,128)S(1)}, f32[1,4,16,256]{3,2,1,0:T(8,128)S(1)}, u32[]{:S(2)}, u32[]{:S(2)}) %collective-permute-start.5) | collective-permute-done | bytes 65568 | tf_op jit(solution)/shard_map/ppermute | solution.py:325
  13.0 0.6 %update.1 = (f32[1,4,16,256]{3,2,1,0:T(8,128)}, f32[3,1,512]{2,1,0:T(1,128)}) custom-call(f32[1,4,16,256]{3,2,1,0:T(8,128)S(1)} %get-tuple-element.22.residual, f32[16,256]{1,0:T(8,128)S(1)} %get-tuple-element.19._.step, f32[16,128]{1,0:T(8,128)S(1)} %get-tuple-element.23.total, f32[1,4,16,256]{3,2,1,0:T(8,128)S(1)} %collective-permute-done.5.refs_0_), custom_call_target="tpu_custom_call" | custom-call | tf_op jit(solution)/shard_map/update/pallas_call | solution.py:308
  (4 shorter events, 0.0 us)
Async XLA Ops:
  0.6 4.1 %copy-start = (f32[1,4,16,256]{3,2,1,0:T(8,128)S(1)}, f32[1,4,16,256]{3,2,1,0:T(8,128)}, u32[]{:S(2)}) copy-start(f32[1,4,16,256]{3,2,1,0:T(8,128)} %state.7) | copy-start | bytes 196612
  0.6 4.1 %copy-start.2 = (s32[768]{0:T(1024)S(1)}, s32[768]{0:T(1024)}, u32[]{:S(2)}) copy-start(s32[768]{0:T(1024)} %param.5) | copy-start | bytes 9220
  0.7 4.1 %copy-start.3 = (s32[768]{0:T(1024)S(1)}, s32[768]{0:T(1024)}, u32[]{:S(2)}) copy-start(s32[768]{0:T(1024)} %param.6) | copy-start | bytes 9220
  0.7 4.1 %copy-start.1 = (f32[3,768]{1,0:T(4,128)S(1)}, f32[3,768]{1,0:T(4,128)}, u32[]{:S(2)}) copy-start(f32[3,768]{1,0:T(4,128)} %area.1) | copy-start | bytes 27652
  0.7 8.0 %collective-permute-start.4 = (f32[1,4,16,256]{3,2,1,0:T(8,128)}, f32[1,4,16,256]{3,2,1,0:T(8,128)S(1)}, u32[]{:S(2)}, u32[]{:S(2)}) collective-permute-start(f32[1,4,16,256]{3,2,1,0:T(8,128)} %state.7), channel_id=1, source_target_pairs={{0,2},{1,3},{2,0},{3,1},{4,6},{5,7},{6,4},{7,5},{8,9},{9,8},{10,11... | collective-permute-start | bytes 196616 | tf_op jit(solution)/shard_map/ppermute | solution.py:325
  5.2 1.8 %collective-permute-start.1 = (f32[2,16,128]{2,1,0:T(8,128)S(1)}, f32[2,16,128]{2,1,0:T(8,128)S(1)}, u32[]{:S(2)}, u32[]{:S(2)}) collective-permute-start(f32[2,16,128]{2,1,0:T(8,128)S(1)} %get-tuple-element.18), channel_id=1, source_target_pairs={{0,4},{4,0},{8,12},{12,8},{16,20},{20,16},{24,28},{28,24},{1,5},{5... | collective-permute-start | bytes 49160 | tf_op jit(solution)/shard_map/ppermute | solution.py:297
  5.2 4.7 %collective-permute-start = (f32[2,16,128]{2,1,0:T(8,128)S(1)}, f32[2,16,128]{2,1,0:T(8,128)S(1)}, u32[]{:S(2)}, u32[]{:S(2)}) collective-permute-start(f32[2,16,128]{2,1,0:T(8,128)S(1)} %get-tuple-element.16), channel_id=1, source_target_pairs={{0,24},{4,28},{8,16},{12,20},{16,8},{20,12},{24,0},{28,4},{1,25},{... | collective-permute-start | bytes 49160 | tf_op jit(solution)/shard_map/ppermute | solution.py:297
  7.0 3.8 %collective-permute-start.2 = (f32[2,16,128]{2,1,0:T(8,128)S(1)}, f32[2,16,128]{2,1,0:T(8,128)S(1)}, u32[]{:S(2)}, u32[]{:S(2)}) collective-permute-start(f32[2,16,128]{2,1,0:T(8,128)S(1)} %chip_sums.1), channel_id=1, source_target_pairs={{0,8},{4,20},{8,0},{12,28},{16,24},{20,4},{24,16},{28,12},{1,9},{5... | collective-permute-start | bytes 49160 | tf_op jit(solution)/shard_map/ppermute | solution.py:305
  8.7 4.3 %collective-permute-start.5 = (f32[1,4,16,256]{3,2,1,0:T(8,128)S(1)}, f32[1,4,16,256]{3,2,1,0:T(8,128)S(1)}, u32[]{:S(2)}, u32[]{:S(2)}) collective-permute-start(f32[1,4,16,256]{3,2,1,0:T(8,128)S(1)} %pair_sums.1), channel_id=1, source_target_pairs={{0,1},{1,0},{2,3},{3,2},{4,5},{5,4},{6,7},{7,6},{8,10},{9,11},{10,... | collective-permute-start | bytes 196616 | tf_op jit(solution)/shard_map/ppermute | solution.py:325
  10.8 1.2 %collective-permute-start.3 = (f32[1,16,128]{2,1,0:T(8,128)S(1)}, f32[1,16,128]{2,1,0:T(8,128)S(1)}, u32[]{:S(2)}, u32[]{:S(2)}) collective-permute-start(f32[1,16,128]{2,1,0:T(8,128)S(1)} %get-tuple-element.21), channel_id=1, source_target_pairs={{0,4},{4,0},{8,12},{12,8},{16,20},{20,16},{24,28},{28,24},{1,5},{5... | collective-permute-start | bytes 24584 | tf_op jit(solution)/shard_map/ppermute | solution.py:297
